TPU v7x, 512 devices: a whole 4x4x16 slice. The times are simulated.
512 devices in a mesh: batch: 4 (over y), tm: 16 (over x, z_lo), space: 8 (over z_hi, core).
Axes of the slice: x: 4, y: 4, z: 16 (z_hi: 4, z_lo: 4; z = z_hi * 4 + z_lo), core: 2. Of those that a mesh axis runs over, the one named last changes fastest.
Arguments:
- tokens: bfloat16 [64, 1024, 1152], P(('batch', 'tm'), 'space'), parts along dimension 0, may hold values from -6 to 6
- frame_qkv: bfloat16 [1152, 3456], P(None, 'space'), may hold values from -4 to 4
- frame_out: bfloat16 [1152, 1152], P('space'), may hold values from -0.375 to 0.375
- time_qkv: bfloat16 [3456, 1152], P('tm'), may hold values from -4 to 4
- time_out: bfloat16 [1152, 1152], replicated, may hold values from -0.375 to 0.375
- modulation: float32 [8, 3, 1152], P('batch'), parts along dimension 0, may hold values from -4 to 4
Outputs:
- blended: bfloat16 [64, 1024, 1152], P(('batch', 'tm'), 'space'), parts along dimension 0
There are 4 independent parts, one for each index of `batch`. A program takes and returns all parts, laid end to end along the dimension named above; an argument that names none is the same for every part. Nothing has to cross between parts.
All inputs are finite; a program needn't handle non-finite values.
Results may differ from a plain program's by a relative error of at most 0.035.
Values may be sent and summed in bfloat16 or wider, within the bound.
No kernel may reach another device: no remote copies, remote signals or barrier semaphores. Data moves between devices by JAX's collectives and lax.ppermute only.
A program may use at most 64 MiB of HBM per device.

v0:
```python
import jax
import jax.numpy as jnp
from jax import lax
from jax.sharding import PartitionSpec as P

HD = 72


eps_norm = 1e-06


def modulate(tokens, offset, stretch):
    values = tokens.astype(jnp.float32)
    center = jnp.mean(values, axis=-1, keepdims=True)
    spread = jnp.mean(jnp.square(values - center), axis=-1, keepdims=True)
    normed = (values - center) * lax.rsqrt(spread + eps_norm)
    return (normed * (1.0 + stretch) + offset).astype(jnp.bfloat16)


def normalized_weights(scores):
    largest = jnp.max(scores, axis=-1, keepdims=True)
    raised = jnp.exp(scores - largest)
    return (raised / jnp.sum(raised, axis=-1, keepdims=True)).astype(jnp.bfloat16)


def frame_block(queries, key_part, value_part, factor):
    scores = (
        jnp.einsum("fqhe,fkhe->fhqk", queries, key_part, preferred_element_type=jnp.float32)
        * factor
    )
    weights = normalized_weights(scores)
    return jnp.einsum(
        "fhqk,fkhe->fqhe", weights, value_part, preferred_element_type=jnp.float32
    ).astype(jnp.bfloat16)


def frame_attention(triples, head_width):
    frames, spatial, head_count = (triples.shape[0], triples.shape[1], triples.shape[2])
    queries = triples[:, :, :, 0]
    key_part = triples[:, :, :, 1]
    value_part = triples[:, :, :, 2]
    block_rows = min(spatial, 512)
    block_count = spatial // block_rows
    grouped = jnp.moveaxis(
        queries.reshape(frames, block_count, block_rows, head_count, head_width), 1, 0
    )
    results = lax.map(
        lambda query_block: frame_block(query_block, key_part, value_part, head_width ** (-0.5)),
        grouped,
    )
    return jnp.moveaxis(results, 0, 1).reshape(frames, spatial, head_count * head_width)


def time_attention(triples, head_width):
    queries = triples[..., :head_width]
    key_part = triples[..., head_width : 2 * head_width]
    value_part = triples[..., 2 * head_width :]
    scores = jnp.einsum(
        "tshe,ushe->shtu", queries, key_part, preferred_element_type=jnp.float32
    ) * head_width ** (-0.5)
    weights = normalized_weights(scores)
    return jnp.einsum(
        "shtu,ushe->tshe", weights, value_part, preferred_element_type=jnp.float32
    ).astype(jnp.bfloat16)


def shards(tokens, frame_qkv, frame_out, time_qkv, time_out, modulation):
    frames, row_count, model_width = tokens.shape
    first_input = modulate(tokens, modulation[0, 0], modulation[0, 1])
    triples = jnp.einsum(
        "fsd,dc->fsc",
        lax.all_gather(first_input, "space", axis=1, tiled=True),
        frame_qkv,
        preferred_element_type=jnp.float32,
    ).astype(jnp.bfloat16)
    local_heads = frame_qkv.shape[1] // (3 * HD)
    triples = triples.reshape(frames, triples.shape[1], local_heads, 3, HD)
    attended = frame_attention(triples, HD)
    frame_source = attended.reshape(-1, attended.shape[2])
    frame_branch = lax.psum_scatter(
        jnp.dot(frame_source, frame_out, preferred_element_type=jnp.float32).astype(jnp.bfloat16),
        "space",
        scatter_dimension=0,
        tiled=True,
    ).astype(jnp.float32)
    frame_branch = frame_branch.reshape(frames, row_count, model_width)
    middle = (tokens.astype(jnp.float32) + modulation[0, 2] * frame_branch).astype(jnp.bfloat16)
    second_input = modulate(middle, modulation[1, 0], modulation[1, 1])
    second_flat = second_input.reshape(frames * row_count, model_width)
    projected = lax.dot_general(
        second_flat,
        lax.all_gather(time_qkv, "tm", axis=0, tiled=True),
        (((1,), (1,)), ((), ())),
        preferred_element_type=jnp.float32,
    ).astype(jnp.bfloat16)
    head_total = projected.shape[1] // (3 * HD)
    projected = projected.reshape(frames, row_count, head_total, 3 * HD)
    attended = time_attention(
        lax.all_to_all(projected, "tm", split_axis=2, concat_axis=0, tiled=True), HD
    )
    total_frames = attended.shape[0]
    attended = attended.reshape(total_frames, row_count, -1)
    returned = lax.all_to_all(attended, "tm", split_axis=0, concat_axis=2, tiled=True)
    time_branch = jnp.dot(
        returned.reshape(frames * row_count, model_width),
        time_out,
        preferred_element_type=jnp.float32,
    )
    time_branch = time_branch.reshape(frames, row_count, model_width)
    return (middle.astype(jnp.float32) + modulation[1, 2] * time_branch).astype(jnp.bfloat16)


def solution(mesh):
    placed = (
        P(("batch", "tm"), "space", None),
        P(None, "space"),
        P("space", None),
        P("tm", None),
        P(),
        P("batch", None, None),
    )
    return jax.shard_map(
        shards,
        mesh=mesh,
        in_specs=placed,
        out_specs=P(("batch", "tm"), "space", None),
        check_vma=False,
    )
```

profile of v0, /device:TPU:1, one launch (start us, length us, event | category | flops | bytes accessed | tf_op | source)
XLA Modules:
  0.0 391.0 jit_solution(1781436888458273317)
XLA Ops:
  7.4 0.0 copy-start
  7.4 0.0 all-gather.3.cloned.1.call-start
  7.4 1.0 slice_reduce_fusion.1
  8.4 1.1 convert_reduce_fusion.1
  9.5 1.2 fusion.52
  10.7 1.9 fusion.55
  12.6 0.0 all-gather.3.cloned.1.call-update
  12.6 0.0 reduce-scatter.2.cloned.1.call-start
  12.7 71.5 %all-gather.3.cloned.1.call-done = bf16[1,1024,1152]{2,1,0:T(8,128)(2,1)} async-done(((bf16[1,128,1152]{2,1,0:T(8,128)(2,1)}), bf16[1,1024,1152]{2,1,0:T(8,128)(2,1)}) %all-gather.3.cloned.1.call-update) | async-done | bytes 2359312 | tf_op jit(solution)/shard_map/all_gather | solution.py:72
  84.2 3.2 fusion.39
  87.4 0.9 slice_bitcast_fusion.6
  88.3 0.2 transpose_reshape_squeeze.3
  88.5 0.8 copy.22
  89.3 0.0 copy-start.2
  89.3 16.3 %while.10 = (s32[]{:T(128)}, bf16[2,1,512,2,72]{2,4,3,1,0:T(8,128)(2,1)}, bf16[2,1,512,2,72]{2,4,3,1,0:T(8,128)(2,1)}, bf16[1,1024,2,72]{1,3,2,0:T(8,128)(2,1)}, bf16[1,1024,2,72]{1,3,2,0:T(8,128)(2,1)}, /*index=5*/s32[]{:T(128)}) while((s32[]{:T(128)}, bf16[2,1,512,2,72]{2,4,3,1,0:T(8,128)(2,1)}, bf16[2,1,512,2,72]{2,4,3,1,0:T(8,128)(2,1)}, ...), condition=%wide.region_5.6_spmd, body=%wide.region_2.5_spmd.sunk | while | flops 307307520 | bytes 10462305 | solution.py:47
  89.3 0.0 copy-start.3
  89.3 4.5 %fusion.91 = (f32[2,512]{1,0:T(2,128)S(1)}, f32[2,512,1024]{2,1,0:T(8,128)}) fusion(bf16[1,1024,2,72]{1,3,2,0:T(8,128)(2,1)} %get-tuple-element.118, bf16[2,1,512,2,72]{2,4,3,1,0:T(8,128)(2,1)} %get-tuple-element.117, s32[]{:T(128)} %get-tuple-element.109), kind=kOutput, calls=%fused_computation.80.clone.1 | convolution fusion | flops 154141696 | bytes 4641280 | tf_op jit(solution)/shard_map/while/body/eval_jaxpr/sub | solution.py:22
  93.7 0.0 copy-done.3
  93.7 3.7 fusion.92
  97.4 0.0 copy-start.3
  97.4 4.4 %fusion.91 = (f32[2,512]{1,0:T(2,128)S(1)}, f32[2,512,1024]{2,1,0:T(8,128)}) fusion(bf16[1,1024,2,72]{1,3,2,0:T(8,128)(2,1)} %get-tuple-element.118, bf16[2,1,512,2,72]{2,4,3,1,0:T(8,128)(2,1)} %get-tuple-element.117, s32[]{:T(128)} %get-tuple-element.109), kind=kOutput, calls=%fused_computation.80.clone.1 | convolution fusion | flops 154141696 | bytes 4641280 | tf_op jit(solution)/shard_map/while/body/eval_jaxpr/sub | solution.py:22
  101.9 0.0 copy-done.3
  101.9 3.7 fusion.92
  105.5 0.0 copy-start.1
  105.6 1.3 copy.23
  106.9 0.0 copy-done.2
  106.9 2.4 convolution_convert_fusion.1
  109.3 0.0 reduce-scatter.2.cloned.1.call-update
  109.3 0.0 all-gather.5.cloned.1.call-start
  109.4 0.5 all-gather.5.cloned.1.call-update
  109.9 130.8 %reduce-scatter.2.cloned.1.call-done = bf16[128,1152]{1,0:T(8,128)(2,1)} async-done(((bf16[1024,1152]{1,0:T(8,128)(2,1)}), bf16[128,1152]{1,0:T(8,128)(2,1)}) %reduce-scatter.2.cloned.1.call-update) | async-done | bytes 294928 | tf_op jit(solution)/shard_map/reduce_scatter | solution.py:80
  240.7 0.0 copy-done.1
  240.7 1.2 convert_reduce_fusion
  241.8 0.2 fusion.48
  242.1 80.0 %all-gather.5.cloned.1.call-done = bf16[3456,1152]{1,0:T(8,128)(2,1)} async-done(((bf16[216,1152]{1,0:T(8,128)(2,1)}), bf16[3456,1152]{1,0:T(8,128)(2,1)}) %all-gather.5.cloned.1.call-update) | async-done | bytes 7962640 | tf_op jit(solution)/shard_map/all_gather | solution.py:92
  322.1 6.8 %convolution_convert_fusion = bf16[128,3456]{1,0:T(8,128)(2,1)} fusion(bf16[3456,1152]{1,0:T(8,128)(2,1)} %all-gather.5.cloned.1.call-done, bf16[1,128,1152]{2,1,0:T(8,128)(2,1)S(1)} %get-tuple-element.60, f32[1152]{0:T(1024)S(1)} %get-tuple-element.47, f32[1152]{0:T(1024)S(1)} %get-tuple-element.48, f32[128]{0:T(128)S(1)} %add_rsqrt_fusion, ...), kind=kOutput, calls=%fused_computation.23 | convolution fusion | flops 1020542976 | bytes 9152512 | tf_op jit(solution)/shard_map/dot_general | solution.py:90
  328.9 2.2 copy.24
  331.1 29.2 %all_to_all.33 = bf16[1,128,16,216]{1,3,0,2:T(8,128)(2,1)} all-to-all(bf16[1,128,16,216]{1,3,0,2:T(8,128)(2,1)} %bitcast.128), channel_id=1, replica_groups=mesh['batch'=4,'tm'=16,'space'=8] {'tm'}, dimensions={2} | all-to-all | bytes 1769472 | tf_op jit(solution)/shard_map/all_to_all | solution.py:99
  360.3 2.7 copy.26
  363.0 3.2 fusion.76
  366.1 2.7 fusion.43
  368.8 1.5 copy.28
  370.3 12.0 %all_to_all.34 = bf16[16,128,72]{1,2,0:T(8,128)(2,1)S(1)} all-to-all(bf16[16,128,72]{1,2,0:T(8,128)(2,1)S(1)} %copy.28), channel_id=1, replica_groups=mesh['batch'=4,'tm'=16,'space'=8] {'tm'}, dimensions={0} | all-to-all | bytes 589824 | tf_op jit(solution)/shard_map/all_to_all | solution.py:103
  382.2 0.0 copy-done
  382.2 1.3 fusion.35
  (6 shorter events, 0.1 us)
Async XLA Ops:
  7.4 374.9 %copy-start = (bf16[1152,1152]{1,0:T(8,128)(2,1)S(1)}, bf16[1152,1152]{1,0:T(8,128)(2,1)}, u32[]{:S(2)}) copy-start(bf16[1152,1152]{1,0:T(8,128)(2,1)} %param.12) | copy-start | bytes 7962628
  7.4 76.8 %all-gather.3.cloned.1.call-start = ((), (), s32[]{:S(2)}) async-start(), calls=%async_computation.3 | async-start | bytes 2654208 | tf_op jit(solution)/shard_map/all_gather | solution.py:72
  12.6 228.0 %reduce-scatter.2.cloned.1.call-start = ((), (), s32[]{:S(2)}) async-start(), calls=%async_computation.4 | async-start | bytes 2654208 | tf_op jit(solution)/shard_map/reduce_scatter | solution.py:80
  89.3 17.6 %copy-start.2 = (bf16[144,1152]{1,0:T(8,128)(2,1)S(1)}, bf16[144,1152]{1,0:T(8,128)(2,1)}, u32[]{:S(2)}) copy-start(bf16[144,1152]{1,0:T(8,128)(2,1)} %param.10) | copy-start | bytes 995332
  89.3 4.5 %copy-start.3 = (bf16[1,1024,2,72]{1,3,2,0:T(8,128)(2,1)S(1)}, bf16[1,1024,2,72]{1,3,2,0:T(8,128)(2,1)}, u32[]{:S(2)}) copy-start(bf16[1,1024,2,72]{1,3,2,0:T(8,128)(2,1)} %get-tuple-element.119) | copy-start | bytes 884740 | tf_op jit(solution)/shard_map/while
  97.4 4.4 %copy-start.3 = (bf16[1,1024,2,72]{1,3,2,0:T(8,128)(2,1)S(1)}, bf16[1,1024,2,72]{1,3,2,0:T(8,128)(2,1)}, u32[]{:S(2)}) copy-start(bf16[1,1024,2,72]{1,3,2,0:T(8,128)(2,1)} %get-tuple-element.119) | copy-start | bytes 884740 | tf_op jit(solution)/shard_map/while
  105.5 135.1 %copy-start.1 = (bf16[1,128,1152]{2,1,0:T(8,128)(2,1)S(1)}, bf16[1,128,1152]{2,1,0:T(8,128)(2,1)}, u32[]{:S(2)}) copy-start(bf16[1,128,1152]{2,1,0:T(8,128)(2,1)} %param.8) | copy-start | bytes 884740
  109.3 212.8 %all-gather.5.cloned.1.call-start = ((), (), s32[]{:S(2)}) async-start(), calls=%async_computation.5 | async-start | bytes 8460288 | tf_op jit(solution)/shard_map/all_gather | solution.py:92
Sparse Core Ops, SparseCore 0:
  12.8 71.3 all-gather.2
  109.4 131.1 reduce-scatter.1
Sparse Core Ops, SparseCore 1:
  111.9 210.2 all-gather.4
where the time goes:
time: 396 us; the launch traced here: 391 us
  waiting for transfers between devices  283 us (71%)
  blocking collectives  41.2 us (10%)
  matrix products  35.8 us (9%)
  between operations  14.9 us (4%)
  local copies, waits for them, and re-layouts  9.56 us (2%)
  other arithmetic  6.63 us (2%)
    reduce_scatter x1, waiting for transfers between devices, shards(): lax.psum_scatter(jnp.dot(frame_source, frame_out, preferred_element_type=...  131 us
    all_gather x1, waiting for transfers between devices, shards(): lax.all_gather(time_qkv, 'tm', axis=0, tiled=True)  80 us
    all_gather x1, waiting for transfers between devices, shards(): lax.all_gather(first_input, 'space', axis=1, tiled=True)  71.5 us
    all_to_all x1, blocking collectives, shards(): lax.all_to_all(projected, 'tm', split_axis=2, concat_axis=0, tiled=True)  29.2 us
    sub x3, matrix products, normalized_weights(): raised = jnp.exp(scores - largest)  12 us
    all_to_all x1, blocking collectives, shards(): lax.all_to_all(attended, 'tm', split_axis=0, concat_axis=2, tiled=True)  12 us
  transfers between devices with their start and end apart: 3, of which 3 were waited for; matrix products, arithmetic and copies ran while one was open for 0% of the time, Pallas kernels for 0%

commit v1 on v0

v1 whole, which is shorter than its diff:
```python
import math

import jax
import jax.numpy as jnp
from jax import lax
from jax.experimental import pallas as pl
from jax.experimental.pallas import tpu as pltpu
from jax.sharding import Mesh
from jax.sharding import PartitionSpec as P

HD = 72
HP = 80
LANES = 128
EPS = 1e-06
EXP2_SCALE = HD ** (-0.5) * math.log2(math.e)
NT = (((1,), (1,)), ((), ()))
TN = (((0,), (0,)), ((), ()))
VMEM_BYTES = 56 * 1024 * 1024


def params(mib=48):
    return pltpu.CompilerParams(vmem_limit_bytes=mib * 1024 * 1024)


def whole():
    return pl.BlockSpec(memory_space=pltpu.VMEM)


def modulated(values, offset, stretch):
    center = jnp.mean(values, axis=-1, keepdims=True)
    values = values - center
    spread = jnp.mean(values * values, axis=-1, keepdims=True)
    return (values * lax.rsqrt(spread + EPS) * (1.0 + stretch) + offset).astype(jnp.bfloat16)


def first_norm_kernel(tokens_ref, modulation_ref, out_ref):
    out_ref[...] = modulated(
        tokens_ref[...].astype(jnp.float32), modulation_ref[0, 0:1], modulation_ref[0, 1:2]
    )


def frame_kernel(*refs):
    pieces, (wqk_ref, wvt_ref, out_ref, qk_ref, vt_ref) = refs[:-5], refs[-5:]
    row = 0
    for piece in pieces:
        count = piece.shape[0]
        step = min(count, 256)
        for start in range(0, count, step):
            part = piece[start : start + step]
            qk_ref[row : row + step] = jnp.dot(
                part, wqk_ref[...], preferred_element_type=jnp.float32
            ).astype(jnp.bfloat16)
            values = lax.dot_general(wvt_ref[...], part, NT, preferred_element_type=jnp.float32)
            index = lax.broadcasted_iota(jnp.int32, values.shape, 0)
            ones = (index == HD) | (index == HP + HD)
            vt_ref[:, row : row + step] = jnp.where(ones, 1.0, values).astype(jnp.bfloat16)
            row += step
    block = 256
    for start in range(0, row, block):
        outs = []
        for head in range(2):
            column = 2 * LANES * head
            queries = qk_ref[start : start + block, column : column + LANES]
            keys = qk_ref[:, column + LANES : column + 2 * LANES]
            scores = lax.dot_general(keys, queries, NT, preferred_element_type=jnp.float32)
            largest = jnp.max(scores, axis=0, keepdims=True)
            raised = jnp.exp2((scores - largest) * EXP2_SCALE).astype(jnp.bfloat16)
            mixed = jnp.dot(
                vt_ref[HP * head : HP * head + HP], raised, preferred_element_type=jnp.float32
            )
            outs.append(mixed[:HD] / mixed[HD : HD + 1])
        both = jnp.concatenate(outs, axis=0).astype(jnp.bfloat16)
        for part in range(block // LANES):
            out_ref[start // LANES + part] = both[:, part * LANES : (part + 1) * LANES]


def middle_kernel(mixed_ref, table_ref, tokens_ref, modulation_ref, out_ref):
    mixed = mixed_ref[...].reshape(-1, LANES)
    branch = lax.dot_general(mixed, table_ref[...], TN, preferred_element_type=jnp.float32)
    out_ref[...] = (
        tokens_ref[...].astype(jnp.float32) + modulation_ref[0, 2:3] * branch
    ).astype(jnp.bfloat16)


def time_kernel(positions, middle_ref, table_ref, out_table_ref, modulation_ref, out_ref, input_ref, mixed_ref):
    step = pl.program_id(0)

    @pl.when(step == 0)
    def _():
        input_ref[...] = modulated(
            middle_ref[...].astype(jnp.float32), modulation_ref[1, 0:1], modulation_ref[1, 1:2]
        )

    rows = input_ref.shape[0]
    one = lax.broadcasted_iota(jnp.int32, (rows, rows), 0) % positions
    two = lax.broadcasted_iota(jnp.int32, (rows, rows), 1) % positions
    same = one == two
    heads = table_ref.shape[0]
    outs = []
    for head in range(heads):
        table = table_ref[head].reshape(-1, table_ref.shape[-1])
        triple = lax.dot_general(
            table, input_ref[...], NT, preferred_element_type=jnp.float32
        ).astype(jnp.bfloat16)
        queries, keys, values = triple[:HP], triple[HP : 2 * HP], triple[2 * HP : 3 * HP]
        scores = lax.dot_general(keys, queries, TN, preferred_element_type=jnp.float32)
        scores = jnp.where(same, scores, -1e30)
        largest = jnp.max(scores, axis=0, keepdims=True)
        raised = jnp.exp2((scores - largest) * EXP2_SCALE)
        total = jnp.sum(raised, axis=0, keepdims=True)
        mixed = jnp.dot(values, raised.astype(jnp.bfloat16), preferred_element_type=jnp.float32)
        outs.append(mixed[:HD] / total)
    mixed_ref[step] = jnp.concatenate(outs, axis=0).astype(jnp.bfloat16)

    @pl.when(step == pl.num_programs(0) - 1)
    def _():
        mixed = mixed_ref[...].reshape(-1, rows)
        branch = lax.dot_general(mixed, out_table_ref[...], TN, preferred_element_type=jnp.float32)
        out_ref[...] = (
            middle_ref[...].astype(jnp.float32) + modulation_ref[1, 2:3] * branch
        ).astype(jnp.bfloat16)


def rotation(count, by):
    return [(index, (index + by) % count) for index in range(count)]


SWAP = [(0, 1), (1, 0)]


def shards(tokens, frame_qkv, frame_out, time_qkv, time_out, modulation):
    tokens = tokens[0]
    rows, width = tokens.shape
    zh = lax.axis_index("zh")

    part = jnp.pad(time_qkv.reshape(3, HD, width), ((0, 0), (0, HP - HD), (0, 0)))
    part = jnp.pad(part.reshape(3 * HP, width), ((0, 256 - 3 * HP), (0, 0)))
    index = lax.axis_index("y") * 2 + lax.axis_index("c")
    part = lax.dynamic_slice_in_dim(part, index * 32, 32, 0)
    time_table = lax.all_gather(part, ("x", "zl", "y", "c"), axis=0)
    time_table = time_table.reshape(16, 8, 32, width)

    index = jnp.minimum(lax.axis_index("x") * 4 + lax.axis_index("y"), 8)
    part = lax.dynamic_slice_in_dim(frame_out, index * 16, 16, 0)
    out_table = lax.all_gather(part, ("zh", "c", "x", "y"), axis=0)
    out_table = out_table.reshape(8, 16, 16, width)[:, :9].reshape(width, width)

    heads = frame_qkv.reshape(width, 2, 3, HD)
    wqk = jnp.pad(heads[:, :, :2], ((0, 0), (0, 0), (0, 0), (0, LANES - HD))).reshape(width, 4 * LANES)
    wvt = jnp.pad(jnp.transpose(heads[:, :, 2], (1, 2, 0)), ((0, 0), (0, HP - HD), (0, 0)))
    wvt = wvt.reshape(2 * HP, width)

    first_input = pl.pallas_call(
        first_norm_kernel,
        out_shape=jax.ShapeDtypeStruct((rows, width), jnp.bfloat16),
        in_specs=[whole(), whole()],
        out_specs=whole(),
        compiler_params=params(),
        name="first_norm",
    )(tokens, modulation)

    gathered = lax.all_gather(first_input, ("zh", "c"), axis=0, tiled=True)

    total = gathered.shape[0]
    mixed = pl.pallas_call(
        frame_kernel,
        out_shape=jax.ShapeDtypeStruct((total // LANES, 2 * HD, LANES), jnp.bfloat16),
        in_specs=[whole()] * 3,
        out_specs=whole(),
        scratch_shapes=[
            pltpu.VMEM((total, 4 * LANES), jnp.bfloat16),
            pltpu.VMEM((2 * HP, total), jnp.bfloat16),
        ],
        compiler_params=params(),
        name="frame_attention",
    )(gathered, wqk, wvt)

    mixed = lax.all_to_all(mixed, ("zh", "c"), 0, 0, tiled=True)
    middle = pl.pallas_call(
        middle_kernel,
        out_shape=jax.ShapeDtypeStruct((rows, width), jnp.bfloat16),
        in_specs=[whole()] * 4,
        out_specs=whole(),
        compiler_params=params(),
        name="middle",
    )(mixed, out_table, tokens, modulation)

    middle = lax.all_to_all(middle, ("x", "zl"), 0, 0, tiled=True)

    positions = rows // 16
    group = 2
    steps = 16 // group
    out = pl.pallas_call(
        lambda *refs: time_kernel(positions, *refs),
        grid=(steps,),
        out_shape=jax.ShapeDtypeStruct((rows, width), jnp.bfloat16),
        in_specs=[
            whole(),
            pl.BlockSpec((group, 8, 32, width), lambda i: (i, 0, 0, 0)),
            whole(),
            whole(),
        ],
        out_specs=whole(),
        scratch_shapes=[
            pltpu.VMEM((rows, width), jnp.bfloat16),
            pltpu.VMEM((steps, group * HD, rows), jnp.bfloat16),
        ],
        compiler_params=params(),
        name="time_block",
    )(middle, time_table, time_out, modulation)
    out = lax.all_to_all(out, ("x", "zl"), 0, 0, tiled=True)
    return out[None]


def solution(mesh):
    fine = Mesh(mesh.devices.reshape(4, 4, 4, 4, 2), ("y", "x", "zl", "zh", "c"))
    frames, space = ("y", "x", "zl"), ("zh", "c")
    placed = (
        P(frames, space, None),
        P(None, space),
        P(space, None),
        P(("x", "zl"), None),
        P(),
        P("y", None, None),
    )
    return jax.shard_map(
        shards,
        mesh=fine,
        in_specs=placed,
        out_specs=P(frames, space, None),
        check_vma=False,
    )
```

time: 396 us -> 451 us (1.14); the launches traced: 391 us -> 451 us
  waiting for transfers between devices: 283 us -> 363 us
  matrix products: 35.8 us -> 0 us
  Pallas kernels: 0 us -> 24.2 us
  blocking collectives: 41.2 us -> 29.3 us
  other arithmetic: 6.63 us -> 0 us
  starting transfers between devices: 0.09 us -> 5.89 us
  local copies, waits for them, and re-layouts: 9.56 us -> 15.2 us
    all_gather x2 -> x3, waiting for transfers between devices: 152 us -> 363 us  [the longest x1 192 us: shards(): time_table = lax.all_gather(part, ('x', 'zl', 'y', 'c'), axis=0)]
    reduce_scatter x1 -> x0, waiting for transfers between devices: 131 us -> none  [shards(): lax.psum_scatter(jnp.dot(frame_source, frame_out, preferred_element_type=...]
    pallas_call x0 -> x4, Pallas kernels: none -> 24.2 us  [the longest x1 13.1 us: shards(): pl.pallas_call(lambda *refs: time_kernel(positions, *refs), grid=(steps,)...]
    dot_general x7 -> x0, matrix products: 23.8 us -> none  [the longest x2 7.38 us: frame_block(): jnp.einsum('fhqk,fkhe->fqhe', weights, value_part, preferred_element_type...]
    sub x3 -> x0, matrix products: 12 us -> none  [normalized_weights(): raised = jnp.exp(scores - largest)]
    all_to_all x2, blocking collectives: 41.2 us -> 29.3 us  [the longest x1 15 us: shards(): out = lax.all_to_all(out, ('x', 'zl'), 0, 0, tiled=True)]
    unnamed x7 -> x15, local copies, waits for them, and re-layouts: 0.04 us -> 8.04 us
    all_to_all x0 -> x1, starting transfers between devices: none -> 5.81 us  [shards(): mixed = lax.all_to_all(mixed, ('zh', 'c'), 0, 0, tiled=True)]
  transfers between devices with their start and end apart: 3 -> 4, of which waited for: 3 -> 3; matrix products, arithmetic and copies ran while one was open for 0% -> 2% of each run, Pallas kernels for 0% -> 2%
where the time goes in v1:
time: 451 us
  waiting for transfers between devices  363 us (80%)
  blocking collectives  29.3 us (6%)
  Pallas kernels  24.2 us (5%)
  local copies, waits for them, and re-layouts  15.2 us (3%)
  between operations  13.2 us (3%)
  starting transfers between devices  5.89 us (1%)
    all_gather x1, waiting for transfers between devices, shards(): time_table = lax.all_gather(part, ('x', 'zl', 'y', 'c'), axis=0)  192 us
    all_gather x1, waiting for transfers between devices, shards(): out_table = lax.all_gather(part, ('zh', 'c', 'x', 'y'), axis=0)  107 us
    all_gather x1, waiting for transfers between devices, shards(): gathered = lax.all_gather(first_input, ('zh', 'c'), axis=0, tiled=True)  63.9 us
    all_to_all x1, blocking collectives, shards(): out = lax.all_to_all(out, ('x', 'zl'), 0, 0, tiled=True)  15 us
    all_to_all x1, blocking collectives, shards(): middle = lax.all_to_all(middle, ('x', 'zl'), 0, 0, tiled=True)  14.3 us
    pallas_call x1, Pallas kernels, shards(): pl.pallas_call(lambda *refs: time_kernel(positions, *refs), grid=(steps,)...  13.1 us
  transfers between devices with their start and end apart: 4, of which 3 were waited for; matrix products, arithmetic and copies ran while one was open for 2% of the time, Pallas kernels for 2%

profile of v1, /device:TPU:1, one launch (start us, length us, event | category | flops | bytes accessed | tf_op | source)
XLA Modules:
  0.0 450.8 jit_solution(11091094069810913682)
XLA Ops:
  6.5 0.0 copy-start
  6.5 0.0 all-gather.6.cloned.1.call-start
  6.5 0.8 copy.7.modulation_ref.refs_3_
  7.3 0.0 copy-start.3
  7.4 1.0 copy-done.3
  8.3 0.0 copy-start.5
  8.3 1.0 first_norm.1
  9.3 0.0 all-gather.6.cloned.1.call-update
  9.3 0.0 all-gather.8.cloned.1.call-start
  9.4 0.0 copy-done
  9.4 0.6 constant_dynamic-slice_fusion
  10.0 0.1 all-gather.8.cloned.1.call-update
  10.1 0.0 all-gather.10.cloned.1.call-start
  10.1 1.1 pad.18
  11.2 0.7 pad_dynamic-slice_fusion
  11.9 0.0 all-gather.10.cloned.1.call-update
  11.9 0.0 copy-done.5
  11.9 0.1 slice.12
  12.0 2.1 copy.12
  14.1 1.3 pad.16
  15.4 0.5 reshape.30.refs_1_
  15.9 1.0 slice_bitcast_fusion
  16.9 63.9 %all-gather.6.cloned.1.call-done.refs_0_ = bf16[1024,1152]{1,0:T(8,128)(2,1)} async-done(((bf16[128,1152]{1,0:T(8,128)(2,1)}), bf16[1024,1152]{1,0:T(8,128)(2,1)}) %all-gather.6.cloned.1.call-update) | async-done | bytes 2359312 | tf_op jit(solution)/shard_map/all_gather | solution.py:162
  80.9 0.0 copy-start.2
  80.9 1.7 copy-done.2
  82.5 8.5 %frame_attention.1 = bf16[8,144,128]{2,1,0:T(8,128)(2,1)} custom-call(bf16[1024,1152]{1,0:T(8,128)(2,1)S(1)} %copy-done.2, bf16[1152,512]{1,0:T(8,128)(2,1)S(1)} %reshape.30.refs_1_, bf16[160,1152]{1,0:T(8,128)(2,1)S(1)} %bitcast.19), custom_call_target="tpu_custom_call" | custom-call | tf_op jit(solution)/shard_map/frame_attention/pallas_call | solution.py:165
  91.1 5.8 %all-to-all-start = ((bf16[8,144,128]{2,1,0:T(8,128)(2,1)}), bf16[8,144,128]{2,1,0:T(8,128)(2,1)}, u32[]{:S(2)}, u32[]{:S(2)}) async-start(bf16[8,144,128]{2,1,0:T(8,128)(2,1)} %frame_attention.1), calls=%async_computation | async-start | bytes 589824 | tf_op jit(solution)/shard_map/all_to_all | solution.py:178
  96.9 106.8 %all-gather.8.cloned.1.call-done = bf16[2048,1152]{1,0:T(8,128)(2,1)} async-done(((bf16[16,1152]{1,0:T(8,128)(2,1)}), bf16[2048,1152]{1,0:T(8,128)(2,1)}) %all-gather.8.cloned.1.call-update) | async-done | bytes 4718608 | tf_op jit(solution)/shard_map/all_gather | solution.py:145
  203.7 0.0 copy-start.4
  203.7 2.0 slice.14
  205.7 0.0 all-to-all-done.mixed_ref
  205.7 0.0 copy-done.4
  205.7 1.6 middle.1
  207.3 14.3 %all_to_all.25 = bf16[16,8,1152]{2,1,0:T(8,128)(2,1)S(1)} all-to-all(bf16[16,8,1152]{2,1,0:T(8,128)(2,1)S(1)} %bitcast.24), channel_id=1, replica_groups=mesh['y'=4,'x'=4,'zl'=4,'zh'=4,'c'=2] {'x','zl'}, dimensions={0} | all-to-all | bytes 589824 | tf_op jit(solution)/shard_map/all_to_all | solution.py:188
  221.5 192.2 %all-gather.10.cloned.1.call-done = bf16[4096,1152]{1,0:T(8,128)(2,1)} async-done(((bf16[32,1152]{1,0:T(8,128)(2,1)}), bf16[4096,1152]{1,0:T(8,128)(2,1)}) %all-gather.10.cloned.1.call-update) | async-done | bytes 9437200 | tf_op jit(solution)/shard_map/all_gather | solution.py:140
  413.7 0.0 copy-start.1
  413.7 1.7 copy-done.1
  415.5 13.1 %time_block.1 = bf16[128,1152]{1,0:T(8,128)(2,1)S(1)} custom-call(bf16[128,1152]{1,0:T(8,128)(2,1)S(1)} %bitcast.20, bf16[16,8,32,1152]{3,2,1,0:T(8,128)(2,1)} %bitcast.25, bf16[1152,1152]{1,0:T(8,128)(2,1)S(1)} %copy-done.1, f32[2,3,1152]{2,1,0:T(4,128)S(1)} %copy.7.modulation_ref.refs_3_), custom_call_target="tpu_custom_call" | custom-call | tf_op jit(solution)/shard_map/time_block/pallas_call | solution.py:193
  428.6 15.0 %all_to_all.26 = bf16[16,8,1152]{2,1,0:T(8,128)(2,1)S(1)} all-to-all(bf16[16,8,1152]{2,1,0:T(8,128)(2,1)S(1)} %bitcast.21), channel_id=1, replica_groups=mesh['y'=4,'x'=4,'zl'=4,'zh'=4,'c'=2] {'x','zl'}, dimensions={0} | all-to-all | bytes 589824 | tf_op jit(solution)/shard_map/all_to_all | solution.py:211
  443.6 0.7 copy.15
  (1 shorter events, 0.0 us)
Async XLA Ops:
  6.5 2.9 copy-start
  6.5 74.3 %all-gather.6.cloned.1.call-start = ((), (), s32[]{:S(2)}) async-start(), calls=%async_computation.3 | async-start | bytes 2654208 | tf_op jit(solution)/shard_map/all_gather | solution.py:162
  7.3 1.0 copy-start.3
  8.3 3.6 copy-start.5
  9.3 194.3 %all-gather.8.cloned.1.call-start = ((), (), s32[]{:S(2)}) async-start(), calls=%async_computation.4 | async-start | bytes 4755456 | tf_op jit(solution)/shard_map/all_gather | solution.py:145
  10.1 403.6 %all-gather.10.cloned.1.call-start = ((), (), s32[]{:S(2)}) async-start(), calls=%async_computation.5 | async-start | bytes 9510912 | tf_op jit(solution)/shard_map/all_gather | solution.py:140
  80.9 1.7 copy-start.2
  91.1 114.6 %all-to-all-start = ((bf16[8,144,128]{2,1,0:T(8,128)(2,1)}), bf16[8,144,128]{2,1,0:T(8,128)(2,1)}, u32[]{:S(2)}, u32[]{:S(2)}) async-start(bf16[8,144,128]{2,1,0:T(8,128)(2,1)} %frame_attention.1), calls=%async_computation | async-start | bytes 589824 | tf_op jit(solution)/shard_map/all_to_all | solution.py:178
  203.7 2.0 copy-start.4
  413.7 1.7 copy-start.1
Sparse Core Ops, SparseCore 0:
  9.5 71.3 all-gather.5
  85.2 118.4 all-gather.7
  205.8 207.8 all-gather.9

commit v2 on v1

v2 whole, which is shorter than its diff:
```python
import functools
import math

import jax
import jax.numpy as jnp
from jax import lax
from jax.experimental import pallas as pl
from jax.experimental.pallas import tpu as pltpu
from jax.sharding import Mesh
from jax.sharding import PartitionSpec as P

HD = 72
HP = 80
LANES = 128
EPS = 1e-06
EXP2_SCALE = HD ** (-0.5) * math.log2(math.e)
NT = (((1,), (1,)), ((), ()))
TN = (((0,), (0,)), ((), ()))


def params(mib=48):
    return pltpu.CompilerParams(vmem_limit_bytes=mib * 1024 * 1024)


def whole():
    return pl.BlockSpec(memory_space=pltpu.VMEM)


def modulated(values, offset, stretch):
    center = jnp.mean(values, axis=-1, keepdims=True)
    values = values - center
    spread = jnp.mean(values * values, axis=-1, keepdims=True)
    return (values * lax.rsqrt(spread + EPS) * (1.0 + stretch) + offset).astype(jnp.bfloat16)


def triples_of(rows, modulation_ref, wqk_ref, wvt_ref):
    normed = modulated(rows, modulation_ref[0, 0:1], modulation_ref[0, 1:2])
    qk = jnp.dot(normed, wqk_ref[...], preferred_element_type=jnp.float32).astype(jnp.bfloat16)
    values = lax.dot_general(wvt_ref[...], normed, NT, preferred_element_type=jnp.float32)
    index = lax.broadcasted_iota(jnp.int32, values.shape, 0)
    ones = (index == HD) | (index == HP + HD)
    return qk, jnp.where(ones, 1.0, values).astype(jnp.bfloat16)


def early_kernel(*refs):
    pieces, (modulation_ref, wqk_ref, wvt_ref, qk_ref, vt_ref) = refs[:-5], refs[-5:]
    for index in range(0, len(pieces), 2):
        rows = jnp.concatenate([pieces[index][...], pieces[index + 1][...]], axis=0)
        qk, vt = triples_of(rows.astype(jnp.float32), modulation_ref, wqk_ref, wvt_ref)
        start = LANES * index
        qk_ref[start : start + 2 * LANES] = qk
        vt_ref[:, start : start + 2 * LANES] = vt


def frame_kernel(
    place_ref, one_ref, two_ref, three_ref, four_ref, qk_ref, vt_ref, modulation_ref, wqk_ref, wvt_ref,
    out_ref, qk_late_ref, vt_late_ref,
):
    rows = jnp.concatenate([one_ref[...], two_ref[...], three_ref[...], four_ref[...]], axis=0)
    qk_late_ref[...], vt_late_ref[...] = triples_of(
        rows.astype(jnp.float32), modulation_ref, wqk_ref, wvt_ref
    )
    parts = ((qk_ref, vt_ref), (qk_late_ref, vt_late_ref))
    block = 2 * LANES
    number = 0
    for qk_part, _ in parts:
        for start in range(0, qk_part.shape[0], block):
            outs = []
            for head in range(2):
                column = 2 * LANES * head
                queries = qk_part[start : start + block, column : column + LANES]
                scores = [
                    lax.dot_general(
                        qk[:, column + LANES : column + 2 * LANES], queries, NT,
                        preferred_element_type=jnp.float32,
                    )
                    for qk, _ in parts
                ]
                largest = jnp.maximum(*[jnp.max(part, axis=0, keepdims=True) for part in scores])
                mixed = sum(
                    jnp.dot(
                        vt[HP * head : HP * head + HP],
                        jnp.exp2((part - largest) * EXP2_SCALE).astype(jnp.bfloat16),
                        preferred_element_type=jnp.float32,
                    )
                    for part, (_, vt) in zip(scores, parts)
                )
                outs.append(mixed[:HD] / mixed[HD : HD + 1])
            both = jnp.concatenate(outs, axis=0).astype(jnp.bfloat16)
            for part in range(2):
                out_ref[place_ref[number]] = both[:, part * LANES : (part + 1) * LANES]
                number += 1


def middle_kernel(place_ref, mixed_ref, tables_ref, tokens_ref, modulation_ref, out_ref, table_ref, sem):
    copy = pltpu.make_async_copy(tables_ref.at[pl.ds(0, 9), :, pl.ds(LANES, 64), :], table_ref, sem)
    copy.start()
    zh = place_ref[8]
    slots = [mixed_ref[((zh + 4 - slot) % 4) * 2 + core] for core in range(2) for slot in range(4)]
    mixed = jnp.concatenate(
        [slot[16 * number : 16 * number + 16] for number in range(9) for slot in slots], axis=0
    )
    copy.wait()
    table = table_ref[...].reshape(-1, table_ref.shape[-1])
    branch = lax.dot_general(mixed, table, TN, preferred_element_type=jnp.float32)
    out_ref[...] = (
        tokens_ref[...].astype(jnp.float32) + modulation_ref[0, 2:3] * branch
    ).astype(jnp.bfloat16)


def time_kernel(
    positions, place_ref, middle_ref, tables_ref, out_table_ref, modulation_ref, out_ref,
    input_ref, mixed_ref, table_ref, sem,
):
    step = pl.program_id(0)
    copy = pltpu.make_async_copy(out_table_ref, table_ref, sem)

    @pl.when(step == 0)
    def _():
        copy.start()
        input_ref[...] = modulated(
            middle_ref[...].astype(jnp.float32), modulation_ref[1, 0:1], modulation_ref[1, 1:2]
        )

    rows, width = input_ref.shape
    zl = place_ref[9]
    one = lax.broadcasted_iota(jnp.int32, (rows, rows), 0) % positions
    two = lax.broadcasted_iota(jnp.int32, (rows, rows), 1) % positions
    same = one == two
    triples = []
    for slot in range(4):
        table = tables_ref[0, 0:7, 32 * slot : 32 * slot + 32].reshape(7 * 32, width)
        triples.append(lax.dot_general(table, input_ref[...], NT, preferred_element_type=jnp.float32))
    scores = []
    for triple in triples:
        queries = triple[:HD].astype(jnp.bfloat16)
        keys = triple[HD : 2 * HD].astype(jnp.bfloat16)
        part = lax.dot_general(keys, queries, TN, preferred_element_type=jnp.float32)
        scores.append(jnp.where(same, part, -1e30))
    raised = [
        jnp.exp2((part - jnp.max(part, axis=0, keepdims=True)) * EXP2_SCALE) for part in scores
    ]
    for slot in range(4):
        values = jnp.concatenate([triples[slot][2 * HD : 192], triples[slot][200:]], axis=0)
        total = jnp.sum(raised[slot], axis=0, keepdims=True)
        mixed = jnp.dot(
            values.astype(jnp.bfloat16), raised[slot].astype(jnp.bfloat16),
            preferred_element_type=jnp.float32,
        )
        mixed_ref[step * 4 + (zl + 4 - slot) % 4] = mixed / total

    @pl.when(step == pl.num_programs(0) - 1)
    def _():
        copy.wait()
        mixed = mixed_ref[...].reshape(-1, rows).astype(jnp.bfloat16)
        branch = lax.dot_general(mixed, table_ref[...], TN, preferred_element_type=jnp.float32)
        out_ref[...] = (
            middle_ref[...].astype(jnp.float32) + modulation_ref[1, 2:3] * branch
        ).astype(jnp.bfloat16)


def rotation(count, by):
    return [(index, (index + by) % count) for index in range(count)]


SWAP = [(0, 1), (1, 0)]


def shards(tokens, frame_qkv, frame_out, time_qkv, time_out, modulation):
    tokens = tokens[0]
    rows, width = tokens.shape
    half = rows // 2
    zh, zl, core = lax.axis_index("zh"), lax.axis_index("zl"), lax.axis_index("c")

    def along(array, axis, by):
        return lax.ppermute(array, axis, rotation(4, by))

    def swapped(array):
        return lax.ppermute(array, "c", SWAP)

    before, after = along(tokens, "zh", 1), along(tokens, "zh", 3)
    beside = swapped(tokens)
    far_top, far_bottom = along(before[:half], "zh", 1), along(after[half:], "zh", 3)
    early = [tokens, beside, before, swapped(before), after, swapped(after)]
    late = [far_top, far_bottom, swapped(far_top), swapped(far_bottom)]
    spots = [zh, (zh + 3) % 4, (zh + 1) % 4, (zh + 2) % 4]
    place = jnp.stack(
        [spot * 2 + side for spot in spots for side in (core, 1 - core)] + [zh, zl]
    ).astype(jnp.int32)

    index = lax.axis_index("y") * 2 + core
    time_part = lax.dynamic_slice_in_dim(time_qkv, jnp.minimum(index * 32, 216 - 32), 32, 0)
    index = lax.axis_index("x") * 4 + lax.axis_index("y")
    out_part = lax.dynamic_slice_in_dim(frame_out, jnp.minimum(index, 8) * 16, 16, 0)
    parts = [time_part] + [along(time_part, "zl", by) for by in (1, 2, 3)]
    parts += [out_part] + [along(out_part, "zh", by) for by in (1, 2, 3)]
    tables = lax.all_gather(jnp.concatenate(parts, axis=0), ("x", "y", "c"), axis=0)
    tables = tables.reshape(4, 8, 192, width)

    heads = frame_qkv.reshape(width, 2, 3, HD)
    wqk = jnp.pad(heads[:, :, :2], ((0, 0), (0, 0), (0, 0), (0, LANES - HD))).reshape(width, 4 * LANES)
    wvt = jnp.pad(jnp.transpose(heads[:, :, 2], (1, 2, 0)), ((0, 0), (0, HP - HD), (0, 0)))
    wvt = wvt.reshape(2 * HP, width)

    soon = rows * len(early)
    qk, vt = pl.pallas_call(
        early_kernel,
        out_shape=(
            jax.ShapeDtypeStruct((soon, 4 * LANES), jnp.bfloat16),
            jax.ShapeDtypeStruct((2 * HP, soon), jnp.bfloat16),
        ),
        in_specs=[whole()] * (len(early) + 3),
        out_specs=(whole(), whole()),
        compiler_params=params(),
        cost_estimate=pl.CostEstimate(flops=2 * 10**9, bytes_accessed=5 * 10**6, transcendentals=0),
        name="early_triples",
    )(*early, modulation, wqk, wvt)

    rest = 2 * rows
    mixed = pl.pallas_call(
        frame_kernel,
        out_shape=jax.ShapeDtypeStruct(((soon + rest) // LANES, 2 * HD, LANES), jnp.bfloat16),
        in_specs=[pl.BlockSpec(memory_space=pltpu.SMEM)] + [whole()] * 9,
        out_specs=whole(),
        scratch_shapes=[
            pltpu.VMEM((rest, 4 * LANES), jnp.bfloat16),
            pltpu.VMEM((2 * HP, rest), jnp.bfloat16),
        ],
        compiler_params=params(),
        name="frame_attention",
    )(place, *late, qk, vt, modulation, wqk, wvt)

    mixed = lax.all_to_all(mixed, ("zh", "c"), 0, 0, tiled=True)
    middle = pl.pallas_call(
        middle_kernel,
        out_shape=jax.ShapeDtypeStruct((rows, width), jnp.bfloat16),
        in_specs=[
            pl.BlockSpec(memory_space=pltpu.SMEM), whole(), pl.BlockSpec(memory_space=pl.ANY), whole(), whole()
        ],
        out_specs=whole(),
        scratch_shapes=[pltpu.VMEM((9, 2, 64, width), jnp.bfloat16), pltpu.SemaphoreType.DMA],
        compiler_params=params(),
        name="middle",
    )(place, mixed, tables.reshape(16, 2, 192, width), tokens, modulation)

    middle = lax.all_to_all(middle, ("x", "zl"), 0, 0, tiled=True)

    out = pl.pallas_call(
        functools.partial(time_kernel, rows // 16),
        grid=(4,),
        out_shape=jax.ShapeDtypeStruct((rows, width), jnp.bfloat16),
        in_specs=[
            pl.BlockSpec(memory_space=pltpu.SMEM),
            whole(),
            pl.BlockSpec((1, 8, LANES, width), lambda i: (i, 0, 0, 0)),
            pl.BlockSpec(memory_space=pl.ANY),
            whole(),
        ],
        out_specs=whole(),
        scratch_shapes=[
            pltpu.VMEM((rows, width), jnp.bfloat16),
            pltpu.VMEM((16, HD, rows), jnp.float32),
            pltpu.VMEM((width, width), jnp.bfloat16),
            pltpu.SemaphoreType.DMA,
        ],
        compiler_params=params(),
        name="time_block",
    )(place, middle, tables, time_out, modulation)
    out = lax.all_to_all(out, ("x", "zl"), 0, 0, tiled=True)
    return out[None]


def solution(mesh):
    fine = Mesh(mesh.devices.reshape(4, 4, 4, 4, 2), ("y", "x", "zl", "zh", "c"))
    frames, space = ("y", "x", "zl"), ("zh", "c")
    placed = (
        P(frames, space, None),
        P(None, space),
        P(space, None),
        P(("x", "zl"), None),
        P(),
        P("y", None, None),
    )
    return jax.shard_map(
        shards,
        mesh=fine,
        in_specs=placed,
        out_specs=P(frames, space, None),
        check_vma=False,
    )
```

time: 451 us -> 199 us (0.44)
  waiting for transfers between devices: 363 us -> 21.9 us
  starting transfers between devices: 5.89 us -> 72.9 us
  blocking collectives: 29.3 us -> 53.2 us
    all_gather x3 -> x1, waiting for transfers between devices: 363 us -> 0.01 us  [shards(): lax.all_gather(jnp.concatenate(parts, axis=0), ('x', 'y', 'c'), axis=0)]
    ppermute x0 -> x15, starting transfers between devices: none -> 72.9 us  [the longest x10 58.6 us: along(): return lax.ppermute(array, axis, rotation(4, by))]
    all_to_all x0 -> x1, blocking collectives: none -> 24.6 us  [shards(): mixed = lax.all_to_all(mixed, ('zh', 'c'), 0, 0, tiled=True)]
    ppermute x0 -> x15, waiting for transfers between devices: none -> 21.9 us  [the longest x10 21.9 us: along(): return lax.ppermute(array, axis, rotation(4, by))]
    pallas_call x3, Pallas kernels: 22.6 us -> 16.7 us  [the longest x1 7.83 us: shards(): pl.pallas_call(functools.partial(time_kernel, rows // 16), grid=(4,), out...]
    all_to_all x1 -> x0, starting transfers between devices: 5.81 us -> none  [shards(): mixed = lax.all_to_all(mixed, ('zh', 'c'), 0, 0, tiled=True)]
  transfers between devices with their start and end apart: 4 -> 16, of which waited for: 3 -> 5; matrix products, arithmetic and copies ran while one was open for 2% -> 6% of each run, Pallas kernels for 2% -> 5%
where the time goes in v2:
time: 199 us; the launch traced here: 197 us
  starting transfers between devices  72.9 us (37%)
  blocking collectives  53.2 us (27%)
  waiting for transfers between devices  21.9 us (11%)
  Pallas kernels  19.9 us (10%)
  local copies, waits for them, and re-layouts  15.5 us (8%)
  between operations  13.7 us (7%)
    ppermute x10, starting transfers between devices, along(): return lax.ppermute(array, axis, rotation(4, by))  58.6 us
    all_to_all x1, blocking collectives, shards(): mixed = lax.all_to_all(mixed, ('zh', 'c'), 0, 0, tiled=True)  24.6 us
    ppermute x10, waiting for transfers between devices, along(): return lax.ppermute(array, axis, rotation(4, by))  21.9 us
    all_to_all x1, blocking collectives, shards(): middle = lax.all_to_all(middle, ('x', 'zl'), 0, 0, tiled=True)  14.8 us
    ppermute x5, starting transfers between devices, swapped(): return lax.ppermute(array, 'c', SWAP)  14.3 us
    all_to_all x1, blocking collectives, shards(): out = lax.all_to_all(out, ('x', 'zl'), 0, 0, tiled=True)  13.8 us
    pallas_call x1, Pallas kernels, shards(): pl.pallas_call(functools.partial(time_kernel, rows // 16), grid=(4,), out...  7.83 us
    unnamed x20, local copies, waits for them, and re-layouts  6.73 us
  transfers between devices with their start and end apart: 16, of which 5 were waited for; matrix products, arithmetic and copies ran while one was open for 6% of the time, Pallas kernels for 5%

profile of v2, /device:TPU:1, one launch (start us, length us, event | category | flops | bytes accessed | tf_op | source)
XLA Modules:
  0.0 197.1 jit_solution(12493452857963292096)
XLA Ops:
  6.5 1.0 constant_dynamic-update-slice_fusion.7
  7.6 4.4 %collective-permute-start.9 = (bf16[32,1152]{1,0:T(8,128)(2,1)S(1)}, bf16[32,1152]{1,0:T(8,128)(2,1)S(1)}, u32[]{:S(2)}, u32[]{:S(2)}) collective-permute-start(bf16[32,1152]{1,0:T(8,128)(2,1)S(1)} %get-tuple-element.12), channel_id=1, source_target_pairs={{0,8},{8,16},{16,24},{24,0},{1,9},{9,17},{17,25},{25,1},{2,10},{10... | collective-permute-start | bytes 221192 | tf_op jit(solution)/shard_map/ppermute | solution.py:176
  11.9 4.9 %collective-permute-start.10 = (bf16[32,1152]{1,0:T(8,128)(2,1)S(1)}, bf16[32,1152]{1,0:T(8,128)(2,1)S(1)}, u32[]{:S(2)}, u32[]{:S(2)}) collective-permute-start(bf16[32,1152]{1,0:T(8,128)(2,1)S(1)} %get-tuple-element.12), channel_id=1, source_target_pairs={{0,16},{8,24},{16,0},{24,8},{1,17},{9,25},{17,1},{25,9},{2,18},{10... | collective-permute-start | bytes 221192 | tf_op jit(solution)/shard_map/ppermute | solution.py:176
  16.8 2.6 %collective-permute-start.11 = (bf16[32,1152]{1,0:T(8,128)(2,1)S(1)}, bf16[32,1152]{1,0:T(8,128)(2,1)S(1)}, u32[]{:S(2)}, u32[]{:S(2)}) collective-permute-start(bf16[32,1152]{1,0:T(8,128)(2,1)S(1)} %get-tuple-element.12), channel_id=1, source_target_pairs={{0,24},{8,0},{16,8},{24,16},{1,25},{9,1},{17,9},{25,17},{2,26},{10... | collective-permute-start | bytes 221192 | tf_op jit(solution)/shard_map/ppermute | solution.py:176
  19.5 0.0 collective-permute-done.9
  19.5 0.0 collective-permute-done.10
  19.6 3.9 %collective-permute-done.11 = bf16[32,1152]{1,0:T(8,128)(2,1)S(1)} collective-permute-done((bf16[32,1152]{1,0:T(8,128)(2,1)S(1)}, bf16[32,1152]{1,0:T(8,128)(2,1)S(1)}, u32[]{:S(2)}, u32[]{:S(2)}) %collective-permute-start.11) | collective-permute-done | bytes 73760 | tf_op jit(solution)/shard_map/ppermute | solution.py:176
  23.4 0.8 constant_dynamic-update-slice_fusion.3
  24.2 7.3 %collective-permute-start.12 = (bf16[16,1152]{1,0:T(8,128)(2,1)S(1)}, bf16[16,1152]{1,0:T(8,128)(2,1)S(1)}, u32[]{:S(2)}, u32[]{:S(2)}) collective-permute-start(bf16[16,1152]{1,0:T(8,128)(2,1)S(1)} %get-tuple-element.10), channel_id=1, source_target_pairs={{0,2},{2,4},{4,6},{6,0},{1,3},{3,5},{5,7},{7,1},{8,10},{10,12},{12... | collective-permute-start | bytes 110600 | tf_op jit(solution)/shard_map/ppermute | solution.py:176
  31.6 8.7 %collective-permute-start.13 = (bf16[16,1152]{1,0:T(8,128)(2,1)S(1)}, bf16[16,1152]{1,0:T(8,128)(2,1)S(1)}, u32[]{:S(2)}, u32[]{:S(2)}) collective-permute-start(bf16[16,1152]{1,0:T(8,128)(2,1)S(1)} %get-tuple-element.10), channel_id=1, source_target_pairs={{0,4},{2,6},{4,0},{6,2},{1,5},{3,7},{5,1},{7,3},{8,12},{10,14},{12... | collective-permute-start | bytes 110600 | tf_op jit(solution)/shard_map/ppermute | solution.py:176
  40.2 5.2 %collective-permute-start.14 = (bf16[16,1152]{1,0:T(8,128)(2,1)S(1)}, bf16[16,1152]{1,0:T(8,128)(2,1)S(1)}, u32[]{:S(2)}, u32[]{:S(2)}) collective-permute-start(bf16[16,1152]{1,0:T(8,128)(2,1)S(1)} %get-tuple-element.10), channel_id=1, source_target_pairs={{0,6},{2,0},{4,2},{6,4},{1,7},{3,1},{5,3},{7,5},{8,14},{10,8},{12,... | collective-permute-start | bytes 110600 | tf_op jit(solution)/shard_map/ppermute | solution.py:176
  45.4 0.0 collective-permute-done.12
  45.5 1.0 collective-permute-done.13
  46.5 3.1 %collective-permute-done.14 = bf16[16,1152]{1,0:T(8,128)(2,1)S(1)} collective-permute-done((bf16[16,1152]{1,0:T(8,128)(2,1)S(1)}, bf16[16,1152]{1,0:T(8,128)(2,1)S(1)}, u32[]{:S(2)}, u32[]{:S(2)}) %collective-permute-start.14) | collective-permute-done | bytes 36896 | tf_op jit(solution)/shard_map/ppermute | solution.py:176
  49.6 0.8 copy-done.3
  50.4 0.0 all-gather.3.cloned.1.call-update
  50.4 2.6 %collective-permute-start = (bf16[128,1152]{1,0:T(8,128)(2,1)S(1)}, bf16[128,1152]{1,0:T(8,128)(2,1)S(1)}, u32[]{:S(2)}, u32[]{:S(2)}) collective-permute-start(bf16[128,1152]{1,0:T(8,128)(2,1)S(1)} %bitcast.30), channel_id=1, source_target_pairs={{0,2},{2,4},{4,6},{6,0},{1,3},{3,5},{5,7},{7,1},{8,10},{10,12},{12... | collective-permute-start | bytes 884744 | tf_op jit(solution)/shard_map/ppermute | solution.py:176
  53.1 6.6 %collective-permute-start.2 = (bf16[128,1152]{1,0:T(8,128)(2,1)S(1)}, bf16[128,1152]{1,0:T(8,128)(2,1)S(1)}, u32[]{:S(2)}, u32[]{:S(2)}) collective-permute-start(bf16[128,1152]{1,0:T(8,128)(2,1)S(1)} %bitcast.31), channel_id=1, source_target_pairs={{0,6},{2,0},{4,2},{6,4},{1,7},{3,1},{5,3},{7,5},{8,14},{10,8},{12,... | collective-permute-start | bytes 884744 | tf_op jit(solution)/shard_map/ppermute | solution.py:176
  59.6 5.1 %collective-permute-start.6 = (bf16[128,1152]{1,0:T(8,128)(2,1)S(1)}, bf16[128,1152]{1,0:T(8,128)(2,1)S(1)}, u32[]{:S(2)}, u32[]{:S(2)}) collective-permute-start(bf16[128,1152]{1,0:T(8,128)(2,1)S(1)} %bitcast.32), channel_id=1, source_target_pairs={{0,1},{1,0},{2,3},{3,2},{4,5},{5,4},{6,7},{7,6},{8,9},{9,8},{10,11... | collective-permute-start | bytes 884744 | tf_op jit(solution)/shard_map/ppermute | solution.py:179
  64.7 12.7 %collective-permute-done.refs_2_ = bf16[128,1152]{1,0:T(8,128)(2,1)S(1)} collective-permute-done((bf16[128,1152]{1,0:T(8,128)(2,1)S(1)}, bf16[128,1152]{1,0:T(8,128)(2,1)S(1)}, u32[]{:S(2)}, u32[]{:S(2)}) %collective-permute-start) | collective-permute-done | bytes 294944 | tf_op jit(solution)/shard_map/ppermute | solution.py:176
  77.4 0.0 copy-start.4
  77.5 10.0 %collective-permute-start.1 = (bf16[64,1152]{1,0:T(8,128)(2,1)S(1)}, bf16[64,1152]{1,0:T(8,128)(2,1)S(1)}, u32[]{:S(2)}, u32[]{:S(2)}) collective-permute-start(bf16[64,1152]{1,0:T(8,128)(2,1)S(1)} %slice.16), channel_id=1, source_target_pairs={{0,2},{2,4},{4,6},{6,0},{1,3},{3,5},{5,7},{7,1},{8,10},{10,12},{12... | collective-permute-start | bytes 442376 | tf_op jit(solution)/shard_map/ppermute | solution.py:176
  87.4 1.1 collective-permute-done.2.refs_4_
  88.6 0.7 slice.17
  89.2 6.4 %collective-permute-start.3 = (bf16[64,1152]{1,0:T(8,128)(2,1)}, bf16[64,1152]{1,0:T(8,128)(2,1)S(1)}, u32[]{:S(2)}, u32[]{:S(2)}) collective-permute-start(bf16[64,1152]{1,0:T(8,128)(2,1)} %slice.17), channel_id=1, source_target_pairs={{0,6},{2,0},{4,2},{6,4},{1,7},{3,1},{5,3},{7,5},{8,14},{10,8},{12,... | collective-permute-start | bytes 442376 | tf_op jit(solution)/shard_map/ppermute | solution.py:176
  95.6 3.0 %collective-permute-start.7 = (bf16[128,1152]{1,0:T(8,128)(2,1)S(1)}, bf16[128,1152]{1,0:T(8,128)(2,1)S(1)}, u32[]{:S(2)}, u32[]{:S(2)}) collective-permute-start(bf16[128,1152]{1,0:T(8,128)(2,1)S(1)} %collective-permute-done.refs_2_), channel_id=1, source_target_pairs={{0,1},{1,0},{2,3},{3,2},{4,5},{5,4},{6,7},{7,6},{8,9},{9,8},{10,11... | collective-permute-start | bytes 884744 | tf_op jit(solution)/shard_map/ppermute | solution.py:179
  98.6 1.9 collective-permute-start.8
  100.5 0.8 slice_bitcast_fusion
  101.3 0.9 slice.18
  102.3 3.4 %copy.13 = bf16[1152,2,2,72]{3,2,1,0:T(2,128)(2,1)S(1)} copy(bf16[1152,2,2,72]{0,3,2,1:T(8,128)(2,1)} %slice.18) | data formatting | bytes 1327104
  105.6 2.1 %pad.8 = bf16[1152,2,2,128]{3,2,1,0:T(2,128)(2,1)} pad(bf16[1152,2,2,72]{3,2,1,0:T(2,128)(2,1)S(1)} %copy.13, bf16[]{:T(256)} %constant.51.clone.1), padding=0_0x0_0x0_0x0_56 | pad | bytes 1843202 | tf_op jit(solution)/shard_map/jit(_pad)/pad | solution.py:201
  107.7 3.1 %reshape.18.refs_7_.wqk_ref = bf16[1152,512]{1,0:T(8,128)(2,1)S(1)} reshape(bf16[1152,2,2,128]{3,2,1,0:T(2,128)(2,1)} %pad.8) | data formatting | bytes 2359296 | tf_op jit(solution)/shard_map/reshape | solution.py:201
  110.9 1.0 pad.9
  111.9 0.1 stack.43.place_ref
  112.0 0.0 collective-permute-done.1.one_ref
  112.0 2.4 %collective-permute-start.4 = (bf16[64,1152]{1,0:T(8,128)(2,1)S(1)}, bf16[64,1152]{1,0:T(8,128)(2,1)S(1)}, u32[]{:S(2)}, u32[]{:S(2)}) collective-permute-start(bf16[64,1152]{1,0:T(8,128)(2,1)S(1)} %collective-permute-done.1.one_ref), channel_id=1, source_target_pairs={{0,1},{1,0},{2,3},{3,2},{4,5},{5,4},{6,7},{7,6},{8,9},{9,8},{10,11... | collective-permute-start | bytes 442376 | tf_op jit(solution)/shard_map/ppermute | solution.py:179
  114.4 1.9 collective-permute-start.5
  116.4 0.0 collective-permute-done.6.refs_1_
  116.4 0.0 collective-permute-done.7.refs_3_
  116.4 3.2 %early_triples.1 = (bf16[768,512]{1,0:T(8,128)(2,1)S(1)}, bf16[160,768]{1,0:T(8,128)(2,1)S(1)}) custom-call(bf16[128,1152]{1,0:T(8,128)(2,1)S(1)} %bitcast.33, bf16[128,1152]{1,0:T(8,128)(2,1)S(1)} %collective-permute-done.6.refs_1_, bf16[128,1152]{1,0:T(8,128)(2,1)S(1)} %collective-permute-done.refs_2_, ...), custom_call_target="tpu_custom_call" | custom-call | flops 2000000000 | bytes 5000000 | tf_op jit(solution)/shard_map/early_triples/pallas_call | solution.py:206
  119.6 0.0 collective-permute-done.5.four_ref
  119.6 5.7 %frame_attention.1 = bf16[8,144,128]{2,1,0:T(8,128)(2,1)S(1)} custom-call(s32[10]{0:T(128)S(1)} %stack.43.place_ref, bf16[64,1152]{1,0:T(8,128)(2,1)S(1)} %collective-permute-done.1.one_ref, bf16[64,1152]{1,0:T(8,128)(2,1)S(1)} %collective-permute-done.3.two_ref, bf16[64,1152]{1,0:T(8,128)(2,1)S(1)} %collective-permute-done.4.three_ref, ...), custom_call_target="tpu_custom_call" | custom-call | tf_op jit(solution)/shard_map/frame_attention/pallas_call | solution.py:220
  125.3 24.6 %all_to_all.25.mixed_ref = bf16[8,144,128]{2,1,0:T(8,128)(2,1)S(1)} all-to-all(bf16[8,144,128]{2,1,0:T(8,128)(2,1)S(1)} %frame_attention.1), channel_id=1, replica_groups=mesh['y'=4,'x'=4,'zl'=4,'zh'=4,'c'=2] {'zh','c'}, dimensions={0} | all-to-all | bytes 589824 | tf_op jit(solution)/shard_map/all_to_all | solution.py:233
  149.9 3.2 %middle.1 = bf16[128,1152]{1,0:T(8,128)(2,1)S(1)} custom-call(s32[10]{0:T(128)S(1)} %stack.43.place_ref, bf16[8,144,128]{2,1,0:T(8,128)(2,1)S(1)} %all_to_all.25.mixed_ref, bf16[16,2,192,1152]{3,2,1,0:T(8,128)(2,1)} %bitcast.35, bf16[128,1152]{1,0:T(8,128)(2,1)S(1)} %bitcast.34, f32[2,3,1152]{2,1,0:T(4,128)S(1)} %copy.9.refs_6_.modulation_ref), custom_call_target="tpu_custom_call" | custom-call | tf_op jit(solution)/shard_map/middle/pallas_call | solution.py:234
  153.1 14.8 %all_to_all.26 = bf16[16,8,1152]{2,1,0:T(8,128)(2,1)S(1)} all-to-all(bf16[16,8,1152]{2,1,0:T(8,128)(2,1)S(1)} %bitcast.29), channel_id=1, replica_groups=mesh['y'=4,'x'=4,'zl'=4,'zh'=4,'c'=2] {'x','zl'}, dimensions={0} | all-to-all | bytes 589824 | tf_op jit(solution)/shard_map/all_to_all | solution.py:246
  167.9 7.8 %time_block.1 = bf16[128,1152]{1,0:T(8,128)(2,1)S(1)} custom-call(s32[10]{0:T(128)S(1)} %stack.43.place_ref, bf16[128,1152]{1,0:T(8,128)(2,1)S(1)} %bitcast.27, bf16[4,8,192,1152]{3,2,1,0:T(8,128)(2,1)} %bitcast.36, bf16[1152,1152]{1,0:T(8,128)(2,1)S(1)} %copy-done, f32[2,3,1152]{2,1,0:T(4,128)S(1)} %copy.9.refs_6_.modulation_ref), custom_call_target="tpu_custom_call" | custom-call | tf_op jit(solution)/shard_map/time_block/pallas_call | solution.py:248
  175.7 13.8 %all_to_all.27 = bf16[16,8,1152]{2,1,0:T(8,128)(2,1)S(1)} all-to-all(bf16[16,8,1152]{2,1,0:T(8,128)(2,1)S(1)} %bitcast.28), channel_id=1, replica_groups=mesh['y'=4,'x'=4,'zl'=4,'zh'=4,'c'=2] {'x','zl'}, dimensions={0} | all-to-all | bytes 589824 | tf_op jit(solution)/shard_map/all_to_all | solution.py:269
  189.5 0.7 copy.23
  (21 shorter events, 0.1 us)
Async XLA Ops:
  6.5 43.9 %copy-start.1 = (bf16[1,128,1152]{2,1,0:T(8,128)(2,1)S(1)}, bf16[1,128,1152]{2,1,0:T(8,128)(2,1)}, u32[]{:S(2)}) copy-start(bf16[1,128,1152]{2,1,0:T(8,128)(2,1)} %param.6) | copy-start | bytes 884740
  6.5 94.0 %copy-start.2 = (bf16[1152,432]{0,1:T(8,128)(2,1)S(1)}, bf16[1152,432]{0,1:T(8,128)(2,1)}, u32[]{:S(2)}) copy-start(bf16[1152,432]{0,1:T(8,128)(2,1)} %param.7) | copy-start | bytes 2985988
  6.5 143.4 %all-gather.3.cloned.1.call-start = ((), (), s32[]{:S(2)}) async-start(), calls=%async_computation.3 | async-start | bytes 14598144 | tf_op jit(solution)/shard_map/all_gather | solution.py:197
  7.6 11.9 %collective-permute-start.9 = (bf16[32,1152]{1,0:T(8,128)(2,1)S(1)}, bf16[32,1152]{1,0:T(8,128)(2,1)S(1)}, u32[]{:S(2)}, u32[]{:S(2)}) collective-permute-start(bf16[32,1152]{1,0:T(8,128)(2,1)S(1)} %get-tuple-element.12), channel_id=1, source_target_pairs={{0,8},{8,16},{16,24},{24,0},{1,9},{9,17},{17,25},{25,1},{2,10},{10... | collective-permute-start | bytes 221192 | tf_op jit(solution)/shard_map/ppermute | solution.py:176
  11.9 7.6 %collective-permute-start.10 = (bf16[32,1152]{1,0:T(8,128)(2,1)S(1)}, bf16[32,1152]{1,0:T(8,128)(2,1)S(1)}, u32[]{:S(2)}, u32[]{:S(2)}) collective-permute-start(bf16[32,1152]{1,0:T(8,128)(2,1)S(1)} %get-tuple-element.12), channel_id=1, source_target_pairs={{0,16},{8,24},{16,0},{24,8},{1,17},{9,25},{17,1},{25,9},{2,18},{10... | collective-permute-start | bytes 221192 | tf_op jit(solution)/shard_map/ppermute | solution.py:176
  16.8 6.6 %collective-permute-start.11 = (bf16[32,1152]{1,0:T(8,128)(2,1)S(1)}, bf16[32,1152]{1,0:T(8,128)(2,1)S(1)}, u32[]{:S(2)}, u32[]{:S(2)}) collective-permute-start(bf16[32,1152]{1,0:T(8,128)(2,1)S(1)} %get-tuple-element.12), channel_id=1, source_target_pairs={{0,24},{8,0},{16,8},{24,16},{1,25},{9,1},{17,9},{25,17},{2,26},{10... | collective-permute-start | bytes 221192 | tf_op jit(solution)/shard_map/ppermute | solution.py:176
  24.2 21.2 %collective-permute-start.12 = (bf16[16,1152]{1,0:T(8,128)(2,1)S(1)}, bf16[16,1152]{1,0:T(8,128)(2,1)S(1)}, u32[]{:S(2)}, u32[]{:S(2)}) collective-permute-start(bf16[16,1152]{1,0:T(8,128)(2,1)S(1)} %get-tuple-element.10), channel_id=1, source_target_pairs={{0,2},{2,4},{4,6},{6,0},{1,3},{3,5},{5,7},{7,1},{8,10},{10,12},{12... | collective-permute-start | bytes 110600 | tf_op jit(solution)/shard_map/ppermute | solution.py:176
  31.6 14.9 %collective-permute-start.13 = (bf16[16,1152]{1,0:T(8,128)(2,1)S(1)}, bf16[16,1152]{1,0:T(8,128)(2,1)S(1)}, u32[]{:S(2)}, u32[]{:S(2)}) collective-permute-start(bf16[16,1152]{1,0:T(8,128)(2,1)S(1)} %get-tuple-element.10), channel_id=1, source_target_pairs={{0,4},{2,6},{4,0},{6,2},{1,5},{3,7},{5,1},{7,3},{8,12},{10,14},{12... | collective-permute-start | bytes 110600 | tf_op jit(solution)/shard_map/ppermute | solution.py:176
  40.2 9.4 %collective-permute-start.14 = (bf16[16,1152]{1,0:T(8,128)(2,1)S(1)}, bf16[16,1152]{1,0:T(8,128)(2,1)S(1)}, u32[]{:S(2)}, u32[]{:S(2)}) collective-permute-start(bf16[16,1152]{1,0:T(8,128)(2,1)S(1)} %get-tuple-element.10), channel_id=1, source_target_pairs={{0,6},{2,0},{4,2},{6,4},{1,7},{3,1},{5,3},{7,5},{8,14},{10,8},{12,... | collective-permute-start | bytes 110600 | tf_op jit(solution)/shard_map/ppermute | solution.py:176
  49.6 0.8 copy-start.3
  50.4 27.0 %collective-permute-start = (bf16[128,1152]{1,0:T(8,128)(2,1)S(1)}, bf16[128,1152]{1,0:T(8,128)(2,1)S(1)}, u32[]{:S(2)}, u32[]{:S(2)}) collective-permute-start(bf16[128,1152]{1,0:T(8,128)(2,1)S(1)} %bitcast.30), channel_id=1, source_target_pairs={{0,2},{2,4},{4,6},{6,0},{1,3},{3,5},{5,7},{7,1},{8,10},{10,12},{12... | collective-permute-start | bytes 884744 | tf_op jit(solution)/shard_map/ppermute | solution.py:176
  53.1 35.5 %collective-permute-start.2 = (bf16[128,1152]{1,0:T(8,128)(2,1)S(1)}, bf16[128,1152]{1,0:T(8,128)(2,1)S(1)}, u32[]{:S(2)}, u32[]{:S(2)}) collective-permute-start(bf16[128,1152]{1,0:T(8,128)(2,1)S(1)} %bitcast.31), channel_id=1, source_target_pairs={{0,6},{2,0},{4,2},{6,4},{1,7},{3,1},{5,3},{7,5},{8,14},{10,8},{12,... | collective-permute-start | bytes 884744 | tf_op jit(solution)/shard_map/ppermute | solution.py:176
  59.6 56.7 %collective-permute-start.6 = (bf16[128,1152]{1,0:T(8,128)(2,1)S(1)}, bf16[128,1152]{1,0:T(8,128)(2,1)S(1)}, u32[]{:S(2)}, u32[]{:S(2)}) collective-permute-start(bf16[128,1152]{1,0:T(8,128)(2,1)S(1)} %bitcast.32), channel_id=1, source_target_pairs={{0,1},{1,0},{2,3},{3,2},{4,5},{5,4},{6,7},{7,6},{8,9},{9,8},{10,11... | collective-permute-start | bytes 884744 | tf_op jit(solution)/shard_map/ppermute | solution.py:179
  77.4 24.8 %copy-start.4 = (f32[2,3,1152]{2,0,1:T(2,128)S(1)}, f32[2,3,1152]{2,0,1:T(2,128)}, u32[]{:S(2)}) copy-start(f32[2,3,1152]{2,0,1:T(2,128)} %param.11) | copy-start | bytes 82948
  77.5 34.5 %collective-permute-start.1 = (bf16[64,1152]{1,0:T(8,128)(2,1)S(1)}, bf16[64,1152]{1,0:T(8,128)(2,1)S(1)}, u32[]{:S(2)}, u32[]{:S(2)}) collective-permute-start(bf16[64,1152]{1,0:T(8,128)(2,1)S(1)} %slice.16), channel_id=1, source_target_pairs={{0,2},{2,4},{4,6},{6,0},{1,3},{3,5},{5,7},{7,1},{8,10},{10,12},{12... | collective-permute-start | bytes 442376 | tf_op jit(solution)/shard_map/ppermute | solution.py:176
  89.2 25.2 %collective-permute-start.3 = (bf16[64,1152]{1,0:T(8,128)(2,1)}, bf16[64,1152]{1,0:T(8,128)(2,1)S(1)}, u32[]{:S(2)}, u32[]{:S(2)}) collective-permute-start(bf16[64,1152]{1,0:T(8,128)(2,1)} %slice.17), channel_id=1, source_target_pairs={{0,6},{2,0},{4,2},{6,4},{1,7},{3,1},{5,3},{7,5},{8,14},{10,8},{12,... | collective-permute-start | bytes 442376 | tf_op jit(solution)/shard_map/ppermute | solution.py:176
  95.6 20.8 %collective-permute-start.7 = (bf16[128,1152]{1,0:T(8,128)(2,1)S(1)}, bf16[128,1152]{1,0:T(8,128)(2,1)S(1)}, u32[]{:S(2)}, u32[]{:S(2)}) collective-permute-start(bf16[128,1152]{1,0:T(8,128)(2,1)S(1)} %collective-permute-done.refs_2_), channel_id=1, source_target_pairs={{0,1},{1,0},{2,3},{3,2},{4,5},{5,4},{6,7},{7,6},{8,9},{9,8},{10,11... | collective-permute-start | bytes 884744 | tf_op jit(solution)/shard_map/ppermute | solution.py:179
  98.6 17.8 %collective-permute-start.8 = (bf16[128,1152]{1,0:T(8,128)(2,1)S(1)}, bf16[128,1152]{1,0:T(8,128)(2,1)}, u32[]{:S(2)}, u32[]{:S(2)}) collective-permute-start(bf16[128,1152]{1,0:T(8,128)(2,1)S(1)} %collective-permute-done.2.refs_4_), channel_id=1, source_target_pairs={{0,1},{1,0},{2,3},{3,2},{4,5},{5,4},{6,7},{7,6},{8,9},{9,8},{10,11... | collective-permute-start | bytes 884744 | tf_op jit(solution)/shard_map/ppermute | solution.py:179
  112.0 7.6 %collective-permute-start.4 = (bf16[64,1152]{1,0:T(8,128)(2,1)S(1)}, bf16[64,1152]{1,0:T(8,128)(2,1)S(1)}, u32[]{:S(2)}, u32[]{:S(2)}) collective-permute-start(bf16[64,1152]{1,0:T(8,128)(2,1)S(1)} %collective-permute-done.1.one_ref), channel_id=1, source_target_pairs={{0,1},{1,0},{2,3},{3,2},{4,5},{5,4},{6,7},{7,6},{8,9},{9,8},{10,11... | collective-permute-start | bytes 442376 | tf_op jit(solution)/shard_map/ppermute | solution.py:179
  114.4 5.2 %collective-permute-start.5 = (bf16[64,1152]{1,0:T(8,128)(2,1)S(1)}, bf16[64,1152]{1,0:T(8,128)(2,1)S(1)}, u32[]{:S(2)}, u32[]{:S(2)}) collective-permute-start(bf16[64,1152]{1,0:T(8,128)(2,1)S(1)} %collective-permute-done.3.two_ref), channel_id=1, source_target_pairs={{0,1},{1,0},{2,3},{3,2},{4,5},{5,4},{6,7},{7,6},{8,9},{9,8},{10,11... | collective-permute-start | bytes 442376 | tf_op jit(solution)/shard_map/ppermute | solution.py:179
  149.9 17.9 %copy-start = (bf16[1152,1152]{1,0:T(8,128)(2,1)S(1)}, bf16[1152,1152]{1,0:T(8,128)(2,1)}, u32[]{:S(2)}) copy-start(bf16[1152,1152]{1,0:T(8,128)(2,1)} %out_table_ref.1) | copy-start | bytes 7962628
Sparse Core Ops, SparseCore 0:
  50.5 80.7 all-gather.2

commit v3 on v2

v3 whole, which is shorter than its diff:
```python
import functools
import math

import jax
import jax.numpy as jnp
from jax import lax
from jax.experimental import pallas as pl
from jax.experimental.pallas import tpu as pltpu
from jax.sharding import Mesh
from jax.sharding import PartitionSpec as P

HD = 72
HP = 80
LANES = 128
EPS = 1e-06
EXP2_SCALE = HD ** (-0.5) * math.log2(math.e)
NT = (((1,), (1,)), ((), ()))
TN = (((0,), (0,)), ((), ()))


def params(mib=48):
    return pltpu.CompilerParams(vmem_limit_bytes=mib * 1024 * 1024)


def whole():
    return pl.BlockSpec(memory_space=pltpu.VMEM)


def modulated(values, offset, stretch):
    center = jnp.mean(values, axis=-1, keepdims=True)
    values = values - center
    spread = jnp.mean(values * values, axis=-1, keepdims=True)
    return (values * lax.rsqrt(spread + EPS) * (1.0 + stretch) + offset).astype(jnp.bfloat16)


def triples_of(rows, modulation_ref, wqk_ref, wvt_ref):
    normed = modulated(rows, modulation_ref[0, 0:1], modulation_ref[0, 1:2])
    qk = jnp.dot(normed, wqk_ref[...], preferred_element_type=jnp.float32).astype(jnp.bfloat16)
    values = lax.dot_general(wvt_ref[...], normed, NT, preferred_element_type=jnp.float32)
    index = lax.broadcasted_iota(jnp.int32, values.shape, 0)
    ones = (index == HD) | (index == HP + HD)
    return qk, jnp.where(ones, 1.0, values).astype(jnp.bfloat16)


def early_kernel(own_ref, beside_ref, near_ref, swapped_ref, modulation_ref, wqk_ref, wvt_ref, qk_ref, vt_ref):
    for index, pair in enumerate(((own_ref, beside_ref), (near_ref, swapped_ref))):
        rows = jnp.concatenate([pair[0][...], pair[1][...]], axis=0)
        qk, vt = triples_of(rows.astype(jnp.float32), modulation_ref, wqk_ref, wvt_ref)
        start = 2 * LANES * index
        qk_ref[start : start + 2 * LANES] = qk
        vt_ref[:, start : start + 2 * LANES] = vt


def frame_kernel(
    place_ref, late_ref, swapped_ref, qk_ref, vt_ref, modulation_ref, wqk_ref, wvt_ref,
    out_ref, qk_late_ref, vt_late_ref,
):
    for index, rows_ref in enumerate((late_ref, swapped_ref)):
        start = 2 * LANES * index
        qk, vt = triples_of(rows_ref[...].astype(jnp.float32), modulation_ref, wqk_ref, wvt_ref)
        qk_late_ref[start : start + 2 * LANES] = qk
        vt_late_ref[:, start : start + 2 * LANES] = vt
    parts = ((qk_ref, vt_ref), (qk_late_ref, vt_late_ref))
    blocks = (
        ((qk_ref, 0), (qk_ref, 64), (qk_ref, 128), (qk_ref, 192)),
        ((qk_ref, 256), (qk_late_ref, 128), (qk_ref, 384), (qk_late_ref, 384)),
        ((qk_late_ref, 192), (qk_ref, 320), (qk_late_ref, 448), (qk_ref, 448)),
        ((qk_late_ref, 0), (qk_late_ref, 64), (qk_late_ref, 256), (qk_late_ref, 320)),
    )
    for number, block in enumerate(blocks):
        outs = []
        for head in range(2):
            column = 2 * LANES * head
            queries = jnp.concatenate(
                [ref[start : start + 64, column : column + LANES] for ref, start in block], axis=0
            )
            scores = [
                lax.dot_general(
                    qk[:, column + LANES : column + 2 * LANES], queries, NT,
                    preferred_element_type=jnp.float32,
                )
                for qk, _ in parts
            ]
            largest = jnp.maximum(*[jnp.max(part, axis=0, keepdims=True) for part in scores])
            mixed = sum(
                jnp.dot(
                    vt[HP * head : HP * head + HP],
                    jnp.exp2((part - largest) * EXP2_SCALE).astype(jnp.bfloat16),
                    preferred_element_type=jnp.float32,
                )
                for part, (_, vt) in zip(scores, parts)
            )
            outs.append(mixed[:HD] / mixed[HD : HD + 1])
        both = jnp.concatenate(outs, axis=0).astype(jnp.bfloat16)
        for part in range(2):
            out_ref[place_ref[2 * number + part]] = both[:, part * LANES : (part + 1) * LANES]


def join_kernel(mixed_ref, tokens_ref, out_ref):
    width = tokens_ref.shape[1]
    mixed = mixed_ref[...].reshape(-1, LANES).astype(jnp.float32)
    out_ref[:, :width] = mixed.T.astype(jnp.bfloat16)
    out_ref[:, width:] = tokens_ref[...]


def time_kernel(
    positions, place_ref, joined_ref, tables_ref, all_ref, out_table_ref, modulation_ref, out_ref,
    middle_ref, input_ref, mixed_ref, frame_table_ref, time_table_ref, frame_sem, time_sem,
):
    step = pl.program_id(0)
    rows, width = input_ref.shape
    zh, zl = place_ref[8], place_ref[9]
    time_copy = pltpu.make_async_copy(out_table_ref, time_table_ref, time_sem)

    @pl.when(step == 0)
    def _():
        frame_copies = [
            pltpu.make_async_copy(
                all_ref.at[pl.ds(0, 9), core, pl.ds(LANES + 16 * slot, 16), :],
                frame_table_ref.at[2 * ((zh + 4 - slot) % 4) + core],
                frame_sem.at[2 * slot + core],
            )
            for slot in range(4)
            for core in range(2)
        ]
        for copy in frame_copies:
            copy.start()
        time_copy.start()
        for copy in frame_copies:
            copy.wait()
        table = frame_table_ref[...].reshape(width, width)
        branch = jnp.dot(joined_ref[:, :width], table, preferred_element_type=jnp.float32)
        middle = joined_ref[:, width:].astype(jnp.float32) + modulation_ref[0, 2:3] * branch
        middle = middle.astype(jnp.bfloat16)
        middle_ref[...] = middle
        input_ref[...] = modulated(
            middle.astype(jnp.float32), modulation_ref[1, 0:1], modulation_ref[1, 1:2]
        )

    @pl.when(step > 0)
    def _():
        one = lax.broadcasted_iota(jnp.int32, (rows, rows), 0) % positions
        two = lax.broadcasted_iota(jnp.int32, (rows, rows), 1) % positions
        same = one == two
        triples = []
        for head in range(4):
            table = tables_ref[0, 0:7, 32 * head : 32 * head + 32].reshape(7 * 32, width)
            triples.append(
                lax.dot_general(table, input_ref[...], NT, preferred_element_type=jnp.float32)
            )
        scores = []
        for triple in triples:
            queries = triple[:HD].astype(jnp.bfloat16)
            keys = triple[HD : 2 * HD].astype(jnp.bfloat16)
            part = lax.dot_general(keys, queries, TN, preferred_element_type=jnp.float32)
            scores.append(jnp.where(same, part, -1e30))
        raised = [
            jnp.exp2((part - jnp.max(part, axis=0, keepdims=True)) * EXP2_SCALE) for part in scores
        ]
        for head in range(4):
            values = jnp.concatenate([triples[head][2 * HD : 192], triples[head][200:]], axis=0)
            total = jnp.sum(raised[head], axis=0, keepdims=True)
            mixed = jnp.dot(
                values.astype(jnp.bfloat16), raised[head].astype(jnp.bfloat16),
                preferred_element_type=jnp.float32,
            )
            mixed_ref[(step - 1) * 4 + (zl + 4 - head) % 4] = mixed / total

    @pl.when(step == pl.num_programs(0) - 1)
    def _():
        time_copy.wait()
        mixed = mixed_ref[...].reshape(-1, rows).astype(jnp.bfloat16)
        branch = lax.dot_general(mixed, time_table_ref[...], TN, preferred_element_type=jnp.float32)
        out_ref[...] = (
            middle_ref[...].astype(jnp.float32) + modulation_ref[1, 2:3] * branch
        ).astype(jnp.bfloat16)


def rotation(count, by):
    return [(index, (index + by) % count) for index in range(count)]


SWAP = [(0, 1), (1, 0)]


def shards(tokens, frame_qkv, frame_out, time_qkv, time_out, modulation):
    tokens = tokens[0]
    rows, width = tokens.shape
    half = rows // 2
    zh, zl, core = lax.axis_index("zh"), lax.axis_index("zl"), lax.axis_index("c")

    def along(array, axis, by):
        return lax.ppermute(array, axis, rotation(4, by))

    def swapped(array):
        return lax.ppermute(array, "c", SWAP)

    index = lax.axis_index("y") * 2 + core
    time_part = lax.dynamic_slice_in_dim(time_qkv, jnp.minimum(index * 32, 216 - 32), 32, 0)
    index = lax.axis_index("x") * 4 + lax.axis_index("y")
    out_part = lax.dynamic_slice_in_dim(frame_out, jnp.minimum(index, 8) * 16, 16, 0)

    beside = swapped(tokens)
    below = along(jnp.concatenate([tokens[:half], out_part], axis=0), "zh", 1)
    above = along(jnp.concatenate([tokens[half:], out_part], axis=0), "zh", 3)
    near = jnp.concatenate([below[:half], above[:half]], axis=0)
    far_top, far_bottom = along(below[:half], "zh", 1), along(above[:half], "zh", 3)
    below_bottom, above_top = along(tokens[half:], "zh", 1), along(tokens[:half], "zh", 3)
    late = jnp.concatenate([far_top, far_bottom, below_bottom, above_top], axis=0)

    parts = [time_part] + [along(time_part, "zl", by) for by in (1, 2, 3)]
    parts += [out_part, below[half:], along(out_part, "zh", 2), above[half:]]
    tables = lax.all_gather(jnp.concatenate(parts, axis=0), ("x", "y", "c"), axis=0)
    tables = tables.reshape(4, 8, 192, width)

    spots = [zh, (zh + 3) % 4, (zh + 1) % 4, (zh + 2) % 4]
    place = [spot * 2 + side for spot in spots for side in (core, 1 - core)]
    place = jnp.stack(place + [zh, zl]).astype(jnp.int32)

    heads = frame_qkv.reshape(width, 2, 3, HD)
    wqk = jnp.pad(heads[:, :, :2], ((0, 0), (0, 0), (0, 0), (0, LANES - HD))).reshape(width, 4 * LANES)
    wvt = jnp.pad(jnp.transpose(heads[:, :, 2], (1, 2, 0)), ((0, 0), (0, HP - HD), (0, 0)))
    wvt = wvt.reshape(2 * HP, width)

    count = 4 * rows
    shapes = (
        jax.ShapeDtypeStruct((count, 4 * LANES), jnp.bfloat16),
        jax.ShapeDtypeStruct((2 * HP, count), jnp.bfloat16),
    )
    qk, vt = pl.pallas_call(
        early_kernel,
        out_shape=shapes,
        in_specs=[whole()] * 7,
        out_specs=(whole(), whole()),
        compiler_params=params(),
        cost_estimate=pl.CostEstimate(flops=10**9, bytes_accessed=5 * 10**6, transcendentals=0),
        name="early_triples",
    )(tokens, beside, near, swapped(near), modulation, wqk, wvt)

    mixed = pl.pallas_call(
        frame_kernel,
        out_shape=jax.ShapeDtypeStruct((2 * count // LANES, 2 * HD, LANES), jnp.bfloat16),
        in_specs=[pl.BlockSpec(memory_space=pltpu.SMEM)] + [whole()] * 7,
        out_specs=whole(),
        scratch_shapes=[pltpu.VMEM(shape.shape, shape.dtype) for shape in shapes],
        compiler_params=params(),
        name="frame_attention",
    )(place, late, swapped(late), qk, vt, modulation, wqk, wvt)

    mixed = lax.all_to_all(mixed, ("zh", "c"), 0, 0, tiled=True)
    joined = pl.pallas_call(
        join_kernel,
        out_shape=jax.ShapeDtypeStruct((rows, 2 * width), jnp.bfloat16),
        in_specs=[whole(), whole()],
        out_specs=whole(),
        compiler_params=params(),
        name="join",
    )(mixed, tokens)
    joined = lax.all_to_all(joined, ("x", "zl"), 0, 0, tiled=True)

    out = pl.pallas_call(
        functools.partial(time_kernel, rows // 16),
        grid=(5,),
        out_shape=jax.ShapeDtypeStruct((rows, width), jnp.bfloat16),
        in_specs=[
            pl.BlockSpec(memory_space=pltpu.SMEM),
            whole(),
            pl.BlockSpec((1, 8, LANES, width), lambda i: (jnp.maximum(i - 1, 0), 0, 0, 0)),
            pl.BlockSpec(memory_space=pl.ANY),
            pl.BlockSpec(memory_space=pl.ANY),
            whole(),
        ],
        out_specs=whole(),
        scratch_shapes=[
            pltpu.VMEM((rows, width), jnp.bfloat16),
            pltpu.VMEM((rows, width), jnp.bfloat16),
            pltpu.VMEM((16, HD, rows), jnp.float32),
            pltpu.VMEM((8, 9, 16, width), jnp.bfloat16),
            pltpu.VMEM((width, width), jnp.bfloat16),
            pltpu.SemaphoreType.DMA((8,)),
            pltpu.SemaphoreType.DMA,
        ],
        compiler_params=params(),
        name="time_block",
    )(place, joined, tables, tables.reshape(16, 2, 192, width), time_out, modulation)
    out = lax.all_to_all(out, ("x", "zl"), 0, 0, tiled=True)
    return out[None]


def solution(mesh):
    fine = Mesh(mesh.devices.reshape(4, 4, 4, 4, 2), ("y", "x", "zl", "zh", "c"))
    frames, space = ("y", "x", "zl"), ("zh", "c")
    placed = (
        P(frames, space, None),
        P(None, space),
        P(space, None),
        P(("x", "zl"), None),
        P(),
        P("y", None, None),
    )
    return jax.shard_map(
        shards,
        mesh=fine,
        in_specs=placed,
        out_specs=P(frames, space, None),
        check_vma=False,
    )
```

time: 199 us -> 198 us (level)
  starting transfers between devices: 72.9 us -> 59.2 us
  waiting for transfers between devices: 21.9 us -> 34.5 us
  blocking collectives: 53.2 us -> 56.6 us
  local copies, waits for them, and re-layouts: 15.5 us -> 12.3 us
    ppermute x10, waiting for transfers between devices: 21.9 us -> 34 us  [along(): return lax.ppermute(array, axis, rotation(4, by))]
    ppermute x10, starting transfers between devices: 58.6 us -> 51.5 us  [along(): return lax.ppermute(array, axis, rotation(4, by))]
    ppermute x5 -> x3, starting transfers between devices: 14.3 us -> 7.75 us  [swapped(): return lax.ppermute(array, 'c', SWAP)]
    all_to_all x1, blocking collectives: 14.8 us -> 21 us  [shards(): joined = lax.all_to_all(joined, ('x', 'zl'), 0, 0, tiled=True)]
    all_to_all x1, blocking collectives: 24.6 us -> 21.4 us  [shards(): mixed = lax.all_to_all(mixed, ('zh', 'c'), 0, 0, tiled=True)]
    reshape x1, local copies, waits for them, and re-layouts: 3.14 us -> 0.49 us  [shards(): jnp.pad(heads[:, :, :2], ((0, 0), (0, 0), (0, 0), (0, LANES - HD)))]
    unnamed x20 -> x27, local copies, waits for them, and re-layouts: 6.73 us -> 7.33 us
  transfers between devices with their start and end apart: 16 -> 14, of which waited for: 5 -> 5; matrix products, arithmetic and copies ran while one was open for 6% -> 5% of each run, Pallas kernels for 5% -> 5%
where the time goes in v3:
time: 198 us; the launch traced here: 196 us
  starting transfers between devices  59.2 us (30%)
  blocking collectives  56.6 us (29%)
  waiting for transfers between devices  34.5 us (17%)
  Pallas kernels  20 us (10%)
  between operations  13.8 us (7%)
  local copies, waits for them, and re-layouts  12.3 us (6%)
    ppermute x10, starting transfers between devices, along(): return lax.ppermute(array, axis, rotation(4, by))  51.5 us
    ppermute x10, waiting for transfers between devices, along(): return lax.ppermute(array, axis, rotation(4, by))  34 us
    all_to_all x1, blocking collectives, shards(): mixed = lax.all_to_all(mixed, ('zh', 'c'), 0, 0, tiled=True)  21.4 us
    all_to_all x1, blocking collectives, shards(): joined = lax.all_to_all(joined, ('x', 'zl'), 0, 0, tiled=True)  21 us
    all_to_all x1, blocking collectives, shards(): out = lax.all_to_all(out, ('x', 'zl'), 0, 0, tiled=True)  14.1 us
    pallas_call x1, Pallas kernels, shards(): pl.pallas_call(functools.partial(time_kernel, rows // 16), grid=(5,), out...  10.5 us
    ppermute x3, starting transfers between devices, swapped(): return lax.ppermute(array, 'c', SWAP)  7.75 us
    unnamed x27, local copies, waits for them, and re-layouts  7.33 us
  transfers between devices with their start and end apart: 14, of which 5 were waited for; matrix products, arithmetic and copies ran while one was open for 5% of the time, Pallas kernels for 5%

profile of v3, /device:TPU:1, one launch (start us, length us, event | category | flops | bytes accessed | tf_op | source)
XLA Modules:
  0.0 196.5 jit_solution(5147303918905174168)
XLA Ops:
  6.5 0.9 constant_dynamic-update-slice_fusion.9
  7.5 4.4 %collective-permute-start.9 = (bf16[32,1152]{1,0:T(8,128)(2,1)S(1)}, bf16[32,1152]{1,0:T(8,128)(2,1)S(1)}, u32[]{:S(2)}, u32[]{:S(2)}) collective-permute-start(bf16[32,1152]{1,0:T(8,128)(2,1)S(1)} %get-tuple-element.12), channel_id=1, source_target_pairs={{0,8},{8,16},{16,24},{24,0},{1,9},{9,17},{17,25},{25,1},{2,10},{10... | collective-permute-start | bytes 221192 | tf_op jit(solution)/shard_map/ppermute | solution.py:193
  11.8 4.9 %collective-permute-start.10 = (bf16[32,1152]{1,0:T(8,128)(2,1)S(1)}, bf16[32,1152]{1,0:T(8,128)(2,1)S(1)}, u32[]{:S(2)}, u32[]{:S(2)}) collective-permute-start(bf16[32,1152]{1,0:T(8,128)(2,1)S(1)} %get-tuple-element.12), channel_id=1, source_target_pairs={{0,16},{8,24},{16,0},{24,8},{1,17},{9,25},{17,1},{25,9},{2,18},{10... | collective-permute-start | bytes 221192 | tf_op jit(solution)/shard_map/ppermute | solution.py:193
  16.7 2.6 %collective-permute-start.11 = (bf16[32,1152]{1,0:T(8,128)(2,1)S(1)}, bf16[32,1152]{1,0:T(8,128)(2,1)S(1)}, u32[]{:S(2)}, u32[]{:S(2)}) collective-permute-start(bf16[32,1152]{1,0:T(8,128)(2,1)S(1)} %get-tuple-element.12), channel_id=1, source_target_pairs={{0,24},{8,0},{16,8},{24,16},{1,25},{9,1},{17,9},{25,17},{2,26},{10... | collective-permute-start | bytes 221192 | tf_op jit(solution)/shard_map/ppermute | solution.py:193
  19.4 1.0 slice_bitcast_fusion.1
  20.4 0.0 copy-start.1
  20.4 0.0 copy-start.4
  20.5 0.0 collective-permute-done.10
  20.5 2.8 %collective-permute-done.11 = bf16[32,1152]{1,0:T(8,128)(2,1)S(1)} collective-permute-done((bf16[32,1152]{1,0:T(8,128)(2,1)S(1)}, bf16[32,1152]{1,0:T(8,128)(2,1)S(1)}, u32[]{:S(2)}, u32[]{:S(2)}) %collective-permute-start.11) | collective-permute-done | bytes 73760 | tf_op jit(solution)/shard_map/ppermute | solution.py:193
  23.3 0.8 constant_dynamic-update-slice_fusion.5
  24.1 7.3 %collective-permute-start = (bf16[80,1152]{1,0:T(8,128)(2,1)S(1)}, bf16[80,1152]{1,0:T(8,128)(2,1)S(1)}, u32[]{:S(2)}, u32[]{:S(2)}) collective-permute-start(bf16[80,1152]{1,0:T(8,128)(2,1)S(1)} %get-tuple-element.16), channel_id=1, source_target_pairs={{0,2},{2,4},{4,6},{6,0},{1,3},{3,5},{5,7},{7,1},{8,10},{10,12},{12... | collective-permute-start | bytes 552968 | tf_op jit(solution)/shard_map/ppermute | solution.py:193
  31.5 8.7 %collective-permute-start.12 = (bf16[16,1152]{1,0:T(8,128)(2,1)S(1)}, bf16[16,1152]{1,0:T(8,128)(2,1)S(1)}, u32[]{:S(2)}, u32[]{:S(2)}) collective-permute-start(bf16[16,1152]{1,0:T(8,128)(2,1)S(1)} %get-tuple-element.10), channel_id=1, source_target_pairs={{0,4},{2,6},{4,0},{6,2},{1,5},{3,7},{5,1},{7,3},{8,12},{10,14},{12... | collective-permute-start | bytes 110600 | tf_op jit(solution)/shard_map/ppermute | solution.py:193
  40.2 5.2 %collective-permute-start.2 = (bf16[80,1152]{1,0:T(8,128)(2,1)S(1)}, bf16[80,1152]{1,0:T(8,128)(2,1)S(1)}, u32[]{:S(2)}, u32[]{:S(2)}) collective-permute-start(bf16[80,1152]{1,0:T(8,128)(2,1)S(1)} %get-tuple-element.15), channel_id=1, source_target_pairs={{0,6},{2,0},{4,2},{6,4},{1,7},{3,1},{5,3},{7,5},{8,14},{10,8},{12,... | collective-permute-start | bytes 552968 | tf_op jit(solution)/shard_map/ppermute | solution.py:193
  45.4 3.8 %collective-permute-done.12 = bf16[16,1152]{1,0:T(8,128)(2,1)S(1)} collective-permute-done((bf16[16,1152]{1,0:T(8,128)(2,1)S(1)}, bf16[16,1152]{1,0:T(8,128)(2,1)S(1)}, u32[]{:S(2)}, u32[]{:S(2)}) %collective-permute-start.12) | collective-permute-done | bytes 36896 | tf_op jit(solution)/shard_map/ppermute | solution.py:193
  49.2 15.5 %collective-permute-done.2 = bf16[80,1152]{1,0:T(8,128)(2,1)S(1)} collective-permute-done((bf16[80,1152]{1,0:T(8,128)(2,1)S(1)}, bf16[80,1152]{1,0:T(8,128)(2,1)S(1)}, u32[]{:S(2)}, u32[]{:S(2)}) %collective-permute-start.2) | collective-permute-done | bytes 184352 | tf_op jit(solution)/shard_map/ppermute | solution.py:193
  64.6 0.8 copy-done.5
  65.4 0.0 all-gather.3.cloned.1.call-update
  65.5 3.5 %collective-permute-start.1 = (bf16[64,1152]{1,0:T(8,128)(2,1)S(1)}, bf16[64,1152]{1,0:T(8,128)(2,1)}, u32[]{:S(2)}, u32[]{:S(2)}) collective-permute-start(bf16[64,1152]{1,0:T(8,128)(2,1)S(1)} %slice.44), channel_id=1, source_target_pairs={{0,2},{2,4},{4,6},{6,0},{1,3},{3,5},{5,7},{7,1},{8,10},{10,12},{12... | collective-permute-start | bytes 442376 | tf_op jit(solution)/shard_map/ppermute | solution.py:193
  69.0 6.4 %collective-permute-start.4 = (bf16[64,1152]{1,0:T(8,128)(2,1)S(1)}, bf16[64,1152]{1,0:T(8,128)(2,1)}, u32[]{:S(2)}, u32[]{:S(2)}) collective-permute-start(bf16[64,1152]{1,0:T(8,128)(2,1)S(1)} %get-tuple-element.13), channel_id=1, source_target_pairs={{0,2},{2,4},{4,6},{6,0},{1,3},{3,5},{5,7},{7,1},{8,10},{10,12},{12... | collective-permute-start | bytes 442376 | tf_op jit(solution)/shard_map/ppermute | solution.py:193
  75.4 2.8 %collective-permute-start.5 = (bf16[64,1152]{1,0:T(8,128)(2,1)S(1)}, bf16[64,1152]{1,0:T(8,128)(2,1)}, u32[]{:S(2)}, u32[]{:S(2)}) collective-permute-start(bf16[64,1152]{1,0:T(8,128)(2,1)S(1)} %get-tuple-element.14), channel_id=1, source_target_pairs={{0,6},{2,0},{4,2},{6,4},{1,7},{3,1},{5,3},{7,5},{8,14},{10,8},{12,... | collective-permute-start | bytes 442376 | tf_op jit(solution)/shard_map/ppermute | solution.py:193
  78.2 3.4 %collective-permute-start.7 = (bf16[128,1152]{1,0:T(8,128)(2,1)S(1)}, bf16[128,1152]{1,0:T(8,128)(2,1)}, u32[]{:S(2)}, u32[]{:S(2)}) collective-permute-start(bf16[128,1152]{1,0:T(8,128)(2,1)S(1)} %bitcast.33), channel_id=1, source_target_pairs={{0,1},{1,0},{2,3},{3,2},{4,5},{5,4},{6,7},{7,6},{8,9},{9,8},{10,11... | collective-permute-start | bytes 884744 | tf_op jit(solution)/shard_map/ppermute | solution.py:196
  81.7 0.1 slice.46
  81.7 2.1 %copy.12 = bf16[1152,2,2,72]{3,2,1,0:T(2,128)(2,1)S(1)} copy(bf16[1152,2,2,72]{0,3,2,1:T(8,128)(2,1)S(1)} %slice.46) | data formatting | bytes 1327104
  83.9 1.3 pad.8
  85.2 0.5 reshape.20.wqk_ref
  85.7 5.7 %collective-permute-start.3 = (bf16[64,1152]{1,0:T(8,128)(2,1)S(1)}, bf16[64,1152]{1,0:T(8,128)(2,1)S(1)}, u32[]{:S(2)}, u32[]{:S(2)}) collective-permute-start(bf16[64,1152]{1,0:T(8,128)(2,1)S(1)} %slice.45), channel_id=1, source_target_pairs={{0,6},{2,0},{4,2},{6,4},{1,7},{3,1},{5,3},{7,5},{8,14},{10,8},{12,... | collective-permute-start | bytes 442376 | tf_op jit(solution)/shard_map/ppermute | solution.py:193
  91.4 0.9 constant_dynamic-update-slice_fusion.3
  92.3 11.9 %collective-permute-done.3 = bf16[64,1152]{1,0:T(8,128)(2,1)S(1)} collective-permute-done((bf16[64,1152]{1,0:T(8,128)(2,1)S(1)}, bf16[64,1152]{1,0:T(8,128)(2,1)S(1)}, u32[]{:S(2)}, u32[]{:S(2)}) %collective-permute-start.3) | collective-permute-done | bytes 147488 | tf_op jit(solution)/shard_map/ppermute | solution.py:193
  104.3 0.9 constant_dynamic-update-slice_fusion.1
  105.2 0.0 copy-start.6
  105.2 0.0 collective-permute-done.5
  105.2 0.9 constant_dynamic-update-slice_fusion.late_ref
  106.1 2.3 %collective-permute-start.6 = (bf16[256,1152]{1,0:T(8,128)(2,1)S(1)}, bf16[256,1152]{1,0:T(8,128)(2,1)S(1)}, u32[]{:S(2)}, u32[]{:S(2)}) collective-permute-start(bf16[256,1152]{1,0:T(8,128)(2,1)S(1)} %constant_dynamic-update-slice_fusion.late_ref), channel_id=1, source_target_pairs={{0,1},{1,0},{2,3},{3,2},{4,5},{5,4},{6,7},{7,6},{8,9},{9,8},{10,11... | collective-permute-start | bytes 1769480 | tf_op jit(solution)/shard_map/ppermute | solution.py:196
  108.5 2.0 %collective-permute-start.8 = (bf16[128,1152]{1,0:T(8,128)(2,1)S(1)}, bf16[128,1152]{1,0:T(8,128)(2,1)}, u32[]{:S(2)}, u32[]{:S(2)}) collective-permute-start(bf16[128,1152]{1,0:T(8,128)(2,1)S(1)} %pad_maximum_fusion.near_ref), channel_id=1, source_target_pairs={{0,1},{1,0},{2,3},{3,2},{4,5},{5,4},{6,7},{7,6},{8,9},{9,8},{10,11... | collective-permute-start | bytes 884744 | tf_op jit(solution)/shard_map/ppermute | solution.py:196
  110.5 1.1 slice_bitcast_fusion
  111.7 0.0 copy-start.2
  111.7 0.1 stack.43.place_ref
  111.8 0.0 collective-permute-done.7.beside_ref
  111.8 0.5 collective-permute-done.8.swapped_ref
  112.3 2.6 %early_triples.1 = (bf16[512,512]{1,0:T(8,128)(2,1)S(1)}, bf16[160,512]{1,0:T(8,128)(2,1)S(1)}) custom-call(bf16[128,1152]{1,0:T(8,128)(2,1)S(1)} %bitcast.34, bf16[128,1152]{1,0:T(8,128)(2,1)} %collective-permute-done.7.beside_ref, bf16[128,1152]{1,0:T(8,128)(2,1)S(1)} %pad_maximum_fusion.near_ref, bf16[128,1152]{1,0:T(8,128)(2,1)} %collective-permute-done.8.swapped_ref, ...), custom_call_target="tpu_custom_call" | custom-call | flops 1000000000 | bytes 5000000 | tf_op jit(solution)/shard_map/early_triples/pallas_call | solution.py:230
  114.9 6.7 %frame_attention.1 = bf16[8,144,128]{2,1,0:T(8,128)(2,1)S(1)} custom-call(s32[10]{0:T(128)S(1)} %stack.43.place_ref, bf16[256,1152]{1,0:T(8,128)(2,1)S(1)} %constant_dynamic-update-slice_fusion.late_ref, bf16[256,1152]{1,0:T(8,128)(2,1)S(1)} %collective-permute-done.6.swapped_ref, bf16[512,512]{1,0:T(8,128)(2,1)S(1)} %get-tuple-element.7.qk_ref, ...), custom_call_target="tpu_custom_call" | custom-call | tf_op jit(solution)/shard_map/frame_attention/pallas_call | solution.py:240
  121.6 0.0 copy-start
  121.6 21.4 %all_to_all.25.mixed_ref = bf16[8,144,128]{2,1,0:T(8,128)(2,1)S(1)} all-to-all(bf16[8,144,128]{2,1,0:T(8,128)(2,1)S(1)} %frame_attention.1), channel_id=1, replica_groups=mesh['y'=4,'x'=4,'zl'=4,'zh'=4,'c'=2] {'zh','c'}, dimensions={0} | all-to-all | bytes 589824 | tf_op jit(solution)/shard_map/all_to_all | solution.py:250
  143.1 0.2 join.1
  143.2 21.0 %all_to_all.26 = bf16[16,8,2304]{2,1,0:T(8,128)(2,1)S(1)} all-to-all(bf16[16,8,2304]{2,1,0:T(8,128)(2,1)S(1)} %bitcast.29), channel_id=1, replica_groups=mesh['y'=4,'x'=4,'zl'=4,'zh'=4,'c'=2] {'x','zl'}, dimensions={0} | all-to-all | bytes 1179648 | tf_op jit(solution)/shard_map/all_to_all | solution.py:259
  164.2 10.5 %time_block.1 = bf16[128,1152]{1,0:T(8,128)(2,1)S(1)} custom-call(s32[10]{0:T(128)S(1)} %stack.43.place_ref, bf16[128,2304]{1,0:T(8,128)(2,1)S(1)} %bitcast.30, bf16[4,8,192,1152]{3,2,1,0:T(8,128)(2,1)} %bitcast.37, bf16[16,2,192,1152]{3,2,1,0:T(8,128)(2,1)} %bitcast.38, bf16[1152,1152]{1,0:T(8,128)(2,1)S(1)} %copy-done, f32[2,3,1152]{2,1,0:T(4,128)S(1)} %copy-done.3), custom_call_target="tpu_custom_call" | custom-call | tf_op jit(solution)/shard_map/time_block/pallas_call | solution.py:261
  174.8 14.1 %all_to_all.27 = bf16[16,8,1152]{2,1,0:T(8,128)(2,1)S(1)} all-to-all(bf16[16,8,1152]{2,1,0:T(8,128)(2,1)S(1)} %bitcast.36), channel_id=1, replica_groups=mesh['y'=4,'x'=4,'zl'=4,'zh'=4,'c'=2] {'x','zl'}, dimensions={0} | all-to-all | bytes 589824 | tf_op jit(solution)/shard_map/all_to_all | solution.py:286
  188.9 0.7 copy.25
  (28 shorter events, 0.2 us)
Async XLA Ops:
  6.5 157.7 %all-gather.3.cloned.1.call-start = ((), (), s32[]{:S(2)}) async-start(), calls=%async_computation.3 | async-start | bytes 14598144 | tf_op jit(solution)/shard_map/all_gather | solution.py:213
  7.5 13.0 %collective-permute-start.9 = (bf16[32,1152]{1,0:T(8,128)(2,1)S(1)}, bf16[32,1152]{1,0:T(8,128)(2,1)S(1)}, u32[]{:S(2)}, u32[]{:S(2)}) collective-permute-start(bf16[32,1152]{1,0:T(8,128)(2,1)S(1)} %get-tuple-element.12), channel_id=1, source_target_pairs={{0,8},{8,16},{16,24},{24,0},{1,9},{9,17},{17,25},{25,1},{2,10},{10... | collective-permute-start | bytes 221192 | tf_op jit(solution)/shard_map/ppermute | solution.py:193
  11.8 8.6 %collective-permute-start.10 = (bf16[32,1152]{1,0:T(8,128)(2,1)S(1)}, bf16[32,1152]{1,0:T(8,128)(2,1)S(1)}, u32[]{:S(2)}, u32[]{:S(2)}) collective-permute-start(bf16[32,1152]{1,0:T(8,128)(2,1)S(1)} %get-tuple-element.12), channel_id=1, source_target_pairs={{0,16},{8,24},{16,0},{24,8},{1,17},{9,25},{17,1},{25,9},{2,18},{10... | collective-permute-start | bytes 221192 | tf_op jit(solution)/shard_map/ppermute | solution.py:193
  16.7 6.6 %collective-permute-start.11 = (bf16[32,1152]{1,0:T(8,128)(2,1)S(1)}, bf16[32,1152]{1,0:T(8,128)(2,1)S(1)}, u32[]{:S(2)}, u32[]{:S(2)}) collective-permute-start(bf16[32,1152]{1,0:T(8,128)(2,1)S(1)} %get-tuple-element.12), channel_id=1, source_target_pairs={{0,24},{8,0},{16,8},{24,16},{1,25},{9,1},{17,9},{25,17},{2,26},{10... | collective-permute-start | bytes 221192 | tf_op jit(solution)/shard_map/ppermute | solution.py:193
  20.4 57.8 %copy-start.1 = (bf16[1,128,1152]{2,1,0:T(8,128)(2,1)S(1)}, bf16[1,128,1152]{2,1,0:T(8,128)(2,1)}, u32[]{:S(2)}) copy-start(bf16[1,128,1152]{2,1,0:T(8,128)(2,1)} %param.6) | copy-start | bytes 884740
  20.4 61.3 %copy-start.4 = (bf16[1152,432]{0,1:T(8,128)(2,1)S(1)}, bf16[1152,432]{0,1:T(8,128)(2,1)}, u32[]{:S(2)}) copy-start(bf16[1152,432]{0,1:T(8,128)(2,1)} %param.7) | copy-start | bytes 2985988
  24.1 21.2 %collective-permute-start = (bf16[80,1152]{1,0:T(8,128)(2,1)S(1)}, bf16[80,1152]{1,0:T(8,128)(2,1)S(1)}, u32[]{:S(2)}, u32[]{:S(2)}) collective-permute-start(bf16[80,1152]{1,0:T(8,128)(2,1)S(1)} %get-tuple-element.16), channel_id=1, source_target_pairs={{0,2},{2,4},{4,6},{6,0},{1,3},{3,5},{5,7},{7,1},{8,10},{10,12},{12... | collective-permute-start | bytes 552968 | tf_op jit(solution)/shard_map/ppermute | solution.py:193
  31.5 17.7 %collective-permute-start.12 = (bf16[16,1152]{1,0:T(8,128)(2,1)S(1)}, bf16[16,1152]{1,0:T(8,128)(2,1)S(1)}, u32[]{:S(2)}, u32[]{:S(2)}) collective-permute-start(bf16[16,1152]{1,0:T(8,128)(2,1)S(1)} %get-tuple-element.10), channel_id=1, source_target_pairs={{0,4},{2,6},{4,0},{6,2},{1,5},{3,7},{5,1},{7,3},{8,12},{10,14},{12... | collective-permute-start | bytes 110600 | tf_op jit(solution)/shard_map/ppermute | solution.py:193
  40.2 24.4 %collective-permute-start.2 = (bf16[80,1152]{1,0:T(8,128)(2,1)S(1)}, bf16[80,1152]{1,0:T(8,128)(2,1)S(1)}, u32[]{:S(2)}, u32[]{:S(2)}) collective-permute-start(bf16[80,1152]{1,0:T(8,128)(2,1)S(1)} %get-tuple-element.15), channel_id=1, source_target_pairs={{0,6},{2,0},{4,2},{6,4},{1,7},{3,1},{5,3},{7,5},{8,14},{10,8},{12,... | collective-permute-start | bytes 552968 | tf_op jit(solution)/shard_map/ppermute | solution.py:193
  64.6 0.8 copy-start.5
  65.5 25.9 %collective-permute-start.1 = (bf16[64,1152]{1,0:T(8,128)(2,1)S(1)}, bf16[64,1152]{1,0:T(8,128)(2,1)}, u32[]{:S(2)}, u32[]{:S(2)}) collective-permute-start(bf16[64,1152]{1,0:T(8,128)(2,1)S(1)} %slice.44), channel_id=1, source_target_pairs={{0,2},{2,4},{4,6},{6,0},{1,3},{3,5},{5,7},{7,1},{8,10},{10,12},{12... | collective-permute-start | bytes 442376 | tf_op jit(solution)/shard_map/ppermute | solution.py:193
  69.0 35.3 %collective-permute-start.4 = (bf16[64,1152]{1,0:T(8,128)(2,1)S(1)}, bf16[64,1152]{1,0:T(8,128)(2,1)}, u32[]{:S(2)}, u32[]{:S(2)}) collective-permute-start(bf16[64,1152]{1,0:T(8,128)(2,1)S(1)} %get-tuple-element.13), channel_id=1, source_target_pairs={{0,2},{2,4},{4,6},{6,0},{1,3},{3,5},{5,7},{7,1},{8,10},{10,12},{12... | collective-permute-start | bytes 442376 | tf_op jit(solution)/shard_map/ppermute | solution.py:193
  75.4 29.8 %collective-permute-start.5 = (bf16[64,1152]{1,0:T(8,128)(2,1)S(1)}, bf16[64,1152]{1,0:T(8,128)(2,1)}, u32[]{:S(2)}, u32[]{:S(2)}) collective-permute-start(bf16[64,1152]{1,0:T(8,128)(2,1)S(1)} %get-tuple-element.14), channel_id=1, source_target_pairs={{0,6},{2,0},{4,2},{6,4},{1,7},{3,1},{5,3},{7,5},{8,14},{10,8},{12,... | collective-permute-start | bytes 442376 | tf_op jit(solution)/shard_map/ppermute | solution.py:193
  78.2 33.6 %collective-permute-start.7 = (bf16[128,1152]{1,0:T(8,128)(2,1)S(1)}, bf16[128,1152]{1,0:T(8,128)(2,1)}, u32[]{:S(2)}, u32[]{:S(2)}) collective-permute-start(bf16[128,1152]{1,0:T(8,128)(2,1)S(1)} %bitcast.33), channel_id=1, source_target_pairs={{0,1},{1,0},{2,3},{3,2},{4,5},{5,4},{6,7},{7,6},{8,9},{9,8},{10,11... | collective-permute-start | bytes 884744 | tf_op jit(solution)/shard_map/ppermute | solution.py:196
  85.7 18.5 %collective-permute-start.3 = (bf16[64,1152]{1,0:T(8,128)(2,1)S(1)}, bf16[64,1152]{1,0:T(8,128)(2,1)S(1)}, u32[]{:S(2)}, u32[]{:S(2)}) collective-permute-start(bf16[64,1152]{1,0:T(8,128)(2,1)S(1)} %slice.45), channel_id=1, source_target_pairs={{0,6},{2,0},{4,2},{6,4},{1,7},{3,1},{5,3},{7,5},{8,14},{10,8},{12,... | collective-permute-start | bytes 442376 | tf_op jit(solution)/shard_map/ppermute | solution.py:193
  105.2 6.5 %copy-start.6 = (f32[2,3,1152]{2,0,1:T(2,128)S(1)}, f32[2,3,1152]{2,0,1:T(2,128)}, u32[]{:S(2)}) copy-start(f32[2,3,1152]{2,0,1:T(2,128)} %param.11) | copy-start | bytes 82948
  106.1 8.8 %collective-permute-start.6 = (bf16[256,1152]{1,0:T(8,128)(2,1)S(1)}, bf16[256,1152]{1,0:T(8,128)(2,1)S(1)}, u32[]{:S(2)}, u32[]{:S(2)}) collective-permute-start(bf16[256,1152]{1,0:T(8,128)(2,1)S(1)} %constant_dynamic-update-slice_fusion.late_ref), channel_id=1, source_target_pairs={{0,1},{1,0},{2,3},{3,2},{4,5},{5,4},{6,7},{7,6},{8,9},{9,8},{10,11... | collective-permute-start | bytes 1769480 | tf_op jit(solution)/shard_map/ppermute | solution.py:196
  108.5 3.7 %collective-permute-start.8 = (bf16[128,1152]{1,0:T(8,128)(2,1)S(1)}, bf16[128,1152]{1,0:T(8,128)(2,1)}, u32[]{:S(2)}, u32[]{:S(2)}) collective-permute-start(bf16[128,1152]{1,0:T(8,128)(2,1)S(1)} %pad_maximum_fusion.near_ref), channel_id=1, source_target_pairs={{0,1},{1,0},{2,3},{3,2},{4,5},{5,4},{6,7},{7,6},{8,9},{9,8},{10,11... | collective-permute-start | bytes 884744 | tf_op jit(solution)/shard_map/ppermute | solution.py:196
  111.7 3.2 %copy-start.2 = (f32[2,3,1152]{2,1,0:T(4,128)}, f32[2,3,1152]{2,1,0:T(4,128)S(1)}, u32[]{:S(2)}) copy-start(f32[2,3,1152]{2,1,0:T(4,128)S(1)} %copy.9.modulation_ref) | copy-start | bytes 82948
  121.6 42.6 %copy-start = (bf16[1152,1152]{1,0:T(8,128)(2,1)S(1)}, bf16[1152,1152]{1,0:T(8,128)(2,1)}, u32[]{:S(2)}) copy-start(bf16[1152,1152]{1,0:T(8,128)(2,1)} %out_table_ref.1) | copy-start | bytes 7962628
  143.1 21.2 %copy-start.3 = (f32[2,3,1152]{2,1,0:T(4,128)S(1)}, f32[2,3,1152]{2,1,0:T(4,128)}, u32[]{:S(2)}) copy-start(f32[2,3,1152]{2,1,0:T(4,128)} %copy-done.2) | copy-start | bytes 82948
Sparse Core Ops, SparseCore 0:
  65.6 78.9 all-gather.2

commit v4 on v3

v4 whole, which is shorter than its diff:
```python
import functools
import math

import jax
import jax.numpy as jnp
from jax import lax
from jax.experimental import pallas as pl
from jax.experimental.pallas import tpu as pltpu
from jax.sharding import Mesh
from jax.sharding import PartitionSpec as P

HD = 72
HP = 80
LANES = 128
EPS = 1e-06
EXP2_SCALE = HD ** (-0.5) * math.log2(math.e)
NT = (((1,), (1,)), ((), ()))
TN = (((0,), (0,)), ((), ()))


def params(mib=48):
    return pltpu.CompilerParams(vmem_limit_bytes=mib * 1024 * 1024)


def whole():
    return pl.BlockSpec(memory_space=pltpu.VMEM)


def modulated(values, offset, stretch):
    center = jnp.mean(values, axis=-1, keepdims=True)
    values = values - center
    spread = jnp.mean(values * values, axis=-1, keepdims=True)
    return (values * lax.rsqrt(spread + EPS) * (1.0 + stretch) + offset).astype(jnp.bfloat16)


def triples_of(rows, modulation_ref, wqk_ref, wvt_ref):
    normed = modulated(rows, modulation_ref[0, 0:1], modulation_ref[0, 1:2])
    qk = jnp.dot(normed, wqk_ref[...], preferred_element_type=jnp.float32).astype(jnp.bfloat16)
    values = lax.dot_general(wvt_ref[...], normed, NT, preferred_element_type=jnp.float32)
    index = lax.broadcasted_iota(jnp.int32, values.shape, 0)
    ones = (index == HD) | (index == HP + HD)
    return qk, jnp.where(ones, 1.0, values).astype(jnp.bfloat16)


def frame_kernel(tokens_ref, modulation_ref, wqk_ref, wvt_ref, out_ref, qk_ref, vt_ref):
    count, block = tokens_ref.shape[0], 2 * LANES
    for start in range(0, count, block):
        rows = tokens_ref[start : start + block].astype(jnp.float32)
        qk, vt = triples_of(rows, modulation_ref, wqk_ref, wvt_ref)
        qk_ref[start : start + block] = qk
        vt_ref[:, start : start + block] = vt
    for start in range(0, count, block):
        outs = []
        for head in range(2):
            column = 2 * LANES * head
            queries = qk_ref[start : start + block, column : column + LANES]
            keys = qk_ref[:, column + LANES : column + 2 * LANES]
            scores = lax.dot_general(keys, queries, NT, preferred_element_type=jnp.float32)
            largest = jnp.max(scores, axis=0, keepdims=True)
            raised = jnp.exp2((scores - largest) * EXP2_SCALE).astype(jnp.bfloat16)
            mixed = jnp.dot(
                vt_ref[HP * head : HP * head + HP], raised, preferred_element_type=jnp.float32
            )
            outs.append(mixed[:HD] / mixed[HD : HD + 1])
        both = jnp.concatenate(outs, axis=0).astype(jnp.bfloat16)
        for part in range(2):
            out_ref[start // LANES + part] = both[:, part * LANES : (part + 1) * LANES]


def join_kernel(mixed_ref, tokens_ref, out_ref):
    width = tokens_ref.shape[1]
    mixed = mixed_ref[...].reshape(-1, LANES).astype(jnp.float32)
    out_ref[:, :width] = mixed.T.astype(jnp.bfloat16)
    out_ref[:, width:] = tokens_ref[...]


def time_kernel(
    positions, joined_ref, tables_ref, all_ref, out_table_ref, modulation_ref, out_ref,
    middle_ref, input_ref, mixed_ref, frame_table_ref, time_table_ref, frame_sem, time_sem,
):
    step = pl.program_id(0)
    rows, width = input_ref.shape
    time_copy = pltpu.make_async_copy(out_table_ref, time_table_ref, time_sem)

    @pl.when(step == 0)
    def _():
        frame_copies = [
            pltpu.make_async_copy(
                all_ref.at[pl.ds(0, 9), core, pl.ds(LANES + 16 * zh, 16), :],
                frame_table_ref.at[2 * zh + core],
                frame_sem.at[2 * zh + core],
            )
            for zh in range(4)
            for core in range(2)
        ]
        for copy in frame_copies:
            copy.start()
        time_copy.start()
        for copy in frame_copies:
            copy.wait()
        table = frame_table_ref[...].reshape(width, width)
        branch = jnp.dot(joined_ref[:, :width], table, preferred_element_type=jnp.float32)
        middle = joined_ref[:, width:].astype(jnp.float32) + modulation_ref[0, 2:3] * branch
        middle = middle.astype(jnp.bfloat16)
        middle_ref[...] = middle
        input_ref[...] = modulated(
            middle.astype(jnp.float32), modulation_ref[1, 0:1], modulation_ref[1, 1:2]
        )

    @pl.when(step > 0)
    def _():
        one = lax.broadcasted_iota(jnp.int32, (rows, rows), 0) % positions
        two = lax.broadcasted_iota(jnp.int32, (rows, rows), 1) % positions
        same = one == two
        triples = []
        for head in range(4):
            table = tables_ref[0, 0:7, 32 * head : 32 * head + 32].reshape(7 * 32, width)
            triples.append(
                lax.dot_general(table, input_ref[...], NT, preferred_element_type=jnp.float32)
            )
        scores = []
        for triple in triples:
            queries = triple[:HD].astype(jnp.bfloat16)
            keys = triple[HD : 2 * HD].astype(jnp.bfloat16)
            part = lax.dot_general(keys, queries, TN, preferred_element_type=jnp.float32)
            scores.append(jnp.where(same, part, -1e30))
        raised = [
            jnp.exp2((part - jnp.max(part, axis=0, keepdims=True)) * EXP2_SCALE) for part in scores
        ]
        for head in range(4):
            values = jnp.concatenate([triples[head][2 * HD : 192], triples[head][200:]], axis=0)
            total = jnp.sum(raised[head], axis=0, keepdims=True)
            mixed = jnp.dot(
                values.astype(jnp.bfloat16), raised[head].astype(jnp.bfloat16),
                preferred_element_type=jnp.float32,
            )
            mixed_ref[(step - 1) * 4 + head] = mixed / total

    @pl.when(step == pl.num_programs(0) - 1)
    def _():
        time_copy.wait()
        mixed = mixed_ref[...].reshape(-1, rows).astype(jnp.bfloat16)
        branch = lax.dot_general(mixed, time_table_ref[...], TN, preferred_element_type=jnp.float32)
        out_ref[...] = (
            middle_ref[...].astype(jnp.float32) + modulation_ref[1, 2:3] * branch
        ).astype(jnp.bfloat16)


def shards(tokens, frame_qkv, frame_out, time_qkv, time_out, modulation):
    tokens = tokens[0]
    rows, width = tokens.shape
    core = lax.axis_index("c")
    gathered = lax.all_gather(tokens, ("zh", "c"), axis=0, tiled=True)

    index = lax.axis_index("y") * 2 + core
    time_part = lax.dynamic_slice_in_dim(time_qkv, jnp.minimum(index * 32, 216 - 32), 32, 0)
    index = lax.axis_index("x") * 4 + lax.axis_index("y")
    out_part = lax.dynamic_slice_in_dim(frame_out, jnp.minimum(index, 8) * 16, 16, 0)
    time_parts = lax.all_gather(time_part, "zl", axis=0, tiled=True)
    out_parts = lax.all_gather(out_part, "zh", axis=0, tiled=True)
    parts = jnp.concatenate([time_parts, out_parts], axis=0)
    tables = lax.all_gather(parts, ("x", "y", "c"), axis=0)
    tables = tables.reshape(4, 8, 192, width)

    heads = frame_qkv.reshape(width, 2, 3, HD)
    wqk = jnp.pad(heads[:, :, :2], ((0, 0), (0, 0), (0, 0), (0, LANES - HD))).reshape(width, 4 * LANES)
    wvt = jnp.pad(jnp.transpose(heads[:, :, 2], (1, 2, 0)), ((0, 0), (0, HP - HD), (0, 0)))
    wvt = wvt.reshape(2 * HP, width)

    total = gathered.shape[0]
    mixed = pl.pallas_call(
        frame_kernel,
        out_shape=jax.ShapeDtypeStruct((total // LANES, 2 * HD, LANES), jnp.bfloat16),
        in_specs=[whole()] * 4,
        out_specs=whole(),
        scratch_shapes=[
            pltpu.VMEM((total, 4 * LANES), jnp.bfloat16),
            pltpu.VMEM((2 * HP, total), jnp.bfloat16),
        ],
        compiler_params=params(),
        name="frame_attention",
    )(gathered, modulation, wqk, wvt)

    mixed = lax.all_to_all(mixed, ("zh", "c"), 0, 0, tiled=True)
    joined = pl.pallas_call(
        join_kernel,
        out_shape=jax.ShapeDtypeStruct((rows, 2 * width), jnp.bfloat16),
        in_specs=[whole(), whole()],
        out_specs=whole(),
        compiler_params=params(),
        name="join",
    )(mixed, tokens)
    joined = lax.all_to_all(joined, ("x", "zl"), 0, 0, tiled=True)

    out = pl.pallas_call(
        functools.partial(time_kernel, rows // 16),
        grid=(5,),
        out_shape=jax.ShapeDtypeStruct((rows, width), jnp.bfloat16),
        in_specs=[
            whole(),
            pl.BlockSpec((1, 8, LANES, width), lambda i: (jnp.maximum(i - 1, 0), 0, 0, 0)),
            pl.BlockSpec(memory_space=pl.ANY),
            pl.BlockSpec(memory_space=pl.ANY),
            whole(),
        ],
        out_specs=whole(),
        scratch_shapes=[
            pltpu.VMEM((rows, width), jnp.bfloat16),
            pltpu.VMEM((rows, width), jnp.bfloat16),
            pltpu.VMEM((16, HD, rows), jnp.float32),
            pltpu.VMEM((8, 9, 16, width), jnp.bfloat16),
            pltpu.VMEM((width, width), jnp.bfloat16),
            pltpu.SemaphoreType.DMA((8,)),
            pltpu.SemaphoreType.DMA,
        ],
        compiler_params=params(),
        name="time_block",
    )(joined, tables, tables.reshape(16, 2, 192, width), time_out, modulation)
    out = lax.all_to_all(out, ("x", "zl"), 0, 0, tiled=True)
    return out[None]


def solution(mesh):
    fine = Mesh(mesh.devices.reshape(4, 4, 4, 4, 2), ("y", "x", "zl", "zh", "c"))
    frames, space = ("y", "x", "zl"), ("zh", "c")
    placed = (
        P(frames, space, None),
        P(None, space),
        P(space, None),
        P(("x", "zl"), None),
        P(),
        P("y", None, None),
    )
    return jax.shard_map(
        shards,
        mesh=fine,
        in_specs=placed,
        out_specs=P(frames, space, None),
        check_vma=False,
    )
```

time: 198 us -> 203 us (1.025)
  blocking collectives: 56.6 us -> 124 us
  starting transfers between devices: 59.2 us -> 0.04 us
  local copies, waits for them, and re-layouts: 12.3 us -> 9.27 us
    ppermute x13 -> x0, starting transfers between devices: 59.2 us -> none  [the longest x10 51.5 us: along(): return lax.ppermute(array, axis, rotation(4, by))]
    all_gather x0 -> x2, blocking collectives: none -> 50.6 us  [the longest x1 26.7 us: shards(): time_parts = lax.all_gather(time_part, 'zl', axis=0, tiled=True)]
    all_gather x1 -> x2, waiting for transfers between devices: 0.01 us -> 34.6 us  [the longest x1 23.9 us: shards(): tables = lax.all_gather(parts, ('x', 'y', 'c'), axis=0)]
    ppermute x13 -> x0, waiting for transfers between devices: 34.4 us -> none  [the longest x10 34 us: along(): return lax.ppermute(array, axis, rotation(4, by))]
    all_to_all x1, blocking collectives: 21.4 us -> 35.1 us  [shards(): mixed = lax.all_to_all(mixed, ('zh', 'c'), 0, 0, tiled=True)]
    all_to_all x1, blocking collectives: 21 us -> 23.4 us  [shards(): joined = lax.all_to_all(joined, ('x', 'zl'), 0, 0, tiled=True)]
    unnamed x27 -> x17, local copies, waits for them, and re-layouts: 7.33 us -> 5.62 us
    pallas_call x2 -> x1, Pallas kernels: 9.34 us -> 8.52 us  [shards(): pl.pallas_call(frame_kernel, out_shape=jax.ShapeDtypeStruct((total // LAN...]
  transfers between devices with their start and end apart: 14 -> 2, of which waited for: 5 -> 2; matrix products, arithmetic and copies ran while one was open for 5% -> 3% of each run, Pallas kernels for 5% -> 4%
where the time goes in v4:
time: 203 us
  blocking collectives  124 us (61%)
  waiting for transfers between devices  35.3 us (17%)
  Pallas kernels  19.2 us (9%)
  between operations  13.5 us (7%)
  local copies, waits for them, and re-layouts  9.27 us (5%)
    all_to_all x1, blocking collectives, shards(): mixed = lax.all_to_all(mixed, ('zh', 'c'), 0, 0, tiled=True)  35.1 us
    all_gather x1, blocking collectives, shards(): time_parts = lax.all_gather(time_part, 'zl', axis=0, tiled=True)  26.7 us
    all_gather x1, blocking collectives, shards(): out_parts = lax.all_gather(out_part, 'zh', axis=0, tiled=True)  23.9 us
    all_gather x1, waiting for transfers between devices, shards(): tables = lax.all_gather(parts, ('x', 'y', 'c'), axis=0)  23.9 us
    all_to_all x1, blocking collectives, shards(): joined = lax.all_to_all(joined, ('x', 'zl'), 0, 0, tiled=True)  23.4 us
    all_to_all x1, blocking collectives, shards(): out = lax.all_to_all(out, ('x', 'zl'), 0, 0, tiled=True)  15.3 us
    all_gather x1, waiting for transfers between devices, shards(): gathered = lax.all_gather(tokens, ('zh', 'c'), axis=0, tiled=True)  10.7 us
    pallas_call x1, Pallas kernels, shards(): pl.pallas_call(functools.partial(time_kernel, rows // 16), grid=(5,), out...  10.5 us
  transfers between devices with their start and end apart: 2, of which 2 were waited for; matrix products, arithmetic and copies ran while one was open for 3% of the time, Pallas kernels for 4%

profile of v4, /device:TPU:1, one launch (start us, length us, event | category | flops | bytes accessed | tf_op | source)
XLA Modules:
  0.0 202.5 jit_solution(1632302253038819724)
XLA Ops:
  6.5 0.0 copy-start
  6.5 0.0 copy-start.6
  6.5 0.0 copy-start.5
  6.5 0.0 all-gather.5.cloned.1.call-start
  6.5 0.7 all-gather.5.cloned.1.call-update
  7.3 0.0 all-gather.7.cloned.1.call-start
  7.3 0.8 constant_dynamic-slice_fusion
  8.1 23.9 %all_gather.17 = bf16[64,1152]{1,0:T(8,128)(2,1)S(1)} all-gather(bf16[16,1152]{1,0:T(8,128)(2,1)S(1)} %constant_dynamic-slice_fusion), channel_id=1, replica_groups=mesh['y'=4,'x'=4,'zl'=4,'zh'=4,'c'=2] {'zh'}, dimensions={0}, use_global_device_ids=true | all-gather | bytes 184320 | tf_op jit(solution)/shard_map/all_gather | solution.py:160
  32.0 0.0 copy-done
  32.0 26.7 %all_gather.16 = bf16[128,1152]{1,0:T(8,128)(2,1)S(1)} all-gather(bf16[32,1152]{1,0:T(8,128)(2,1)S(1)} %constant_dynamic-slice_fusion.1), channel_id=1, replica_groups=mesh['y'=4,'x'=4,'zl'=4,'zh'=4,'c'=2] {'zl'}, dimensions={0}, use_global_device_ids=true | all-gather | bytes 368640 | tf_op jit(solution)/shard_map/all_gather | solution.py:159
  58.8 0.8 pad_maximum_fusion
  59.5 0.0 all-gather.7.cloned.1.call-update
  59.6 0.0 copy-done.6
  59.6 0.0 copy-done.5
  59.6 0.1 slice.8
  59.7 2.1 %copy.11 = bf16[1152,2,2,72]{3,2,1,0:T(2,128)(2,1)S(1)} copy(bf16[1152,2,2,72]{0,3,2,1:T(8,128)(2,1)S(1)} %slice.8) | data formatting | bytes 1327104
  61.8 1.3 pad.8
  63.1 0.5 reshape.18.wqk_ref
  63.6 1.0 slice_bitcast_fusion
  64.6 10.7 %all-gather.5.cloned.1.call-done = bf16[1,1024,1152]{2,1,0:T(8,128)(2,1)} async-done(((bf16[1,128,1152]{2,1,0:T(8,128)(2,1)}), bf16[1,1024,1152]{2,1,0:T(8,128)(2,1)}) %all-gather.5.cloned.1.call-update) | async-done | bytes 2359312 | tf_op jit(solution)/shard_map/all_gather | solution.py:153
  75.4 0.0 copy-start.2
  75.4 1.7 copy-done.2
  77.0 0.0 copy-start.4
  77.1 8.5 %frame_attention.1 = bf16[8,144,128]{2,1,0:T(8,128)(2,1)S(1)} custom-call(bf16[1024,1152]{1,0:T(8,128)(2,1)S(1)} %bitcast.16, f32[2,3,1152]{2,1,0:T(4,128)S(1)} %copy.9.modulation_ref, bf16[1152,512]{1,0:T(8,128)(2,1)S(1)} %reshape.18.wqk_ref, bf16[160,1152]{1,0:T(8,128)(2,1)S(1)} %bitcast.19), custom_call_target="tpu_custom_call" | custom-call | tf_op jit(solution)/shard_map/frame_attention/pallas_call | solution.py:171
  85.6 0.0 copy-start.1
  85.6 35.1 %all_to_all.25.mixed_ref = bf16[8,144,128]{2,1,0:T(8,128)(2,1)S(1)} all-to-all(bf16[8,144,128]{2,1,0:T(8,128)(2,1)S(1)} %frame_attention.1), channel_id=1, replica_groups=mesh['y'=4,'x'=4,'zl'=4,'zh'=4,'c'=2] {'zh','c'}, dimensions={0} | all-to-all | bytes 589824 | tf_op jit(solution)/shard_map/all_to_all | solution.py:184
  120.7 0.0 copy-done.4
  120.7 0.2 join.1
  120.9 23.4 %all_to_all.26 = bf16[16,8,2304]{2,1,0:T(8,128)(2,1)} all-to-all(bf16[16,8,2304]{2,1,0:T(8,128)(2,1)S(1)} %bitcast.17), channel_id=1, replica_groups=mesh['y'=4,'x'=4,'zl'=4,'zh'=4,'c'=2] {'x','zl'}, dimensions={0} | all-to-all | bytes 1179648 | tf_op jit(solution)/shard_map/all_to_all | solution.py:193
  144.3 23.9 %all-gather.7.cloned.1.call-done = bf16[6144,1152]{1,0:T(8,128)(2,1)} async-done(((bf16[192,1152]{1,0:T(8,128)(2,1)}), bf16[6144,1152]{1,0:T(8,128)(2,1)}) %all-gather.7.cloned.1.call-update) | async-done | bytes 14155792 | tf_op jit(solution)/shard_map/all_gather | solution.py:162
  168.2 0.0 copy-done.1
  168.2 0.0 copy-start.3
  168.2 1.1 copy-done.3
  169.2 10.5 %time_block.1 = bf16[128,1152]{1,0:T(8,128)(2,1)S(1)} custom-call(bf16[128,2304]{1,0:T(8,128)(2,1)S(1)} %bitcast.18, bf16[4,8,192,1152]{3,2,1,0:T(8,128)(2,1)} %bitcast.22, bf16[16,2,192,1152]{3,2,1,0:T(8,128)(2,1)} %bitcast.23, bf16[1152,1152]{1,0:T(8,128)(2,1)S(1)} %copy-done.1, f32[2,3,1152]{2,1,0:T(4,128)S(1)} %copy.9.modulation_ref), custom_call_target="tpu_custom_call" | custom-call | tf_op jit(solution)/shard_map/time_block/pallas_call | solution.py:195
  179.7 15.3 %all_to_all.27 = bf16[16,8,1152]{2,1,0:T(8,128)(2,1)S(1)} all-to-all(bf16[16,8,1152]{2,1,0:T(8,128)(2,1)S(1)} %bitcast.20), channel_id=1, replica_groups=mesh['y'=4,'x'=4,'zl'=4,'zh'=4,'c'=2] {'x','zl'}, dimensions={0} | all-to-all | bytes 589824 | tf_op jit(solution)/shard_map/all_to_all | solution.py:219
  195.0 0.7 copy.14
  (3 shorter events, 0.1 us)
Async XLA Ops:
  6.5 25.5 %copy-start = (bf16[216,1152]{1,0:T(8,128)(2,1)S(1)}, bf16[216,1152]{1,0:T(8,128)(2,1)}, u32[]{:S(2)}) copy-start(bf16[216,1152]{1,0:T(8,128)(2,1)} %param.9) | copy-start | bytes 1492996
  6.5 53.0 %copy-start.6 = (f32[2,3,1152]{2,0,1:T(2,128)S(1)}, f32[2,3,1152]{2,0,1:T(2,128)}, u32[]{:S(2)}) copy-start(f32[2,3,1152]{2,0,1:T(2,128)} %param.11) | copy-start | bytes 82948
  6.5 53.1 %copy-start.5 = (bf16[1152,432]{0,1:T(8,128)(2,1)S(1)}, bf16[1152,432]{0,1:T(8,128)(2,1)}, u32[]{:S(2)}) copy-start(bf16[1152,432]{0,1:T(8,128)(2,1)} %param.7) | copy-start | bytes 2985988
  6.5 68.8 %all-gather.5.cloned.1.call-start = ((), (), s32[]{:S(2)}) async-start(), calls=%async_computation.3 | async-start | bytes 2654208 | tf_op jit(solution)/shard_map/all_gather | solution.py:153
  7.3 160.9 %all-gather.7.cloned.1.call-start = ((), (), s32[]{:S(2)}) async-start(), calls=%async_computation.4 | async-start | bytes 14598144 | tf_op jit(solution)/shard_map/all_gather | solution.py:162
  75.4 1.7 copy-start.2
  77.0 43.7 %copy-start.4 = (bf16[1,128,1152]{2,1,0:T(8,128)(2,1)S(1)}, bf16[1,128,1152]{2,1,0:T(8,128)(2,1)}, u32[]{:S(2)}) copy-start(bf16[1,128,1152]{2,1,0:T(8,128)(2,1)} %param.6) | copy-start | bytes 884740
  85.6 82.6 %copy-start.1 = (bf16[1152,1152]{1,0:T(8,128)(2,1)S(1)}, bf16[1152,1152]{1,0:T(8,128)(2,1)}, u32[]{:S(2)}) copy-start(bf16[1152,1152]{1,0:T(8,128)(2,1)} %out_table_ref.1) | copy-start | bytes 7962628
  168.2 1.1 copy-start.3
Sparse Core Ops, SparseCore 0:
  9.5 65.8 all-gather.4
  78.5 89.6 all-gather.6

commit v5 on v2

--- a/solution.py
+++ b/solution.py
@@ -35,11 +35,22 @@
 
 def triples_of(rows, modulation_ref, wqk_ref, wvt_ref):
     normed = modulated(rows, modulation_ref[0, 0:1], modulation_ref[0, 1:2])
-    qk = jnp.dot(normed, wqk_ref[...], preferred_element_type=jnp.float32).astype(jnp.bfloat16)
+    qk = lax.dot_general(normed, wqk_ref[...], NT, preferred_element_type=jnp.float32).astype(jnp.bfloat16)
     values = lax.dot_general(wvt_ref[...], normed, NT, preferred_element_type=jnp.float32)
     index = lax.broadcasted_iota(jnp.int32, values.shape, 0)
     ones = (index == HD) | (index == HP + HD)
     return qk, jnp.where(ones, 1.0, values).astype(jnp.bfloat16)
+
+
+def spread_kernel(table_ref, wqk_ref, wvt_ref):
+    table = table_ref[...].astype(jnp.float32)
+    width = table.shape[1]
+    wide, narrow = jnp.zeros((LANES - HD, width)), jnp.zeros((HP - HD, width))
+    pieces = [table[HD * index : HD * index + HD] for index in range(6)]
+    wqk_ref[...] = jnp.concatenate(
+        [pieces[0], wide, pieces[1], wide, pieces[3], wide, pieces[4], wide], axis=0
+    ).astype(jnp.bfloat16)
+    wvt_ref[...] = jnp.concatenate([pieces[2], narrow, pieces[5], narrow], axis=0).astype(jnp.bfloat16)
 
 
 def early_kernel(*refs):
@@ -53,50 +64,56 @@
 
 
 def frame_kernel(
-    place_ref, one_ref, two_ref, three_ref, four_ref, qk_ref, vt_ref, modulation_ref, wqk_ref, wvt_ref,
-    out_ref, qk_late_ref, vt_late_ref,
+    place_ref, below_ref, above_ref, one_ref, two_ref, three_ref, four_ref, qk_ref, vt_ref, modulation_ref,
+    wqk_ref, wvt_ref, out_ref, qk_late_ref, vt_late_ref,
 ):
-    rows = jnp.concatenate([one_ref[...], two_ref[...], three_ref[...], four_ref[...]], axis=0)
-    qk_late_ref[...], vt_late_ref[...] = triples_of(
-        rows.astype(jnp.float32), modulation_ref, wqk_ref, wvt_ref
+    groups = ((below_ref, above_ref), (three_ref, four_ref, one_ref, two_ref))
+    for index, group in enumerate(groups):
+        rows = jnp.concatenate([ref[...] for ref in group], axis=0).astype(jnp.float32)
+        qk, vt = triples_of(rows, modulation_ref, wqk_ref, wvt_ref)
+        start = 2 * LANES * index
+        qk_late_ref[start : start + 2 * LANES] = qk
+        vt_late_ref[:, start : start + 2 * LANES] = vt
+    parts = ((qk_ref, vt_ref), (qk_late_ref, vt_late_ref))
+    blocks = (
+        ((qk_ref, 0), (qk_ref, 128)),
+        ((qk_ref, 256), (qk_late_ref, 0)),
+        ((qk_ref, 384), (qk_late_ref, 128)),
+        ((qk_late_ref, 384), (qk_late_ref, 256)),
     )
-    parts = ((qk_ref, vt_ref), (qk_late_ref, vt_late_ref))
-    block = 2 * LANES
-    number = 0
-    for qk_part, _ in parts:
-        for start in range(0, qk_part.shape[0], block):
-            outs = []
-            for head in range(2):
-                column = 2 * LANES * head
-                queries = qk_part[start : start + block, column : column + LANES]
-                scores = [
-                    lax.dot_general(
-                        qk[:, column + LANES : column + 2 * LANES], queries, NT,
-                        preferred_element_type=jnp.float32,
-                    )
-                    for qk, _ in parts
-                ]
-                largest = jnp.maximum(*[jnp.max(part, axis=0, keepdims=True) for part in scores])
-                mixed = sum(
-                    jnp.dot(
-                        vt[HP * head : HP * head + HP],
-                        jnp.exp2((part - largest) * EXP2_SCALE).astype(jnp.bfloat16),
-                        preferred_element_type=jnp.float32,
-                    )
-                    for part, (_, vt) in zip(scores, parts)
+    for number, block in enumerate(blocks):
+        outs = []
+        for head in range(2):
+            column = 2 * LANES * head
+            queries = jnp.concatenate(
+                [ref[start : start + LANES, column : column + LANES] for ref, start in block], axis=0
+            )
+            scores = [
+                lax.dot_general(
+                    qk[:, column + LANES : column + 2 * LANES], queries, NT,
+                    preferred_element_type=jnp.float32,
                 )
-                outs.append(mixed[:HD] / mixed[HD : HD + 1])
-            both = jnp.concatenate(outs, axis=0).astype(jnp.bfloat16)
-            for part in range(2):
-                out_ref[place_ref[number]] = both[:, part * LANES : (part + 1) * LANES]
-                number += 1
-
-
-def middle_kernel(place_ref, mixed_ref, tables_ref, tokens_ref, modulation_ref, out_ref, table_ref, sem):
+                for qk, _ in parts
+            ]
+            largest = jnp.maximum(*[jnp.max(part, axis=0, keepdims=True) for part in scores])
+            mixed = sum(
+                jnp.dot(
+                    vt[HP * head : HP * head + HP],
+                    jnp.exp2((part - largest) * EXP2_SCALE).astype(jnp.bfloat16),
+                    preferred_element_type=jnp.float32,
+                )
+                for part, (_, vt) in zip(scores, parts)
+            )
+            outs.append(mixed[:HD] / mixed[HD : HD + 1])
+        both = jnp.concatenate(outs, axis=0).astype(jnp.bfloat16)
+        for part in range(2):
+            out_ref[place_ref[2 * number + part]] = both[:, part * LANES : (part + 1) * LANES]
+
+
+def middle_kernel(mixed_ref, tables_ref, tokens_ref, modulation_ref, out_ref, table_ref, sem):
     copy = pltpu.make_async_copy(tables_ref.at[pl.ds(0, 9), :, pl.ds(LANES, 64), :], table_ref, sem)
     copy.start()
-    zh = place_ref[8]
-    slots = [mixed_ref[((zh + 4 - slot) % 4) * 2 + core] for core in range(2) for slot in range(4)]
+    slots = [mixed_ref[2 * zh + core] for core in range(2) for zh in range(4)]
     mixed = jnp.concatenate(
         [slot[16 * number : 16 * number + 16] for number in range(9) for slot in slots], axis=0
     )
@@ -109,7 +126,7 @@
 
 
 def time_kernel(
-    positions, place_ref, middle_ref, tables_ref, out_table_ref, modulation_ref, out_ref,
+    positions, middle_ref, tables_ref, out_table_ref, modulation_ref, out_ref,
     input_ref, mixed_ref, table_ref, sem,
 ):
     step = pl.program_id(0)
@@ -123,7 +140,6 @@
         )
 
     rows, width = input_ref.shape
-    zl = place_ref[9]
     one = lax.broadcasted_iota(jnp.int32, (rows, rows), 0) % positions
     two = lax.broadcasted_iota(jnp.int32, (rows, rows), 1) % positions
     same = one == two
@@ -147,7 +163,7 @@
             values.astype(jnp.bfloat16), raised[slot].astype(jnp.bfloat16),
             preferred_element_type=jnp.float32,
         )
-        mixed_ref[step * 4 + (zl + 4 - slot) % 4] = mixed / total
+        mixed_ref[step * 4 + slot] = mixed / total
 
     @pl.when(step == pl.num_programs(0) - 1)
     def _():
@@ -170,7 +186,7 @@
     tokens = tokens[0]
     rows, width = tokens.shape
     half = rows // 2
-    zh, zl, core = lax.axis_index("zh"), lax.axis_index("zl"), lax.axis_index("c")
+    zh, core = lax.axis_index("zh"), lax.axis_index("c")
 
     def along(array, axis, by):
         return lax.ppermute(array, axis, rotation(4, by))
@@ -181,26 +197,34 @@
     before, after = along(tokens, "zh", 1), along(tokens, "zh", 3)
     beside = swapped(tokens)
     far_top, far_bottom = along(before[:half], "zh", 1), along(after[half:], "zh", 3)
-    early = [tokens, beside, before, swapped(before), after, swapped(after)]
-    late = [far_top, far_bottom, swapped(far_top), swapped(far_bottom)]
+    early = [tokens, beside, before, after]
+    late = [swapped(before), swapped(after), far_top, far_bottom, swapped(far_top), swapped(far_bottom)]
     spots = [zh, (zh + 3) % 4, (zh + 1) % 4, (zh + 2) % 4]
     place = jnp.stack(
-        [spot * 2 + side for spot in spots for side in (core, 1 - core)] + [zh, zl]
+        [spot * 2 + side for spot in spots for side in (core, 1 - core)]
     ).astype(jnp.int32)
 
     index = lax.axis_index("y") * 2 + core
     time_part = lax.dynamic_slice_in_dim(time_qkv, jnp.minimum(index * 32, 216 - 32), 32, 0)
     index = lax.axis_index("x") * 4 + lax.axis_index("y")
     out_part = lax.dynamic_slice_in_dim(frame_out, jnp.minimum(index, 8) * 16, 16, 0)
-    parts = [time_part] + [along(time_part, "zl", by) for by in (1, 2, 3)]
-    parts += [out_part] + [along(out_part, "zh", by) for by in (1, 2, 3)]
+    time_parts = lax.all_gather(time_part, "zl", axis=0, tiled=True)
+    out_parts = lax.all_gather(out_part, "zh", axis=0, tiled=True)
+    parts = [time_parts, out_parts]
     tables = lax.all_gather(jnp.concatenate(parts, axis=0), ("x", "y", "c"), axis=0)
     tables = tables.reshape(4, 8, 192, width)
 
-    heads = frame_qkv.reshape(width, 2, 3, HD)
-    wqk = jnp.pad(heads[:, :, :2], ((0, 0), (0, 0), (0, 0), (0, LANES - HD))).reshape(width, 4 * LANES)
-    wvt = jnp.pad(jnp.transpose(heads[:, :, 2], (1, 2, 0)), ((0, 0), (0, HP - HD), (0, 0)))
-    wvt = wvt.reshape(2 * HP, width)
+    wqk, wvt = pl.pallas_call(
+        spread_kernel,
+        out_shape=(
+            jax.ShapeDtypeStruct((4 * LANES, width), jnp.bfloat16),
+            jax.ShapeDtypeStruct((2 * HP, width), jnp.bfloat16),
+        ),
+        in_specs=[whole()],
+        out_specs=(whole(), whole()),
+        compiler_params=params(),
+        name="spread",
+    )(frame_qkv.T)
 
     soon = rows * len(early)
     qk, vt = pl.pallas_call(
@@ -216,11 +240,11 @@
         name="early_triples",
     )(*early, modulation, wqk, wvt)
 
-    rest = 2 * rows
+    rest = 4 * rows
     mixed = pl.pallas_call(
         frame_kernel,
         out_shape=jax.ShapeDtypeStruct(((soon + rest) // LANES, 2 * HD, LANES), jnp.bfloat16),
-        in_specs=[pl.BlockSpec(memory_space=pltpu.SMEM)] + [whole()] * 9,
+        in_specs=[pl.BlockSpec(memory_space=pltpu.SMEM)] + [whole()] * 11,
         out_specs=whole(),
         scratch_shapes=[
             pltpu.VMEM((rest, 4 * LANES), jnp.bfloat16),
@@ -234,14 +258,12 @@
     middle = pl.pallas_call(
         middle_kernel,
         out_shape=jax.ShapeDtypeStruct((rows, width), jnp.bfloat16),
-        in_specs=[
-            pl.BlockSpec(memory_space=pltpu.SMEM), whole(), pl.BlockSpec(memory_space=pl.ANY), whole(), whole()
-        ],
+        in_specs=[whole(), pl.BlockSpec(memory_space=pl.ANY), whole(), whole()],
         out_specs=whole(),
         scratch_shapes=[pltpu.VMEM((9, 2, 64, width), jnp.bfloat16), pltpu.SemaphoreType.DMA],
         compiler_params=params(),
         name="middle",
-    )(place, mixed, tables.reshape(16, 2, 192, width), tokens, modulation)
+    )(mixed, tables.reshape(16, 2, 192, width), tokens, modulation)
 
     middle = lax.all_to_all(middle, ("x", "zl"), 0, 0, tiled=True)
 
@@ -250,7 +272,6 @@
         grid=(4,),
         out_shape=jax.ShapeDtypeStruct((rows, width), jnp.bfloat16),
         in_specs=[
-            pl.BlockSpec(memory_space=pltpu.SMEM),
             whole(),
             pl.BlockSpec((1, 8, LANES, width), lambda i: (i, 0, 0, 0)),
             pl.BlockSpec(memory_space=pl.ANY),
@@ -265,7 +286,7 @@
         ],
         compiler_params=params(),
         name="time_block",
-    )(place, middle, tables, time_out, modulation)
+    )(middle, tables, time_out, modulation)
     out = lax.all_to_all(out, ("x", "zl"), 0, 0, tiled=True)
     return out[None]
 

time: 199 us -> 188 us (0.945)
  blocking collectives: 53.2 us -> 97 us
  starting transfers between devices: 72.9 us -> 33.5 us
  local copies, waits for them, and re-layouts: 15.5 us -> 6.73 us
  waiting for transfers between devices: 21.9 us -> 14.6 us
    ppermute x10 -> x4, starting transfers between devices: 58.6 us -> 14 us  [along(): return lax.ppermute(array, axis, rotation(4, by))]
    all_gather x0 -> x2, blocking collectives: none -> 36.3 us  [the longest x1 22.5 us: shards(): out_parts = lax.all_gather(out_part, 'zh', axis=0, tiled=True)]
    all_to_all x1, blocking collectives: 14.8 us -> 24.6 us  [shards(): middle = lax.all_to_all(middle, ('x', 'zl'), 0, 0, tiled=True)]
    ppermute x10 -> x4, waiting for transfers between devices: 21.9 us -> 14.5 us  [along(): return lax.ppermute(array, axis, rotation(4, by))]
    ppermute x5, starting transfers between devices: 14.3 us -> 19.5 us  [swapped(): return lax.ppermute(array, 'c', SWAP)]
    unnamed x20 -> x12, local copies, waits for them, and re-layouts: 6.73 us -> 2.7 us
    reshape x1 -> x0, local copies, waits for them, and re-layouts: 3.14 us -> none  [shards(): jnp.pad(heads[:, :, :2], ((0, 0), (0, 0), (0, 0), (0, LANES - HD)))]
    pad x2 -> x0, local copies, waits for them, and re-layouts: 3.12 us -> none  [the longest x1 2.1 us: shards(): jnp.pad(heads[:, :, :2], ((0, 0), (0, 0), (0, 0), (0, LANES - HD)))]
  transfers between devices with their start and end apart: 16 -> 10, of which waited for: 5 -> 2; matrix products, arithmetic and copies ran while one was open for 6% -> 2% of each run, Pallas kernels for 5% -> 5%
where the time goes in v5:
time: 188 us; the launch traced here: 187 us
  blocking collectives  97 us (52%)
  starting transfers between devices  33.5 us (18%)
  Pallas kernels  20.6 us (11%)
  waiting for transfers between devices  14.6 us (8%)
  between operations  13.6 us (7%)
  local copies, waits for them, and re-layouts  6.73 us (4%)
    all_to_all x1, blocking collectives, shards(): middle = lax.all_to_all(middle, ('x', 'zl'), 0, 0, tiled=True)  24.6 us
    all_gather x1, blocking collectives, shards(): out_parts = lax.all_gather(out_part, 'zh', axis=0, tiled=True)  22.5 us
    all_to_all x1, blocking collectives, shards(): mixed = lax.all_to_all(mixed, ('zh', 'c'), 0, 0, tiled=True)  22.2 us
    ppermute x5, starting transfers between devices, swapped(): return lax.ppermute(array, 'c', SWAP)  19.5 us
    ppermute x4, waiting for transfers between devices, along(): return lax.ppermute(array, axis, rotation(4, by))  14.5 us
    ppermute x4, starting transfers between devices, along(): return lax.ppermute(array, axis, rotation(4, by))  14 us
    all_to_all x1, blocking collectives, shards(): out = lax.all_to_all(out, ('x', 'zl'), 0, 0, tiled=True)  13.9 us
    all_gather x1, blocking collectives, shards(): time_parts = lax.all_gather(time_part, 'zl', axis=0, tiled=True)  13.8 us
  transfers between devices with their start and end apart: 10, of which 2 were waited for; matrix products, arithmetic and copies ran while one was open for 2% of the time, Pallas kernels for 5%

profile of v5, /device:TPU:1, one launch (start us, length us, event | category | flops | bytes accessed | tf_op | source)
XLA Modules:
  0.0 186.8 jit_solution(759575562714767814)
XLA Ops:
  6.5 0.0 copy-start
  6.5 0.0 copy-start.4
  6.5 0.0 copy-start.2
  6.5 0.0 all-gather.3.cloned.1.call-start
  6.6 1.0 copy-done
  7.6 13.8 %all_gather.12 = bf16[128,1152]{1,0:T(8,128)(2,1)S(1)} all-gather(bf16[32,1152]{1,0:T(8,128)(2,1)S(1)} %constant_dynamic-slice_fusion.1), channel_id=1, replica_groups=mesh['y'=4,'x'=4,'zl'=4,'zh'=4,'c'=2] {'zl'}, dimensions={0}, use_global_device_ids=true | all-gather | bytes 368640 | tf_op jit(solution)/shard_map/all_gather | solution.py:211
  21.4 0.8 constant_dynamic-slice_fusion
  22.2 22.5 %all_gather.13 = bf16[64,1152]{1,0:T(8,128)(2,1)S(1)} all-gather(bf16[16,1152]{1,0:T(8,128)(2,1)S(1)} %constant_dynamic-slice_fusion), channel_id=1, replica_groups=mesh['y'=4,'x'=4,'zl'=4,'zh'=4,'c'=2] {'zh'}, dimensions={0}, use_global_device_ids=true | all-gather | bytes 184320 | tf_op jit(solution)/shard_map/all_gather | solution.py:212
  44.7 0.8 pad_maximum_fusion
  45.5 0.0 all-gather.3.cloned.1.call-update
  45.5 3.0 %collective-permute-start = (bf16[128,1152]{1,0:T(8,128)(2,1)}, bf16[128,1152]{1,0:T(8,128)(2,1)}, u32[]{:S(2)}, u32[]{:S(2)}) collective-permute-start(bf16[128,1152]{1,0:T(8,128)(2,1)} %bitcast.20), channel_id=1, source_target_pairs={{0,2},{2,4},{4,6},{6,0},{1,3},{3,5},{5,7},{7,1},{8,10},{10,12},{12... | collective-permute-start | bytes 884744 | tf_op jit(solution)/shard_map/ppermute | solution.py:192
  48.5 6.2 %collective-permute-start.2 = (bf16[128,1152]{1,0:T(8,128)(2,1)}, bf16[128,1152]{1,0:T(8,128)(2,1)}, u32[]{:S(2)}, u32[]{:S(2)}) collective-permute-start(bf16[128,1152]{1,0:T(8,128)(2,1)} %bitcast.21), channel_id=1, source_target_pairs={{0,6},{2,0},{4,2},{6,4},{1,7},{3,1},{5,3},{7,5},{8,14},{10,8},{12,... | collective-permute-start | bytes 884744 | tf_op jit(solution)/shard_map/ppermute | solution.py:192
  54.7 8.4 %collective-permute-start.8 = (bf16[128,1152]{1,0:T(8,128)(2,1)}, bf16[128,1152]{1,0:T(8,128)(2,1)}, u32[]{:S(2)}, u32[]{:S(2)}) collective-permute-start(bf16[128,1152]{1,0:T(8,128)(2,1)} %bitcast.22), channel_id=1, source_target_pairs={{0,1},{1,0},{2,3},{3,2},{4,5},{5,4},{6,7},{7,6},{8,9},{9,8},{10,11... | collective-permute-start | bytes 884744 | tf_op jit(solution)/shard_map/ppermute | solution.py:195
  63.1 3.7 %collective-permute-done.refs_2_ = bf16[128,1152]{1,0:T(8,128)(2,1)} collective-permute-done((bf16[128,1152]{1,0:T(8,128)(2,1)}, bf16[128,1152]{1,0:T(8,128)(2,1)}, u32[]{:S(2)}, u32[]{:S(2)}) %collective-permute-start) | collective-permute-done | bytes 294944 | tf_op jit(solution)/shard_map/ppermute | solution.py:192
  66.8 1.6 slice.8
  68.4 1.9 %collective-permute-start.4 = (bf16[64,1152]{1,0:T(8,128)(2,1)}, bf16[64,1152]{1,0:T(8,128)(2,1)S(1)}, u32[]{:S(2)}, u32[]{:S(2)}) collective-permute-start(bf16[64,1152]{1,0:T(8,128)(2,1)} %slice.8), channel_id=1, source_target_pairs={{0,2},{2,4},{4,6},{6,0},{1,3},{3,5},{5,7},{7,1},{8,10},{10,12},{12... | collective-permute-start | bytes 442376 | tf_op jit(solution)/shard_map/ppermute | solution.py:192
  70.3 10.8 %collective-permute-done.2.refs_3_ = bf16[128,1152]{1,0:T(8,128)(2,1)} collective-permute-done((bf16[128,1152]{1,0:T(8,128)(2,1)}, bf16[128,1152]{1,0:T(8,128)(2,1)}, u32[]{:S(2)}, u32[]{:S(2)}) %collective-permute-start.2) | collective-permute-done | bytes 294944 | tf_op jit(solution)/shard_map/ppermute | solution.py:192
  81.1 1.6 slice.9
  82.7 2.9 %collective-permute-start.5 = (bf16[64,1152]{1,0:T(8,128)(2,1)}, bf16[64,1152]{1,0:T(8,128)(2,1)}, u32[]{:S(2)}, u32[]{:S(2)}) collective-permute-start(bf16[64,1152]{1,0:T(8,128)(2,1)} %slice.9), channel_id=1, source_target_pairs={{0,6},{2,0},{4,2},{6,4},{1,7},{3,1},{5,3},{7,5},{8,14},{10,8},{12,... | collective-permute-start | bytes 442376 | tf_op jit(solution)/shard_map/ppermute | solution.py:192
  85.6 4.7 %collective-permute-start.1 = (bf16[128,1152]{1,0:T(8,128)(2,1)}, bf16[128,1152]{1,0:T(8,128)(2,1)S(1)}, u32[]{:S(2)}, u32[]{:S(2)}) collective-permute-start(bf16[128,1152]{1,0:T(8,128)(2,1)} %collective-permute-done.refs_2_), channel_id=1, source_target_pairs={{0,1},{1,0},{2,3},{3,2},{4,5},{5,4},{6,7},{7,6},{8,9},{9,8},{10,11... | collective-permute-start | bytes 884744 | tf_op jit(solution)/shard_map/ppermute | solution.py:195
  90.4 1.9 %collective-permute-start.3 = (bf16[128,1152]{1,0:T(8,128)(2,1)}, bf16[128,1152]{1,0:T(8,128)(2,1)}, u32[]{:S(2)}, u32[]{:S(2)}) collective-permute-start(bf16[128,1152]{1,0:T(8,128)(2,1)} %collective-permute-done.2.refs_3_), channel_id=1, source_target_pairs={{0,1},{1,0},{2,3},{3,2},{4,5},{5,4},{6,7},{7,6},{8,9},{9,8},{10,11... | collective-permute-start | bytes 884744 | tf_op jit(solution)/shard_map/ppermute | solution.py:195
  92.4 0.0 copy-done.4
  92.4 0.0 copy-done.2
  92.4 0.1 spread.1
  92.5 0.1 stack.35.place_ref
  92.6 0.0 collective-permute-done.4.one_ref
  92.6 2.4 %collective-permute-start.6 = (bf16[64,1152]{1,0:T(8,128)(2,1)S(1)}, bf16[64,1152]{1,0:T(8,128)(2,1)S(1)}, u32[]{:S(2)}, u32[]{:S(2)}) collective-permute-start(bf16[64,1152]{1,0:T(8,128)(2,1)S(1)} %collective-permute-done.4.one_ref), channel_id=1, source_target_pairs={{0,1},{1,0},{2,3},{3,2},{4,5},{5,4},{6,7},{7,6},{8,9},{9,8},{10,11... | collective-permute-start | bytes 442376 | tf_op jit(solution)/shard_map/ppermute | solution.py:195
  95.0 0.0 collective-permute-done.5.two_ref
  95.0 2.0 %collective-permute-start.7 = (bf16[64,1152]{1,0:T(8,128)(2,1)}, bf16[64,1152]{1,0:T(8,128)(2,1)S(1)}, u32[]{:S(2)}, u32[]{:S(2)}) collective-permute-start(bf16[64,1152]{1,0:T(8,128)(2,1)} %collective-permute-done.5.two_ref), channel_id=1, source_target_pairs={{0,1},{1,0},{2,3},{3,2},{4,5},{5,4},{6,7},{7,6},{8,9},{9,8},{10,11... | collective-permute-start | bytes 442376 | tf_op jit(solution)/shard_map/ppermute | solution.py:195
  97.1 0.0 collective-permute-done.8.refs_1_
  97.1 0.0 copy-start.3
  97.1 1.0 copy-done.3
  98.1 2.8 %early_triples.1 = (bf16[512,512]{1,0:T(8,128)(2,1)S(1)}, bf16[160,512]{1,0:T(8,128)(2,1)S(1)}) custom-call(bf16[128,1152]{1,0:T(8,128)(2,1)S(1)} %bitcast.23, bf16[128,1152]{1,0:T(8,128)(2,1)} %collective-permute-done.8.refs_1_, bf16[128,1152]{1,0:T(8,128)(2,1)} %collective-permute-done.refs_2_, bf16[128,1152]{1,0:T(8,128)(2,1)} %collective-permute-done.2.refs_3_, ...), custom_call_target="tpu_custom_call" | custom-call | flops 2000000000 | bytes 5000000 | tf_op jit(solution)/shard_map/early_triples/pallas_call | solution.py:230
  100.9 0.0 collective-permute-done.6.three_ref
  100.9 0.0 collective-permute-done.7.four_ref
  100.9 0.0 collective-permute-done.1.below_ref
  100.9 0.0 collective-permute-done.3.above_ref
  100.9 7.4 %frame_attention.1 = bf16[8,144,128]{2,1,0:T(8,128)(2,1)S(1)} custom-call(s32[8]{0:T(128)S(1)} %stack.35.place_ref, bf16[128,1152]{1,0:T(8,128)(2,1)S(1)} %collective-permute-done.1.below_ref, bf16[128,1152]{1,0:T(8,128)(2,1)} %collective-permute-done.3.above_ref, bf16[64,1152]{1,0:T(8,128)(2,1)S(1)} %collective-permute-done.4.one_ref, ...), custom_call_target="tpu_custom_call" | custom-call | tf_op jit(solution)/shard_map/frame_attention/pallas_call | solution.py:244
  108.3 22.2 %all_to_all.25.mixed_ref = bf16[8,144,128]{2,1,0:T(8,128)(2,1)S(1)} all-to-all(bf16[8,144,128]{2,1,0:T(8,128)(2,1)S(1)} %frame_attention.1), channel_id=1, replica_groups=mesh['y'=4,'x'=4,'zl'=4,'zh'=4,'c'=2] {'zh','c'}, dimensions={0} | all-to-all | bytes 589824 | tf_op jit(solution)/shard_map/all_to_all | solution.py:257
  130.4 0.0 all-gather.3.cloned.1.call-done
  130.4 0.0 copy-start.1
  130.4 2.5 %middle.1 = bf16[128,1152]{1,0:T(8,128)(2,1)S(1)} custom-call(bf16[8,144,128]{2,1,0:T(8,128)(2,1)S(1)} %all_to_all.25.mixed_ref, bf16[16,2,192,1152]{3,2,1,0:T(8,128)(2,1)} %bitcast.25, bf16[128,1152]{1,0:T(8,128)(2,1)S(1)} %bitcast.24, f32[2,3,1152]{2,1,0:T(4,128)S(1)} %copy.7.refs_4_.modulation_ref), custom_call_target="tpu_custom_call" | custom-call | tf_op jit(solution)/shard_map/middle/pallas_call | solution.py:258
  133.0 24.6 %all_to_all.26 = bf16[16,8,1152]{2,1,0:T(8,128)(2,1)S(1)} all-to-all(bf16[16,8,1152]{2,1,0:T(8,128)(2,1)S(1)} %bitcast.18), channel_id=1, replica_groups=mesh['y'=4,'x'=4,'zl'=4,'zh'=4,'c'=2] {'x','zl'}, dimensions={0} | all-to-all | bytes 589824 | tf_op jit(solution)/shard_map/all_to_all | solution.py:268
  157.6 0.0 copy-done.1
  157.6 7.8 %time_block.1 = bf16[128,1152]{1,0:T(8,128)(2,1)S(1)} custom-call(bf16[128,1152]{1,0:T(8,128)(2,1)S(1)} %bitcast.16, bf16[4,8,192,1152]{3,2,1,0:T(8,128)(2,1)} %bitcast.26, bf16[1152,1152]{1,0:T(8,128)(2,1)S(1)} %copy-done.1, f32[2,3,1152]{2,1,0:T(4,128)S(1)} %copy.7.refs_4_.modulation_ref), custom_call_target="tpu_custom_call" | custom-call | tf_op jit(solution)/shard_map/time_block/pallas_call | solution.py:270
  165.4 13.9 %all_to_all.27 = bf16[16,8,1152]{2,1,0:T(8,128)(2,1)S(1)} all-to-all(bf16[16,8,1152]{2,1,0:T(8,128)(2,1)S(1)} %bitcast.17), channel_id=1, replica_groups=mesh['y'=4,'x'=4,'zl'=4,'zh'=4,'c'=2] {'x','zl'}, dimensions={0} | all-to-all | bytes 589824 | tf_op jit(solution)/shard_map/all_to_all | solution.py:290
  179.3 0.7 copy.12
  (2 shorter events, 0.0 us)
Async XLA Ops:
  6.5 1.0 copy-start
  6.5 85.8 %copy-start.4 = (f32[2,3,1152]{2,0,1:T(2,128)S(1)}, f32[2,3,1152]{2,0,1:T(2,128)}, u32[]{:S(2)}) copy-start(f32[2,3,1152]{2,0,1:T(2,128)} %param.11) | copy-start | bytes 82948
  6.5 85.8 %copy-start.2 = (bf16[1152,432]{0,1:T(8,128)(2,1)S(1)}, bf16[1152,432]{0,1:T(8,128)(2,1)}, u32[]{:S(2)}) copy-start(bf16[1152,432]{0,1:T(8,128)(2,1)} %param.7) | copy-start | bytes 2985988
  6.5 123.9 %all-gather.3.cloned.1.call-start = ((), (), s32[]{:S(2)}) async-start(), calls=%async_computation.3 | async-start | bytes 14598144 | tf_op jit(solution)/shard_map/all_gather | solution.py:214
  45.5 21.3 %collective-permute-start = (bf16[128,1152]{1,0:T(8,128)(2,1)}, bf16[128,1152]{1,0:T(8,128)(2,1)}, u32[]{:S(2)}, u32[]{:S(2)}) collective-permute-start(bf16[128,1152]{1,0:T(8,128)(2,1)} %bitcast.20), channel_id=1, source_target_pairs={{0,2},{2,4},{4,6},{6,0},{1,3},{3,5},{5,7},{7,1},{8,10},{10,12},{12... | collective-permute-start | bytes 884744 | tf_op jit(solution)/shard_map/ppermute | solution.py:192
  48.5 32.6 %collective-permute-start.2 = (bf16[128,1152]{1,0:T(8,128)(2,1)}, bf16[128,1152]{1,0:T(8,128)(2,1)}, u32[]{:S(2)}, u32[]{:S(2)}) collective-permute-start(bf16[128,1152]{1,0:T(8,128)(2,1)} %bitcast.21), channel_id=1, source_target_pairs={{0,6},{2,0},{4,2},{6,4},{1,7},{3,1},{5,3},{7,5},{8,14},{10,8},{12,... | collective-permute-start | bytes 884744 | tf_op jit(solution)/shard_map/ppermute | solution.py:192
  54.7 42.4 %collective-permute-start.8 = (bf16[128,1152]{1,0:T(8,128)(2,1)}, bf16[128,1152]{1,0:T(8,128)(2,1)}, u32[]{:S(2)}, u32[]{:S(2)}) collective-permute-start(bf16[128,1152]{1,0:T(8,128)(2,1)} %bitcast.22), channel_id=1, source_target_pairs={{0,1},{1,0},{2,3},{3,2},{4,5},{5,4},{6,7},{7,6},{8,9},{9,8},{10,11... | collective-permute-start | bytes 884744 | tf_op jit(solution)/shard_map/ppermute | solution.py:195
  68.4 24.2 %collective-permute-start.4 = (bf16[64,1152]{1,0:T(8,128)(2,1)}, bf16[64,1152]{1,0:T(8,128)(2,1)S(1)}, u32[]{:S(2)}, u32[]{:S(2)}) collective-permute-start(bf16[64,1152]{1,0:T(8,128)(2,1)} %slice.8), channel_id=1, source_target_pairs={{0,2},{2,4},{4,6},{6,0},{1,3},{3,5},{5,7},{7,1},{8,10},{10,12},{12... | collective-permute-start | bytes 442376 | tf_op jit(solution)/shard_map/ppermute | solution.py:192
  82.7 12.3 %collective-permute-start.5 = (bf16[64,1152]{1,0:T(8,128)(2,1)}, bf16[64,1152]{1,0:T(8,128)(2,1)}, u32[]{:S(2)}, u32[]{:S(2)}) collective-permute-start(bf16[64,1152]{1,0:T(8,128)(2,1)} %slice.9), channel_id=1, source_target_pairs={{0,6},{2,0},{4,2},{6,4},{1,7},{3,1},{5,3},{7,5},{8,14},{10,8},{12,... | collective-permute-start | bytes 442376 | tf_op jit(solution)/shard_map/ppermute | solution.py:192
  85.6 15.2 %collective-permute-start.1 = (bf16[128,1152]{1,0:T(8,128)(2,1)}, bf16[128,1152]{1,0:T(8,128)(2,1)S(1)}, u32[]{:S(2)}, u32[]{:S(2)}) collective-permute-start(bf16[128,1152]{1,0:T(8,128)(2,1)} %collective-permute-done.refs_2_), channel_id=1, source_target_pairs={{0,1},{1,0},{2,3},{3,2},{4,5},{5,4},{6,7},{7,6},{8,9},{9,8},{10,11... | collective-permute-start | bytes 884744 | tf_op jit(solution)/shard_map/ppermute | solution.py:195
  90.4 10.5 %collective-permute-start.3 = (bf16[128,1152]{1,0:T(8,128)(2,1)}, bf16[128,1152]{1,0:T(8,128)(2,1)}, u32[]{:S(2)}, u32[]{:S(2)}) collective-permute-start(bf16[128,1152]{1,0:T(8,128)(2,1)} %collective-permute-done.2.refs_3_), channel_id=1, source_target_pairs={{0,1},{1,0},{2,3},{3,2},{4,5},{5,4},{6,7},{7,6},{8,9},{9,8},{10,11... | collective-permute-start | bytes 884744 | tf_op jit(solution)/shard_map/ppermute | solution.py:195
  92.6 8.2 %collective-permute-start.6 = (bf16[64,1152]{1,0:T(8,128)(2,1)S(1)}, bf16[64,1152]{1,0:T(8,128)(2,1)S(1)}, u32[]{:S(2)}, u32[]{:S(2)}) collective-permute-start(bf16[64,1152]{1,0:T(8,128)(2,1)S(1)} %collective-permute-done.4.one_ref), channel_id=1, source_target_pairs={{0,1},{1,0},{2,3},{3,2},{4,5},{5,4},{6,7},{7,6},{8,9},{9,8},{10,11... | collective-permute-start | bytes 442376 | tf_op jit(solution)/shard_map/ppermute | solution.py:195
  95.0 5.8 %collective-permute-start.7 = (bf16[64,1152]{1,0:T(8,128)(2,1)}, bf16[64,1152]{1,0:T(8,128)(2,1)S(1)}, u32[]{:S(2)}, u32[]{:S(2)}) collective-permute-start(bf16[64,1152]{1,0:T(8,128)(2,1)} %collective-permute-done.5.two_ref), channel_id=1, source_target_pairs={{0,1},{1,0},{2,3},{3,2},{4,5},{5,4},{6,7},{7,6},{8,9},{9,8},{10,11... | collective-permute-start | bytes 442376 | tf_op jit(solution)/shard_map/ppermute | solution.py:195
  97.1 1.0 copy-start.3
  130.4 27.1 %copy-start.1 = (bf16[1152,1152]{1,0:T(8,128)(2,1)S(1)}, bf16[1152,1152]{1,0:T(8,128)(2,1)}, u32[]{:S(2)}) copy-start(bf16[1152,1152]{1,0:T(8,128)(2,1)} %out_table_ref.1) | copy-start | bytes 7962628
Sparse Core Ops, SparseCore 0:
  45.6 83.4 all-gather.2

commit v6 on v3

--- a/solution.py
+++ b/solution.py
@@ -35,44 +35,58 @@
 
 def triples_of(rows, modulation_ref, wqk_ref, wvt_ref):
     normed = modulated(rows, modulation_ref[0, 0:1], modulation_ref[0, 1:2])
-    qk = jnp.dot(normed, wqk_ref[...], preferred_element_type=jnp.float32).astype(jnp.bfloat16)
+    qk = lax.dot_general(normed, wqk_ref[...], NT, preferred_element_type=jnp.float32).astype(jnp.bfloat16)
     values = lax.dot_general(wvt_ref[...], normed, NT, preferred_element_type=jnp.float32)
     index = lax.broadcasted_iota(jnp.int32, values.shape, 0)
     ones = (index == HD) | (index == HP + HD)
     return qk, jnp.where(ones, 1.0, values).astype(jnp.bfloat16)
 
 
-def early_kernel(own_ref, beside_ref, near_ref, swapped_ref, modulation_ref, wqk_ref, wvt_ref, qk_ref, vt_ref):
-    for index, pair in enumerate(((own_ref, beside_ref), (near_ref, swapped_ref))):
-        rows = jnp.concatenate([pair[0][...], pair[1][...]], axis=0)
+def spread_kernel(table_ref, wqk_ref, wvt_ref):
+    table = table_ref[...].astype(jnp.float32)
+    width = table.shape[1]
+    wide, narrow = jnp.zeros((LANES - HD, width)), jnp.zeros((HP - HD, width))
+    pieces = [table[HD * index : HD * index + HD] for index in range(6)]
+    wqk_ref[...] = jnp.concatenate(
+        [pieces[0], wide, pieces[1], wide, pieces[3], wide, pieces[4], wide], axis=0
+    ).astype(jnp.bfloat16)
+    wvt_ref[...] = jnp.concatenate([pieces[2], narrow, pieces[5], narrow], axis=0).astype(jnp.bfloat16)
+
+
+def early_kernel(*refs):
+    pieces, (modulation_ref, wqk_ref, wvt_ref, qk_ref, vt_ref) = refs[:-5], refs[-5:]
+    for index in range(0, len(pieces), 2):
+        rows = jnp.concatenate([pieces[index][...], pieces[index + 1][...]], axis=0)
         qk, vt = triples_of(rows.astype(jnp.float32), modulation_ref, wqk_ref, wvt_ref)
-        start = 2 * LANES * index
+        start = LANES * index
         qk_ref[start : start + 2 * LANES] = qk
         vt_ref[:, start : start + 2 * LANES] = vt
 
 
 def frame_kernel(
-    place_ref, late_ref, swapped_ref, qk_ref, vt_ref, modulation_ref, wqk_ref, wvt_ref,
-    out_ref, qk_late_ref, vt_late_ref,
+    place_ref, below_ref, above_ref, one_ref, two_ref, three_ref, four_ref, qk_ref, vt_ref, modulation_ref,
+    wqk_ref, wvt_ref, out_ref, qk_late_ref, vt_late_ref,
 ):
-    for index, rows_ref in enumerate((late_ref, swapped_ref)):
+    groups = ((below_ref, above_ref), (three_ref, four_ref, one_ref, two_ref))
+    for index, group in enumerate(groups):
+        rows = jnp.concatenate([ref[...] for ref in group], axis=0).astype(jnp.float32)
+        qk, vt = triples_of(rows, modulation_ref, wqk_ref, wvt_ref)
         start = 2 * LANES * index
-        qk, vt = triples_of(rows_ref[...].astype(jnp.float32), modulation_ref, wqk_ref, wvt_ref)
         qk_late_ref[start : start + 2 * LANES] = qk
         vt_late_ref[:, start : start + 2 * LANES] = vt
     parts = ((qk_ref, vt_ref), (qk_late_ref, vt_late_ref))
     blocks = (
-        ((qk_ref, 0), (qk_ref, 64), (qk_ref, 128), (qk_ref, 192)),
-        ((qk_ref, 256), (qk_late_ref, 128), (qk_ref, 384), (qk_late_ref, 384)),
-        ((qk_late_ref, 192), (qk_ref, 320), (qk_late_ref, 448), (qk_ref, 448)),
-        ((qk_late_ref, 0), (qk_late_ref, 64), (qk_late_ref, 256), (qk_late_ref, 320)),
+        ((qk_ref, 0), (qk_ref, 128)),
+        ((qk_ref, 256), (qk_late_ref, 0)),
+        ((qk_ref, 384), (qk_late_ref, 128)),
+        ((qk_late_ref, 384), (qk_late_ref, 256)),
     )
     for number, block in enumerate(blocks):
         outs = []
         for head in range(2):
             column = 2 * LANES * head
             queries = jnp.concatenate(
-                [ref[start : start + 64, column : column + LANES] for ref, start in block], axis=0
+                [ref[start : start + LANES, column : column + LANES] for ref, start in block], axis=0
             )
             scores = [
                 lax.dot_general(
@@ -96,6 +110,13 @@
             out_ref[place_ref[2 * number + part]] = both[:, part * LANES : (part + 1) * LANES]
 
 
+def pack_kernel(parts_ref, below_ref, above_ref, out_ref):
+    parts = parts_ref[...].astype(jnp.float32)
+    rows = [parts[16 * (4 * zh + zl) : 16 * (4 * zh + zl) + 8] for zl in range(4) for zh in range(4)]
+    rows += [parts[16 * (4 * zh + zl) + 8 : 16 * (4 * zh + zl) + 16] for zh in range(4) for zl in range(2)]
+    out_ref[...] = jnp.concatenate(rows, axis=0).astype(jnp.bfloat16)
+
+
 def join_kernel(mixed_ref, tokens_ref, out_ref):
     width = tokens_ref.shape[1]
     mixed = mixed_ref[...].reshape(-1, LANES).astype(jnp.float32)
@@ -104,23 +125,22 @@
 
 
 def time_kernel(
-    positions, place_ref, joined_ref, tables_ref, all_ref, out_table_ref, modulation_ref, out_ref,
+    positions, joined_ref, tables_ref, all_ref, out_table_ref, modulation_ref, out_ref,
     middle_ref, input_ref, mixed_ref, frame_table_ref, time_table_ref, frame_sem, time_sem,
 ):
     step = pl.program_id(0)
     rows, width = input_ref.shape
-    zh, zl = place_ref[8], place_ref[9]
     time_copy = pltpu.make_async_copy(out_table_ref, time_table_ref, time_sem)
 
     @pl.when(step == 0)
     def _():
         frame_copies = [
             pltpu.make_async_copy(
-                all_ref.at[pl.ds(0, 9), core, pl.ds(LANES + 16 * slot, 16), :],
-                frame_table_ref.at[2 * ((zh + 4 - slot) % 4) + core],
-                frame_sem.at[2 * slot + core],
-            )
-            for slot in range(4)
+                all_ref.at[pl.ds(0, 9), core, pl.ds(LANES + 16 * zh, 16), :],
+                frame_table_ref.at[2 * zh + core],
+                frame_sem.at[2 * zh + core],
+            )
+            for zh in range(4)
             for core in range(2)
         ]
         for copy in frame_copies:
@@ -164,7 +184,7 @@
                 values.astype(jnp.bfloat16), raised[head].astype(jnp.bfloat16),
                 preferred_element_type=jnp.float32,
             )
-            mixed_ref[(step - 1) * 4 + (zl + 4 - head) % 4] = mixed / total
+            mixed_ref[(step - 1) * 4 + head] = mixed / total
 
     @pl.when(step == pl.num_programs(0) - 1)
     def _():
@@ -187,7 +207,7 @@
     tokens = tokens[0]
     rows, width = tokens.shape
     half = rows // 2
-    zh, zl, core = lax.axis_index("zh"), lax.axis_index("zl"), lax.axis_index("c")
+    zh, core = lax.axis_index("zh"), lax.axis_index("c")
 
     def along(array, axis, by):
         return lax.ppermute(array, axis, rotation(4, by))
@@ -195,57 +215,72 @@
     def swapped(array):
         return lax.ppermute(array, "c", SWAP)
 
-    index = lax.axis_index("y") * 2 + core
-    time_part = lax.dynamic_slice_in_dim(time_qkv, jnp.minimum(index * 32, 216 - 32), 32, 0)
-    index = lax.axis_index("x") * 4 + lax.axis_index("y")
-    out_part = lax.dynamic_slice_in_dim(frame_out, jnp.minimum(index, 8) * 16, 16, 0)
-
+    x, y, zl = lax.axis_index("x"), lax.axis_index("y"), lax.axis_index("zl")
+    start = jnp.minimum(32 * (2 * y + core), 216 - 32) + 8 * zh
+    time_part = lax.dynamic_slice_in_dim(time_qkv, start, 8, 0)
+    start = 16 * jnp.minimum(4 * x + y, 8) + 8 * (zl % 2)
+    out_part = lax.dynamic_slice_in_dim(frame_out, start, 8, 0)
+    part = jnp.concatenate([time_part, out_part], axis=0)
+    parts = lax.all_gather(part, ("zh", "zl"), axis=0, tiled=True)
+
+    before, after = along(tokens, "zh", 1), along(tokens, "zh", 3)
     beside = swapped(tokens)
-    below = along(jnp.concatenate([tokens[:half], out_part], axis=0), "zh", 1)
-    above = along(jnp.concatenate([tokens[half:], out_part], axis=0), "zh", 3)
-    near = jnp.concatenate([below[:half], above[:half]], axis=0)
-    far_top, far_bottom = along(below[:half], "zh", 1), along(above[:half], "zh", 3)
-    below_bottom, above_top = along(tokens[half:], "zh", 1), along(tokens[:half], "zh", 3)
-    late = jnp.concatenate([far_top, far_bottom, below_bottom, above_top], axis=0)
-
-    parts = [time_part] + [along(time_part, "zl", by) for by in (1, 2, 3)]
-    parts += [out_part, below[half:], along(out_part, "zh", 2), above[half:]]
-    tables = lax.all_gather(jnp.concatenate(parts, axis=0), ("x", "y", "c"), axis=0)
+    parts = pl.pallas_call(
+        pack_kernel,
+        out_shape=jax.ShapeDtypeStruct((4 * 32 + 4 * 16, width), parts.dtype),
+        in_specs=[whole(), pl.BlockSpec(memory_space=pl.ANY), pl.BlockSpec(memory_space=pl.ANY)],
+        out_specs=whole(),
+        compiler_params=params(),
+        name="pack",
+    )(parts, before, after)
+    tables = lax.all_gather(parts, ("x", "y", "c"), axis=0)
+    far_top, far_bottom = along(before[:half], "zh", 1), along(after[half:], "zh", 3)
+    early = [tokens, beside, before, after]
+    late = [swapped(before), swapped(after), far_top, far_bottom, swapped(far_top), swapped(far_bottom)]
+    spots = [zh, (zh + 3) % 4, (zh + 1) % 4, (zh + 2) % 4]
+    place = jnp.stack([spot * 2 + side for spot in spots for side in (core, 1 - core)]).astype(jnp.int32)
+
     tables = tables.reshape(4, 8, 192, width)
 
-    spots = [zh, (zh + 3) % 4, (zh + 1) % 4, (zh + 2) % 4]
-    place = [spot * 2 + side for spot in spots for side in (core, 1 - core)]
-    place = jnp.stack(place + [zh, zl]).astype(jnp.int32)
-
-    heads = frame_qkv.reshape(width, 2, 3, HD)
-    wqk = jnp.pad(heads[:, :, :2], ((0, 0), (0, 0), (0, 0), (0, LANES - HD))).reshape(width, 4 * LANES)
-    wvt = jnp.pad(jnp.transpose(heads[:, :, 2], (1, 2, 0)), ((0, 0), (0, HP - HD), (0, 0)))
-    wvt = wvt.reshape(2 * HP, width)
-
-    count = 4 * rows
-    shapes = (
-        jax.ShapeDtypeStruct((count, 4 * LANES), jnp.bfloat16),
-        jax.ShapeDtypeStruct((2 * HP, count), jnp.bfloat16),
-    )
+    wqk, wvt = pl.pallas_call(
+        spread_kernel,
+        out_shape=(
+            jax.ShapeDtypeStruct((4 * LANES, width), jnp.bfloat16),
+            jax.ShapeDtypeStruct((2 * HP, width), jnp.bfloat16),
+        ),
+        in_specs=[whole()],
+        out_specs=(whole(), whole()),
+        compiler_params=params(),
+        name="spread",
+    )(frame_qkv.T)
+
+    soon = rows * len(early)
     qk, vt = pl.pallas_call(
         early_kernel,
-        out_shape=shapes,
-        in_specs=[whole()] * 7,
+        out_shape=(
+            jax.ShapeDtypeStruct((soon, 4 * LANES), jnp.bfloat16),
+            jax.ShapeDtypeStruct((2 * HP, soon), jnp.bfloat16),
+        ),
+        in_specs=[whole()] * (len(early) + 3),
         out_specs=(whole(), whole()),
         compiler_params=params(),
-        cost_estimate=pl.CostEstimate(flops=10**9, bytes_accessed=5 * 10**6, transcendentals=0),
+        cost_estimate=pl.CostEstimate(flops=2 * 10**9, bytes_accessed=5 * 10**6, transcendentals=0),
         name="early_triples",
-    )(tokens, beside, near, swapped(near), modulation, wqk, wvt)
-
+    )(*early, modulation, wqk, wvt)
+
+    rest = 4 * rows
     mixed = pl.pallas_call(
         frame_kernel,
-        out_shape=jax.ShapeDtypeStruct((2 * count // LANES, 2 * HD, LANES), jnp.bfloat16),
-        in_specs=[pl.BlockSpec(memory_space=pltpu.SMEM)] + [whole()] * 7,
+        out_shape=jax.ShapeDtypeStruct(((soon + rest) // LANES, 2 * HD, LANES), jnp.bfloat16),
+        in_specs=[pl.BlockSpec(memory_space=pltpu.SMEM)] + [whole()] * 11,
         out_specs=whole(),
-        scratch_shapes=[pltpu.VMEM(shape.shape, shape.dtype) for shape in shapes],
+        scratch_shapes=[
+            pltpu.VMEM((rest, 4 * LANES), jnp.bfloat16),
+            pltpu.VMEM((2 * HP, rest), jnp.bfloat16),
+        ],
         compiler_params=params(),
         name="frame_attention",
-    )(place, late, swapped(late), qk, vt, modulation, wqk, wvt)
+    )(place, *late, qk, vt, modulation, wqk, wvt)
 
     mixed = lax.all_to_all(mixed, ("zh", "c"), 0, 0, tiled=True)
     joined = pl.pallas_call(
@@ -263,7 +298,6 @@
         grid=(5,),
         out_shape=jax.ShapeDtypeStruct((rows, width), jnp.bfloat16),
         in_specs=[
-            pl.BlockSpec(memory_space=pltpu.SMEM),
             whole(),
             pl.BlockSpec((1, 8, LANES, width), lambda i: (jnp.maximum(i - 1, 0), 0, 0, 0)),
             pl.BlockSpec(memory_space=pl.ANY),
@@ -282,7 +316,7 @@
         ],
         compiler_params=params(),
         name="time_block",
-    )(place, joined, tables, tables.reshape(16, 2, 192, width), time_out, modulation)
+    )(joined, tables, tables.reshape(16, 2, 192, width), time_out, modulation)
     out = lax.all_to_all(out, ("x", "zl"), 0, 0, tiled=True)
     return out[None]
 

time: 198 us -> 203 us (1.025)
  blocking collectives: 56.6 us -> 110 us
  waiting for transfers between devices: 34.5 us -> 8.6 us
  starting transfers between devices: 59.2 us -> 43.2 us
  local copies, waits for them, and re-layouts: 12.3 us -> 4.23 us
  Pallas kernels: 20 us -> 22.7 us
    all_gather x0 -> x1, blocking collectives: none -> 47.3 us  [shards(): parts = lax.all_gather(part, ('zh', 'zl'), axis=0, tiled=True)]
    ppermute x10 -> x4, starting transfers between devices: 51.5 us -> 24.5 us  [along(): return lax.ppermute(array, axis, rotation(4, by))]
    ppermute x10 -> x4, waiting for transfers between devices: 34 us -> 8.57 us  [along(): return lax.ppermute(array, axis, rotation(4, by))]
    ppermute x3 -> x5, starting transfers between devices: 7.75 us -> 18.7 us  [swapped(): return lax.ppermute(array, 'c', SWAP)]
    unnamed x27 -> x12, local copies, waits for them, and re-layouts: 7.33 us -> 2 us
    all_to_all x1, blocking collectives: 21.4 us -> 25.8 us  [shards(): mixed = lax.all_to_all(mixed, ('zh', 'c'), 0, 0, tiled=True)]
    pallas_call x2 -> x4, Pallas kernels: 9.34 us -> 11 us  [the longest x1 7.42 us: shards(): pl.pallas_call(frame_kernel, out_shape=jax.ShapeDtypeStruct(((soon + rest...]
  transfers between devices with their start and end apart: 14 -> 10, of which waited for: 5 -> 2; matrix products, arithmetic and copies ran while one was open for 5% -> 1% of each run, Pallas kernels for 5% -> 6%
where the time goes in v6:
time: 203 us; the launch traced here: 202 us
  blocking collectives  110 us (54%)
  starting transfers between devices  43.2 us (21%)
  Pallas kernels  22.7 us (11%)
  between operations  13.7 us (7%)
  waiting for transfers between devices  8.6 us (4%)
  local copies, waits for them, and re-layouts  4.23 us (2%)
    all_gather x1, blocking collectives, shards(): parts = lax.all_gather(part, ('zh', 'zl'), axis=0, tiled=True)  47.3 us
    all_to_all x1, blocking collectives, shards(): mixed = lax.all_to_all(mixed, ('zh', 'c'), 0, 0, tiled=True)  25.8 us
    ppermute x4, starting transfers between devices, along(): return lax.ppermute(array, axis, rotation(4, by))  24.5 us
    all_to_all x1, blocking collectives, shards(): joined = lax.all_to_all(joined, ('x', 'zl'), 0, 0, tiled=True)  22.5 us
    ppermute x5, starting transfers between devices, swapped(): return lax.ppermute(array, 'c', SWAP)  18.7 us
    all_to_all x1, blocking collectives, shards(): out = lax.all_to_all(out, ('x', 'zl'), 0, 0, tiled=True)  14.2 us
    pallas_call x1, Pallas kernels, shards(): pl.pallas_call(functools.partial(time_kernel, rows // 16), grid=(5,), out...  10.4 us
    ppermute x4, waiting for transfers between devices, along(): return lax.ppermute(array, axis, rotation(4, by))  8.57 us
  transfers between devices with their start and end apart: 10, of which 2 were waited for; matrix products, arithmetic and copies ran while one was open for 1% of the time, Pallas kernels for 6%

profile of v6, /device:TPU:1, one launch (start us, length us, event | category | flops | bytes accessed | tf_op | source)
XLA Modules:
  0.0 202.1 jit_solution(1845870831995239264)
XLA Ops:
  6.5 0.0 copy-start.3
  6.5 0.0 copy-start.4
  6.5 0.0 all-gather.3.cloned.1.call-start
  6.5 9.8 %collective-permute-start = (bf16[128,1152]{1,0:T(8,128)(2,1)}, bf16[128,1152]{1,0:T(8,128)(2,1)S(1)}, u32[]{:S(2)}, u32[]{:S(2)}) collective-permute-start(bf16[128,1152]{1,0:T(8,128)(2,1)} %bitcast.8.refs_0_.tokens_ref), channel_id=1, source_target_pairs={{0,2},{2,4},{4,6},{6,0},{1,3},{3,5},{5,7},{7,1},{8,10},{10,12},{12... | collective-permute-start | bytes 884744 | tf_op jit(solution)/shard_map/ppermute | solution.py:213
  16.3 5.6 %collective-permute-start.2 = (bf16[128,1152]{1,0:T(8,128)(2,1)}, bf16[128,1152]{1,0:T(8,128)(2,1)S(1)}, u32[]{:S(2)}, u32[]{:S(2)}) collective-permute-start(bf16[128,1152]{1,0:T(8,128)(2,1)} %bitcast.8.refs_0_.tokens_ref), channel_id=1, source_target_pairs={{0,6},{2,0},{4,2},{6,4},{1,7},{3,1},{5,3},{7,5},{8,14},{10,8},{12,... | collective-permute-start | bytes 884744 | tf_op jit(solution)/shard_map/ppermute | solution.py:213
  21.9 0.8 constant_dynamic-slice_fusion
  22.7 47.3 %all_gather.9.parts_ref = bf16[256,1152]{1,0:T(8,128)(2,1)S(1)} all-gather(bf16[16,1152]{1,0:T(8,128)(2,1)S(1)} %pad_maximum_fusion), channel_id=1, replica_groups=mesh['y'=4,'x'=4,'zl'=4,'zh'=4,'c'=2] {'zh','zl'}, dimensions={0}, use_global_device_ids=true | all-gather | bytes 626688 | tf_op jit(solution)/shard_map/all_gather | solution.py:224
  70.0 0.0 collective-permute-done.refs_2_.below_ref
  70.0 0.0 collective-permute-done.2.refs_3_.above_ref
  70.0 0.8 pack.1
  70.8 0.0 all-gather.3.cloned.1.call-update
  70.9 9.4 %collective-permute-start.8 = (bf16[128,1152]{1,0:T(8,128)(2,1)}, bf16[128,1152]{1,0:T(8,128)(2,1)}, u32[]{:S(2)}, u32[]{:S(2)}) collective-permute-start(bf16[128,1152]{1,0:T(8,128)(2,1)} %bitcast.8.refs_0_.tokens_ref), channel_id=1, source_target_pairs={{0,1},{1,0},{2,3},{3,2},{4,5},{5,4},{6,7},{7,6},{8,9},{9,8},{10,11... | collective-permute-start | bytes 884744 | tf_op jit(solution)/shard_map/ppermute | solution.py:216
  80.3 0.7 slice.8
  81.0 4.5 %collective-permute-start.4 = (bf16[64,1152]{1,0:T(8,128)(2,1)}, bf16[64,1152]{1,0:T(8,128)(2,1)S(1)}, u32[]{:S(2)}, u32[]{:S(2)}) collective-permute-start(bf16[64,1152]{1,0:T(8,128)(2,1)} %slice.8), channel_id=1, source_target_pairs={{0,2},{2,4},{4,6},{6,0},{1,3},{3,5},{5,7},{7,1},{8,10},{10,12},{12... | collective-permute-start | bytes 442376 | tf_op jit(solution)/shard_map/ppermute | solution.py:213
  85.4 0.7 slice.9
  86.1 4.7 %collective-permute-start.5 = (bf16[64,1152]{1,0:T(8,128)(2,1)}, bf16[64,1152]{1,0:T(8,128)(2,1)}, u32[]{:S(2)}, u32[]{:S(2)}) collective-permute-start(bf16[64,1152]{1,0:T(8,128)(2,1)} %slice.9), channel_id=1, source_target_pairs={{0,6},{2,0},{4,2},{6,4},{1,7},{3,1},{5,3},{7,5},{8,14},{10,8},{12,... | collective-permute-start | bytes 442376 | tf_op jit(solution)/shard_map/ppermute | solution.py:213
  90.8 2.5 %collective-permute-start.1 = (bf16[128,1152]{1,0:T(8,128)(2,1)S(1)}, bf16[128,1152]{1,0:T(8,128)(2,1)}, u32[]{:S(2)}, u32[]{:S(2)}) collective-permute-start(bf16[128,1152]{1,0:T(8,128)(2,1)S(1)} %collective-permute-done.refs_2_.below_ref), channel_id=1, source_target_pairs={{0,1},{1,0},{2,3},{3,2},{4,5},{5,4},{6,7},{7,6},{8,9},{9,8},{10,11... | collective-permute-start | bytes 884744 | tf_op jit(solution)/shard_map/ppermute | solution.py:216
  93.3 1.9 collective-permute-start.3
  95.3 0.0 copy-done.3
  95.3 0.1 spread.1
  95.4 0.0 copy-done.4
  95.4 0.0 copy-start.1
  95.5 0.1 stack.35.place_ref
  95.5 5.8 %collective-permute-done.4.one_ref = bf16[64,1152]{1,0:T(8,128)(2,1)S(1)} collective-permute-done((bf16[64,1152]{1,0:T(8,128)(2,1)}, bf16[64,1152]{1,0:T(8,128)(2,1)S(1)}, u32[]{:S(2)}, u32[]{:S(2)}) %collective-permute-start.4) | collective-permute-done | bytes 147488 | tf_op jit(solution)/shard_map/ppermute | solution.py:213
  101.3 2.5 %collective-permute-start.6 = (bf16[64,1152]{1,0:T(8,128)(2,1)S(1)}, bf16[64,1152]{1,0:T(8,128)(2,1)S(1)}, u32[]{:S(2)}, u32[]{:S(2)}) collective-permute-start(bf16[64,1152]{1,0:T(8,128)(2,1)S(1)} %collective-permute-done.4.one_ref), channel_id=1, source_target_pairs={{0,1},{1,0},{2,3},{3,2},{4,5},{5,4},{6,7},{7,6},{8,9},{9,8},{10,11... | collective-permute-start | bytes 442376 | tf_op jit(solution)/shard_map/ppermute | solution.py:216
  103.9 2.8 %collective-permute-done.5.two_ref = bf16[64,1152]{1,0:T(8,128)(2,1)} collective-permute-done((bf16[64,1152]{1,0:T(8,128)(2,1)}, bf16[64,1152]{1,0:T(8,128)(2,1)}, u32[]{:S(2)}, u32[]{:S(2)}) %collective-permute-start.5) | collective-permute-done | bytes 147488 | tf_op jit(solution)/shard_map/ppermute | solution.py:213
  106.6 2.4 %collective-permute-start.7 = (bf16[64,1152]{1,0:T(8,128)(2,1)}, bf16[64,1152]{1,0:T(8,128)(2,1)S(1)}, u32[]{:S(2)}, u32[]{:S(2)}) collective-permute-start(bf16[64,1152]{1,0:T(8,128)(2,1)} %collective-permute-done.5.two_ref), channel_id=1, source_target_pairs={{0,1},{1,0},{2,3},{3,2},{4,5},{5,4},{6,7},{7,6},{8,9},{9,8},{10,11... | collective-permute-start | bytes 442376 | tf_op jit(solution)/shard_map/ppermute | solution.py:216
  109.0 0.0 collective-permute-done.8.refs_1_
  109.0 2.7 %early_triples.1 = (bf16[512,512]{1,0:T(8,128)(2,1)S(1)}, bf16[160,512]{1,0:T(8,128)(2,1)S(1)}) custom-call(bf16[128,1152]{1,0:T(8,128)(2,1)} %bitcast.8.refs_0_.tokens_ref, bf16[128,1152]{1,0:T(8,128)(2,1)} %collective-permute-done.8.refs_1_, bf16[128,1152]{1,0:T(8,128)(2,1)S(1)} %collective-permute-done.refs_2_.below_ref, ...), custom_call_target="tpu_custom_call" | custom-call | flops 2000000000 | bytes 5000000 | tf_op jit(solution)/shard_map/early_triples/pallas_call | solution.py:258
  111.7 0.0 copy-done.1
  111.7 0.0 collective-permute-done.6.three_ref
  111.7 0.0 collective-permute-done.7.four_ref
  111.7 0.0 collective-permute-done.1.below_ref
  111.7 0.0 collective-permute-done.3.above_ref
  111.7 0.0 copy-start.2
  111.8 1.3 copy-done.2
  113.0 0.0 copy-start
  113.0 7.4 %frame_attention.1 = bf16[8,144,128]{2,1,0:T(8,128)(2,1)S(1)} custom-call(s32[8]{0:T(128)S(1)} %stack.35.place_ref, bf16[128,1152]{1,0:T(8,128)(2,1)} %collective-permute-done.1.below_ref, bf16[128,1152]{1,0:T(8,128)(2,1)} %collective-permute-done.3.above_ref, bf16[64,1152]{1,0:T(8,128)(2,1)S(1)} %collective-permute-done.4.one_ref, ...), custom_call_target="tpu_custom_call" | custom-call | tf_op jit(solution)/shard_map/frame_attention/pallas_call | solution.py:272
  120.4 25.8 %all_to_all.25.mixed_ref = bf16[8,144,128]{2,1,0:T(8,128)(2,1)S(1)} all-to-all(bf16[8,144,128]{2,1,0:T(8,128)(2,1)S(1)} %frame_attention.1), channel_id=1, replica_groups=mesh['y'=4,'x'=4,'zl'=4,'zh'=4,'c'=2] {'zh','c'}, dimensions={0} | all-to-all | bytes 589824 | tf_op jit(solution)/shard_map/all_to_all | solution.py:285
  146.2 1.2 join.1
  147.5 22.5 %all_to_all.26 = bf16[16,8,2304]{2,1,0:T(8,128)(2,1)S(1)} all-to-all(bf16[16,8,2304]{2,1,0:T(8,128)(2,1)S(1)} %bitcast.16), channel_id=1, replica_groups=mesh['y'=4,'x'=4,'zl'=4,'zh'=4,'c'=2] {'x','zl'}, dimensions={0} | all-to-all | bytes 1179648 | tf_op jit(solution)/shard_map/all_to_all | solution.py:294
  169.9 0.0 all-gather.3.cloned.1.call-done
  169.9 0.0 copy-done
  169.9 10.4 %time_block.1 = bf16[128,1152]{1,0:T(8,128)(2,1)S(1)} custom-call(bf16[128,2304]{1,0:T(8,128)(2,1)S(1)} %bitcast.17, bf16[4,8,192,1152]{3,2,1,0:T(8,128)(2,1)} %bitcast.20, bf16[16,2,192,1152]{3,2,1,0:T(8,128)(2,1)} %bitcast.21, bf16[1152,1152]{1,0:T(8,128)(2,1)S(1)} %copy-done, f32[2,3,1152]{2,1,0:T(4,128)S(1)} %copy.7.refs_4_.modulation_ref), custom_call_target="tpu_custom_call" | custom-call | tf_op jit(solution)/shard_map/time_block/pallas_call | solution.py:296
  180.4 14.2 %all_to_all.27 = bf16[16,8,1152]{2,1,0:T(8,128)(2,1)S(1)} all-to-all(bf16[16,8,1152]{2,1,0:T(8,128)(2,1)S(1)} %bitcast.18), channel_id=1, replica_groups=mesh['y'=4,'x'=4,'zl'=4,'zh'=4,'c'=2] {'x','zl'}, dimensions={0} | all-to-all | bytes 589824 | tf_op jit(solution)/shard_map/all_to_all | solution.py:320
  194.5 0.7 copy.11
  (2 shorter events, 0.0 us)
Async XLA Ops:
  6.5 88.8 %copy-start.3 = (bf16[1152,432]{0,1:T(8,128)(2,1)S(1)}, bf16[1152,432]{0,1:T(8,128)(2,1)}, u32[]{:S(2)}) copy-start(bf16[1152,432]{0,1:T(8,128)(2,1)} %param.7) | copy-start | bytes 2985988
  6.5 88.9 %copy-start.4 = (f32[2,3,1152]{2,0,1:T(2,128)S(1)}, f32[2,3,1152]{2,0,1:T(2,128)}, u32[]{:S(2)}) copy-start(f32[2,3,1152]{2,0,1:T(2,128)} %param.11) | copy-start | bytes 82948
  6.5 163.4 %all-gather.3.cloned.1.call-start = ((), (), s32[]{:S(2)}) async-start(), calls=%async_computation.3 | async-start | bytes 14598144 | tf_op jit(solution)/shard_map/all_gather | solution.py:236
  6.5 63.5 %collective-permute-start = (bf16[128,1152]{1,0:T(8,128)(2,1)}, bf16[128,1152]{1,0:T(8,128)(2,1)S(1)}, u32[]{:S(2)}, u32[]{:S(2)}) collective-permute-start(bf16[128,1152]{1,0:T(8,128)(2,1)} %bitcast.8.refs_0_.tokens_ref), channel_id=1, source_target_pairs={{0,2},{2,4},{4,6},{6,0},{1,3},{3,5},{5,7},{7,1},{8,10},{10,12},{12... | collective-permute-start | bytes 884744 | tf_op jit(solution)/shard_map/ppermute | solution.py:213
  16.3 53.7 %collective-permute-start.2 = (bf16[128,1152]{1,0:T(8,128)(2,1)}, bf16[128,1152]{1,0:T(8,128)(2,1)S(1)}, u32[]{:S(2)}, u32[]{:S(2)}) collective-permute-start(bf16[128,1152]{1,0:T(8,128)(2,1)} %bitcast.8.refs_0_.tokens_ref), channel_id=1, source_target_pairs={{0,6},{2,0},{4,2},{6,4},{1,7},{3,1},{5,3},{7,5},{8,14},{10,8},{12,... | collective-permute-start | bytes 884744 | tf_op jit(solution)/shard_map/ppermute | solution.py:213
  70.9 38.2 %collective-permute-start.8 = (bf16[128,1152]{1,0:T(8,128)(2,1)}, bf16[128,1152]{1,0:T(8,128)(2,1)}, u32[]{:S(2)}, u32[]{:S(2)}) collective-permute-start(bf16[128,1152]{1,0:T(8,128)(2,1)} %bitcast.8.refs_0_.tokens_ref), channel_id=1, source_target_pairs={{0,1},{1,0},{2,3},{3,2},{4,5},{5,4},{6,7},{7,6},{8,9},{9,8},{10,11... | collective-permute-start | bytes 884744 | tf_op jit(solution)/shard_map/ppermute | solution.py:216
  81.0 20.3 %collective-permute-start.4 = (bf16[64,1152]{1,0:T(8,128)(2,1)}, bf16[64,1152]{1,0:T(8,128)(2,1)S(1)}, u32[]{:S(2)}, u32[]{:S(2)}) collective-permute-start(bf16[64,1152]{1,0:T(8,128)(2,1)} %slice.8), channel_id=1, source_target_pairs={{0,2},{2,4},{4,6},{6,0},{1,3},{3,5},{5,7},{7,1},{8,10},{10,12},{12... | collective-permute-start | bytes 442376 | tf_op jit(solution)/shard_map/ppermute | solution.py:213
  86.1 20.5 %collective-permute-start.5 = (bf16[64,1152]{1,0:T(8,128)(2,1)}, bf16[64,1152]{1,0:T(8,128)(2,1)}, u32[]{:S(2)}, u32[]{:S(2)}) collective-permute-start(bf16[64,1152]{1,0:T(8,128)(2,1)} %slice.9), channel_id=1, source_target_pairs={{0,6},{2,0},{4,2},{6,4},{1,7},{3,1},{5,3},{7,5},{8,14},{10,8},{12,... | collective-permute-start | bytes 442376 | tf_op jit(solution)/shard_map/ppermute | solution.py:213
  90.8 20.9 %collective-permute-start.1 = (bf16[128,1152]{1,0:T(8,128)(2,1)S(1)}, bf16[128,1152]{1,0:T(8,128)(2,1)}, u32[]{:S(2)}, u32[]{:S(2)}) collective-permute-start(bf16[128,1152]{1,0:T(8,128)(2,1)S(1)} %collective-permute-done.refs_2_.below_ref), channel_id=1, source_target_pairs={{0,1},{1,0},{2,3},{3,2},{4,5},{5,4},{6,7},{7,6},{8,9},{9,8},{10,11... | collective-permute-start | bytes 884744 | tf_op jit(solution)/shard_map/ppermute | solution.py:216
  93.3 18.4 %collective-permute-start.3 = (bf16[128,1152]{1,0:T(8,128)(2,1)S(1)}, bf16[128,1152]{1,0:T(8,128)(2,1)}, u32[]{:S(2)}, u32[]{:S(2)}) collective-permute-start(bf16[128,1152]{1,0:T(8,128)(2,1)S(1)} %collective-permute-done.2.refs_3_.above_ref), channel_id=1, source_target_pairs={{0,1},{1,0},{2,3},{3,2},{4,5},{5,4},{6,7},{7,6},{8,9},{9,8},{10,11... | collective-permute-start | bytes 884744 | tf_op jit(solution)/shard_map/ppermute | solution.py:216
  95.4 16.3 %copy-start.1 = (bf16[512,1152]{1,0:T(8,128)(2,1)}, bf16[512,1152]{1,0:T(8,128)(2,1)S(1)}, u32[]{:S(2)}) copy-start(bf16[512,1152]{1,0:T(8,128)(2,1)S(1)} %get-tuple-element.9.refs_5_.wqk_ref) | copy-start | bytes 3538948
  101.3 10.4 %collective-permute-start.6 = (bf16[64,1152]{1,0:T(8,128)(2,1)S(1)}, bf16[64,1152]{1,0:T(8,128)(2,1)S(1)}, u32[]{:S(2)}, u32[]{:S(2)}) collective-permute-start(bf16[64,1152]{1,0:T(8,128)(2,1)S(1)} %collective-permute-done.4.one_ref), channel_id=1, source_target_pairs={{0,1},{1,0},{2,3},{3,2},{4,5},{5,4},{6,7},{7,6},{8,9},{9,8},{10,11... | collective-permute-start | bytes 442376 | tf_op jit(solution)/shard_map/ppermute | solution.py:216
  106.6 5.1 %collective-permute-start.7 = (bf16[64,1152]{1,0:T(8,128)(2,1)}, bf16[64,1152]{1,0:T(8,128)(2,1)S(1)}, u32[]{:S(2)}, u32[]{:S(2)}) collective-permute-start(bf16[64,1152]{1,0:T(8,128)(2,1)} %collective-permute-done.5.two_ref), channel_id=1, source_target_pairs={{0,1},{1,0},{2,3},{3,2},{4,5},{5,4},{6,7},{7,6},{8,9},{9,8},{10,11... | collective-permute-start | bytes 442376 | tf_op jit(solution)/shard_map/ppermute | solution.py:216
  111.7 1.3 copy-start.2
  113.0 56.9 %copy-start = (bf16[1152,1152]{1,0:T(8,128)(2,1)S(1)}, bf16[1152,1152]{1,0:T(8,128)(2,1)}, u32[]{:S(2)}) copy-start(bf16[1152,1152]{1,0:T(8,128)(2,1)} %out_table_ref.1) | copy-start | bytes 7962628
Sparse Core Ops, SparseCore 0:
  71.0 86.7 all-gather.2

commit v7 on v5

--- a/solution.py
+++ b/solution.py
@@ -110,6 +110,13 @@
             out_ref[place_ref[2 * number + part]] = both[:, part * LANES : (part + 1) * LANES]
 
 
+def pack_kernel(parts_ref, out_ref):
+    parts = parts_ref[...].astype(jnp.float32)
+    rows = [parts[16 * (4 * zh + zl) : 16 * (4 * zh + zl) + 8] for zl in range(4) for zh in range(4)]
+    rows += [parts[16 * (4 * zh + zl) + 8 : 16 * (4 * zh + zl) + 16] for zh in range(4) for zl in range(2)]
+    out_ref[...] = jnp.concatenate(rows, axis=0).astype(jnp.bfloat16)
+
+
 def middle_kernel(mixed_ref, tables_ref, tokens_ref, modulation_ref, out_ref, table_ref, sem):
     copy = pltpu.make_async_copy(tables_ref.at[pl.ds(0, 9), :, pl.ds(LANES, 64), :], table_ref, sem)
     copy.start()
@@ -204,14 +211,22 @@
         [spot * 2 + side for spot in spots for side in (core, 1 - core)]
     ).astype(jnp.int32)
 
-    index = lax.axis_index("y") * 2 + core
-    time_part = lax.dynamic_slice_in_dim(time_qkv, jnp.minimum(index * 32, 216 - 32), 32, 0)
-    index = lax.axis_index("x") * 4 + lax.axis_index("y")
-    out_part = lax.dynamic_slice_in_dim(frame_out, jnp.minimum(index, 8) * 16, 16, 0)
-    time_parts = lax.all_gather(time_part, "zl", axis=0, tiled=True)
-    out_parts = lax.all_gather(out_part, "zh", axis=0, tiled=True)
-    parts = [time_parts, out_parts]
-    tables = lax.all_gather(jnp.concatenate(parts, axis=0), ("x", "y", "c"), axis=0)
+    x, y, zl = lax.axis_index("x"), lax.axis_index("y"), lax.axis_index("zl")
+    start = jnp.minimum(32 * (2 * y + core), 216 - 32) + 8 * zh
+    time_part = lax.dynamic_slice_in_dim(time_qkv, start, 8, 0)
+    start = 16 * jnp.minimum(4 * x + y, 8) + 8 * (zl % 2)
+    out_part = lax.dynamic_slice_in_dim(frame_out, start, 8, 0)
+    part = jnp.concatenate([time_part, out_part], axis=0)
+    parts = lax.all_gather(part, ("zh", "zl"), axis=0, tiled=True)
+    parts = pl.pallas_call(
+        pack_kernel,
+        out_shape=jax.ShapeDtypeStruct((4 * 32 + 4 * 16, width), parts.dtype),
+        in_specs=[whole()],
+        out_specs=whole(),
+        compiler_params=params(),
+        name="pack",
+    )(parts)
+    tables = lax.all_gather(parts, ("x", "y", "c"), axis=0)
     tables = tables.reshape(4, 8, 192, width)
 
     wqk, wvt = pl.pallas_call(

time: 188 us -> 181 us (0.963)
  starting transfers between devices: 33.5 us -> 43.6 us
  blocking collectives: 97 us -> 87.2 us
  waiting for transfers between devices: 14.6 us -> 9.5 us
    all_to_all x1, blocking collectives: 24.6 us -> 15.7 us  [shards(): middle = lax.all_to_all(middle, ('x', 'zl'), 0, 0, tiled=True)]
    ppermute x5, starting transfers between devices: 19.5 us -> 25.3 us  [swapped(): return lax.ppermute(array, 'c', SWAP)]
    ppermute x4, waiting for transfers between devices: 14.5 us -> 9.47 us  [along(): return lax.ppermute(array, axis, rotation(4, by))]
    ppermute x4, starting transfers between devices: 14 us -> 18.4 us  [along(): return lax.ppermute(array, axis, rotation(4, by))]
    all_gather x2 -> x1, blocking collectives: 36.3 us -> 32.1 us  [shards(): parts = lax.all_gather(part, ('zh', 'zl'), axis=0, tiled=True)]
    all_to_all x1, blocking collectives: 22.2 us -> 24.9 us  [shards(): mixed = lax.all_to_all(mixed, ('zh', 'c'), 0, 0, tiled=True)]
    unnamed x12 -> x10, local copies, waits for them, and re-layouts: 2.7 us -> 0.74 us
  transfers between devices with their start and end apart: 10 -> 10, of which waited for: 2 -> 1; matrix products, arithmetic and copies ran while one was open for 2% -> 2% of each run, Pallas kernels for 5% -> 6%
where the time goes in v7:
time: 181 us; the launch traced here: 180 us
  blocking collectives  87.2 us (48%)
  starting transfers between devices  43.6 us (24%)
  Pallas kernels  21.1 us (12%)
  between operations  13.6 us (8%)
  waiting for transfers between devices  9.5 us (5%)
  local copies, waits for them, and re-layouts  4.89 us (3%)
    all_gather x1, blocking collectives, shards(): parts = lax.all_gather(part, ('zh', 'zl'), axis=0, tiled=True)  32.1 us
    ppermute x5, starting transfers between devices, swapped(): return lax.ppermute(array, 'c', SWAP)  25.3 us
    all_to_all x1, blocking collectives, shards(): mixed = lax.all_to_all(mixed, ('zh', 'c'), 0, 0, tiled=True)  24.9 us
    ppermute x4, starting transfers between devices, along(): return lax.ppermute(array, axis, rotation(4, by))  18.4 us
    all_to_all x1, blocking collectives, shards(): middle = lax.all_to_all(middle, ('x', 'zl'), 0, 0, tiled=True)  15.7 us
    all_to_all x1, blocking collectives, shards(): out = lax.all_to_all(out, ('x', 'zl'), 0, 0, tiled=True)  14.4 us
    ppermute x4, waiting for transfers between devices, along(): return lax.ppermute(array, axis, rotation(4, by))  9.47 us
    pallas_call x1, Pallas kernels, shards(): pl.pallas_call(functools.partial(time_kernel, rows // 16), grid=(4,), out...  7.81 us
  transfers between devices with their start and end apart: 10, of which 1 were waited for; matrix products, arithmetic and copies ran while one was open for 2% of the time, Pallas kernels for 6%

profile of v7, /device:TPU:1, one launch (start us, length us, event | category | flops | bytes accessed | tf_op | source)
XLA Modules:
  0.0 180.0 jit_solution(15574156959778866267)
XLA Ops:
  6.5 0.0 copy-start.2
  6.5 0.0 copy-start.3
  6.5 0.0 copy-start.1
  6.5 0.0 all-gather.3.cloned.1.call-start
  6.5 0.9 constant_dynamic-slice_fusion
  7.4 32.1 %all_gather.9.parts_ref = bf16[256,1152]{1,0:T(8,128)(2,1)S(1)} all-gather(bf16[16,1152]{1,0:T(8,128)(2,1)S(1)} %pad_maximum_fusion), channel_id=1, replica_groups=mesh['y'=4,'x'=4,'zl'=4,'zh'=4,'c'=2] {'zh','zl'}, dimensions={0}, use_global_device_ids=true | all-gather | bytes 626688 | tf_op jit(solution)/shard_map/all_gather | solution.py:220
  39.6 0.8 pack.1
  40.4 0.0 all-gather.3.cloned.1.call-update
  40.4 3.7 %collective-permute-start = (bf16[128,1152]{1,0:T(8,128)(2,1)}, bf16[128,1152]{1,0:T(8,128)(2,1)}, u32[]{:S(2)}, u32[]{:S(2)}) collective-permute-start(bf16[128,1152]{1,0:T(8,128)(2,1)} %bitcast.20), channel_id=1, source_target_pairs={{0,2},{2,4},{4,6},{6,0},{1,3},{3,5},{5,7},{7,1},{8,10},{10,12},{12... | collective-permute-start | bytes 884744 | tf_op jit(solution)/shard_map/ppermute | solution.py:199
  44.1 5.5 %collective-permute-start.2 = (bf16[128,1152]{1,0:T(8,128)(2,1)}, bf16[128,1152]{1,0:T(8,128)(2,1)}, u32[]{:S(2)}, u32[]{:S(2)}) collective-permute-start(bf16[128,1152]{1,0:T(8,128)(2,1)} %bitcast.21), channel_id=1, source_target_pairs={{0,6},{2,0},{4,2},{6,4},{1,7},{3,1},{5,3},{7,5},{8,14},{10,8},{12,... | collective-permute-start | bytes 884744 | tf_op jit(solution)/shard_map/ppermute | solution.py:199
  49.6 14.1 %collective-permute-start.8 = (bf16[128,1152]{1,0:T(8,128)(2,1)}, bf16[128,1152]{1,0:T(8,128)(2,1)}, u32[]{:S(2)}, u32[]{:S(2)}) collective-permute-start(bf16[128,1152]{1,0:T(8,128)(2,1)} %bitcast.22), channel_id=1, source_target_pairs={{0,1},{1,0},{2,3},{3,2},{4,5},{5,4},{6,7},{7,6},{8,9},{9,8},{10,11... | collective-permute-start | bytes 884744 | tf_op jit(solution)/shard_map/ppermute | solution.py:202
  63.7 9.5 %collective-permute-done.refs_2_ = bf16[128,1152]{1,0:T(8,128)(2,1)} collective-permute-done((bf16[128,1152]{1,0:T(8,128)(2,1)}, bf16[128,1152]{1,0:T(8,128)(2,1)}, u32[]{:S(2)}, u32[]{:S(2)}) %collective-permute-start) | collective-permute-done | bytes 294944 | tf_op jit(solution)/shard_map/ppermute | solution.py:199
  73.2 1.6 slice.8
  74.8 3.8 %collective-permute-start.4 = (bf16[64,1152]{1,0:T(8,128)(2,1)}, bf16[64,1152]{1,0:T(8,128)(2,1)}, u32[]{:S(2)}, u32[]{:S(2)}) collective-permute-start(bf16[64,1152]{1,0:T(8,128)(2,1)} %slice.8), channel_id=1, source_target_pairs={{0,2},{2,4},{4,6},{6,0},{1,3},{3,5},{5,7},{7,1},{8,10},{10,12},{12... | collective-permute-start | bytes 442376 | tf_op jit(solution)/shard_map/ppermute | solution.py:199
  78.6 0.0 collective-permute-done.2.refs_3_
  78.6 1.6 slice.9
  80.2 5.4 %collective-permute-start.5 = (bf16[64,1152]{1,0:T(8,128)(2,1)}, bf16[64,1152]{1,0:T(8,128)(2,1)}, u32[]{:S(2)}, u32[]{:S(2)}) collective-permute-start(bf16[64,1152]{1,0:T(8,128)(2,1)} %slice.9), channel_id=1, source_target_pairs={{0,6},{2,0},{4,2},{6,4},{1,7},{3,1},{5,3},{7,5},{8,14},{10,8},{12,... | collective-permute-start | bytes 442376 | tf_op jit(solution)/shard_map/ppermute | solution.py:199
  85.5 4.9 %collective-permute-start.1 = (bf16[128,1152]{1,0:T(8,128)(2,1)}, bf16[128,1152]{1,0:T(8,128)(2,1)S(1)}, u32[]{:S(2)}, u32[]{:S(2)}) collective-permute-start(bf16[128,1152]{1,0:T(8,128)(2,1)} %collective-permute-done.refs_2_), channel_id=1, source_target_pairs={{0,1},{1,0},{2,3},{3,2},{4,5},{5,4},{6,7},{7,6},{8,9},{9,8},{10,11... | collective-permute-start | bytes 884744 | tf_op jit(solution)/shard_map/ppermute | solution.py:202
  90.5 1.9 %collective-permute-start.3 = (bf16[128,1152]{1,0:T(8,128)(2,1)}, bf16[128,1152]{1,0:T(8,128)(2,1)S(1)}, u32[]{:S(2)}, u32[]{:S(2)}) collective-permute-start(bf16[128,1152]{1,0:T(8,128)(2,1)} %collective-permute-done.2.refs_3_), channel_id=1, source_target_pairs={{0,1},{1,0},{2,3},{3,2},{4,5},{5,4},{6,7},{7,6},{8,9},{9,8},{10,11... | collective-permute-start | bytes 884744 | tf_op jit(solution)/shard_map/ppermute | solution.py:202
  92.4 0.0 copy-done.3
  92.5 0.0 copy-done.1
  92.5 0.1 spread.1
  92.6 0.1 stack.35.place_ref
  92.7 0.0 collective-permute-done.4.one_ref
  92.7 2.4 %collective-permute-start.6 = (bf16[64,1152]{1,0:T(8,128)(2,1)}, bf16[64,1152]{1,0:T(8,128)(2,1)S(1)}, u32[]{:S(2)}, u32[]{:S(2)}) collective-permute-start(bf16[64,1152]{1,0:T(8,128)(2,1)} %collective-permute-done.4.one_ref), channel_id=1, source_target_pairs={{0,1},{1,0},{2,3},{3,2},{4,5},{5,4},{6,7},{7,6},{8,9},{9,8},{10,11... | collective-permute-start | bytes 442376 | tf_op jit(solution)/shard_map/ppermute | solution.py:202
  95.1 0.0 collective-permute-done.5.two_ref
  95.1 1.9 %collective-permute-start.7 = (bf16[64,1152]{1,0:T(8,128)(2,1)}, bf16[64,1152]{1,0:T(8,128)(2,1)S(1)}, u32[]{:S(2)}, u32[]{:S(2)}) collective-permute-start(bf16[64,1152]{1,0:T(8,128)(2,1)} %collective-permute-done.5.two_ref), channel_id=1, source_target_pairs={{0,1},{1,0},{2,3},{3,2},{4,5},{5,4},{6,7},{7,6},{8,9},{9,8},{10,11... | collective-permute-start | bytes 442376 | tf_op jit(solution)/shard_map/ppermute | solution.py:202
  97.0 0.0 collective-permute-done.8.refs_1_
  97.1 0.0 copy-done.2
  97.1 2.7 %early_triples.1 = (bf16[512,512]{1,0:T(8,128)(2,1)S(1)}, bf16[160,512]{1,0:T(8,128)(2,1)S(1)}) custom-call(bf16[128,1152]{1,0:T(8,128)(2,1)S(1)} %bitcast.23, bf16[128,1152]{1,0:T(8,128)(2,1)} %collective-permute-done.8.refs_1_, bf16[128,1152]{1,0:T(8,128)(2,1)} %collective-permute-done.refs_2_, bf16[128,1152]{1,0:T(8,128)(2,1)} %collective-permute-done.2.refs_3_, ...), custom_call_target="tpu_custom_call" | custom-call | flops 2000000000 | bytes 5000000 | tf_op jit(solution)/shard_map/early_triples/pallas_call | solution.py:245
  99.8 0.0 collective-permute-done.6.three_ref
  99.8 0.0 collective-permute-done.7.four_ref
  99.8 0.0 collective-permute-done.1.below_ref
  99.8 0.0 collective-permute-done.3.above_ref
  99.9 7.2 %frame_attention.1 = bf16[8,144,128]{2,1,0:T(8,128)(2,1)S(1)} custom-call(s32[8]{0:T(128)S(1)} %stack.35.place_ref, bf16[128,1152]{1,0:T(8,128)(2,1)S(1)} %collective-permute-done.1.below_ref, bf16[128,1152]{1,0:T(8,128)(2,1)S(1)} %collective-permute-done.3.above_ref, bf16[64,1152]{1,0:T(8,128)(2,1)} %collective-permute-done.4.one_ref, ...), custom_call_target="tpu_custom_call" | custom-call | tf_op jit(solution)/shard_map/frame_attention/pallas_call | solution.py:259
  107.0 24.9 %all_to_all.25.mixed_ref = bf16[8,144,128]{2,1,0:T(8,128)(2,1)S(1)} all-to-all(bf16[8,144,128]{2,1,0:T(8,128)(2,1)S(1)} %frame_attention.1), channel_id=1, replica_groups=mesh['y'=4,'x'=4,'zl'=4,'zh'=4,'c'=2] {'zh','c'}, dimensions={0} | all-to-all | bytes 589824 | tf_op jit(solution)/shard_map/all_to_all | solution.py:272
  132.0 0.0 all-gather.3.cloned.1.call-done
  132.0 0.0 copy-start
  132.0 2.5 %middle.1 = bf16[128,1152]{1,0:T(8,128)(2,1)S(1)} custom-call(bf16[8,144,128]{2,1,0:T(8,128)(2,1)S(1)} %all_to_all.25.mixed_ref, bf16[16,2,192,1152]{3,2,1,0:T(8,128)(2,1)} %bitcast.25, bf16[128,1152]{1,0:T(8,128)(2,1)S(1)} %bitcast.24, f32[2,3,1152]{2,1,0:T(4,128)S(1)} %copy.7.refs_4_.modulation_ref), custom_call_target="tpu_custom_call" | custom-call | tf_op jit(solution)/shard_map/middle/pallas_call | solution.py:273
  134.5 15.7 %all_to_all.26 = bf16[16,8,1152]{2,1,0:T(8,128)(2,1)S(1)} all-to-all(bf16[16,8,1152]{2,1,0:T(8,128)(2,1)S(1)} %bitcast.18), channel_id=1, replica_groups=mesh['y'=4,'x'=4,'zl'=4,'zh'=4,'c'=2] {'x','zl'}, dimensions={0} | all-to-all | bytes 589824 | tf_op jit(solution)/shard_map/all_to_all | solution.py:283
  150.2 0.0 copy-done
  150.2 7.8 %time_block.1 = bf16[128,1152]{1,0:T(8,128)(2,1)S(1)} custom-call(bf16[128,1152]{1,0:T(8,128)(2,1)S(1)} %bitcast.16, bf16[4,8,192,1152]{3,2,1,0:T(8,128)(2,1)} %bitcast.26, bf16[1152,1152]{1,0:T(8,128)(2,1)S(1)} %copy-done, f32[2,3,1152]{2,1,0:T(4,128)S(1)} %copy.7.refs_4_.modulation_ref), custom_call_target="tpu_custom_call" | custom-call | tf_op jit(solution)/shard_map/time_block/pallas_call | solution.py:285
  158.0 14.4 %all_to_all.27 = bf16[16,8,1152]{2,1,0:T(8,128)(2,1)S(1)} all-to-all(bf16[16,8,1152]{2,1,0:T(8,128)(2,1)S(1)} %bitcast.17), channel_id=1, replica_groups=mesh['y'=4,'x'=4,'zl'=4,'zh'=4,'c'=2] {'x','zl'}, dimensions={0} | all-to-all | bytes 589824 | tf_op jit(solution)/shard_map/all_to_all | solution.py:305
  172.4 0.7 copy.12
  (2 shorter events, 0.0 us)
Async XLA Ops:
  6.5 90.5 %copy-start.2 = (bf16[1,128,1152]{2,1,0:T(8,128)(2,1)S(1)}, bf16[1,128,1152]{2,1,0:T(8,128)(2,1)}, u32[]{:S(2)}) copy-start(bf16[1,128,1152]{2,1,0:T(8,128)(2,1)} %param.6) | copy-start | bytes 884740
  6.5 85.9 %copy-start.3 = (f32[2,3,1152]{2,0,1:T(2,128)S(1)}, f32[2,3,1152]{2,0,1:T(2,128)}, u32[]{:S(2)}) copy-start(f32[2,3,1152]{2,0,1:T(2,128)} %param.11) | copy-start | bytes 82948
  6.5 85.9 %copy-start.1 = (bf16[1152,432]{0,1:T(8,128)(2,1)S(1)}, bf16[1152,432]{0,1:T(8,128)(2,1)}, u32[]{:S(2)}) copy-start(bf16[1152,432]{0,1:T(8,128)(2,1)} %param.7) | copy-start | bytes 2985988
  6.5 125.4 %all-gather.3.cloned.1.call-start = ((), (), s32[]{:S(2)}) async-start(), calls=%async_computation.3 | async-start | bytes 14598144 | tf_op jit(solution)/shard_map/all_gather | solution.py:229
  40.4 32.8 %collective-permute-start = (bf16[128,1152]{1,0:T(8,128)(2,1)}, bf16[128,1152]{1,0:T(8,128)(2,1)}, u32[]{:S(2)}, u32[]{:S(2)}) collective-permute-start(bf16[128,1152]{1,0:T(8,128)(2,1)} %bitcast.20), channel_id=1, source_target_pairs={{0,2},{2,4},{4,6},{6,0},{1,3},{3,5},{5,7},{7,1},{8,10},{10,12},{12... | collective-permute-start | bytes 884744 | tf_op jit(solution)/shard_map/ppermute | solution.py:199
  44.1 34.5 %collective-permute-start.2 = (bf16[128,1152]{1,0:T(8,128)(2,1)}, bf16[128,1152]{1,0:T(8,128)(2,1)}, u32[]{:S(2)}, u32[]{:S(2)}) collective-permute-start(bf16[128,1152]{1,0:T(8,128)(2,1)} %bitcast.21), channel_id=1, source_target_pairs={{0,6},{2,0},{4,2},{6,4},{1,7},{3,1},{5,3},{7,5},{8,14},{10,8},{12,... | collective-permute-start | bytes 884744 | tf_op jit(solution)/shard_map/ppermute | solution.py:199
  49.6 47.4 %collective-permute-start.8 = (bf16[128,1152]{1,0:T(8,128)(2,1)}, bf16[128,1152]{1,0:T(8,128)(2,1)}, u32[]{:S(2)}, u32[]{:S(2)}) collective-permute-start(bf16[128,1152]{1,0:T(8,128)(2,1)} %bitcast.22), channel_id=1, source_target_pairs={{0,1},{1,0},{2,3},{3,2},{4,5},{5,4},{6,7},{7,6},{8,9},{9,8},{10,11... | collective-permute-start | bytes 884744 | tf_op jit(solution)/shard_map/ppermute | solution.py:202
  74.8 17.9 %collective-permute-start.4 = (bf16[64,1152]{1,0:T(8,128)(2,1)}, bf16[64,1152]{1,0:T(8,128)(2,1)}, u32[]{:S(2)}, u32[]{:S(2)}) collective-permute-start(bf16[64,1152]{1,0:T(8,128)(2,1)} %slice.8), channel_id=1, source_target_pairs={{0,2},{2,4},{4,6},{6,0},{1,3},{3,5},{5,7},{7,1},{8,10},{10,12},{12... | collective-permute-start | bytes 442376 | tf_op jit(solution)/shard_map/ppermute | solution.py:199
  80.2 14.9 %collective-permute-start.5 = (bf16[64,1152]{1,0:T(8,128)(2,1)}, bf16[64,1152]{1,0:T(8,128)(2,1)}, u32[]{:S(2)}, u32[]{:S(2)}) collective-permute-start(bf16[64,1152]{1,0:T(8,128)(2,1)} %slice.9), channel_id=1, source_target_pairs={{0,6},{2,0},{4,2},{6,4},{1,7},{3,1},{5,3},{7,5},{8,14},{10,8},{12,... | collective-permute-start | bytes 442376 | tf_op jit(solution)/shard_map/ppermute | solution.py:199
  85.5 14.3 %collective-permute-start.1 = (bf16[128,1152]{1,0:T(8,128)(2,1)}, bf16[128,1152]{1,0:T(8,128)(2,1)S(1)}, u32[]{:S(2)}, u32[]{:S(2)}) collective-permute-start(bf16[128,1152]{1,0:T(8,128)(2,1)} %collective-permute-done.refs_2_), channel_id=1, source_target_pairs={{0,1},{1,0},{2,3},{3,2},{4,5},{5,4},{6,7},{7,6},{8,9},{9,8},{10,11... | collective-permute-start | bytes 884744 | tf_op jit(solution)/shard_map/ppermute | solution.py:202
  90.5 9.4 %collective-permute-start.3 = (bf16[128,1152]{1,0:T(8,128)(2,1)}, bf16[128,1152]{1,0:T(8,128)(2,1)S(1)}, u32[]{:S(2)}, u32[]{:S(2)}) collective-permute-start(bf16[128,1152]{1,0:T(8,128)(2,1)} %collective-permute-done.2.refs_3_), channel_id=1, source_target_pairs={{0,1},{1,0},{2,3},{3,2},{4,5},{5,4},{6,7},{7,6},{8,9},{9,8},{10,11... | collective-permute-start | bytes 884744 | tf_op jit(solution)/shard_map/ppermute | solution.py:202
  92.7 7.1 %collective-permute-start.6 = (bf16[64,1152]{1,0:T(8,128)(2,1)}, bf16[64,1152]{1,0:T(8,128)(2,1)S(1)}, u32[]{:S(2)}, u32[]{:S(2)}) collective-permute-start(bf16[64,1152]{1,0:T(8,128)(2,1)} %collective-permute-done.4.one_ref), channel_id=1, source_target_pairs={{0,1},{1,0},{2,3},{3,2},{4,5},{5,4},{6,7},{7,6},{8,9},{9,8},{10,11... | collective-permute-start | bytes 442376 | tf_op jit(solution)/shard_map/ppermute | solution.py:202
  95.1 4.7 %collective-permute-start.7 = (bf16[64,1152]{1,0:T(8,128)(2,1)}, bf16[64,1152]{1,0:T(8,128)(2,1)S(1)}, u32[]{:S(2)}, u32[]{:S(2)}) collective-permute-start(bf16[64,1152]{1,0:T(8,128)(2,1)} %collective-permute-done.5.two_ref), channel_id=1, source_target_pairs={{0,1},{1,0},{2,3},{3,2},{4,5},{5,4},{6,7},{7,6},{8,9},{9,8},{10,11... | collective-permute-start | bytes 442376 | tf_op jit(solution)/shard_map/ppermute | solution.py:202
  132.0 18.3 %copy-start = (bf16[1152,1152]{1,0:T(8,128)(2,1)S(1)}, bf16[1152,1152]{1,0:T(8,128)(2,1)}, u32[]{:S(2)}) copy-start(bf16[1152,1152]{1,0:T(8,128)(2,1)} %out_table_ref.1) | copy-start | bytes 7962628
Sparse Core Ops, SparseCore 0:
  40.5 89.7 all-gather.2

commit v8 on v5

--- a/solution.py
+++ b/solution.py
@@ -126,7 +126,7 @@
 
 
 def time_kernel(
-    positions, middle_ref, tables_ref, out_table_ref, modulation_ref, out_ref,
+    positions, place_ref, middle_ref, tables_ref, out_table_ref, modulation_ref, out_ref,
     input_ref, mixed_ref, table_ref, sem,
 ):
     step = pl.program_id(0)
@@ -163,7 +163,7 @@
             values.astype(jnp.bfloat16), raised[slot].astype(jnp.bfloat16),
             preferred_element_type=jnp.float32,
         )
-        mixed_ref[step * 4 + slot] = mixed / total
+        mixed_ref[step * 4 + (place_ref[8] + 4 - slot) % 4] = mixed / total
 
     @pl.when(step == pl.num_programs(0) - 1)
     def _():
@@ -200,18 +200,16 @@
     early = [tokens, beside, before, after]
     late = [swapped(before), swapped(after), far_top, far_bottom, swapped(far_top), swapped(far_bottom)]
     spots = [zh, (zh + 3) % 4, (zh + 1) % 4, (zh + 2) % 4]
-    place = jnp.stack(
-        [spot * 2 + side for spot in spots for side in (core, 1 - core)]
-    ).astype(jnp.int32)
-
-    index = lax.axis_index("y") * 2 + core
-    time_part = lax.dynamic_slice_in_dim(time_qkv, jnp.minimum(index * 32, 216 - 32), 32, 0)
-    index = lax.axis_index("x") * 4 + lax.axis_index("y")
-    out_part = lax.dynamic_slice_in_dim(frame_out, jnp.minimum(index, 8) * 16, 16, 0)
-    time_parts = lax.all_gather(time_part, "zl", axis=0, tiled=True)
+    place = [spot * 2 + side for spot in spots for side in (core, 1 - core)]
+    place = jnp.stack(place + [lax.axis_index("zl")]).astype(jnp.int32)
+
+    x, y, zl = lax.axis_index("x"), lax.axis_index("y"), lax.axis_index("zl")
+    time_part = lax.dynamic_slice_in_dim(time_qkv, jnp.minimum(32 * (2 * y + core), 216 - 32), 32, 0)
+    out_part = lax.dynamic_slice_in_dim(frame_out, 16 * jnp.minimum(4 * x + y, 8), 16, 0)
+    time_parts = [time_part] + [along(time_part, "zl", by) for by in (1, 2, 3)]
     out_parts = lax.all_gather(out_part, "zh", axis=0, tiled=True)
-    parts = [time_parts, out_parts]
-    tables = lax.all_gather(jnp.concatenate(parts, axis=0), ("x", "y", "c"), axis=0)
+    parts = jnp.concatenate(time_parts + [out_parts], axis=0)
+    tables = lax.all_gather(parts, ("x", "y", "c"), axis=0)
     tables = tables.reshape(4, 8, 192, width)
 
     wqk, wvt = pl.pallas_call(
@@ -272,6 +270,7 @@
         grid=(4,),
         out_shape=jax.ShapeDtypeStruct((rows, width), jnp.bfloat16),
         in_specs=[
+            pl.BlockSpec(memory_space=pltpu.SMEM),
             whole(),
             pl.BlockSpec((1, 8, LANES, width), lambda i: (i, 0, 0, 0)),
             pl.BlockSpec(memory_space=pl.ANY),
@@ -286,7 +285,7 @@
         ],
         compiler_params=params(),
         name="time_block",
-    )(middle, tables, time_out, modulation)
+    )(place, middle, tables, time_out, modulation)
     out = lax.all_to_all(out, ("x", "zl"), 0, 0, tiled=True)
     return out[None]
 

time: 188 us -> 184 us (0.979)
  blocking collectives: 97 us -> 78.8 us
  starting transfers between devices: 33.5 us -> 46.5 us
    ppermute x4 -> x7, starting transfers between devices: 14 us -> 30 us  [along(): return lax.ppermute(array, axis, rotation(4, by))]
    all_gather x1 -> x0, blocking collectives: 13.8 us -> none  [shards(): time_parts = lax.all_gather(time_part, 'zl', axis=0, tiled=True)]
    all_to_all x1, blocking collectives: 24.6 us -> 16 us  [shards(): middle = lax.all_to_all(middle, ('x', 'zl'), 0, 0, tiled=True)]
    all_to_all x1, blocking collectives: 22.2 us -> 27.6 us  [shards(): mixed = lax.all_to_all(mixed, ('zh', 'c'), 0, 0, tiled=True)]
    ppermute x5, starting transfers between devices: 19.5 us -> 16.5 us  [swapped(): return lax.ppermute(array, 'c', SWAP)]
    unnamed x12 -> x16, local copies, waits for them, and re-layouts: 2.7 us -> 4.28 us
    ppermute x4 -> x7, waiting for transfers between devices: 14.5 us -> 15.9 us  [along(): return lax.ppermute(array, axis, rotation(4, by))]
  transfers between devices with their start and end apart: 10 -> 13, of which waited for: 2 -> 2; matrix products, arithmetic and copies ran while one was open for 2% -> 2% of each run, Pallas kernels for 5% -> 6%
where the time goes in v8:
time: 184 us; the launch traced here: 183 us
  blocking collectives  78.8 us (43%)
  starting transfers between devices  46.5 us (25%)
  Pallas kernels  20.5 us (11%)
  waiting for transfers between devices  15.9 us (9%)
  between operations  13.7 us (7%)
  local copies, waits for them, and re-layouts  7.55 us (4%)
    ppermute x7, starting transfers between devices, along(): return lax.ppermute(array, axis, rotation(4, by))  30 us
    all_to_all x1, blocking collectives, shards(): mixed = lax.all_to_all(mixed, ('zh', 'c'), 0, 0, tiled=True)  27.6 us
    all_gather x1, blocking collectives, shards(): out_parts = lax.all_gather(out_part, 'zh', axis=0, tiled=True)  21.3 us
    ppermute x5, starting transfers between devices, swapped(): return lax.ppermute(array, 'c', SWAP)  16.5 us
    all_to_all x1, blocking collectives, shards(): middle = lax.all_to_all(middle, ('x', 'zl'), 0, 0, tiled=True)  16 us
    ppermute x7, waiting for transfers between devices, along(): return lax.ppermute(array, axis, rotation(4, by))  15.9 us
    all_to_all x1, blocking collectives, shards(): out = lax.all_to_all(out, ('x', 'zl'), 0, 0, tiled=True)  14 us
    pallas_call x1, Pallas kernels, shards(): pl.pallas_call(functools.partial(time_kernel, rows // 16), grid=(4,), out...  7.84 us
  transfers between devices with their start and end apart: 13, of which 2 were waited for; matrix products, arithmetic and copies ran while one was open for 2% of the time, Pallas kernels for 6%

profile of v8, /device:TPU:1, one launch (start us, length us, event | category | flops | bytes accessed | tf_op | source)
XLA Modules:
  0.0 182.9 jit_solution(2647694552736540912)
XLA Ops:
  6.5 0.0 copy-start
  6.5 0.0 all-gather.3.cloned.1.call-start
  6.5 1.0 constant_dynamic-update-slice_fusion.4
  7.6 4.4 %collective-permute-start.9 = (bf16[32,1152]{1,0:T(8,128)(2,1)S(1)}, bf16[32,1152]{1,0:T(8,128)(2,1)S(1)}, u32[]{:S(2)}, u32[]{:S(2)}) collective-permute-start(bf16[32,1152]{1,0:T(8,128)(2,1)S(1)} %get-tuple-element.14), channel_id=1, source_target_pairs={{0,8},{8,16},{16,24},{24,0},{1,9},{9,17},{17,25},{25,1},{2,10},{10... | collective-permute-start | bytes 221192 | tf_op jit(solution)/shard_map/ppermute | solution.py:192
  11.9 4.9 %collective-permute-start.10 = (bf16[32,1152]{1,0:T(8,128)(2,1)S(1)}, bf16[32,1152]{1,0:T(8,128)(2,1)S(1)}, u32[]{:S(2)}, u32[]{:S(2)}) collective-permute-start(bf16[32,1152]{1,0:T(8,128)(2,1)S(1)} %get-tuple-element.14), channel_id=1, source_target_pairs={{0,16},{8,24},{16,0},{24,8},{1,17},{9,25},{17,1},{25,9},{2,18},{10... | collective-permute-start | bytes 221192 | tf_op jit(solution)/shard_map/ppermute | solution.py:192
  16.9 2.6 %collective-permute-start.11 = (bf16[32,1152]{1,0:T(8,128)(2,1)S(1)}, bf16[32,1152]{1,0:T(8,128)(2,1)S(1)}, u32[]{:S(2)}, u32[]{:S(2)}) collective-permute-start(bf16[32,1152]{1,0:T(8,128)(2,1)S(1)} %get-tuple-element.14), channel_id=1, source_target_pairs={{0,24},{8,0},{16,8},{24,16},{1,25},{9,1},{17,9},{25,17},{2,26},{10... | collective-permute-start | bytes 221192 | tf_op jit(solution)/shard_map/ppermute | solution.py:192
  19.5 0.0 copy-done
  19.5 21.3 %all_gather.9 = bf16[64,1152]{1,0:T(8,128)(2,1)S(1)} all-gather(bf16[16,1152]{1,0:T(8,128)(2,1)S(1)} %constant_dynamic-slice_fusion), channel_id=1, replica_groups=mesh['y'=4,'x'=4,'zl'=4,'zh'=4,'c'=2] {'zh'}, dimensions={0}, use_global_device_ids=true | all-gather | bytes 184320 | tf_op jit(solution)/shard_map/all_gather | solution.py:210
  40.8 0.0 collective-permute-done.9
  40.8 0.0 collective-permute-done.10
  40.8 0.0 collective-permute-done.11
  40.9 0.0 copy-start.4
  40.9 0.8 copy-done.4
  41.7 0.0 all-gather.3.cloned.1.call-update
  41.7 4.3 %collective-permute-start = (bf16[128,1152]{1,0:T(8,128)(2,1)}, bf16[128,1152]{1,0:T(8,128)(2,1)}, u32[]{:S(2)}, u32[]{:S(2)}) collective-permute-start(bf16[128,1152]{1,0:T(8,128)(2,1)} %bitcast.21), channel_id=1, source_target_pairs={{0,2},{2,4},{4,6},{6,0},{1,3},{3,5},{5,7},{7,1},{8,10},{10,12},{12... | collective-permute-start | bytes 884744 | tf_op jit(solution)/shard_map/ppermute | solution.py:192
  46.0 4.9 %collective-permute-start.2 = (bf16[128,1152]{1,0:T(8,128)(2,1)}, bf16[128,1152]{1,0:T(8,128)(2,1)}, u32[]{:S(2)}, u32[]{:S(2)}) collective-permute-start(bf16[128,1152]{1,0:T(8,128)(2,1)} %bitcast.22), channel_id=1, source_target_pairs={{0,6},{2,0},{4,2},{6,4},{1,7},{3,1},{5,3},{7,5},{8,14},{10,8},{12,... | collective-permute-start | bytes 884744 | tf_op jit(solution)/shard_map/ppermute | solution.py:192
  50.9 7.0 %collective-permute-start.8 = (bf16[128,1152]{1,0:T(8,128)(2,1)}, bf16[128,1152]{1,0:T(8,128)(2,1)}, u32[]{:S(2)}, u32[]{:S(2)}) collective-permute-start(bf16[128,1152]{1,0:T(8,128)(2,1)} %bitcast.23), channel_id=1, source_target_pairs={{0,1},{1,0},{2,3},{3,2},{4,5},{5,4},{6,7},{7,6},{8,9},{9,8},{10,11... | collective-permute-start | bytes 884744 | tf_op jit(solution)/shard_map/ppermute | solution.py:195
  57.9 9.1 %collective-permute-done.refs_2_ = bf16[128,1152]{1,0:T(8,128)(2,1)} collective-permute-done((bf16[128,1152]{1,0:T(8,128)(2,1)}, bf16[128,1152]{1,0:T(8,128)(2,1)}, u32[]{:S(2)}, u32[]{:S(2)}) %collective-permute-start) | collective-permute-done | bytes 294944 | tf_op jit(solution)/shard_map/ppermute | solution.py:192
  66.9 1.6 slice.8
  68.5 4.1 %collective-permute-start.4 = (bf16[64,1152]{1,0:T(8,128)(2,1)}, bf16[64,1152]{1,0:T(8,128)(2,1)}, u32[]{:S(2)}, u32[]{:S(2)}) collective-permute-start(bf16[64,1152]{1,0:T(8,128)(2,1)} %slice.8), channel_id=1, source_target_pairs={{0,2},{2,4},{4,6},{6,0},{1,3},{3,5},{5,7},{7,1},{8,10},{10,12},{12... | collective-permute-start | bytes 442376 | tf_op jit(solution)/shard_map/ppermute | solution.py:192
  72.7 6.8 %collective-permute-done.2.refs_3_ = bf16[128,1152]{1,0:T(8,128)(2,1)} collective-permute-done((bf16[128,1152]{1,0:T(8,128)(2,1)}, bf16[128,1152]{1,0:T(8,128)(2,1)}, u32[]{:S(2)}, u32[]{:S(2)}) %collective-permute-start.2) | collective-permute-done | bytes 294944 | tf_op jit(solution)/shard_map/ppermute | solution.py:192
  79.5 1.6 slice.9
  81.0 4.7 %collective-permute-start.5 = (bf16[64,1152]{1,0:T(8,128)(2,1)}, bf16[64,1152]{1,0:T(8,128)(2,1)}, u32[]{:S(2)}, u32[]{:S(2)}) collective-permute-start(bf16[64,1152]{1,0:T(8,128)(2,1)} %slice.9), channel_id=1, source_target_pairs={{0,6},{2,0},{4,2},{6,4},{1,7},{3,1},{5,3},{7,5},{8,14},{10,8},{12,... | collective-permute-start | bytes 442376 | tf_op jit(solution)/shard_map/ppermute | solution.py:192
  85.8 3.3 %collective-permute-start.1 = (bf16[128,1152]{1,0:T(8,128)(2,1)}, bf16[128,1152]{1,0:T(8,128)(2,1)S(1)}, u32[]{:S(2)}, u32[]{:S(2)}) collective-permute-start(bf16[128,1152]{1,0:T(8,128)(2,1)} %collective-permute-done.refs_2_), channel_id=1, source_target_pairs={{0,1},{1,0},{2,3},{3,2},{4,5},{5,4},{6,7},{7,6},{8,9},{9,8},{10,11... | collective-permute-start | bytes 884744 | tf_op jit(solution)/shard_map/ppermute | solution.py:195
  89.1 1.9 %collective-permute-start.3 = (bf16[128,1152]{1,0:T(8,128)(2,1)}, bf16[128,1152]{1,0:T(8,128)(2,1)S(1)}, u32[]{:S(2)}, u32[]{:S(2)}) collective-permute-start(bf16[128,1152]{1,0:T(8,128)(2,1)} %collective-permute-done.2.refs_3_), channel_id=1, source_target_pairs={{0,1},{1,0},{2,3},{3,2},{4,5},{5,4},{6,7},{7,6},{8,9},{9,8},{10,11... | collective-permute-start | bytes 884744 | tf_op jit(solution)/shard_map/ppermute | solution.py:195
  91.1 0.8 copy.7.refs_4_.modulation_ref
  91.8 0.0 copy-done.2
  91.8 0.1 spread.1
  92.0 0.1 stack.39.place_ref
  92.0 0.0 collective-permute-done.4.one_ref
  92.0 2.4 %collective-permute-start.6 = (bf16[64,1152]{1,0:T(8,128)(2,1)}, bf16[64,1152]{1,0:T(8,128)(2,1)S(1)}, u32[]{:S(2)}, u32[]{:S(2)}) collective-permute-start(bf16[64,1152]{1,0:T(8,128)(2,1)} %collective-permute-done.4.one_ref), channel_id=1, source_target_pairs={{0,1},{1,0},{2,3},{3,2},{4,5},{5,4},{6,7},{7,6},{8,9},{9,8},{10,11... | collective-permute-start | bytes 442376 | tf_op jit(solution)/shard_map/ppermute | solution.py:195
  94.5 0.0 collective-permute-done.5.two_ref
  94.5 1.9 %collective-permute-start.7 = (bf16[64,1152]{1,0:T(8,128)(2,1)}, bf16[64,1152]{1,0:T(8,128)(2,1)S(1)}, u32[]{:S(2)}, u32[]{:S(2)}) collective-permute-start(bf16[64,1152]{1,0:T(8,128)(2,1)} %collective-permute-done.5.two_ref), channel_id=1, source_target_pairs={{0,1},{1,0},{2,3},{3,2},{4,5},{5,4},{6,7},{7,6},{8,9},{9,8},{10,11... | collective-permute-start | bytes 442376 | tf_op jit(solution)/shard_map/ppermute | solution.py:195
  96.4 0.0 collective-permute-done.8.refs_1_
  96.4 0.0 copy-start.3
  96.4 1.0 copy-done.3
  97.4 2.8 %early_triples.1 = (bf16[512,512]{1,0:T(8,128)(2,1)S(1)}, bf16[160,512]{1,0:T(8,128)(2,1)S(1)}) custom-call(bf16[128,1152]{1,0:T(8,128)(2,1)S(1)} %bitcast.24, bf16[128,1152]{1,0:T(8,128)(2,1)} %collective-permute-done.8.refs_1_, bf16[128,1152]{1,0:T(8,128)(2,1)} %collective-permute-done.refs_2_, bf16[128,1152]{1,0:T(8,128)(2,1)} %collective-permute-done.2.refs_3_, ...), custom_call_target="tpu_custom_call" | custom-call | flops 2000000000 | bytes 5000000 | tf_op jit(solution)/shard_map/early_triples/pallas_call | solution.py:228
  100.2 0.0 collective-permute-done.6.three_ref
  100.2 0.0 collective-permute-done.7.four_ref
  100.2 0.0 collective-permute-done.1.below_ref
  100.2 0.0 collective-permute-done.3.above_ref
  100.2 7.2 %frame_attention.1 = bf16[8,144,128]{2,1,0:T(8,128)(2,1)S(1)} custom-call(s32[9]{0:T(128)S(1)} %stack.39.place_ref, bf16[128,1152]{1,0:T(8,128)(2,1)S(1)} %collective-permute-done.1.below_ref, bf16[128,1152]{1,0:T(8,128)(2,1)S(1)} %collective-permute-done.3.above_ref, bf16[64,1152]{1,0:T(8,128)(2,1)} %collective-permute-done.4.one_ref, ...), custom_call_target="tpu_custom_call" | custom-call | tf_op jit(solution)/shard_map/frame_attention/pallas_call | solution.py:242
  107.4 27.6 %all_to_all.25.mixed_ref = bf16[8,144,128]{2,1,0:T(8,128)(2,1)S(1)} all-to-all(bf16[8,144,128]{2,1,0:T(8,128)(2,1)S(1)} %frame_attention.1), channel_id=1, replica_groups=mesh['y'=4,'x'=4,'zl'=4,'zh'=4,'c'=2] {'zh','c'}, dimensions={0} | all-to-all | bytes 589824 | tf_op jit(solution)/shard_map/all_to_all | solution.py:255
  135.0 2.5 %middle.1 = bf16[128,1152]{1,0:T(8,128)(2,1)S(1)} custom-call(bf16[8,144,128]{2,1,0:T(8,128)(2,1)S(1)} %all_to_all.25.mixed_ref, bf16[16,2,192,1152]{3,2,1,0:T(8,128)(2,1)} %bitcast.26, bf16[128,1152]{1,0:T(8,128)(2,1)S(1)} %bitcast.25, f32[2,3,1152]{2,1,0:T(4,128)S(1)} %copy.7.refs_4_.modulation_ref), custom_call_target="tpu_custom_call" | custom-call | tf_op jit(solution)/shard_map/middle/pallas_call | solution.py:256
  137.6 16.0 %all_to_all.26 = bf16[16,8,1152]{2,1,0:T(8,128)(2,1)S(1)} all-to-all(bf16[16,8,1152]{2,1,0:T(8,128)(2,1)S(1)} %bitcast.19), channel_id=1, replica_groups=mesh['y'=4,'x'=4,'zl'=4,'zh'=4,'c'=2] {'x','zl'}, dimensions={0} | all-to-all | bytes 589824 | tf_op jit(solution)/shard_map/all_to_all | solution.py:266
  153.5 7.8 %time_block.1 = bf16[128,1152]{1,0:T(8,128)(2,1)S(1)} custom-call(s32[9]{0:T(128)S(1)} %stack.39.place_ref, bf16[128,1152]{1,0:T(8,128)(2,1)S(1)} %bitcast.17, bf16[4,8,192,1152]{3,2,1,0:T(8,128)(2,1)} %bitcast.27, bf16[1152,1152]{1,0:T(8,128)(2,1)S(1)} %copy-done.1, f32[2,3,1152]{2,1,0:T(4,128)S(1)} %copy.7.refs_4_.modulation_ref), custom_call_target="tpu_custom_call" | custom-call | tf_op jit(solution)/shard_map/time_block/pallas_call | solution.py:268
  161.4 14.0 %all_to_all.27 = bf16[16,8,1152]{2,1,0:T(8,128)(2,1)S(1)} all-to-all(bf16[16,8,1152]{2,1,0:T(8,128)(2,1)S(1)} %bitcast.18), channel_id=1, replica_groups=mesh['y'=4,'x'=4,'zl'=4,'zh'=4,'c'=2] {'x','zl'}, dimensions={0} | all-to-all | bytes 589824 | tf_op jit(solution)/shard_map/all_to_all | solution.py:289
  175.3 0.7 copy.16
  (9 shorter events, 0.1 us)
Async XLA Ops:
  6.5 13.0 %copy-start = (bf16[144,1152]{1,0:T(8,128)(2,1)S(1)}, bf16[144,1152]{1,0:T(8,128)(2,1)}, u32[]{:S(2)}) copy-start(bf16[144,1152]{1,0:T(8,128)(2,1)} %param.8) | copy-start | bytes 995332
  6.5 85.3 %copy-start.2 = (bf16[1152,432]{0,1:T(8,128)(2,1)S(1)}, bf16[1152,432]{0,1:T(8,128)(2,1)}, u32[]{:S(2)}) copy-start(bf16[1152,432]{0,1:T(8,128)(2,1)} %param.7) | copy-start | bytes 2985988
  6.5 128.5 %all-gather.3.cloned.1.call-start = ((), (), s32[]{:S(2)}) async-start(), calls=%async_computation.3 | async-start | bytes 14598144 | tf_op jit(solution)/shard_map/all_gather | solution.py:212
  7.6 33.2 %collective-permute-start.9 = (bf16[32,1152]{1,0:T(8,128)(2,1)S(1)}, bf16[32,1152]{1,0:T(8,128)(2,1)S(1)}, u32[]{:S(2)}, u32[]{:S(2)}) collective-permute-start(bf16[32,1152]{1,0:T(8,128)(2,1)S(1)} %get-tuple-element.14), channel_id=1, source_target_pairs={{0,8},{8,16},{16,24},{24,0},{1,9},{9,17},{17,25},{25,1},{2,10},{10... | collective-permute-start | bytes 221192 | tf_op jit(solution)/shard_map/ppermute | solution.py:192
  11.9 28.9 %collective-permute-start.10 = (bf16[32,1152]{1,0:T(8,128)(2,1)S(1)}, bf16[32,1152]{1,0:T(8,128)(2,1)S(1)}, u32[]{:S(2)}, u32[]{:S(2)}) collective-permute-start(bf16[32,1152]{1,0:T(8,128)(2,1)S(1)} %get-tuple-element.14), channel_id=1, source_target_pairs={{0,16},{8,24},{16,0},{24,8},{1,17},{9,25},{17,1},{25,9},{2,18},{10... | collective-permute-start | bytes 221192 | tf_op jit(solution)/shard_map/ppermute | solution.py:192
  16.9 24.0 %collective-permute-start.11 = (bf16[32,1152]{1,0:T(8,128)(2,1)S(1)}, bf16[32,1152]{1,0:T(8,128)(2,1)S(1)}, u32[]{:S(2)}, u32[]{:S(2)}) collective-permute-start(bf16[32,1152]{1,0:T(8,128)(2,1)S(1)} %get-tuple-element.14), channel_id=1, source_target_pairs={{0,24},{8,0},{16,8},{24,16},{1,25},{9,1},{17,9},{25,17},{2,26},{10... | collective-permute-start | bytes 221192 | tf_op jit(solution)/shard_map/ppermute | solution.py:192
  40.9 0.8 copy-start.4
  41.7 25.3 %collective-permute-start = (bf16[128,1152]{1,0:T(8,128)(2,1)}, bf16[128,1152]{1,0:T(8,128)(2,1)}, u32[]{:S(2)}, u32[]{:S(2)}) collective-permute-start(bf16[128,1152]{1,0:T(8,128)(2,1)} %bitcast.21), channel_id=1, source_target_pairs={{0,2},{2,4},{4,6},{6,0},{1,3},{3,5},{5,7},{7,1},{8,10},{10,12},{12... | collective-permute-start | bytes 884744 | tf_op jit(solution)/shard_map/ppermute | solution.py:192
  46.0 33.5 %collective-permute-start.2 = (bf16[128,1152]{1,0:T(8,128)(2,1)}, bf16[128,1152]{1,0:T(8,128)(2,1)}, u32[]{:S(2)}, u32[]{:S(2)}) collective-permute-start(bf16[128,1152]{1,0:T(8,128)(2,1)} %bitcast.22), channel_id=1, source_target_pairs={{0,6},{2,0},{4,2},{6,4},{1,7},{3,1},{5,3},{7,5},{8,14},{10,8},{12,... | collective-permute-start | bytes 884744 | tf_op jit(solution)/shard_map/ppermute | solution.py:192
  50.9 45.5 %collective-permute-start.8 = (bf16[128,1152]{1,0:T(8,128)(2,1)}, bf16[128,1152]{1,0:T(8,128)(2,1)}, u32[]{:S(2)}, u32[]{:S(2)}) collective-permute-start(bf16[128,1152]{1,0:T(8,128)(2,1)} %bitcast.23), channel_id=1, source_target_pairs={{0,1},{1,0},{2,3},{3,2},{4,5},{5,4},{6,7},{7,6},{8,9},{9,8},{10,11... | collective-permute-start | bytes 884744 | tf_op jit(solution)/shard_map/ppermute | solution.py:195
  68.5 23.5 %collective-permute-start.4 = (bf16[64,1152]{1,0:T(8,128)(2,1)}, bf16[64,1152]{1,0:T(8,128)(2,1)}, u32[]{:S(2)}, u32[]{:S(2)}) collective-permute-start(bf16[64,1152]{1,0:T(8,128)(2,1)} %slice.8), channel_id=1, source_target_pairs={{0,2},{2,4},{4,6},{6,0},{1,3},{3,5},{5,7},{7,1},{8,10},{10,12},{12... | collective-permute-start | bytes 442376 | tf_op jit(solution)/shard_map/ppermute | solution.py:192
  81.0 13.4 %collective-permute-start.5 = (bf16[64,1152]{1,0:T(8,128)(2,1)}, bf16[64,1152]{1,0:T(8,128)(2,1)}, u32[]{:S(2)}, u32[]{:S(2)}) collective-permute-start(bf16[64,1152]{1,0:T(8,128)(2,1)} %slice.9), channel_id=1, source_target_pairs={{0,6},{2,0},{4,2},{6,4},{1,7},{3,1},{5,3},{7,5},{8,14},{10,8},{12,... | collective-permute-start | bytes 442376 | tf_op jit(solution)/shard_map/ppermute | solution.py:192
  85.8 14.4 %collective-permute-start.1 = (bf16[128,1152]{1,0:T(8,128)(2,1)}, bf16[128,1152]{1,0:T(8,128)(2,1)S(1)}, u32[]{:S(2)}, u32[]{:S(2)}) collective-permute-start(bf16[128,1152]{1,0:T(8,128)(2,1)} %collective-permute-done.refs_2_), channel_id=1, source_target_pairs={{0,1},{1,0},{2,3},{3,2},{4,5},{5,4},{6,7},{7,6},{8,9},{9,8},{10,11... | collective-permute-start | bytes 884744 | tf_op jit(solution)/shard_map/ppermute | solution.py:195
  89.1 11.1 %collective-permute-start.3 = (bf16[128,1152]{1,0:T(8,128)(2,1)}, bf16[128,1152]{1,0:T(8,128)(2,1)S(1)}, u32[]{:S(2)}, u32[]{:S(2)}) collective-permute-start(bf16[128,1152]{1,0:T(8,128)(2,1)} %collective-permute-done.2.refs_3_), channel_id=1, source_target_pairs={{0,1},{1,0},{2,3},{3,2},{4,5},{5,4},{6,7},{7,6},{8,9},{9,8},{10,11... | collective-permute-start | bytes 884744 | tf_op jit(solution)/shard_map/ppermute | solution.py:195
  92.0 8.1 %collective-permute-start.6 = (bf16[64,1152]{1,0:T(8,128)(2,1)}, bf16[64,1152]{1,0:T(8,128)(2,1)S(1)}, u32[]{:S(2)}, u32[]{:S(2)}) collective-permute-start(bf16[64,1152]{1,0:T(8,128)(2,1)} %collective-permute-done.4.one_ref), channel_id=1, source_target_pairs={{0,1},{1,0},{2,3},{3,2},{4,5},{5,4},{6,7},{7,6},{8,9},{9,8},{10,11... | collective-permute-start | bytes 442376 | tf_op jit(solution)/shard_map/ppermute | solution.py:195
  94.5 5.7 %collective-permute-start.7 = (bf16[64,1152]{1,0:T(8,128)(2,1)}, bf16[64,1152]{1,0:T(8,128)(2,1)S(1)}, u32[]{:S(2)}, u32[]{:S(2)}) collective-permute-start(bf16[64,1152]{1,0:T(8,128)(2,1)} %collective-permute-done.5.two_ref), channel_id=1, source_target_pairs={{0,1},{1,0},{2,3},{3,2},{4,5},{5,4},{6,7},{7,6},{8,9},{9,8},{10,11... | collective-permute-start | bytes 442376 | tf_op jit(solution)/shard_map/ppermute | solution.py:195
  96.4 1.0 copy-start.3
  135.0 18.5 %copy-start.1 = (bf16[1152,1152]{1,0:T(8,128)(2,1)S(1)}, bf16[1152,1152]{1,0:T(8,128)(2,1)}, u32[]{:S(2)}) copy-start(bf16[1152,1152]{1,0:T(8,128)(2,1)} %out_table_ref.1) | copy-start | bytes 7962628
Sparse Core Ops, SparseCore 0:
  41.8 82.0 all-gather.2

commit v9 on v6

--- a/solution.py
+++ b/solution.py
@@ -18,7 +18,7 @@
 TN = (((0,), (0,)), ((), ()))
 
 
-def params(mib=48):
+def params(mib=28):
     return pltpu.CompilerParams(vmem_limit_bytes=mib * 1024 * 1024)
 
 
@@ -56,7 +56,7 @@
 def early_kernel(*refs):
     pieces, (modulation_ref, wqk_ref, wvt_ref, qk_ref, vt_ref) = refs[:-5], refs[-5:]
     for index in range(0, len(pieces), 2):
-        rows = jnp.concatenate([pieces[index][...], pieces[index + 1][...]], axis=0)
+        rows = jnp.concatenate([pieces[index][:LANES], pieces[index + 1][:LANES]], axis=0)
         qk, vt = triples_of(rows.astype(jnp.float32), modulation_ref, wqk_ref, wvt_ref)
         start = LANES * index
         qk_ref[start : start + 2 * LANES] = qk
@@ -69,7 +69,7 @@
 ):
     groups = ((below_ref, above_ref), (three_ref, four_ref, one_ref, two_ref))
     for index, group in enumerate(groups):
-        rows = jnp.concatenate([ref[...] for ref in group], axis=0).astype(jnp.float32)
+        rows = jnp.concatenate([ref[:LANES] for ref in group], axis=0).astype(jnp.float32)
         qk, vt = triples_of(rows, modulation_ref, wqk_ref, wvt_ref)
         start = 2 * LANES * index
         qk_late_ref[start : start + 2 * LANES] = qk
@@ -110,11 +110,12 @@
             out_ref[place_ref[2 * number + part]] = both[:, part * LANES : (part + 1) * LANES]
 
 
-def pack_kernel(parts_ref, below_ref, above_ref, out_ref):
-    parts = parts_ref[...].astype(jnp.float32)
-    rows = [parts[16 * (4 * zh + zl) : 16 * (4 * zh + zl) + 8] for zl in range(4) for zh in range(4)]
-    rows += [parts[16 * (4 * zh + zl) + 8 : 16 * (4 * zh + zl) + 16] for zh in range(4) for zl in range(2)]
-    out_ref[...] = jnp.concatenate(rows, axis=0).astype(jnp.bfloat16)
+def pack_kernel(times_ref, own_ref, below_ref, across_ref, above_ref, out_ref):
+    count, rows = times_ref.shape[0], own_ref.shape[0]
+    out_ref[:count] = times_ref[...]
+    slots = (own_ref[...], below_ref[LANES:], across_ref[...], above_ref[LANES:])
+    for index, slot in enumerate(slots):
+        out_ref[count + rows * index : count + rows * index + rows] = slot
 
 
 def join_kernel(mixed_ref, tokens_ref, out_ref):
@@ -125,22 +126,23 @@
 
 
 def time_kernel(
-    positions, joined_ref, tables_ref, all_ref, out_table_ref, modulation_ref, out_ref,
+    positions, place_ref, joined_ref, tables_ref, all_ref, out_table_ref, modulation_ref, out_ref,
     middle_ref, input_ref, mixed_ref, frame_table_ref, time_table_ref, frame_sem, time_sem,
 ):
     step = pl.program_id(0)
     rows, width = input_ref.shape
+    zh = place_ref[8]
     time_copy = pltpu.make_async_copy(out_table_ref, time_table_ref, time_sem)
 
     @pl.when(step == 0)
     def _():
         frame_copies = [
             pltpu.make_async_copy(
-                all_ref.at[pl.ds(0, 9), core, pl.ds(LANES + 16 * zh, 16), :],
-                frame_table_ref.at[2 * zh + core],
-                frame_sem.at[2 * zh + core],
-            )
-            for zh in range(4)
+                all_ref.at[pl.ds(0, 9), core, pl.ds(LANES + 16 * slot, 16), :],
+                frame_table_ref.at[2 * ((zh + 4 - slot) % 4) + core],
+                frame_sem.at[2 * slot + core],
+            )
+            for slot in range(4)
             for core in range(2)
         ]
         for copy in frame_copies:
@@ -215,30 +217,30 @@
     def swapped(array):
         return lax.ppermute(array, "c", SWAP)
 
-    x, y, zl = lax.axis_index("x"), lax.axis_index("y"), lax.axis_index("zl")
-    start = jnp.minimum(32 * (2 * y + core), 216 - 32) + 8 * zh
-    time_part = lax.dynamic_slice_in_dim(time_qkv, start, 8, 0)
-    start = 16 * jnp.minimum(4 * x + y, 8) + 8 * (zl % 2)
-    out_part = lax.dynamic_slice_in_dim(frame_out, start, 8, 0)
-    part = jnp.concatenate([time_part, out_part], axis=0)
-    parts = lax.all_gather(part, ("zh", "zl"), axis=0, tiled=True)
-
-    before, after = along(tokens, "zh", 1), along(tokens, "zh", 3)
+    x, y = lax.axis_index("x"), lax.axis_index("y")
+    time_part = lax.dynamic_slice_in_dim(time_qkv, jnp.minimum(32 * (2 * y + core), 216 - 32), 32, 0)
+    out_part = lax.dynamic_slice_in_dim(frame_out, 16 * jnp.minimum(4 * x + y, 8), 16, 0)
+    across = along(out_part, "zh", 2)
+
+    sent = jnp.concatenate([tokens, out_part], axis=0)
+    before, after = along(sent, "zh", 1), along(sent, "zh", 3)
     beside = swapped(tokens)
+    times = lax.all_gather(time_part, "zl", axis=0, tiled=True)
     parts = pl.pallas_call(
         pack_kernel,
-        out_shape=jax.ShapeDtypeStruct((4 * 32 + 4 * 16, width), parts.dtype),
-        in_specs=[whole(), pl.BlockSpec(memory_space=pl.ANY), pl.BlockSpec(memory_space=pl.ANY)],
+        out_shape=jax.ShapeDtypeStruct((4 * 32 + 4 * 16, width), times.dtype),
+        in_specs=[whole()] * 5,
         out_specs=whole(),
         compiler_params=params(),
         name="pack",
-    )(parts, before, after)
+    )(times, out_part, before, across, after)
     tables = lax.all_gather(parts, ("x", "y", "c"), axis=0)
-    far_top, far_bottom = along(before[:half], "zh", 1), along(after[half:], "zh", 3)
+    far_top, far_bottom = along(before[:half], "zh", 1), along(after[half:rows], "zh", 3)
     early = [tokens, beside, before, after]
     late = [swapped(before), swapped(after), far_top, far_bottom, swapped(far_top), swapped(far_bottom)]
     spots = [zh, (zh + 3) % 4, (zh + 1) % 4, (zh + 2) % 4]
-    place = jnp.stack([spot * 2 + side for spot in spots for side in (core, 1 - core)]).astype(jnp.int32)
+    place = [spot * 2 + side for spot in spots for side in (core, 1 - core)]
+    place = jnp.stack(place + [zh]).astype(jnp.int32)
 
     tables = tables.reshape(4, 8, 192, width)
 
@@ -298,6 +300,7 @@
         grid=(5,),
         out_shape=jax.ShapeDtypeStruct((rows, width), jnp.bfloat16),
         in_specs=[
+            pl.BlockSpec(memory_space=pltpu.SMEM),
             whole(),
             pl.BlockSpec((1, 8, LANES, width), lambda i: (jnp.maximum(i - 1, 0), 0, 0, 0)),
             pl.BlockSpec(memory_space=pl.ANY),
@@ -314,9 +317,9 @@
             pltpu.SemaphoreType.DMA((8,)),
             pltpu.SemaphoreType.DMA,
         ],
-        compiler_params=params(),
+        compiler_params=params(56),
         name="time_block",
-    )(joined, tables, tables.reshape(16, 2, 192, width), time_out, modulation)
+    )(place, joined, tables, tables.reshape(16, 2, 192, width), time_out, modulation)
     out = lax.all_to_all(out, ("x", "zl"), 0, 0, tiled=True)
     return out[None]
 

time: 203 us -> 197 us (0.970)
  blocking collectives: 110 us -> 93.7 us
  starting transfers between devices: 43.2 us -> 52.1 us
  waiting for transfers between devices: 8.6 us -> 4.68 us
    all_gather x1, blocking collectives: 47.3 us -> 28 us  [shards(): times = lax.all_gather(time_part, 'zl', axis=0, tiled=True)]
    ppermute x4 -> x5, starting transfers between devices: 24.5 us -> 34.6 us  [along(): return lax.ppermute(array, axis, rotation(4, by))]
    ppermute x4 -> x5, waiting for transfers between devices: 8.57 us -> 4.65 us  [along(): return lax.ppermute(array, axis, rotation(4, by))]
    all_to_all x1, blocking collectives: 25.8 us -> 28.9 us  [shards(): mixed = lax.all_to_all(mixed, ('zh', 'c'), 0, 0, tiled=True)]
  transfers between devices with their start and end apart: 10 -> 11, of which waited for: 2 -> 2; matrix products, arithmetic and copies ran while one was open for 1% -> 1% of each run, Pallas kernels for 6% -> 5%
where the time goes in v9:
time: 197 us; the launch traced here: 195 us
  blocking collectives  93.7 us (48%)
  starting transfers between devices  52.1 us (26%)
  Pallas kernels  24.2 us (12%)
  between operations  13.7 us (7%)
  local copies, waits for them, and re-layouts  5.74 us (3%)
  waiting for transfers between devices  4.68 us (2%)
    ppermute x5, starting transfers between devices, along(): return lax.ppermute(array, axis, rotation(4, by))  34.6 us
    all_to_all x1, blocking collectives, shards(): mixed = lax.all_to_all(mixed, ('zh', 'c'), 0, 0, tiled=True)  28.9 us
    all_gather x1, blocking collectives, shards(): times = lax.all_gather(time_part, 'zl', axis=0, tiled=True)  28 us
    all_to_all x1, blocking collectives, shards(): joined = lax.all_to_all(joined, ('x', 'zl'), 0, 0, tiled=True)  22.5 us
    ppermute x5, starting transfers between devices, swapped(): return lax.ppermute(array, 'c', SWAP)  17.4 us
    all_to_all x1, blocking collectives, shards(): out = lax.all_to_all(out, ('x', 'zl'), 0, 0, tiled=True)  14.4 us
    pallas_call x1, Pallas kernels, shards(): pl.pallas_call(functools.partial(time_kernel, rows // 16), grid=(5,), out...  12.1 us
    pallas_call x1, Pallas kernels, shards(): pl.pallas_call(frame_kernel, out_shape=jax.ShapeDtypeStruct(((soon + rest...  7.32 us
  transfers between devices with their start and end apart: 11, of which 2 were waited for; matrix products, arithmetic and copies ran while one was open for 1% of the time, Pallas kernels for 5%

profile of v9, /device:TPU:1, one launch (start us, length us, event | category | flops | bytes accessed | tf_op | source)
XLA Modules:
  0.0 195.2 jit_solution(11886181853415224035)
XLA Ops:
  6.5 0.0 copy-start
  6.5 0.0 all-gather.3.cloned.1.call-start
  6.6 0.9 constant_dynamic-slice_fusion.1.own_ref
  7.5 1.0 pad_maximum_fusion
  8.5 9.6 %collective-permute-start = (bf16[144,1152]{1,0:T(8,128)(2,1)S(1)}, bf16[144,1152]{1,0:T(8,128)(2,1)S(1)}, u32[]{:S(2)}, u32[]{:S(2)}) collective-permute-start(bf16[144,1152]{1,0:T(8,128)(2,1)S(1)} %pad_maximum_fusion), channel_id=1, source_target_pairs={{0,2},{2,4},{4,6},{6,0},{1,3},{3,5},{5,7},{7,1},{8,10},{10,12},{12... | collective-permute-start | bytes 995336 | tf_op jit(solution)/shard_map/ppermute | solution.py:215
  18.1 5.6 %collective-permute-start.2 = (bf16[144,1152]{1,0:T(8,128)(2,1)S(1)}, bf16[144,1152]{1,0:T(8,128)(2,1)}, u32[]{:S(2)}, u32[]{:S(2)}) collective-permute-start(bf16[144,1152]{1,0:T(8,128)(2,1)S(1)} %pad_maximum_fusion), channel_id=1, source_target_pairs={{0,6},{2,0},{4,2},{6,4},{1,7},{3,1},{5,3},{7,5},{8,14},{10,8},{12,... | collective-permute-start | bytes 995336 | tf_op jit(solution)/shard_map/ppermute | solution.py:215
  23.7 10.3 %collective-permute-start.9 = (bf16[16,1152]{1,0:T(8,128)(2,1)S(1)}, bf16[16,1152]{1,0:T(8,128)(2,1)S(1)}, u32[]{:S(2)}, u32[]{:S(2)}) collective-permute-start(bf16[16,1152]{1,0:T(8,128)(2,1)S(1)} %constant_dynamic-slice_fusion.1.own_ref), channel_id=1, source_target_pairs={{0,4},{2,6},{4,0},{6,2},{1,5},{3,7},{5,1},{7,3},{8,12},{10,14},{12... | collective-permute-start | bytes 110600 | tf_op jit(solution)/shard_map/ppermute | solution.py:215
  34.0 0.0 copy-done
  34.0 28.0 %all_gather.9.times_ref = bf16[128,1152]{1,0:T(8,128)(2,1)S(1)} all-gather(bf16[32,1152]{1,0:T(8,128)(2,1)S(1)} %constant_dynamic-slice_fusion), channel_id=1, replica_groups=mesh['y'=4,'x'=4,'zl'=4,'zh'=4,'c'=2] {'zl'}, dimensions={0}, use_global_device_ids=true | all-gather | bytes 368640 | tf_op jit(solution)/shard_map/all_gather | solution.py:228
  62.0 0.0 collective-permute-done.9.across_ref
  62.0 0.0 collective-permute-done.refs_2_.below_ref
  62.0 0.0 collective-permute-done.2.refs_3_.above_ref
  62.0 1.8 pack.1
  63.8 0.0 all-gather.3.cloned.1.call-update
  63.8 0.0 copy-done.1
  63.9 8.0 %collective-permute-start.8 = (bf16[128,1152]{1,0:T(8,128)(2,1)S(1)}, bf16[128,1152]{1,0:T(8,128)(2,1)}, u32[]{:S(2)}, u32[]{:S(2)}) collective-permute-start(bf16[128,1152]{1,0:T(8,128)(2,1)S(1)} %bitcast.19), channel_id=1, source_target_pairs={{0,1},{1,0},{2,3},{3,2},{4,5},{5,4},{6,7},{7,6},{8,9},{9,8},{10,11... | collective-permute-start | bytes 884744 | tf_op jit(solution)/shard_map/ppermute | solution.py:218
  71.9 0.7 slice.8
  72.5 1.9 collective-permute-start.4
  74.5 1.6 slice.9
  76.0 7.3 %collective-permute-start.5 = (bf16[64,1152]{1,0:T(8,128)(2,1)}, bf16[64,1152]{1,0:T(8,128)(2,1)}, u32[]{:S(2)}, u32[]{:S(2)}) collective-permute-start(bf16[64,1152]{1,0:T(8,128)(2,1)} %slice.9), channel_id=1, source_target_pairs={{0,6},{2,0},{4,2},{6,4},{1,7},{3,1},{5,3},{7,5},{8,14},{10,8},{12,... | collective-permute-start | bytes 442376 | tf_op jit(solution)/shard_map/ppermute | solution.py:215
  83.3 2.5 %collective-permute-start.1 = (bf16[144,1152]{1,0:T(8,128)(2,1)S(1)}, bf16[144,1152]{1,0:T(8,128)(2,1)}, u32[]{:S(2)}, u32[]{:S(2)}) collective-permute-start(bf16[144,1152]{1,0:T(8,128)(2,1)S(1)} %collective-permute-done.refs_2_.below_ref), channel_id=1, source_target_pairs={{0,1},{1,0},{2,3},{3,2},{4,5},{5,4},{6,7},{7,6},{8,9},{9,8},{10,11... | collective-permute-start | bytes 995336 | tf_op jit(solution)/shard_map/ppermute | solution.py:218
  85.8 1.9 collective-permute-start.3
  87.8 0.0 copy-done.2
  87.8 0.1 spread.1
  87.9 0.0 copy-start.3
  87.9 0.7 copy-done.3
  88.7 0.0 copy-done.7
  88.7 0.1 stack.39.place_ref
  88.8 3.5 %collective-permute-done.4.one_ref = bf16[64,1152]{1,0:T(8,128)(2,1)S(1)} collective-permute-done((bf16[64,1152]{1,0:T(8,128)(2,1)}, bf16[64,1152]{1,0:T(8,128)(2,1)S(1)}, u32[]{:S(2)}, u32[]{:S(2)}) %collective-permute-start.4) | collective-permute-done | bytes 147488 | tf_op jit(solution)/shard_map/ppermute | solution.py:215
  92.3 2.6 %collective-permute-start.6 = (bf16[64,1152]{1,0:T(8,128)(2,1)S(1)}, bf16[64,1152]{1,0:T(8,128)(2,1)S(1)}, u32[]{:S(2)}, u32[]{:S(2)}) collective-permute-start(bf16[64,1152]{1,0:T(8,128)(2,1)S(1)} %collective-permute-done.4.one_ref), channel_id=1, source_target_pairs={{0,1},{1,0},{2,3},{3,2},{4,5},{5,4},{6,7},{7,6},{8,9},{9,8},{10,11... | collective-permute-start | bytes 442376 | tf_op jit(solution)/shard_map/ppermute | solution.py:218
  94.9 1.1 collective-permute-done.5.two_ref
  96.0 2.4 %collective-permute-start.7 = (bf16[64,1152]{1,0:T(8,128)(2,1)}, bf16[64,1152]{1,0:T(8,128)(2,1)S(1)}, u32[]{:S(2)}, u32[]{:S(2)}) collective-permute-start(bf16[64,1152]{1,0:T(8,128)(2,1)} %collective-permute-done.5.two_ref), channel_id=1, source_target_pairs={{0,1},{1,0},{2,3},{3,2},{4,5},{5,4},{6,7},{7,6},{8,9},{9,8},{10,11... | collective-permute-start | bytes 442376 | tf_op jit(solution)/shard_map/ppermute | solution.py:218
  98.5 0.0 collective-permute-done.8.refs_1_
  98.5 1.0 copy-done.4
  99.5 2.7 %early_triples.1 = (bf16[512,512]{1,0:T(8,128)(2,1)S(1)}, bf16[160,512]{1,0:T(8,128)(2,1)S(1)}) custom-call(bf16[128,1152]{1,0:T(8,128)(2,1)S(1)} %bitcast.20, bf16[128,1152]{1,0:T(8,128)(2,1)} %collective-permute-done.8.refs_1_, bf16[144,1152]{1,0:T(8,128)(2,1)S(1)} %collective-permute-done.refs_2_.below_ref, ...), custom_call_target="tpu_custom_call" | custom-call | flops 2000000000 | bytes 5000000 | tf_op jit(solution)/shard_map/early_triples/pallas_call | solution.py:260
  102.2 0.0 collective-permute-done.6.three_ref
  102.2 0.0 collective-permute-done.7.four_ref
  102.2 0.0 collective-permute-done.1.below_ref
  102.2 0.0 collective-permute-done.3.above_ref
  102.3 0.0 copy-done.5
  102.3 0.0 copy-done.6
  102.3 7.3 %frame_attention.1 = bf16[8,144,128]{2,1,0:T(8,128)(2,1)S(1)} custom-call(s32[9]{0:T(128)S(1)} %stack.39.place_ref, bf16[144,1152]{1,0:T(8,128)(2,1)} %collective-permute-done.1.below_ref, bf16[144,1152]{1,0:T(8,128)(2,1)} %collective-permute-done.3.above_ref, bf16[64,1152]{1,0:T(8,128)(2,1)S(1)} %collective-permute-done.4.one_ref, ...), custom_call_target="tpu_custom_call" | custom-call | tf_op jit(solution)/shard_map/frame_attention/pallas_call | solution.py:274
  109.6 28.9 %all_to_all.25.mixed_ref = bf16[8,144,128]{2,1,0:T(8,128)(2,1)S(1)} all-to-all(bf16[8,144,128]{2,1,0:T(8,128)(2,1)S(1)} %frame_attention.1), channel_id=1, replica_groups=mesh['y'=4,'x'=4,'zl'=4,'zh'=4,'c'=2] {'zh','c'}, dimensions={0} | all-to-all | bytes 589824 | tf_op jit(solution)/shard_map/all_to_all | solution.py:287
  138.5 0.2 join.1
  138.7 22.5 %all_to_all.26 = bf16[16,8,2304]{2,1,0:T(8,128)(2,1)} all-to-all(bf16[16,8,2304]{2,1,0:T(8,128)(2,1)S(1)} %bitcast.17), channel_id=1, replica_groups=mesh['y'=4,'x'=4,'zl'=4,'zh'=4,'c'=2] {'x','zl'}, dimensions={0} | all-to-all | bytes 1179648 | tf_op jit(solution)/shard_map/all_to_all | solution.py:296
  161.2 12.1 %time_block.1 = bf16[128,1152]{1,0:T(8,128)(2,1)} custom-call(s32[9]{0:T(128)} %copy-done.6, bf16[128,2304]{1,0:T(8,128)(2,1)} %bitcast.25, bf16[4,8,192,1152]{3,2,1,0:T(8,128)(2,1)} %bitcast.23, bf16[16,2,192,1152]{3,2,1,0:T(8,128)(2,1)} %bitcast.24, bf16[1152,1152]{1,0:T(8,128)(2,1)} %out_table_ref.1, f32[2,3,1152]{2,1,0:T(4,128)} %copy-done.5), custom_call_target="tpu_custom_call" | custom-call | tf_op jit(solution)/shard_map/time_block/pallas_call | solution.py:298
  173.3 14.4 %all_to_all.27 = bf16[16,8,1152]{2,1,0:T(8,128)(2,1)S(1)} all-to-all(bf16[16,8,1152]{2,1,0:T(8,128)(2,1)} %bitcast.27), channel_id=1, replica_groups=mesh['y'=4,'x'=4,'zl'=4,'zh'=4,'c'=2] {'x','zl'}, dimensions={0} | all-to-all | bytes 589824 | tf_op jit(solution)/shard_map/all_to_all | solution.py:323
  187.6 0.7 copy.11
  (9 shorter events, 0.1 us)
Async XLA Ops:
  6.5 27.4 %copy-start = (bf16[216,1152]{1,0:T(8,128)(2,1)S(1)}, bf16[216,1152]{1,0:T(8,128)(2,1)}, u32[]{:S(2)}) copy-start(bf16[216,1152]{1,0:T(8,128)(2,1)} %param.9) | copy-start | bytes 1492996
  6.5 57.3 %copy-start.1 = (bf16[1,128,1152]{2,1,0:T(8,128)(2,1)S(1)}, bf16[1,128,1152]{2,1,0:T(8,128)(2,1)}, u32[]{:S(2)}) copy-start(bf16[1,128,1152]{2,1,0:T(8,128)(2,1)} %param.6) | copy-start | bytes 884740
  6.5 81.2 %copy-start.2 = (bf16[1152,432]{0,1:T(8,128)(2,1)S(1)}, bf16[1152,432]{0,1:T(8,128)(2,1)}, u32[]{:S(2)}) copy-start(bf16[1152,432]{0,1:T(8,128)(2,1)} %param.7) | copy-start | bytes 2985988
  6.5 82.1 %copy-start.7 = (f32[2,3,1152]{2,0,1:T(2,128)S(1)}, f32[2,3,1152]{2,0,1:T(2,128)}, u32[]{:S(2)}) copy-start(f32[2,3,1152]{2,0,1:T(2,128)} %param.11) | copy-start | bytes 82948
  6.5 154.6 %all-gather.3.cloned.1.call-start = ((), (), s32[]{:S(2)}) async-start(), calls=%async_computation.3 | async-start | bytes 14598144 | tf_op jit(solution)/shard_map/all_gather | solution.py:237
  8.5 53.6 %collective-permute-start = (bf16[144,1152]{1,0:T(8,128)(2,1)S(1)}, bf16[144,1152]{1,0:T(8,128)(2,1)S(1)}, u32[]{:S(2)}, u32[]{:S(2)}) collective-permute-start(bf16[144,1152]{1,0:T(8,128)(2,1)S(1)} %pad_maximum_fusion), channel_id=1, source_target_pairs={{0,2},{2,4},{4,6},{6,0},{1,3},{3,5},{5,7},{7,1},{8,10},{10,12},{12... | collective-permute-start | bytes 995336 | tf_op jit(solution)/shard_map/ppermute | solution.py:215
  18.1 43.9 %collective-permute-start.2 = (bf16[144,1152]{1,0:T(8,128)(2,1)S(1)}, bf16[144,1152]{1,0:T(8,128)(2,1)}, u32[]{:S(2)}, u32[]{:S(2)}) collective-permute-start(bf16[144,1152]{1,0:T(8,128)(2,1)S(1)} %pad_maximum_fusion), channel_id=1, source_target_pairs={{0,6},{2,0},{4,2},{6,4},{1,7},{3,1},{5,3},{7,5},{8,14},{10,8},{12,... | collective-permute-start | bytes 995336 | tf_op jit(solution)/shard_map/ppermute | solution.py:215
  23.7 38.3 %collective-permute-start.9 = (bf16[16,1152]{1,0:T(8,128)(2,1)S(1)}, bf16[16,1152]{1,0:T(8,128)(2,1)S(1)}, u32[]{:S(2)}, u32[]{:S(2)}) collective-permute-start(bf16[16,1152]{1,0:T(8,128)(2,1)S(1)} %constant_dynamic-slice_fusion.1.own_ref), channel_id=1, source_target_pairs={{0,4},{2,6},{4,0},{6,2},{1,5},{3,7},{5,1},{7,3},{8,12},{10,14},{12... | collective-permute-start | bytes 110600 | tf_op jit(solution)/shard_map/ppermute | solution.py:215
  63.9 34.6 %collective-permute-start.8 = (bf16[128,1152]{1,0:T(8,128)(2,1)S(1)}, bf16[128,1152]{1,0:T(8,128)(2,1)}, u32[]{:S(2)}, u32[]{:S(2)}) collective-permute-start(bf16[128,1152]{1,0:T(8,128)(2,1)S(1)} %bitcast.19), channel_id=1, source_target_pairs={{0,1},{1,0},{2,3},{3,2},{4,5},{5,4},{6,7},{7,6},{8,9},{9,8},{10,11... | collective-permute-start | bytes 884744 | tf_op jit(solution)/shard_map/ppermute | solution.py:218
  72.5 19.8 %collective-permute-start.4 = (bf16[64,1152]{1,0:T(8,128)(2,1)}, bf16[64,1152]{1,0:T(8,128)(2,1)S(1)}, u32[]{:S(2)}, u32[]{:S(2)}) collective-permute-start(bf16[64,1152]{1,0:T(8,128)(2,1)} %slice.8), channel_id=1, source_target_pairs={{0,2},{2,4},{4,6},{6,0},{1,3},{3,5},{5,7},{7,1},{8,10},{10,12},{12... | collective-permute-start | bytes 442376 | tf_op jit(solution)/shard_map/ppermute | solution.py:215
  76.0 20.0 %collective-permute-start.5 = (bf16[64,1152]{1,0:T(8,128)(2,1)}, bf16[64,1152]{1,0:T(8,128)(2,1)}, u32[]{:S(2)}, u32[]{:S(2)}) collective-permute-start(bf16[64,1152]{1,0:T(8,128)(2,1)} %slice.9), channel_id=1, source_target_pairs={{0,6},{2,0},{4,2},{6,4},{1,7},{3,1},{5,3},{7,5},{8,14},{10,8},{12,... | collective-permute-start | bytes 442376 | tf_op jit(solution)/shard_map/ppermute | solution.py:215
  83.3 18.9 %collective-permute-start.1 = (bf16[144,1152]{1,0:T(8,128)(2,1)S(1)}, bf16[144,1152]{1,0:T(8,128)(2,1)}, u32[]{:S(2)}, u32[]{:S(2)}) collective-permute-start(bf16[144,1152]{1,0:T(8,128)(2,1)S(1)} %collective-permute-done.refs_2_.below_ref), channel_id=1, source_target_pairs={{0,1},{1,0},{2,3},{3,2},{4,5},{5,4},{6,7},{7,6},{8,9},{9,8},{10,11... | collective-permute-start | bytes 995336 | tf_op jit(solution)/shard_map/ppermute | solution.py:218
  85.8 16.4 %collective-permute-start.3 = (bf16[144,1152]{1,0:T(8,128)(2,1)}, bf16[144,1152]{1,0:T(8,128)(2,1)}, u32[]{:S(2)}, u32[]{:S(2)}) collective-permute-start(bf16[144,1152]{1,0:T(8,128)(2,1)} %collective-permute-done.2.refs_3_.above_ref), channel_id=1, source_target_pairs={{0,1},{1,0},{2,3},{3,2},{4,5},{5,4},{6,7},{7,6},{8,9},{9,8},{10,11... | collective-permute-start | bytes 995336 | tf_op jit(solution)/shard_map/ppermute | solution.py:218
  87.9 0.7 copy-start.3
  88.7 13.6 %copy-start.5 = (f32[2,3,1152]{2,1,0:T(4,128)}, f32[2,3,1152]{2,1,0:T(4,128)S(1)}, u32[]{:S(2)}) copy-start(f32[2,3,1152]{2,1,0:T(4,128)S(1)} %copy.7.refs_4_.modulation_ref) | copy-start | bytes 82948
  88.8 13.5 %copy-start.6 = (s32[9]{0:T(128)}, s32[9]{0:T(128)S(1)}, u32[]{:S(2)}) copy-start(s32[9]{0:T(128)S(1)} %stack.39.place_ref) | copy-start | bytes 112
  92.3 9.9 %collective-permute-start.6 = (bf16[64,1152]{1,0:T(8,128)(2,1)S(1)}, bf16[64,1152]{1,0:T(8,128)(2,1)S(1)}, u32[]{:S(2)}, u32[]{:S(2)}) collective-permute-start(bf16[64,1152]{1,0:T(8,128)(2,1)S(1)} %collective-permute-done.4.one_ref), channel_id=1, source_target_pairs={{0,1},{1,0},{2,3},{3,2},{4,5},{5,4},{6,7},{7,6},{8,9},{9,8},{10,11... | collective-permute-start | bytes 442376 | tf_op jit(solution)/shard_map/ppermute | solution.py:218
  96.0 6.2 %collective-permute-start.7 = (bf16[64,1152]{1,0:T(8,128)(2,1)}, bf16[64,1152]{1,0:T(8,128)(2,1)S(1)}, u32[]{:S(2)}, u32[]{:S(2)}) collective-permute-start(bf16[64,1152]{1,0:T(8,128)(2,1)} %collective-permute-done.5.two_ref), channel_id=1, source_target_pairs={{0,1},{1,0},{2,3},{3,2},{4,5},{5,4},{6,7},{7,6},{8,9},{9,8},{10,11... | collective-permute-start | bytes 442376 | tf_op jit(solution)/shard_map/ppermute | solution.py:218
  98.5 1.0 copy-start.4
Sparse Core Ops, SparseCore 0:
  64.0 87.4 all-gather.2

commit v10 on v7

--- a/solution.py
+++ b/solution.py
@@ -132,54 +132,46 @@
     ).astype(jnp.bfloat16)
 
 
-def time_kernel(
-    positions, middle_ref, tables_ref, out_table_ref, modulation_ref, out_ref,
-    input_ref, mixed_ref, table_ref, sem,
-):
-    step = pl.program_id(0)
-    copy = pltpu.make_async_copy(out_table_ref, table_ref, sem)
-
-    @pl.when(step == 0)
-    def _():
-        copy.start()
-        input_ref[...] = modulated(
-            middle_ref[...].astype(jnp.float32), modulation_ref[1, 0:1], modulation_ref[1, 1:2]
-        )
-
-    rows, width = input_ref.shape
+def time_attention(positions, triples, mixed_ref, first):
+    rows = triples.shape[1]
     one = lax.broadcasted_iota(jnp.int32, (rows, rows), 0) % positions
     two = lax.broadcasted_iota(jnp.int32, (rows, rows), 1) % positions
     same = one == two
-    triples = []
-    for slot in range(4):
-        table = tables_ref[0, 0:7, 32 * slot : 32 * slot + 32].reshape(7 * 32, width)
-        triples.append(lax.dot_general(table, input_ref[...], NT, preferred_element_type=jnp.float32))
-    scores = []
-    for triple in triples:
+    scores, values = [], []
+    for head in range(4):
+        triple = jnp.concatenate(
+            [triples[LANES * part + 32 * head : LANES * part + 32 * head + 32] for part in range(7)], axis=0
+        )
         queries = triple[:HD].astype(jnp.bfloat16)
         keys = triple[HD : 2 * HD].astype(jnp.bfloat16)
+        values.append(jnp.concatenate([triple[2 * HD : 192], triple[200:]], axis=0).astype(jnp.bfloat16))
         part = lax.dot_general(keys, queries, TN, preferred_element_type=jnp.float32)
         scores.append(jnp.where(same, part, -1e30))
     raised = [
         jnp.exp2((part - jnp.max(part, axis=0, keepdims=True)) * EXP2_SCALE) for part in scores
     ]
-    for slot in range(4):
-        values = jnp.concatenate([triples[slot][2 * HD : 192], triples[slot][200:]], axis=0)
-        total = jnp.sum(raised[slot], axis=0, keepdims=True)
-        mixed = jnp.dot(
-            values.astype(jnp.bfloat16), raised[slot].astype(jnp.bfloat16),
-            preferred_element_type=jnp.float32,
-        )
-        mixed_ref[step * 4 + slot] = mixed / total
-
-    @pl.when(step == pl.num_programs(0) - 1)
-    def _():
-        copy.wait()
-        mixed = mixed_ref[...].reshape(-1, rows).astype(jnp.bfloat16)
-        branch = lax.dot_general(mixed, table_ref[...], TN, preferred_element_type=jnp.float32)
-        out_ref[...] = (
-            middle_ref[...].astype(jnp.float32) + modulation_ref[1, 2:3] * branch
-        ).astype(jnp.bfloat16)
+    for head in range(4):
+        total = jnp.sum(raised[head], axis=0, keepdims=True)
+        mixed = jnp.dot(values[head], raised[head].astype(jnp.bfloat16), preferred_element_type=jnp.float32)
+        mixed_ref[first + head] = mixed / total
+
+
+def time_kernel(
+    positions, middle_ref, tables_ref, out_table_ref, modulation_ref, out_ref, mixed_ref,
+):
+    rows, width = middle_ref.shape
+    second = modulated(
+        middle_ref[...].astype(jnp.float32), modulation_ref[1, 0:1], modulation_ref[1, 1:2]
+    )
+    for group in range(4):
+        table = tables_ref[group, 0:7, 0:LANES].reshape(7 * LANES, width)
+        triples = lax.dot_general(table, second, NT, preferred_element_type=jnp.float32)
+        time_attention(positions, triples, mixed_ref, 4 * group)
+    mixed = mixed_ref[...].reshape(-1, rows).astype(jnp.bfloat16)
+    branch = lax.dot_general(mixed, out_table_ref[...], TN, preferred_element_type=jnp.float32)
+    out_ref[...] = (
+        middle_ref[...].astype(jnp.float32) + modulation_ref[1, 2:3] * branch
+    ).astype(jnp.bfloat16)
 
 
 def rotation(count, by):
@@ -276,7 +268,7 @@
         in_specs=[whole(), pl.BlockSpec(memory_space=pl.ANY), whole(), whole()],
         out_specs=whole(),
         scratch_shapes=[pltpu.VMEM((9, 2, 64, width), jnp.bfloat16), pltpu.SemaphoreType.DMA],
-        compiler_params=params(),
+        compiler_params=params(44),
         name="middle",
     )(mixed, tables.reshape(16, 2, 192, width), tokens, modulation)
 
@@ -284,22 +276,11 @@
 
     out = pl.pallas_call(
         functools.partial(time_kernel, rows // 16),
-        grid=(4,),
         out_shape=jax.ShapeDtypeStruct((rows, width), jnp.bfloat16),
-        in_specs=[
-            whole(),
-            pl.BlockSpec((1, 8, LANES, width), lambda i: (i, 0, 0, 0)),
-            pl.BlockSpec(memory_space=pl.ANY),
-            whole(),
-        ],
+        in_specs=[whole()] * 4,
         out_specs=whole(),
-        scratch_shapes=[
-            pltpu.VMEM((rows, width), jnp.bfloat16),
-            pltpu.VMEM((16, HD, rows), jnp.float32),
-            pltpu.VMEM((width, width), jnp.bfloat16),
-            pltpu.SemaphoreType.DMA,
-        ],
-        compiler_params=params(),
+        scratch_shapes=[pltpu.VMEM((16, HD, rows), jnp.float32)],
+        compiler_params=params(28),
         name="time_block",
     )(middle, tables, time_out, modulation)
     out = lax.all_to_all(out, ("x", "zl"), 0, 0, tiled=True)

time: 181 us -> 183 us (1.011)
  local copies, waits for them, and re-layouts: 4.89 us -> 10.7 us
  Pallas kernels: 21.1 us -> 18.9 us
    unnamed x10 -> x26, local copies, waits for them, and re-layouts: 0.74 us -> 6.53 us
    pallas_call x1, Pallas kernels: 7.81 us -> 5.96 us  [shards(): pl.pallas_call(functools.partial(time_kernel, rows // 16), out_shape=jax....]
  transfers between devices with their start and end apart: 10 -> 10, of which waited for: 1 -> 1; matrix products, arithmetic and copies ran while one was open for 2% -> 2% of each run, Pallas kernels for 6% -> 5%
where the time goes in v10:
time: 183 us; the launch traced here: 182 us
  blocking collectives  85.6 us (47%)
  starting transfers between devices  43.6 us (24%)
  Pallas kernels  18.9 us (10%)
  between operations  13.7 us (7%)
  local copies, waits for them, and re-layouts  10.7 us (6%)
  waiting for transfers between devices  9.5 us (5%)
    all_gather x1, blocking collectives, shards(): parts = lax.all_gather(part, ('zh', 'zl'), axis=0, tiled=True)  32.1 us
    ppermute x5, starting transfers between devices, swapped(): return lax.ppermute(array, 'c', SWAP)  25.3 us
    all_to_all x1, blocking collectives, shards(): mixed = lax.all_to_all(mixed, ('zh', 'c'), 0, 0, tiled=True)  24.6 us
    ppermute x4, starting transfers between devices, along(): return lax.ppermute(array, axis, rotation(4, by))  18.4 us
    all_to_all x1, blocking collectives, shards(): middle = lax.all_to_all(middle, ('x', 'zl'), 0, 0, tiled=True)  15 us
    all_to_all x1, blocking collectives, shards(): out = lax.all_to_all(out, ('x', 'zl'), 0, 0, tiled=True)  13.8 us
    ppermute x4, waiting for transfers between devices, along(): return lax.ppermute(array, axis, rotation(4, by))  9.47 us
    pallas_call x1, Pallas kernels, shards(): pl.pallas_call(frame_kernel, out_shape=jax.ShapeDtypeStruct(((soon + rest...  6.73 us
  transfers between devices with their start and end apart: 10, of which 1 were waited for; matrix products, arithmetic and copies ran while one was open for 2% of the time, Pallas kernels for 5%

profile of v10, /device:TPU:1, one launch (start us, length us, event | category | flops | bytes accessed | tf_op | source)
XLA Modules:
  0.0 182.0 jit_solution(15911648528062831141)
XLA Ops:
  6.5 0.0 all-gather.3.cloned.1.call-start
  6.5 0.9 constant_dynamic-slice_fusion
  7.4 32.1 %all_gather.9.parts_ref = bf16[256,1152]{1,0:T(8,128)(2,1)S(1)} all-gather(bf16[16,1152]{1,0:T(8,128)(2,1)S(1)} %pad_maximum_fusion), channel_id=1, replica_groups=mesh['y'=4,'x'=4,'zl'=4,'zh'=4,'c'=2] {'zh','zl'}, dimensions={0}, use_global_device_ids=true | all-gather | bytes 626688 | tf_op jit(solution)/shard_map/all_gather | solution.py:212
  39.6 0.8 pack.1
  40.4 0.0 all-gather.3.cloned.1.call-update
  40.4 3.7 %collective-permute-start = (bf16[128,1152]{1,0:T(8,128)(2,1)}, bf16[128,1152]{1,0:T(8,128)(2,1)}, u32[]{:S(2)}, u32[]{:S(2)}) collective-permute-start(bf16[128,1152]{1,0:T(8,128)(2,1)} %bitcast.22), channel_id=1, source_target_pairs={{0,2},{2,4},{4,6},{6,0},{1,3},{3,5},{5,7},{7,1},{8,10},{10,12},{12... | collective-permute-start | bytes 884744 | tf_op jit(solution)/shard_map/ppermute | solution.py:191
  44.0 5.5 %collective-permute-start.2 = (bf16[128,1152]{1,0:T(8,128)(2,1)}, bf16[128,1152]{1,0:T(8,128)(2,1)}, u32[]{:S(2)}, u32[]{:S(2)}) collective-permute-start(bf16[128,1152]{1,0:T(8,128)(2,1)} %bitcast.23), channel_id=1, source_target_pairs={{0,6},{2,0},{4,2},{6,4},{1,7},{3,1},{5,3},{7,5},{8,14},{10,8},{12,... | collective-permute-start | bytes 884744 | tf_op jit(solution)/shard_map/ppermute | solution.py:191
  49.6 14.1 %collective-permute-start.8 = (bf16[128,1152]{1,0:T(8,128)(2,1)}, bf16[128,1152]{1,0:T(8,128)(2,1)}, u32[]{:S(2)}, u32[]{:S(2)}) collective-permute-start(bf16[128,1152]{1,0:T(8,128)(2,1)} %bitcast.24), channel_id=1, source_target_pairs={{0,1},{1,0},{2,3},{3,2},{4,5},{5,4},{6,7},{7,6},{8,9},{9,8},{10,11... | collective-permute-start | bytes 884744 | tf_op jit(solution)/shard_map/ppermute | solution.py:194
  63.7 9.5 %collective-permute-done.refs_2_ = bf16[128,1152]{1,0:T(8,128)(2,1)} collective-permute-done((bf16[128,1152]{1,0:T(8,128)(2,1)}, bf16[128,1152]{1,0:T(8,128)(2,1)}, u32[]{:S(2)}, u32[]{:S(2)}) %collective-permute-start) | collective-permute-done | bytes 294944 | tf_op jit(solution)/shard_map/ppermute | solution.py:191
  73.2 1.6 slice.8
  74.7 3.8 %collective-permute-start.4 = (bf16[64,1152]{1,0:T(8,128)(2,1)}, bf16[64,1152]{1,0:T(8,128)(2,1)S(1)}, u32[]{:S(2)}, u32[]{:S(2)}) collective-permute-start(bf16[64,1152]{1,0:T(8,128)(2,1)} %slice.8), channel_id=1, source_target_pairs={{0,2},{2,4},{4,6},{6,0},{1,3},{3,5},{5,7},{7,1},{8,10},{10,12},{12... | collective-permute-start | bytes 442376 | tf_op jit(solution)/shard_map/ppermute | solution.py:191
  78.5 0.0 collective-permute-done.2.refs_3_
  78.6 1.6 slice.9
  80.1 5.4 %collective-permute-start.5 = (bf16[64,1152]{1,0:T(8,128)(2,1)}, bf16[64,1152]{1,0:T(8,128)(2,1)S(1)}, u32[]{:S(2)}, u32[]{:S(2)}) collective-permute-start(bf16[64,1152]{1,0:T(8,128)(2,1)} %slice.9), channel_id=1, source_target_pairs={{0,6},{2,0},{4,2},{6,4},{1,7},{3,1},{5,3},{7,5},{8,14},{10,8},{12,... | collective-permute-start | bytes 442376 | tf_op jit(solution)/shard_map/ppermute | solution.py:191
  85.5 4.9 %collective-permute-start.1 = (bf16[128,1152]{1,0:T(8,128)(2,1)}, bf16[128,1152]{1,0:T(8,128)(2,1)S(1)}, u32[]{:S(2)}, u32[]{:S(2)}) collective-permute-start(bf16[128,1152]{1,0:T(8,128)(2,1)} %collective-permute-done.refs_2_), channel_id=1, source_target_pairs={{0,1},{1,0},{2,3},{3,2},{4,5},{5,4},{6,7},{7,6},{8,9},{9,8},{10,11... | collective-permute-start | bytes 884744 | tf_op jit(solution)/shard_map/ppermute | solution.py:194
  90.4 1.9 %collective-permute-start.3 = (bf16[128,1152]{1,0:T(8,128)(2,1)}, bf16[128,1152]{1,0:T(8,128)(2,1)S(1)}, u32[]{:S(2)}, u32[]{:S(2)}) collective-permute-start(bf16[128,1152]{1,0:T(8,128)(2,1)} %collective-permute-done.2.refs_3_), channel_id=1, source_target_pairs={{0,1},{1,0},{2,3},{3,2},{4,5},{5,4},{6,7},{7,6},{8,9},{9,8},{10,11... | collective-permute-start | bytes 884744 | tf_op jit(solution)/shard_map/ppermute | solution.py:194
  92.4 0.0 copy-done.11
  92.4 0.0 copy-done.4
  92.5 0.1 spread.1
  92.6 0.0 copy-start.2
  92.6 0.1 stack.35.place_ref
  92.7 0.0 collective-permute-done.4.one_ref
  92.7 2.4 %collective-permute-start.6 = (bf16[64,1152]{1,0:T(8,128)(2,1)S(1)}, bf16[64,1152]{1,0:T(8,128)(2,1)S(1)}, u32[]{:S(2)}, u32[]{:S(2)}) collective-permute-start(bf16[64,1152]{1,0:T(8,128)(2,1)S(1)} %collective-permute-done.4.one_ref), channel_id=1, source_target_pairs={{0,1},{1,0},{2,3},{3,2},{4,5},{5,4},{6,7},{7,6},{8,9},{9,8},{10,11... | collective-permute-start | bytes 442376 | tf_op jit(solution)/shard_map/ppermute | solution.py:194
  95.1 0.0 collective-permute-done.5.two_ref
  95.1 0.0 copy-start.9
  95.1 1.9 %collective-permute-start.7 = (bf16[64,1152]{1,0:T(8,128)(2,1)S(1)}, bf16[64,1152]{1,0:T(8,128)(2,1)S(1)}, u32[]{:S(2)}, u32[]{:S(2)}) collective-permute-start(bf16[64,1152]{1,0:T(8,128)(2,1)S(1)} %collective-permute-done.5.two_ref), channel_id=1, source_target_pairs={{0,1},{1,0},{2,3},{3,2},{4,5},{5,4},{6,7},{7,6},{8,9},{9,8},{10,11... | collective-permute-start | bytes 442376 | tf_op jit(solution)/shard_map/ppermute | solution.py:194
  97.0 0.0 collective-permute-done.8.refs_1_
  97.1 0.0 copy-start.7
  97.1 1.0 copy-done.7
  98.0 2.8 %early_triples.1 = (bf16[512,512]{1,0:T(8,128)(2,1)S(1)}, bf16[160,512]{1,0:T(8,128)(2,1)S(1)}) custom-call(bf16[128,1152]{1,0:T(8,128)(2,1)S(1)} %bitcast.25, bf16[128,1152]{1,0:T(8,128)(2,1)} %collective-permute-done.8.refs_1_, bf16[128,1152]{1,0:T(8,128)(2,1)} %collective-permute-done.refs_2_, bf16[128,1152]{1,0:T(8,128)(2,1)} %collective-permute-done.2.refs_3_, ...), custom_call_target="tpu_custom_call" | custom-call | flops 2000000000 | bytes 5000000 | tf_op jit(solution)/shard_map/early_triples/pallas_call | solution.py:237
  100.8 0.0 copy-done.2
  100.8 0.0 collective-permute-done.6.three_ref
  100.8 0.0 collective-permute-done.7.four_ref
  100.8 0.0 collective-permute-done.1.below_ref
  100.8 0.0 collective-permute-done.3.above_ref
  100.8 0.0 copy-start.5
  100.9 0.7 copy-done.5
  101.6 1.3 copy-done.3
  102.8 1.0 copy-done.6
  103.8 0.9 copy-done.10
  104.7 6.7 %frame_attention.1 = bf16[8,144,128]{2,1,0:T(8,128)(2,1)S(1)} custom-call(s32[8]{0:T(128)S(1)} %stack.35.place_ref, bf16[128,1152]{1,0:T(8,128)(2,1)S(1)} %collective-permute-done.1.below_ref, bf16[128,1152]{1,0:T(8,128)(2,1)S(1)} %copy-done.6, bf16[64,1152]{1,0:T(8,128)(2,1)S(1)} %collective-permute-done.4.one_ref, bf16[64,1152]{1,0:T(8,128)(2,1)S(1)} %copy-done.10, ...), custom_call_target="tpu_custom_call" | custom-call | tf_op jit(solution)/shard_map/frame_attention/pallas_call | solution.py:251
  111.5 24.6 %all_to_all.25.mixed_ref = bf16[8,144,128]{2,1,0:T(8,128)(2,1)S(1)} all-to-all(bf16[8,144,128]{2,1,0:T(8,128)(2,1)S(1)} %frame_attention.1), channel_id=1, replica_groups=mesh['y'=4,'x'=4,'zl'=4,'zh'=4,'c'=2] {'zh','c'}, dimensions={0} | all-to-all | bytes 589824 | tf_op jit(solution)/shard_map/all_to_all | solution.py:264
  136.1 1.0 copy-done.8
  137.1 2.5 %middle.1 = bf16[128,1152]{1,0:T(8,128)(2,1)S(1)} custom-call(bf16[8,144,128]{2,1,0:T(8,128)(2,1)S(1)} %all_to_all.25.mixed_ref, bf16[16,2,192,1152]{3,2,1,0:T(8,128)(2,1)} %bitcast.16, bf16[128,1152]{1,0:T(8,128)(2,1)S(1)} %bitcast.26, f32[2,3,1152]{2,1,0:T(4,128)S(1)} %copy.7.refs_4_.modulation_ref), custom_call_target="tpu_custom_call" | custom-call | tf_op jit(solution)/shard_map/middle/pallas_call | solution.py:265
  139.6 15.0 %all_to_all.26 = bf16[16,8,1152]{2,1,0:T(8,128)(2,1)S(1)} all-to-all(bf16[16,8,1152]{2,1,0:T(8,128)(2,1)S(1)} %bitcast.20), channel_id=1, replica_groups=mesh['y'=4,'x'=4,'zl'=4,'zh'=4,'c'=2] {'x','zl'}, dimensions={0} | all-to-all | bytes 589824 | tf_op jit(solution)/shard_map/all_to_all | solution.py:275
  154.7 6.0 %time_block.1 = bf16[128,1152]{1,0:T(8,128)(2,1)S(1)} custom-call(bf16[128,1152]{1,0:T(8,128)(2,1)S(1)} %bitcast.18, bf16[4,8,192,1152]{3,2,1,0:T(8,128)(2,1)S(1)} %bitcast.17, bf16[1152,1152]{1,0:T(8,128)(2,1)S(1)} %copy-done.1, f32[2,3,1152]{2,1,0:T(4,128)S(1)} %copy.7.refs_4_.modulation_ref), custom_call_target="tpu_custom_call" | custom-call | tf_op jit(solution)/shard_map/time_block/pallas_call | solution.py:277
  160.6 13.8 %all_to_all.27 = bf16[16,8,1152]{2,1,0:T(8,128)(2,1)S(1)} all-to-all(bf16[16,8,1152]{2,1,0:T(8,128)(2,1)S(1)} %bitcast.19), channel_id=1, replica_groups=mesh['y'=4,'x'=4,'zl'=4,'zh'=4,'c'=2] {'x','zl'}, dimensions={0} | all-to-all | bytes 589824 | tf_op jit(solution)/shard_map/all_to_all | solution.py:286
  174.4 0.7 copy.12
  (14 shorter events, 0.0 us)
Async XLA Ops:
  6.5 85.9 %copy-start.11 = (f32[2,3,1152]{2,0,1:T(2,128)S(1)}, f32[2,3,1152]{2,0,1:T(2,128)}, u32[]{:S(2)}) copy-start(f32[2,3,1152]{2,0,1:T(2,128)} %param.11) | copy-start | bytes 82948
  6.5 85.9 %copy-start.4 = (bf16[1152,432]{0,1:T(8,128)(2,1)S(1)}, bf16[1152,432]{0,1:T(8,128)(2,1)}, u32[]{:S(2)}) copy-start(bf16[1152,432]{0,1:T(8,128)(2,1)} %param.7) | copy-start | bytes 2985988
  6.5 129.6 %all-gather.3.cloned.1.call-start = ((), (), s32[]{:S(2)}) async-start(), calls=%async_computation.3 | async-start | bytes 14598144 | tf_op jit(solution)/shard_map/all_gather | solution.py:221
  40.4 32.8 %collective-permute-start = (bf16[128,1152]{1,0:T(8,128)(2,1)}, bf16[128,1152]{1,0:T(8,128)(2,1)}, u32[]{:S(2)}, u32[]{:S(2)}) collective-permute-start(bf16[128,1152]{1,0:T(8,128)(2,1)} %bitcast.22), channel_id=1, source_target_pairs={{0,2},{2,4},{4,6},{6,0},{1,3},{3,5},{5,7},{7,1},{8,10},{10,12},{12... | collective-permute-start | bytes 884744 | tf_op jit(solution)/shard_map/ppermute | solution.py:191
  44.0 34.5 %collective-permute-start.2 = (bf16[128,1152]{1,0:T(8,128)(2,1)}, bf16[128,1152]{1,0:T(8,128)(2,1)}, u32[]{:S(2)}, u32[]{:S(2)}) collective-permute-start(bf16[128,1152]{1,0:T(8,128)(2,1)} %bitcast.23), channel_id=1, source_target_pairs={{0,6},{2,0},{4,2},{6,4},{1,7},{3,1},{5,3},{7,5},{8,14},{10,8},{12,... | collective-permute-start | bytes 884744 | tf_op jit(solution)/shard_map/ppermute | solution.py:191
  49.6 47.5 %collective-permute-start.8 = (bf16[128,1152]{1,0:T(8,128)(2,1)}, bf16[128,1152]{1,0:T(8,128)(2,1)}, u32[]{:S(2)}, u32[]{:S(2)}) collective-permute-start(bf16[128,1152]{1,0:T(8,128)(2,1)} %bitcast.24), channel_id=1, source_target_pairs={{0,1},{1,0},{2,3},{3,2},{4,5},{5,4},{6,7},{7,6},{8,9},{9,8},{10,11... | collective-permute-start | bytes 884744 | tf_op jit(solution)/shard_map/ppermute | solution.py:194
  74.7 17.9 %collective-permute-start.4 = (bf16[64,1152]{1,0:T(8,128)(2,1)}, bf16[64,1152]{1,0:T(8,128)(2,1)S(1)}, u32[]{:S(2)}, u32[]{:S(2)}) collective-permute-start(bf16[64,1152]{1,0:T(8,128)(2,1)} %slice.8), channel_id=1, source_target_pairs={{0,2},{2,4},{4,6},{6,0},{1,3},{3,5},{5,7},{7,1},{8,10},{10,12},{12... | collective-permute-start | bytes 442376 | tf_op jit(solution)/shard_map/ppermute | solution.py:191
  80.1 15.0 %collective-permute-start.5 = (bf16[64,1152]{1,0:T(8,128)(2,1)}, bf16[64,1152]{1,0:T(8,128)(2,1)S(1)}, u32[]{:S(2)}, u32[]{:S(2)}) collective-permute-start(bf16[64,1152]{1,0:T(8,128)(2,1)} %slice.9), channel_id=1, source_target_pairs={{0,6},{2,0},{4,2},{6,4},{1,7},{3,1},{5,3},{7,5},{8,14},{10,8},{12,... | collective-permute-start | bytes 442376 | tf_op jit(solution)/shard_map/ppermute | solution.py:191
  85.5 15.3 %collective-permute-start.1 = (bf16[128,1152]{1,0:T(8,128)(2,1)}, bf16[128,1152]{1,0:T(8,128)(2,1)S(1)}, u32[]{:S(2)}, u32[]{:S(2)}) collective-permute-start(bf16[128,1152]{1,0:T(8,128)(2,1)} %collective-permute-done.refs_2_), channel_id=1, source_target_pairs={{0,1},{1,0},{2,3},{3,2},{4,5},{5,4},{6,7},{7,6},{8,9},{9,8},{10,11... | collective-permute-start | bytes 884744 | tf_op jit(solution)/shard_map/ppermute | solution.py:194
  90.4 10.4 %collective-permute-start.3 = (bf16[128,1152]{1,0:T(8,128)(2,1)}, bf16[128,1152]{1,0:T(8,128)(2,1)S(1)}, u32[]{:S(2)}, u32[]{:S(2)}) collective-permute-start(bf16[128,1152]{1,0:T(8,128)(2,1)} %collective-permute-done.2.refs_3_), channel_id=1, source_target_pairs={{0,1},{1,0},{2,3},{3,2},{4,5},{5,4},{6,7},{7,6},{8,9},{9,8},{10,11... | collective-permute-start | bytes 884744 | tf_op jit(solution)/shard_map/ppermute | solution.py:194
  92.6 8.2 %copy-start.2 = (bf16[512,1152]{1,0:T(8,128)(2,1)}, bf16[512,1152]{1,0:T(8,128)(2,1)S(1)}, u32[]{:S(2)}) copy-start(bf16[512,1152]{1,0:T(8,128)(2,1)S(1)} %get-tuple-element.9.refs_5_.wqk_ref) | copy-start | bytes 3538948
  92.7 8.1 %collective-permute-start.6 = (bf16[64,1152]{1,0:T(8,128)(2,1)S(1)}, bf16[64,1152]{1,0:T(8,128)(2,1)S(1)}, u32[]{:S(2)}, u32[]{:S(2)}) collective-permute-start(bf16[64,1152]{1,0:T(8,128)(2,1)S(1)} %collective-permute-done.4.one_ref), channel_id=1, source_target_pairs={{0,1},{1,0},{2,3},{3,2},{4,5},{5,4},{6,7},{7,6},{8,9},{9,8},{10,11... | collective-permute-start | bytes 442376 | tf_op jit(solution)/shard_map/ppermute | solution.py:194
  95.1 5.7 %copy-start.9 = (bf16[64,1152]{1,0:T(8,128)(2,1)}, bf16[64,1152]{1,0:T(8,128)(2,1)S(1)}, u32[]{:S(2)}) copy-start(bf16[64,1152]{1,0:T(8,128)(2,1)S(1)} %collective-permute-done.5.two_ref) | copy-start | bytes 442372
  95.1 5.7 %collective-permute-start.7 = (bf16[64,1152]{1,0:T(8,128)(2,1)S(1)}, bf16[64,1152]{1,0:T(8,128)(2,1)S(1)}, u32[]{:S(2)}, u32[]{:S(2)}) collective-permute-start(bf16[64,1152]{1,0:T(8,128)(2,1)S(1)} %collective-permute-done.5.two_ref), channel_id=1, source_target_pairs={{0,1},{1,0},{2,3},{3,2},{4,5},{5,4},{6,7},{7,6},{8,9},{9,8},{10,11... | collective-permute-start | bytes 442376 | tf_op jit(solution)/shard_map/ppermute | solution.py:194
  97.1 1.0 copy-start.7
  100.8 0.7 copy-start.5
  101.6 1.3 copy-start.3
  102.8 1.0 copy-start.6
  103.8 0.9 copy-start.10
  104.7 49.9 %copy-start.1 = (bf16[1152,1152]{1,0:T(8,128)(2,1)S(1)}, bf16[1152,1152]{1,0:T(8,128)(2,1)}, u32[]{:S(2)}) copy-start(bf16[1152,1152]{1,0:T(8,128)(2,1)} %out_table_ref.1) | copy-start | bytes 7962628
  136.1 1.0 copy-start.8
  137.1 17.6 %copy-start = (bf16[6144,1152]{1,0:T(8,128)(2,1)S(1)}, bf16[6144,1152]{1,0:T(8,128)(2,1)}, u32[]{:S(2)}) copy-start(bf16[6144,1152]{1,0:T(8,128)(2,1)} %all-gather.3.cloned.1.call-done) | copy-start | bytes 42467332
Sparse Core Ops, SparseCore 0:
  40.5 89.7 all-gather.2

commit v11 on v10

--- a/solution.py
+++ b/solution.py
@@ -18,7 +18,7 @@
 TN = (((0,), (0,)), ((), ()))
 
 
-def params(mib=48):
+def params(mib=16):
     return pltpu.CompilerParams(vmem_limit_bytes=mib * 1024 * 1024)
 
 
@@ -53,61 +53,49 @@
     wvt_ref[...] = jnp.concatenate([pieces[2], narrow, pieces[5], narrow], axis=0).astype(jnp.bfloat16)
 
 
-def early_kernel(*refs):
-    pieces, (modulation_ref, wqk_ref, wvt_ref, qk_ref, vt_ref) = refs[:-5], refs[-5:]
-    for index in range(0, len(pieces), 2):
-        rows = jnp.concatenate([pieces[index][...], pieces[index + 1][...]], axis=0)
-        qk, vt = triples_of(rows.astype(jnp.float32), modulation_ref, wqk_ref, wvt_ref)
-        start = LANES * index
-        qk_ref[start : start + 2 * LANES] = qk
-        vt_ref[:, start : start + 2 * LANES] = vt
-
-
-def frame_kernel(
-    place_ref, below_ref, above_ref, one_ref, two_ref, three_ref, four_ref, qk_ref, vt_ref, modulation_ref,
-    wqk_ref, wvt_ref, out_ref, qk_late_ref, vt_late_ref,
-):
-    groups = ((below_ref, above_ref), (three_ref, four_ref, one_ref, two_ref))
+def frame_kernel(*refs):
+    place_ref, pieces = refs[0], refs[1:11]
+    modulation_in, wqk_in, wvt_in, out_ref = refs[11:15]
+    rows_ref, modulation_ref, wqk_ref, wvt_ref, qk_ref, vt_ref, sems = refs[15:]
+    copies, start = [], 0
+    for index, piece in enumerate(pieces):
+        count = piece.shape[0]
+        copies.append(pltpu.make_async_copy(piece, rows_ref.at[pl.ds(start, count)], sems.at[index]))
+        start += count
+    tables = [
+        pltpu.make_async_copy(modulation_in, modulation_ref, sems.at[10]),
+        pltpu.make_async_copy(wqk_in, wqk_ref, sems.at[11]),
+        pltpu.make_async_copy(wvt_in, wvt_ref, sems.at[12]),
+    ]
+    for copy in copies[:2] + tables + copies[2:]:
+        copy.start()
+    block = 2 * LANES
+    groups = (copies[0:2] + tables, copies[2:4], copies[4:6], copies[6:10])
     for index, group in enumerate(groups):
-        rows = jnp.concatenate([ref[...] for ref in group], axis=0).astype(jnp.float32)
+        for copy in group:
+            copy.wait()
+        start = block * index
+        rows = rows_ref[start : start + block].astype(jnp.float32)
         qk, vt = triples_of(rows, modulation_ref, wqk_ref, wvt_ref)
-        start = 2 * LANES * index
-        qk_late_ref[start : start + 2 * LANES] = qk
-        vt_late_ref[:, start : start + 2 * LANES] = vt
-    parts = ((qk_ref, vt_ref), (qk_late_ref, vt_late_ref))
-    blocks = (
-        ((qk_ref, 0), (qk_ref, 128)),
-        ((qk_ref, 256), (qk_late_ref, 0)),
-        ((qk_ref, 384), (qk_late_ref, 128)),
-        ((qk_late_ref, 384), (qk_late_ref, 256)),
-    )
-    for number, block in enumerate(blocks):
+        qk_ref[start : start + block] = qk
+        vt_ref[:, start : start + block] = vt
+    for index in range(len(groups)):
+        start = block * index
         outs = []
         for head in range(2):
             column = 2 * LANES * head
-            queries = jnp.concatenate(
-                [ref[start : start + LANES, column : column + LANES] for ref, start in block], axis=0
-            )
-            scores = [
-                lax.dot_general(
-                    qk[:, column + LANES : column + 2 * LANES], queries, NT,
-                    preferred_element_type=jnp.float32,
-                )
-                for qk, _ in parts
-            ]
-            largest = jnp.maximum(*[jnp.max(part, axis=0, keepdims=True) for part in scores])
-            mixed = sum(
-                jnp.dot(
-                    vt[HP * head : HP * head + HP],
-                    jnp.exp2((part - largest) * EXP2_SCALE).astype(jnp.bfloat16),
-                    preferred_element_type=jnp.float32,
-                )
-                for part, (_, vt) in zip(scores, parts)
+            queries = qk_ref[start : start + block, column : column + LANES]
+            keys = qk_ref[:, column + LANES : column + 2 * LANES]
+            scores = lax.dot_general(keys, queries, NT, preferred_element_type=jnp.float32)
+            largest = jnp.max(scores, axis=0, keepdims=True)
+            raised = jnp.exp2((scores - largest) * EXP2_SCALE).astype(jnp.bfloat16)
+            mixed = jnp.dot(
+                vt_ref[HP * head : HP * head + HP], raised, preferred_element_type=jnp.float32
             )
             outs.append(mixed[:HD] / mixed[HD : HD + 1])
         both = jnp.concatenate(outs, axis=0).astype(jnp.bfloat16)
         for part in range(2):
-            out_ref[place_ref[2 * number + part]] = both[:, part * LANES : (part + 1) * LANES]
+            out_ref[place_ref[2 * index + part]] = both[:, part * LANES : (part + 1) * LANES]
 
 
 def pack_kernel(parts_ref, out_ref):
@@ -117,18 +105,23 @@
     out_ref[...] = jnp.concatenate(rows, axis=0).astype(jnp.bfloat16)
 
 
-def middle_kernel(mixed_ref, tables_ref, tokens_ref, modulation_ref, out_ref, table_ref, sem):
-    copy = pltpu.make_async_copy(tables_ref.at[pl.ds(0, 9), :, pl.ds(LANES, 64), :], table_ref, sem)
+def middle_kernel(
+    mixed_ref, tables_ref, tokens_ref, modulation_ref, out_ref, table_ref, held_ref, table_sem, held_sem
+):
+    copy = pltpu.make_async_copy(tables_ref.at[pl.ds(0, 9), :, pl.ds(LANES, 64), :], table_ref, table_sem)
+    held_copy = pltpu.make_async_copy(tokens_ref, held_ref, held_sem)
     copy.start()
+    held_copy.start()
     slots = [mixed_ref[2 * zh + core] for core in range(2) for zh in range(4)]
     mixed = jnp.concatenate(
         [slot[16 * number : 16 * number + 16] for number in range(9) for slot in slots], axis=0
     )
     copy.wait()
+    held_copy.wait()
     table = table_ref[...].reshape(-1, table_ref.shape[-1])
     branch = lax.dot_general(mixed, table, TN, preferred_element_type=jnp.float32)
     out_ref[...] = (
-        tokens_ref[...].astype(jnp.float32) + modulation_ref[0, 2:3] * branch
+        held_ref[...].astype(jnp.float32) + modulation_ref[0, 2:3] * branch
     ).astype(jnp.bfloat16)
 
 
@@ -196,8 +189,8 @@
     before, after = along(tokens, "zh", 1), along(tokens, "zh", 3)
     beside = swapped(tokens)
     far_top, far_bottom = along(before[:half], "zh", 1), along(after[half:], "zh", 3)
-    early = [tokens, beside, before, after]
-    late = [swapped(before), swapped(after), far_top, far_bottom, swapped(far_top), swapped(far_bottom)]
+    pieces = [tokens, beside, before, swapped(before), after, swapped(after)]
+    pieces += [far_top, far_bottom, swapped(far_top), swapped(far_bottom)]
     spots = [zh, (zh + 3) % 4, (zh + 1) % 4, (zh + 2) % 4]
     place = jnp.stack(
         [spot * 2 + side for spot in spots for side in (core, 1 - core)]
@@ -233,41 +226,37 @@
         name="spread",
     )(frame_qkv.T)
 
-    soon = rows * len(early)
-    qk, vt = pl.pallas_call(
-        early_kernel,
-        out_shape=(
-            jax.ShapeDtypeStruct((soon, 4 * LANES), jnp.bfloat16),
-            jax.ShapeDtypeStruct((2 * HP, soon), jnp.bfloat16),
-        ),
-        in_specs=[whole()] * (len(early) + 3),
-        out_specs=(whole(), whole()),
-        compiler_params=params(),
-        cost_estimate=pl.CostEstimate(flops=2 * 10**9, bytes_accessed=5 * 10**6, transcendentals=0),
-        name="early_triples",
-    )(*early, modulation, wqk, wvt)
-
-    rest = 4 * rows
+    count = 8 * rows
     mixed = pl.pallas_call(
         frame_kernel,
-        out_shape=jax.ShapeDtypeStruct(((soon + rest) // LANES, 2 * HD, LANES), jnp.bfloat16),
-        in_specs=[pl.BlockSpec(memory_space=pltpu.SMEM)] + [whole()] * 11,
+        out_shape=jax.ShapeDtypeStruct((count // LANES, 2 * HD, LANES), jnp.bfloat16),
+        in_specs=[pl.BlockSpec(memory_space=pltpu.SMEM)] + [pl.BlockSpec(memory_space=pl.ANY)] * 13,
         out_specs=whole(),
         scratch_shapes=[
-            pltpu.VMEM((rest, 4 * LANES), jnp.bfloat16),
-            pltpu.VMEM((2 * HP, rest), jnp.bfloat16),
+            pltpu.VMEM((count, width), jnp.bfloat16),
+            pltpu.VMEM(modulation.shape, modulation.dtype),
+            pltpu.VMEM(wqk.shape, wqk.dtype),
+            pltpu.VMEM(wvt.shape, wvt.dtype),
+            pltpu.VMEM((count, 4 * LANES), jnp.bfloat16),
+            pltpu.VMEM((2 * HP, count), jnp.bfloat16),
+            pltpu.SemaphoreType.DMA((13,)),
         ],
-        compiler_params=params(),
+        compiler_params=params(60),
         name="frame_attention",
-    )(place, *late, qk, vt, modulation, wqk, wvt)
+    )(place, *pieces, modulation, wqk, wvt)
 
     mixed = lax.all_to_all(mixed, ("zh", "c"), 0, 0, tiled=True)
     middle = pl.pallas_call(
         middle_kernel,
         out_shape=jax.ShapeDtypeStruct((rows, width), jnp.bfloat16),
-        in_specs=[whole(), pl.BlockSpec(memory_space=pl.ANY), whole(), whole()],
-        out_specs=whole(),
-        scratch_shapes=[pltpu.VMEM((9, 2, 64, width), jnp.bfloat16), pltpu.SemaphoreType.DMA],
+        in_specs=[whole(), pl.BlockSpec(memory_space=pl.ANY), pl.BlockSpec(memory_space=pl.ANY), whole()],
+        out_specs=whole(),
+        scratch_shapes=[
+            pltpu.VMEM((9, 2, 64, width), jnp.bfloat16),
+            pltpu.VMEM((rows, width), jnp.bfloat16),
+            pltpu.SemaphoreType.DMA,
+            pltpu.SemaphoreType.DMA,
+        ],
         compiler_params=params(44),
         name="middle",
     )(mixed, tables.reshape(16, 2, 192, width), tokens, modulation)

time: 183 us -> 185 us (1.011)
  local copies, waits for them, and re-layouts: 10.7 us -> 5.64 us
  Pallas kernels: 18.9 us -> 22.7 us
  waiting for transfers between devices: 9.5 us -> 12.3 us
    pallas_call x2 -> x1, Pallas kernels: 9.49 us -> 13.3 us  [shards(): pl.pallas_call(frame_kernel, out_shape=jax.ShapeDtypeStruct((count // LAN...]
    ppermute x4, waiting for transfers between devices: 9.47 us -> 12.3 us  [along(): return lax.ppermute(array, axis, rotation(4, by))]
    unnamed x26 -> x36, local copies, waits for them, and re-layouts: 6.53 us -> 4.07 us
  transfers between devices with their start and end apart: 10 -> 10, of which waited for: 1 -> 1; matrix products, arithmetic and copies ran while one was open for 2% -> 1% of each run, Pallas kernels for 5% -> 7%
where the time goes in v11:
time: 185 us; the launch traced here: 183 us
  blocking collectives  84.9 us (46%)
  starting transfers between devices  44.2 us (24%)
  Pallas kernels  22.7 us (12%)
  between operations  13.7 us (7%)
  waiting for transfers between devices  12.3 us (7%)
  local copies, waits for them, and re-layouts  5.64 us (3%)
    all_gather x1, blocking collectives, shards(): parts = lax.all_gather(part, ('zh', 'zl'), axis=0, tiled=True)  32.1 us
    ppermute x5, starting transfers between devices, swapped(): return lax.ppermute(array, 'c', SWAP)  25.8 us
    all_to_all x1, blocking collectives, shards(): mixed = lax.all_to_all(mixed, ('zh', 'c'), 0, 0, tiled=True)  24 us
    ppermute x4, starting transfers between devices, along(): return lax.ppermute(array, axis, rotation(4, by))  18.4 us
    all_to_all x1, blocking collectives, shards(): middle = lax.all_to_all(middle, ('x', 'zl'), 0, 0, tiled=True)  15 us
    all_to_all x1, blocking collectives, shards(): out = lax.all_to_all(out, ('x', 'zl'), 0, 0, tiled=True)  13.8 us
    pallas_call x1, Pallas kernels, shards(): pl.pallas_call(frame_kernel, out_shape=jax.ShapeDtypeStruct((count // LAN...  13.3 us
    ppermute x4, waiting for transfers between devices, along(): return lax.ppermute(array, axis, rotation(4, by))  12.3 us
  transfers between devices with their start and end apart: 10, of which 1 were waited for; matrix products, arithmetic and copies ran while one was open for 1% of the time, Pallas kernels for 7%

profile of v11, /device:TPU:1, one launch (start us, length us, event | category | flops | bytes accessed | tf_op | source)
XLA Modules:
  0.0 183.5 jit_solution(11185656857489696153)
XLA Ops:
  6.5 0.0 all-gather.3.cloned.1.call-start
  6.5 0.9 constant_dynamic-slice_fusion
  7.4 32.1 %all_gather.9.parts_ref = bf16[256,1152]{1,0:T(8,128)(2,1)S(1)} all-gather(bf16[16,1152]{1,0:T(8,128)(2,1)S(1)} %pad_maximum_fusion), channel_id=1, replica_groups=mesh['y'=4,'x'=4,'zl'=4,'zh'=4,'c'=2] {'zh','zl'}, dimensions={0}, use_global_device_ids=true | all-gather | bytes 626688 | tf_op jit(solution)/shard_map/all_gather | solution.py:205
  39.6 0.8 pack.1
  40.4 0.0 all-gather.3.cloned.1.call-update
  40.4 3.7 %collective-permute-start.1 = (bf16[128,1152]{1,0:T(8,128)(2,1)}, bf16[128,1152]{1,0:T(8,128)(2,1)S(1)}, u32[]{:S(2)}, u32[]{:S(2)}) collective-permute-start(bf16[128,1152]{1,0:T(8,128)(2,1)} %bitcast.18), channel_id=1, source_target_pairs={{0,2},{2,4},{4,6},{6,0},{1,3},{3,5},{5,7},{7,1},{8,10},{10,12},{12... | collective-permute-start | bytes 884744 | tf_op jit(solution)/shard_map/ppermute | solution.py:184
  44.0 5.5 %collective-permute-start.3 = (bf16[128,1152]{1,0:T(8,128)(2,1)}, bf16[128,1152]{1,0:T(8,128)(2,1)S(1)}, u32[]{:S(2)}, u32[]{:S(2)}) collective-permute-start(bf16[128,1152]{1,0:T(8,128)(2,1)} %bitcast.19), channel_id=1, source_target_pairs={{0,6},{2,0},{4,2},{6,4},{1,7},{3,1},{5,3},{7,5},{8,14},{10,8},{12,... | collective-permute-start | bytes 884744 | tf_op jit(solution)/shard_map/ppermute | solution.py:184
  49.6 14.1 %collective-permute-start = (bf16[128,1152]{1,0:T(8,128)(2,1)}, bf16[128,1152]{1,0:T(8,128)(2,1)S(1)}, u32[]{:S(2)}, u32[]{:S(2)}) collective-permute-start(bf16[128,1152]{1,0:T(8,128)(2,1)} %bitcast.20), channel_id=1, source_target_pairs={{0,1},{1,0},{2,3},{3,2},{4,5},{5,4},{6,7},{7,6},{8,9},{9,8},{10,11... | collective-permute-start | bytes 884744 | tf_op jit(solution)/shard_map/ppermute | solution.py:187
  63.7 12.3 %collective-permute-done.1.refs_3_ = bf16[128,1152]{1,0:T(8,128)(2,1)S(1)} collective-permute-done((bf16[128,1152]{1,0:T(8,128)(2,1)}, bf16[128,1152]{1,0:T(8,128)(2,1)S(1)}, u32[]{:S(2)}, u32[]{:S(2)}) %collective-permute-start.1) | collective-permute-done | bytes 294944 | tf_op jit(solution)/shard_map/ppermute | solution.py:184
  76.0 2.2 %collective-permute-start.5 = (bf16[64,1152]{1,0:T(8,128)(2,1)S(1)}, bf16[64,1152]{1,0:T(8,128)(2,1)S(1)}, u32[]{:S(2)}, u32[]{:S(2)}) collective-permute-start(bf16[64,1152]{1,0:T(8,128)(2,1)S(1)} %slice.8), channel_id=1, source_target_pairs={{0,2},{2,4},{4,6},{6,0},{1,3},{3,5},{5,7},{7,1},{8,10},{10,12},{12... | collective-permute-start | bytes 442376 | tf_op jit(solution)/shard_map/ppermute | solution.py:184
  78.2 0.0 collective-permute-done.3.refs_5_
  78.2 0.0 copy-start.8
  78.3 7.0 %collective-permute-start.6 = (bf16[64,1152]{1,0:T(8,128)(2,1)S(1)}, bf16[64,1152]{1,0:T(8,128)(2,1)S(1)}, u32[]{:S(2)}, u32[]{:S(2)}) collective-permute-start(bf16[64,1152]{1,0:T(8,128)(2,1)S(1)} %slice.9), channel_id=1, source_target_pairs={{0,6},{2,0},{4,2},{6,4},{1,7},{3,1},{5,3},{7,5},{8,14},{10,8},{12,... | collective-permute-start | bytes 442376 | tf_op jit(solution)/shard_map/ppermute | solution.py:184
  85.2 5.5 %collective-permute-start.2 = (bf16[128,1152]{1,0:T(8,128)(2,1)S(1)}, bf16[128,1152]{1,0:T(8,128)(2,1)S(1)}, u32[]{:S(2)}, u32[]{:S(2)}) collective-permute-start(bf16[128,1152]{1,0:T(8,128)(2,1)S(1)} %collective-permute-done.1.refs_3_), channel_id=1, source_target_pairs={{0,1},{1,0},{2,3},{3,2},{4,5},{5,4},{6,7},{7,6},{8,9},{9,8},{10,11... | collective-permute-start | bytes 884744 | tf_op jit(solution)/shard_map/ppermute | solution.py:187
  90.8 1.9 %collective-permute-start.4 = (bf16[128,1152]{1,0:T(8,128)(2,1)S(1)}, bf16[128,1152]{1,0:T(8,128)(2,1)S(1)}, u32[]{:S(2)}, u32[]{:S(2)}) collective-permute-start(bf16[128,1152]{1,0:T(8,128)(2,1)S(1)} %collective-permute-done.3.refs_5_), channel_id=1, source_target_pairs={{0,1},{1,0},{2,3},{3,2},{4,5},{5,4},{6,7},{7,6},{8,9},{9,8},{10,11... | collective-permute-start | bytes 884744 | tf_op jit(solution)/shard_map/ppermute | solution.py:187
  92.7 0.0 collective-permute-done.5.refs_7_
  92.7 0.0 copy-start.12
  92.7 2.4 %collective-permute-start.7 = (bf16[64,1152]{1,0:T(8,128)(2,1)S(1)}, bf16[64,1152]{1,0:T(8,128)(2,1)S(1)}, u32[]{:S(2)}, u32[]{:S(2)}) collective-permute-start(bf16[64,1152]{1,0:T(8,128)(2,1)S(1)} %collective-permute-done.5.refs_7_), channel_id=1, source_target_pairs={{0,1},{1,0},{2,3},{3,2},{4,5},{5,4},{6,7},{7,6},{8,9},{9,8},{10,11... | collective-permute-start | bytes 442376 | tf_op jit(solution)/shard_map/ppermute | solution.py:187
  95.1 0.0 collective-permute-done.6.refs_8_
  95.1 0.0 copy-start.13
  95.1 1.9 %collective-permute-start.8 = (bf16[64,1152]{1,0:T(8,128)(2,1)S(1)}, bf16[64,1152]{1,0:T(8,128)(2,1)S(1)}, u32[]{:S(2)}, u32[]{:S(2)}) collective-permute-start(bf16[64,1152]{1,0:T(8,128)(2,1)S(1)} %collective-permute-done.6.refs_8_), channel_id=1, source_target_pairs={{0,1},{1,0},{2,3},{3,2},{4,5},{5,4},{6,7},{7,6},{8,9},{9,8},{10,11... | collective-permute-start | bytes 442376 | tf_op jit(solution)/shard_map/ppermute | solution.py:187
  97.1 0.0 copy-done.16
  97.1 0.6 copy.7.refs_11_.modulation_ref
  97.8 0.0 copy-done.4
  97.8 0.1 spread.1
  97.9 0.0 copy-start.2
  97.9 1.0 copy-done.2
  98.9 0.7 copy-done.6
  99.6 0.7 stack.35.refs_0_
  100.3 0.0 collective-permute-done.refs_2_
  100.3 0.0 collective-permute-done.7.refs_9_
  100.3 0.0 collective-permute-done.8.refs_10_
  100.4 0.0 collective-permute-done.2.refs_4_
  100.4 0.0 copy-start.10
  100.4 0.0 collective-permute-done.4.refs_6_
  100.4 0.6 copy-done.9
  101.0 0.0 copy-done.14
  101.1 0.0 copy-done.15
  101.1 0.1 copy-done.10
  101.2 0.1 copy-done.11
  101.3 0.0 copy-done.7
  101.3 13.3 %frame_attention.1 = bf16[8,144,128]{2,1,0:T(8,128)(2,1)} custom-call(s32[8]{0:T(128)} %stack.35.refs_0_, bf16[128,1152]{1,0:T(8,128)(2,1)} %bitcast.21, bf16[128,1152]{1,0:T(8,128)(2,1)} %copy-done.9, bf16[128,1152]{1,0:T(8,128)(2,1)} %copy-done.7, bf16[128,1152]{1,0:T(8,128)(2,1)} %copy-done.10, bf16[128,1152]{1,0:T(8,128)(2,1)} %copy-done.8, ...), custom_call_target="tpu_custom_call" | custom-call | tf_op jit(solution)/shard_map/frame_attention/pallas_call | solution.py:230
  114.6 24.0 %all_to_all.25.mixed_ref = bf16[8,144,128]{2,1,0:T(8,128)(2,1)S(1)} all-to-all(bf16[8,144,128]{2,1,0:T(8,128)(2,1)} %frame_attention.1), channel_id=1, replica_groups=mesh['y'=4,'x'=4,'zl'=4,'zh'=4,'c'=2] {'zh','c'}, dimensions={0} | all-to-all | bytes 589824 | tf_op jit(solution)/shard_map/all_to_all | solution.py:248
  138.6 2.5 %middle.1 = bf16[128,1152]{1,0:T(8,128)(2,1)S(1)} custom-call(bf16[8,144,128]{2,1,0:T(8,128)(2,1)S(1)} %all_to_all.25.mixed_ref, bf16[16,2,192,1152]{3,2,1,0:T(8,128)(2,1)} %bitcast.16, bf16[128,1152]{1,0:T(8,128)(2,1)S(1)} %bitcast.22, f32[2,3,1152]{2,1,0:T(4,128)S(1)} %copy-done.5), custom_call_target="tpu_custom_call" | custom-call | tf_op jit(solution)/shard_map/middle/pallas_call | solution.py:249
  141.1 15.0 %all_to_all.26 = bf16[16,8,1152]{2,1,0:T(8,128)(2,1)S(1)} all-to-all(bf16[16,8,1152]{2,1,0:T(8,128)(2,1)S(1)} %bitcast.25), channel_id=1, replica_groups=mesh['y'=4,'x'=4,'zl'=4,'zh'=4,'c'=2] {'x','zl'}, dimensions={0} | all-to-all | bytes 589824 | tf_op jit(solution)/shard_map/all_to_all | solution.py:264
  156.2 6.0 %time_block.1 = bf16[128,1152]{1,0:T(8,128)(2,1)S(1)} custom-call(bf16[128,1152]{1,0:T(8,128)(2,1)S(1)} %bitcast.23, bf16[4,8,192,1152]{3,2,1,0:T(8,128)(2,1)S(1)} %bitcast.17, bf16[1152,1152]{1,0:T(8,128)(2,1)S(1)} %copy-done.1, f32[2,3,1152]{2,1,0:T(4,128)S(1)} %copy-done.5), custom_call_target="tpu_custom_call" | custom-call | tf_op jit(solution)/shard_map/time_block/pallas_call | solution.py:266
  162.1 13.8 %all_to_all.27 = bf16[16,8,1152]{2,1,0:T(8,128)(2,1)S(1)} all-to-all(bf16[16,8,1152]{2,1,0:T(8,128)(2,1)S(1)} %bitcast.24), channel_id=1, replica_groups=mesh['y'=4,'x'=4,'zl'=4,'zh'=4,'c'=2] {'x','zl'}, dimensions={0} | all-to-all | bytes 589824 | tf_op jit(solution)/shard_map/all_to_all | solution.py:275
  175.9 0.7 copy.11
  (23 shorter events, 0.1 us)
Async XLA Ops:
  6.5 90.6 %copy-start.16 = (f32[2,3,1152]{2,0,1:T(2,128)S(1)}, f32[2,3,1152]{2,0,1:T(2,128)}, u32[]{:S(2)}) copy-start(f32[2,3,1152]{2,0,1:T(2,128)} %param.11) | copy-start | bytes 82948
  6.5 91.2 %copy-start.4 = (bf16[1152,432]{0,1:T(8,128)(2,1)S(1)}, bf16[1152,432]{0,1:T(8,128)(2,1)}, u32[]{:S(2)}) copy-start(bf16[1152,432]{0,1:T(8,128)(2,1)} %param.7) | copy-start | bytes 2985988
  6.5 132.0 %all-gather.3.cloned.1.call-start = ((), (), s32[]{:S(2)}) async-start(), calls=%async_computation.3 | async-start | bytes 14598144 | tf_op jit(solution)/shard_map/all_gather | solution.py:214
  40.4 35.6 %collective-permute-start.1 = (bf16[128,1152]{1,0:T(8,128)(2,1)}, bf16[128,1152]{1,0:T(8,128)(2,1)S(1)}, u32[]{:S(2)}, u32[]{:S(2)}) collective-permute-start(bf16[128,1152]{1,0:T(8,128)(2,1)} %bitcast.18), channel_id=1, source_target_pairs={{0,2},{2,4},{4,6},{6,0},{1,3},{3,5},{5,7},{7,1},{8,10},{10,12},{12... | collective-permute-start | bytes 884744 | tf_op jit(solution)/shard_map/ppermute | solution.py:184
  44.0 34.2 %collective-permute-start.3 = (bf16[128,1152]{1,0:T(8,128)(2,1)}, bf16[128,1152]{1,0:T(8,128)(2,1)S(1)}, u32[]{:S(2)}, u32[]{:S(2)}) collective-permute-start(bf16[128,1152]{1,0:T(8,128)(2,1)} %bitcast.19), channel_id=1, source_target_pairs={{0,6},{2,0},{4,2},{6,4},{1,7},{3,1},{5,3},{7,5},{8,14},{10,8},{12,... | collective-permute-start | bytes 884744 | tf_op jit(solution)/shard_map/ppermute | solution.py:184
  49.6 50.7 %collective-permute-start = (bf16[128,1152]{1,0:T(8,128)(2,1)}, bf16[128,1152]{1,0:T(8,128)(2,1)S(1)}, u32[]{:S(2)}, u32[]{:S(2)}) collective-permute-start(bf16[128,1152]{1,0:T(8,128)(2,1)} %bitcast.20), channel_id=1, source_target_pairs={{0,1},{1,0},{2,3},{3,2},{4,5},{5,4},{6,7},{7,6},{8,9},{9,8},{10,11... | collective-permute-start | bytes 884744 | tf_op jit(solution)/shard_map/ppermute | solution.py:187
  76.0 25.4 %copy-start.7 = (bf16[128,1152]{1,0:T(8,128)(2,1)}, bf16[128,1152]{1,0:T(8,128)(2,1)S(1)}, u32[]{:S(2)}) copy-start(bf16[128,1152]{1,0:T(8,128)(2,1)S(1)} %collective-permute-done.1.refs_3_) | copy-start | bytes 884740
  76.0 16.7 %collective-permute-start.5 = (bf16[64,1152]{1,0:T(8,128)(2,1)S(1)}, bf16[64,1152]{1,0:T(8,128)(2,1)S(1)}, u32[]{:S(2)}, u32[]{:S(2)}) collective-permute-start(bf16[64,1152]{1,0:T(8,128)(2,1)S(1)} %slice.8), channel_id=1, source_target_pairs={{0,2},{2,4},{4,6},{6,0},{1,3},{3,5},{5,7},{7,1},{8,10},{10,12},{12... | collective-permute-start | bytes 442376 | tf_op jit(solution)/shard_map/ppermute | solution.py:184
  78.2 22.2 %copy-start.8 = (bf16[128,1152]{1,0:T(8,128)(2,1)}, bf16[128,1152]{1,0:T(8,128)(2,1)S(1)}, u32[]{:S(2)}) copy-start(bf16[128,1152]{1,0:T(8,128)(2,1)S(1)} %collective-permute-done.3.refs_5_) | copy-start | bytes 884740
  78.3 16.8 %collective-permute-start.6 = (bf16[64,1152]{1,0:T(8,128)(2,1)S(1)}, bf16[64,1152]{1,0:T(8,128)(2,1)S(1)}, u32[]{:S(2)}, u32[]{:S(2)}) collective-permute-start(bf16[64,1152]{1,0:T(8,128)(2,1)S(1)} %slice.9), channel_id=1, source_target_pairs={{0,6},{2,0},{4,2},{6,4},{1,7},{3,1},{5,3},{7,5},{8,14},{10,8},{12,... | collective-permute-start | bytes 442376 | tf_op jit(solution)/shard_map/ppermute | solution.py:184
  85.2 15.1 %collective-permute-start.2 = (bf16[128,1152]{1,0:T(8,128)(2,1)S(1)}, bf16[128,1152]{1,0:T(8,128)(2,1)S(1)}, u32[]{:S(2)}, u32[]{:S(2)}) collective-permute-start(bf16[128,1152]{1,0:T(8,128)(2,1)S(1)} %collective-permute-done.1.refs_3_), channel_id=1, source_target_pairs={{0,1},{1,0},{2,3},{3,2},{4,5},{5,4},{6,7},{7,6},{8,9},{9,8},{10,11... | collective-permute-start | bytes 884744 | tf_op jit(solution)/shard_map/ppermute | solution.py:187
  90.8 9.6 %collective-permute-start.4 = (bf16[128,1152]{1,0:T(8,128)(2,1)S(1)}, bf16[128,1152]{1,0:T(8,128)(2,1)S(1)}, u32[]{:S(2)}, u32[]{:S(2)}) collective-permute-start(bf16[128,1152]{1,0:T(8,128)(2,1)S(1)} %collective-permute-done.3.refs_5_), channel_id=1, source_target_pairs={{0,1},{1,0},{2,3},{3,2},{4,5},{5,4},{6,7},{7,6},{8,9},{9,8},{10,11... | collective-permute-start | bytes 884744 | tf_op jit(solution)/shard_map/ppermute | solution.py:187
  92.7 8.6 %copy-start.12 = (bf16[64,1152]{1,0:T(8,128)(2,1)}, bf16[64,1152]{1,0:T(8,128)(2,1)S(1)}, u32[]{:S(2)}) copy-start(bf16[64,1152]{1,0:T(8,128)(2,1)S(1)} %collective-permute-done.5.refs_7_) | copy-start | bytes 442372
  92.7 7.6 %collective-permute-start.7 = (bf16[64,1152]{1,0:T(8,128)(2,1)S(1)}, bf16[64,1152]{1,0:T(8,128)(2,1)S(1)}, u32[]{:S(2)}, u32[]{:S(2)}) collective-permute-start(bf16[64,1152]{1,0:T(8,128)(2,1)S(1)} %collective-permute-done.5.refs_7_), channel_id=1, source_target_pairs={{0,1},{1,0},{2,3},{3,2},{4,5},{5,4},{6,7},{7,6},{8,9},{9,8},{10,11... | collective-permute-start | bytes 442376 | tf_op jit(solution)/shard_map/ppermute | solution.py:187
  95.1 5.3 %copy-start.13 = (bf16[64,1152]{1,0:T(8,128)(2,1)}, bf16[64,1152]{1,0:T(8,128)(2,1)S(1)}, u32[]{:S(2)}) copy-start(bf16[64,1152]{1,0:T(8,128)(2,1)S(1)} %collective-permute-done.6.refs_8_) | copy-start | bytes 442372
  95.1 5.2 %collective-permute-start.8 = (bf16[64,1152]{1,0:T(8,128)(2,1)S(1)}, bf16[64,1152]{1,0:T(8,128)(2,1)S(1)}, u32[]{:S(2)}, u32[]{:S(2)}) collective-permute-start(bf16[64,1152]{1,0:T(8,128)(2,1)S(1)} %collective-permute-done.6.refs_8_), channel_id=1, source_target_pairs={{0,1},{1,0},{2,3},{3,2},{4,5},{5,4},{6,7},{7,6},{8,9},{9,8},{10,11... | collective-permute-start | bytes 442376 | tf_op jit(solution)/shard_map/ppermute | solution.py:187
  97.9 1.0 copy-start.2
  98.9 0.7 copy-start.6
  99.6 38.9 %copy-start.3 = (bf16[1,128,1152]{2,1,0:T(8,128)(2,1)S(1)}, bf16[1,128,1152]{2,1,0:T(8,128)(2,1)}, u32[]{:S(2)}) copy-start(bf16[1,128,1152]{2,1,0:T(8,128)(2,1)} %param.6) | copy-start | bytes 884740
  99.6 38.9 %copy-start.5 = (f32[2,3,1152]{2,1,0:T(4,128)S(1)}, f32[2,3,1152]{2,1,0:T(4,128)}, u32[]{:S(2)}) copy-start(f32[2,3,1152]{2,1,0:T(4,128)} %copy.7.refs_11_.modulation_ref) | copy-start | bytes 82948
  100.3 0.7 copy-start.9
  100.3 0.7 copy-start.14
  100.3 0.8 copy-start.15
  100.4 0.9 copy-start.10
  100.4 0.9 copy-start.11
  101.3 54.8 %copy-start.1 = (bf16[1152,1152]{1,0:T(8,128)(2,1)S(1)}, bf16[1152,1152]{1,0:T(8,128)(2,1)}, u32[]{:S(2)}) copy-start(bf16[1152,1152]{1,0:T(8,128)(2,1)} %out_table_ref.1) | copy-start | bytes 7962628
  138.6 17.6 %copy-start = (bf16[6144,1152]{1,0:T(8,128)(2,1)S(1)}, bf16[6144,1152]{1,0:T(8,128)(2,1)}, u32[]{:S(2)}) copy-start(bf16[6144,1152]{1,0:T(8,128)(2,1)} %all-gather.3.cloned.1.call-done) | copy-start | bytes 42467332
Sparse Core Ops, SparseCore 0:
  40.5 89.7 all-gather.2

commit v12 on v10

--- a/solution.py
+++ b/solution.py
@@ -157,18 +157,29 @@
 
 
 def time_kernel(
-    positions, middle_ref, tables_ref, out_table_ref, modulation_ref, out_ref, mixed_ref,
+    positions, middle_ref, tables_ref, out_table_ref, modulation_ref, out_ref, held_ref, mixed_ref, out_held_ref, sems
 ):
     rows, width = middle_ref.shape
+    copies = [
+        pltpu.make_async_copy(
+            tables_ref.at[group, pl.ds(0, 7), pl.ds(0, LANES), :], held_ref.at[group], sems.at[group]
+        )
+        for group in range(4)
+    ]
+    copies.append(pltpu.make_async_copy(out_table_ref, out_held_ref, sems.at[4]))
+    for copy in copies:
+        copy.start()
     second = modulated(
         middle_ref[...].astype(jnp.float32), modulation_ref[1, 0:1], modulation_ref[1, 1:2]
     )
     for group in range(4):
-        table = tables_ref[group, 0:7, 0:LANES].reshape(7 * LANES, width)
+        copies[group].wait()
+        table = held_ref[group].reshape(7 * LANES, width)
         triples = lax.dot_general(table, second, NT, preferred_element_type=jnp.float32)
         time_attention(positions, triples, mixed_ref, 4 * group)
+    copies[4].wait()
     mixed = mixed_ref[...].reshape(-1, rows).astype(jnp.bfloat16)
-    branch = lax.dot_general(mixed, out_table_ref[...], TN, preferred_element_type=jnp.float32)
+    branch = lax.dot_general(mixed, out_held_ref[...], TN, preferred_element_type=jnp.float32)
     out_ref[...] = (
         middle_ref[...].astype(jnp.float32) + modulation_ref[1, 2:3] * branch
     ).astype(jnp.bfloat16)
@@ -268,7 +279,7 @@
         in_specs=[whole(), pl.BlockSpec(memory_space=pl.ANY), whole(), whole()],
         out_specs=whole(),
         scratch_shapes=[pltpu.VMEM((9, 2, 64, width), jnp.bfloat16), pltpu.SemaphoreType.DMA],
-        compiler_params=params(44),
+        compiler_params=params(),
         name="middle",
     )(mixed, tables.reshape(16, 2, 192, width), tokens, modulation)
 
@@ -277,10 +288,15 @@
     out = pl.pallas_call(
         functools.partial(time_kernel, rows // 16),
         out_shape=jax.ShapeDtypeStruct((rows, width), jnp.bfloat16),
-        in_specs=[whole()] * 4,
+        in_specs=[whole(), pl.BlockSpec(memory_space=pl.ANY), pl.BlockSpec(memory_space=pl.ANY), whole()],
         out_specs=whole(),
-        scratch_shapes=[pltpu.VMEM((16, HD, rows), jnp.float32)],
-        compiler_params=params(28),
+        scratch_shapes=[
+            pltpu.VMEM((4, 7, LANES, width), jnp.bfloat16),
+            pltpu.VMEM((16, HD, rows), jnp.float32),
+            pltpu.VMEM((width, width), jnp.bfloat16),
+            pltpu.SemaphoreType.DMA((5,)),
+        ],
+        compiler_params=params(),
         name="time_block",
     )(middle, tables, time_out, modulation)
     out = lax.all_to_all(out, ("x", "zl"), 0, 0, tiled=True)

time: 183 us -> 181 us (0.989)
  local copies, waits for them, and re-layouts: 10.7 us -> 4.89 us
  Pallas kernels: 18.9 us -> 21.2 us
    unnamed x26 -> x10, local copies, waits for them, and re-layouts: 6.53 us -> 0.74 us
    pallas_call x1, Pallas kernels: 5.96 us -> 7.91 us  [shards(): pl.pallas_call(functools.partial(time_kernel, rows // 16), out_shape=jax....]
  transfers between devices with their start and end apart: 10 -> 10, of which waited for: 1 -> 1; matrix products, arithmetic and copies ran while one was open for 2% -> 2% of each run, Pallas kernels for 5% -> 6%
where the time goes in v12:
time: 181 us; the launch traced here: 180 us
  blocking collectives  87.2 us (48%)
  starting transfers between devices  43.6 us (24%)
  Pallas kernels  21.2 us (12%)
  between operations  13.6 us (8%)
  waiting for transfers between devices  9.5 us (5%)
  local copies, waits for them, and re-layouts  4.89 us (3%)
    all_gather x1, blocking collectives, shards(): parts = lax.all_gather(part, ('zh', 'zl'), axis=0, tiled=True)  32.1 us
    ppermute x5, starting transfers between devices, swapped(): return lax.ppermute(array, 'c', SWAP)  25.3 us
    all_to_all x1, blocking collectives, shards(): mixed = lax.all_to_all(mixed, ('zh', 'c'), 0, 0, tiled=True)  24.9 us
    ppermute x4, starting transfers between devices, along(): return lax.ppermute(array, axis, rotation(4, by))  18.4 us
    all_to_all x1, blocking collectives, shards(): middle = lax.all_to_all(middle, ('x', 'zl'), 0, 0, tiled=True)  15.7 us
    all_to_all x1, blocking collectives, shards(): out = lax.all_to_all(out, ('x', 'zl'), 0, 0, tiled=True)  14.4 us
    ppermute x4, waiting for transfers between devices, along(): return lax.ppermute(array, axis, rotation(4, by))  9.47 us
    pallas_call x1, Pallas kernels, shards(): pl.pallas_call(functools.partial(time_kernel, rows // 16), out_shape=jax....  7.91 us
  transfers between devices with their start and end apart: 10, of which 1 were waited for; matrix products, arithmetic and copies ran while one was open for 2% of the time, Pallas kernels for 6%

profile of v12, /device:TPU:1, one launch (start us, length us, event | category | flops | bytes accessed | tf_op | source)
XLA Modules:
  0.0 180.1 jit_solution(7620802522698575600)
XLA Ops:
  6.5 0.0 copy-start.2
  6.5 0.0 copy-start.3
  6.5 0.0 copy-start.1
  6.5 0.0 all-gather.3.cloned.1.call-start
  6.5 0.9 constant_dynamic-slice_fusion
  7.4 32.1 %all_gather.9.parts_ref = bf16[256,1152]{1,0:T(8,128)(2,1)S(1)} all-gather(bf16[16,1152]{1,0:T(8,128)(2,1)S(1)} %pad_maximum_fusion), channel_id=1, replica_groups=mesh['y'=4,'x'=4,'zl'=4,'zh'=4,'c'=2] {'zh','zl'}, dimensions={0}, use_global_device_ids=true | all-gather | bytes 626688 | tf_op jit(solution)/shard_map/all_gather | solution.py:223
  39.6 0.8 pack.1
  40.4 0.0 all-gather.3.cloned.1.call-update
  40.4 3.7 %collective-permute-start = (bf16[128,1152]{1,0:T(8,128)(2,1)}, bf16[128,1152]{1,0:T(8,128)(2,1)}, u32[]{:S(2)}, u32[]{:S(2)}) collective-permute-start(bf16[128,1152]{1,0:T(8,128)(2,1)} %bitcast.20), channel_id=1, source_target_pairs={{0,2},{2,4},{4,6},{6,0},{1,3},{3,5},{5,7},{7,1},{8,10},{10,12},{12... | collective-permute-start | bytes 884744 | tf_op jit(solution)/shard_map/ppermute | solution.py:202
  44.1 5.5 %collective-permute-start.2 = (bf16[128,1152]{1,0:T(8,128)(2,1)}, bf16[128,1152]{1,0:T(8,128)(2,1)}, u32[]{:S(2)}, u32[]{:S(2)}) collective-permute-start(bf16[128,1152]{1,0:T(8,128)(2,1)} %bitcast.21), channel_id=1, source_target_pairs={{0,6},{2,0},{4,2},{6,4},{1,7},{3,1},{5,3},{7,5},{8,14},{10,8},{12,... | collective-permute-start | bytes 884744 | tf_op jit(solution)/shard_map/ppermute | solution.py:202
  49.6 14.1 %collective-permute-start.8 = (bf16[128,1152]{1,0:T(8,128)(2,1)}, bf16[128,1152]{1,0:T(8,128)(2,1)}, u32[]{:S(2)}, u32[]{:S(2)}) collective-permute-start(bf16[128,1152]{1,0:T(8,128)(2,1)} %bitcast.22), channel_id=1, source_target_pairs={{0,1},{1,0},{2,3},{3,2},{4,5},{5,4},{6,7},{7,6},{8,9},{9,8},{10,11... | collective-permute-start | bytes 884744 | tf_op jit(solution)/shard_map/ppermute | solution.py:205
  63.7 9.5 %collective-permute-done.refs_2_ = bf16[128,1152]{1,0:T(8,128)(2,1)} collective-permute-done((bf16[128,1152]{1,0:T(8,128)(2,1)}, bf16[128,1152]{1,0:T(8,128)(2,1)}, u32[]{:S(2)}, u32[]{:S(2)}) %collective-permute-start) | collective-permute-done | bytes 294944 | tf_op jit(solution)/shard_map/ppermute | solution.py:202
  73.2 1.6 slice.8
  74.8 3.8 %collective-permute-start.4 = (bf16[64,1152]{1,0:T(8,128)(2,1)}, bf16[64,1152]{1,0:T(8,128)(2,1)}, u32[]{:S(2)}, u32[]{:S(2)}) collective-permute-start(bf16[64,1152]{1,0:T(8,128)(2,1)} %slice.8), channel_id=1, source_target_pairs={{0,2},{2,4},{4,6},{6,0},{1,3},{3,5},{5,7},{7,1},{8,10},{10,12},{12... | collective-permute-start | bytes 442376 | tf_op jit(solution)/shard_map/ppermute | solution.py:202
  78.6 0.0 collective-permute-done.2.refs_3_
  78.6 1.6 slice.9
  80.2 5.4 %collective-permute-start.5 = (bf16[64,1152]{1,0:T(8,128)(2,1)}, bf16[64,1152]{1,0:T(8,128)(2,1)}, u32[]{:S(2)}, u32[]{:S(2)}) collective-permute-start(bf16[64,1152]{1,0:T(8,128)(2,1)} %slice.9), channel_id=1, source_target_pairs={{0,6},{2,0},{4,2},{6,4},{1,7},{3,1},{5,3},{7,5},{8,14},{10,8},{12,... | collective-permute-start | bytes 442376 | tf_op jit(solution)/shard_map/ppermute | solution.py:202
  85.5 4.9 %collective-permute-start.1 = (bf16[128,1152]{1,0:T(8,128)(2,1)}, bf16[128,1152]{1,0:T(8,128)(2,1)S(1)}, u32[]{:S(2)}, u32[]{:S(2)}) collective-permute-start(bf16[128,1152]{1,0:T(8,128)(2,1)} %collective-permute-done.refs_2_), channel_id=1, source_target_pairs={{0,1},{1,0},{2,3},{3,2},{4,5},{5,4},{6,7},{7,6},{8,9},{9,8},{10,11... | collective-permute-start | bytes 884744 | tf_op jit(solution)/shard_map/ppermute | solution.py:205
  90.5 1.9 %collective-permute-start.3 = (bf16[128,1152]{1,0:T(8,128)(2,1)}, bf16[128,1152]{1,0:T(8,128)(2,1)S(1)}, u32[]{:S(2)}, u32[]{:S(2)}) collective-permute-start(bf16[128,1152]{1,0:T(8,128)(2,1)} %collective-permute-done.2.refs_3_), channel_id=1, source_target_pairs={{0,1},{1,0},{2,3},{3,2},{4,5},{5,4},{6,7},{7,6},{8,9},{9,8},{10,11... | collective-permute-start | bytes 884744 | tf_op jit(solution)/shard_map/ppermute | solution.py:205
  92.4 0.0 copy-done.3
  92.5 0.0 copy-done.1
  92.5 0.1 spread.1
  92.6 0.1 stack.35.place_ref
  92.7 0.0 collective-permute-done.4.one_ref
  92.7 2.4 %collective-permute-start.6 = (bf16[64,1152]{1,0:T(8,128)(2,1)}, bf16[64,1152]{1,0:T(8,128)(2,1)S(1)}, u32[]{:S(2)}, u32[]{:S(2)}) collective-permute-start(bf16[64,1152]{1,0:T(8,128)(2,1)} %collective-permute-done.4.one_ref), channel_id=1, source_target_pairs={{0,1},{1,0},{2,3},{3,2},{4,5},{5,4},{6,7},{7,6},{8,9},{9,8},{10,11... | collective-permute-start | bytes 442376 | tf_op jit(solution)/shard_map/ppermute | solution.py:205
  95.1 0.0 collective-permute-done.5.two_ref
  95.1 1.9 %collective-permute-start.7 = (bf16[64,1152]{1,0:T(8,128)(2,1)}, bf16[64,1152]{1,0:T(8,128)(2,1)S(1)}, u32[]{:S(2)}, u32[]{:S(2)}) collective-permute-start(bf16[64,1152]{1,0:T(8,128)(2,1)} %collective-permute-done.5.two_ref), channel_id=1, source_target_pairs={{0,1},{1,0},{2,3},{3,2},{4,5},{5,4},{6,7},{7,6},{8,9},{9,8},{10,11... | collective-permute-start | bytes 442376 | tf_op jit(solution)/shard_map/ppermute | solution.py:205
  97.0 0.0 collective-permute-done.8.refs_1_
  97.1 0.0 copy-done.2
  97.1 2.7 %early_triples.1 = (bf16[512,512]{1,0:T(8,128)(2,1)S(1)}, bf16[160,512]{1,0:T(8,128)(2,1)S(1)}) custom-call(bf16[128,1152]{1,0:T(8,128)(2,1)S(1)} %bitcast.23, bf16[128,1152]{1,0:T(8,128)(2,1)} %collective-permute-done.8.refs_1_, bf16[128,1152]{1,0:T(8,128)(2,1)} %collective-permute-done.refs_2_, bf16[128,1152]{1,0:T(8,128)(2,1)} %collective-permute-done.2.refs_3_, ...), custom_call_target="tpu_custom_call" | custom-call | flops 2000000000 | bytes 5000000 | tf_op jit(solution)/shard_map/early_triples/pallas_call | solution.py:248
  99.8 0.0 collective-permute-done.6.three_ref
  99.8 0.0 collective-permute-done.7.four_ref
  99.8 0.0 collective-permute-done.1.below_ref
  99.8 0.0 collective-permute-done.3.above_ref
  99.9 7.2 %frame_attention.1 = bf16[8,144,128]{2,1,0:T(8,128)(2,1)S(1)} custom-call(s32[8]{0:T(128)S(1)} %stack.35.place_ref, bf16[128,1152]{1,0:T(8,128)(2,1)S(1)} %collective-permute-done.1.below_ref, bf16[128,1152]{1,0:T(8,128)(2,1)S(1)} %collective-permute-done.3.above_ref, bf16[64,1152]{1,0:T(8,128)(2,1)} %collective-permute-done.4.one_ref, ...), custom_call_target="tpu_custom_call" | custom-call | tf_op jit(solution)/shard_map/frame_attention/pallas_call | solution.py:262
  107.0 24.9 %all_to_all.25.mixed_ref = bf16[8,144,128]{2,1,0:T(8,128)(2,1)S(1)} all-to-all(bf16[8,144,128]{2,1,0:T(8,128)(2,1)S(1)} %frame_attention.1), channel_id=1, replica_groups=mesh['y'=4,'x'=4,'zl'=4,'zh'=4,'c'=2] {'zh','c'}, dimensions={0} | all-to-all | bytes 589824 | tf_op jit(solution)/shard_map/all_to_all | solution.py:275
  132.0 0.0 all-gather.3.cloned.1.call-done
  132.0 0.0 copy-start
  132.0 2.5 %middle.1 = bf16[128,1152]{1,0:T(8,128)(2,1)S(1)} custom-call(bf16[8,144,128]{2,1,0:T(8,128)(2,1)S(1)} %all_to_all.25.mixed_ref, bf16[16,2,192,1152]{3,2,1,0:T(8,128)(2,1)} %bitcast.25, bf16[128,1152]{1,0:T(8,128)(2,1)S(1)} %bitcast.24, f32[2,3,1152]{2,1,0:T(4,128)S(1)} %copy.7.refs_4_.modulation_ref), custom_call_target="tpu_custom_call" | custom-call | tf_op jit(solution)/shard_map/middle/pallas_call | solution.py:276
  134.5 15.7 %all_to_all.26 = bf16[16,8,1152]{2,1,0:T(8,128)(2,1)S(1)} all-to-all(bf16[16,8,1152]{2,1,0:T(8,128)(2,1)S(1)} %bitcast.18), channel_id=1, replica_groups=mesh['y'=4,'x'=4,'zl'=4,'zh'=4,'c'=2] {'x','zl'}, dimensions={0} | all-to-all | bytes 589824 | tf_op jit(solution)/shard_map/all_to_all | solution.py:286
  150.2 0.0 copy-done
  150.2 7.9 %time_block.1 = bf16[128,1152]{1,0:T(8,128)(2,1)S(1)} custom-call(bf16[128,1152]{1,0:T(8,128)(2,1)S(1)} %bitcast.16, bf16[4,8,192,1152]{3,2,1,0:T(8,128)(2,1)} %bitcast.26, bf16[1152,1152]{1,0:T(8,128)(2,1)S(1)} %copy-done, f32[2,3,1152]{2,1,0:T(4,128)S(1)} %copy.7.refs_4_.modulation_ref), custom_call_target="tpu_custom_call" | custom-call | tf_op jit(solution)/shard_map/time_block/pallas_call | solution.py:288
  158.1 14.4 %all_to_all.27 = bf16[16,8,1152]{2,1,0:T(8,128)(2,1)S(1)} all-to-all(bf16[16,8,1152]{2,1,0:T(8,128)(2,1)S(1)} %bitcast.17), channel_id=1, replica_groups=mesh['y'=4,'x'=4,'zl'=4,'zh'=4,'c'=2] {'x','zl'}, dimensions={0} | all-to-all | bytes 589824 | tf_op jit(solution)/shard_map/all_to_all | solution.py:302
  172.5 0.7 copy.12
  (2 shorter events, 0.0 us)
Async XLA Ops:
  6.5 90.5 %copy-start.2 = (bf16[1,128,1152]{2,1,0:T(8,128)(2,1)S(1)}, bf16[1,128,1152]{2,1,0:T(8,128)(2,1)}, u32[]{:S(2)}) copy-start(bf16[1,128,1152]{2,1,0:T(8,128)(2,1)} %param.6) | copy-start | bytes 884740
  6.5 85.9 %copy-start.3 = (f32[2,3,1152]{2,0,1:T(2,128)S(1)}, f32[2,3,1152]{2,0,1:T(2,128)}, u32[]{:S(2)}) copy-start(f32[2,3,1152]{2,0,1:T(2,128)} %param.11) | copy-start | bytes 82948
  6.5 85.9 %copy-start.1 = (bf16[1152,432]{0,1:T(8,128)(2,1)S(1)}, bf16[1152,432]{0,1:T(8,128)(2,1)}, u32[]{:S(2)}) copy-start(bf16[1152,432]{0,1:T(8,128)(2,1)} %param.7) | copy-start | bytes 2985988
  6.5 125.4 %all-gather.3.cloned.1.call-start = ((), (), s32[]{:S(2)}) async-start(), calls=%async_computation.3 | async-start | bytes 14598144 | tf_op jit(solution)/shard_map/all_gather | solution.py:232
  40.4 32.8 %collective-permute-start = (bf16[128,1152]{1,0:T(8,128)(2,1)}, bf16[128,1152]{1,0:T(8,128)(2,1)}, u32[]{:S(2)}, u32[]{:S(2)}) collective-permute-start(bf16[128,1152]{1,0:T(8,128)(2,1)} %bitcast.20), channel_id=1, source_target_pairs={{0,2},{2,4},{4,6},{6,0},{1,3},{3,5},{5,7},{7,1},{8,10},{10,12},{12... | collective-permute-start | bytes 884744 | tf_op jit(solution)/shard_map/ppermute | solution.py:202
  44.1 34.5 %collective-permute-start.2 = (bf16[128,1152]{1,0:T(8,128)(2,1)}, bf16[128,1152]{1,0:T(8,128)(2,1)}, u32[]{:S(2)}, u32[]{:S(2)}) collective-permute-start(bf16[128,1152]{1,0:T(8,128)(2,1)} %bitcast.21), channel_id=1, source_target_pairs={{0,6},{2,0},{4,2},{6,4},{1,7},{3,1},{5,3},{7,5},{8,14},{10,8},{12,... | collective-permute-start | bytes 884744 | tf_op jit(solution)/shard_map/ppermute | solution.py:202
  49.6 47.4 %collective-permute-start.8 = (bf16[128,1152]{1,0:T(8,128)(2,1)}, bf16[128,1152]{1,0:T(8,128)(2,1)}, u32[]{:S(2)}, u32[]{:S(2)}) collective-permute-start(bf16[128,1152]{1,0:T(8,128)(2,1)} %bitcast.22), channel_id=1, source_target_pairs={{0,1},{1,0},{2,3},{3,2},{4,5},{5,4},{6,7},{7,6},{8,9},{9,8},{10,11... | collective-permute-start | bytes 884744 | tf_op jit(solution)/shard_map/ppermute | solution.py:205
  74.8 17.9 %collective-permute-start.4 = (bf16[64,1152]{1,0:T(8,128)(2,1)}, bf16[64,1152]{1,0:T(8,128)(2,1)}, u32[]{:S(2)}, u32[]{:S(2)}) collective-permute-start(bf16[64,1152]{1,0:T(8,128)(2,1)} %slice.8), channel_id=1, source_target_pairs={{0,2},{2,4},{4,6},{6,0},{1,3},{3,5},{5,7},{7,1},{8,10},{10,12},{12... | collective-permute-start | bytes 442376 | tf_op jit(solution)/shard_map/ppermute | solution.py:202
  80.2 14.9 %collective-permute-start.5 = (bf16[64,1152]{1,0:T(8,128)(2,1)}, bf16[64,1152]{1,0:T(8,128)(2,1)}, u32[]{:S(2)}, u32[]{:S(2)}) collective-permute-start(bf16[64,1152]{1,0:T(8,128)(2,1)} %slice.9), channel_id=1, source_target_pairs={{0,6},{2,0},{4,2},{6,4},{1,7},{3,1},{5,3},{7,5},{8,14},{10,8},{12,... | collective-permute-start | bytes 442376 | tf_op jit(solution)/shard_map/ppermute | solution.py:202
  85.5 14.3 %collective-permute-start.1 = (bf16[128,1152]{1,0:T(8,128)(2,1)}, bf16[128,1152]{1,0:T(8,128)(2,1)S(1)}, u32[]{:S(2)}, u32[]{:S(2)}) collective-permute-start(bf16[128,1152]{1,0:T(8,128)(2,1)} %collective-permute-done.refs_2_), channel_id=1, source_target_pairs={{0,1},{1,0},{2,3},{3,2},{4,5},{5,4},{6,7},{7,6},{8,9},{9,8},{10,11... | collective-permute-start | bytes 884744 | tf_op jit(solution)/shard_map/ppermute | solution.py:205
  90.5 9.4 %collective-permute-start.3 = (bf16[128,1152]{1,0:T(8,128)(2,1)}, bf16[128,1152]{1,0:T(8,128)(2,1)S(1)}, u32[]{:S(2)}, u32[]{:S(2)}) collective-permute-start(bf16[128,1152]{1,0:T(8,128)(2,1)} %collective-permute-done.2.refs_3_), channel_id=1, source_target_pairs={{0,1},{1,0},{2,3},{3,2},{4,5},{5,4},{6,7},{7,6},{8,9},{9,8},{10,11... | collective-permute-start | bytes 884744 | tf_op jit(solution)/shard_map/ppermute | solution.py:205
  92.7 7.1 %collective-permute-start.6 = (bf16[64,1152]{1,0:T(8,128)(2,1)}, bf16[64,1152]{1,0:T(8,128)(2,1)S(1)}, u32[]{:S(2)}, u32[]{:S(2)}) collective-permute-start(bf16[64,1152]{1,0:T(8,128)(2,1)} %collective-permute-done.4.one_ref), channel_id=1, source_target_pairs={{0,1},{1,0},{2,3},{3,2},{4,5},{5,4},{6,7},{7,6},{8,9},{9,8},{10,11... | collective-permute-start | bytes 442376 | tf_op jit(solution)/shard_map/ppermute | solution.py:205
  95.1 4.7 %collective-permute-start.7 = (bf16[64,1152]{1,0:T(8,128)(2,1)}, bf16[64,1152]{1,0:T(8,128)(2,1)S(1)}, u32[]{:S(2)}, u32[]{:S(2)}) collective-permute-start(bf16[64,1152]{1,0:T(8,128)(2,1)} %collective-permute-done.5.two_ref), channel_id=1, source_target_pairs={{0,1},{1,0},{2,3},{3,2},{4,5},{5,4},{6,7},{7,6},{8,9},{9,8},{10,11... | collective-permute-start | bytes 442376 | tf_op jit(solution)/shard_map/ppermute | solution.py:205
  132.0 18.3 %copy-start = (bf16[1152,1152]{1,0:T(8,128)(2,1)S(1)}, bf16[1152,1152]{1,0:T(8,128)(2,1)}, u32[]{:S(2)}) copy-start(bf16[1152,1152]{1,0:T(8,128)(2,1)} %out_table_ref.1) | copy-start | bytes 7962628
Sparse Core Ops, SparseCore 0:
  40.5 89.7 all-gather.2

commit v13 on v12

--- a/solution.py
+++ b/solution.py
@@ -40,6 +40,12 @@
     index = lax.broadcasted_iota(jnp.int32, values.shape, 0)
     ones = (index == HD) | (index == HP + HD)
     return qk, jnp.where(ones, 1.0, values).astype(jnp.bfloat16)
+
+
+def turn_kernel(below_ref, above_ref, top_ref, bottom_ref):
+    half = top_ref.shape[0]
+    top_ref[...] = below_ref[:half]
+    bottom_ref[...] = above_ref[half:]
 
 
 def spread_kernel(table_ref, wqk_ref, wvt_ref):
@@ -206,7 +212,15 @@
 
     before, after = along(tokens, "zh", 1), along(tokens, "zh", 3)
     beside = swapped(tokens)
-    far_top, far_bottom = along(before[:half], "zh", 1), along(after[half:], "zh", 3)
+    top, bottom = pl.pallas_call(
+        turn_kernel,
+        out_shape=(jax.ShapeDtypeStruct((half, width), tokens.dtype),) * 2,
+        in_specs=[whole(), whole()],
+        out_specs=(whole(),) * 2,
+        compiler_params=params(16),
+        name="turn",
+    )(before, after)
+    far_top, far_bottom = along(top, "zh", 1), along(bottom, "zh", 3)
     early = [tokens, beside, before, after]
     late = [swapped(before), swapped(after), far_top, far_bottom, swapped(far_top), swapped(far_bottom)]
     spots = [zh, (zh + 3) % 4, (zh + 1) % 4, (zh + 2) % 4]

time: 181 us -> 184 us (1.017)
  waiting for transfers between devices: 9.5 us -> 11.8 us
  local copies, waits for them, and re-layouts: 4.89 us -> 2.73 us
    all_to_all x1, blocking collectives: 15.7 us -> 20.2 us  [shards(): middle = lax.all_to_all(middle, ('x', 'zl'), 0, 0, tiled=True)]
    slice x2 -> x0, local copies, waits for them, and re-layouts: 3.16 us -> none  [the longest x1 1.59 us: shards(): before[:half]]
    all_to_all x1, blocking collectives: 24.9 us -> 21.8 us  [shards(): mixed = lax.all_to_all(mixed, ('zh', 'c'), 0, 0, tiled=True)]
  transfers between devices with their start and end apart: 10 -> 10, of which waited for: 1 -> 3; matrix products, arithmetic and copies ran while one was open for 2% -> 0% of each run, Pallas kernels for 6% -> 6%
where the time goes in v13:
time: 184 us; the launch traced here: 182 us
  blocking collectives  88 us (48%)
  starting transfers between devices  43.4 us (24%)
  Pallas kernels  22.9 us (12%)
  between operations  13.6 us (7%)
  waiting for transfers between devices  11.8 us (6%)
  local copies, waits for them, and re-layouts  2.73 us (1%)
    all_gather x1, blocking collectives, shards(): parts = lax.all_gather(part, ('zh', 'zl'), axis=0, tiled=True)  32.1 us
    ppermute x5, starting transfers between devices, swapped(): return lax.ppermute(array, 'c', SWAP)  25.1 us
    all_to_all x1, blocking collectives, shards(): mixed = lax.all_to_all(mixed, ('zh', 'c'), 0, 0, tiled=True)  21.8 us
    all_to_all x1, blocking collectives, shards(): middle = lax.all_to_all(middle, ('x', 'zl'), 0, 0, tiled=True)  20.2 us
    ppermute x4, starting transfers between devices, along(): return lax.ppermute(array, axis, rotation(4, by))  18.4 us
    all_to_all x1, blocking collectives, shards(): out = lax.all_to_all(out, ('x', 'zl'), 0, 0, tiled=True)  13.9 us
    ppermute x4, waiting for transfers between devices, along(): return lax.ppermute(array, axis, rotation(4, by))  10.9 us
    pallas_call x1, Pallas kernels, shards(): pl.pallas_call(functools.partial(time_kernel, rows // 16), out_shape=jax....  7.91 us
  transfers between devices with their start and end apart: 10, of which 3 were waited for; matrix products, arithmetic and copies ran while one was open for 0% of the time, Pallas kernels for 6%

profile of v13, /device:TPU:1, one launch (start us, length us, event | category | flops | bytes accessed | tf_op | source)
XLA Modules:
  0.0 182.5 jit_solution(12513510832114887765)
XLA Ops:
  6.5 0.0 copy-start.4
  6.5 0.0 copy-start.1
  6.5 0.0 all-gather.3.cloned.1.call-start
  6.5 0.9 constant_dynamic-slice_fusion
  7.4 32.1 %all_gather.9.parts_ref = bf16[256,1152]{1,0:T(8,128)(2,1)S(1)} all-gather(bf16[16,1152]{1,0:T(8,128)(2,1)S(1)} %pad_maximum_fusion), channel_id=1, replica_groups=mesh['y'=4,'x'=4,'zl'=4,'zh'=4,'c'=2] {'zh','zl'}, dimensions={0}, use_global_device_ids=true | all-gather | bytes 626688 | tf_op jit(solution)/shard_map/all_gather | solution.py:237
  39.6 0.8 pack.1
  40.4 0.0 all-gather.3.cloned.1.call-update
  40.4 3.7 %collective-permute-start = (bf16[128,1152]{1,0:T(8,128)(2,1)}, bf16[128,1152]{1,0:T(8,128)(2,1)S(1)}, u32[]{:S(2)}, u32[]{:S(2)}) collective-permute-start(bf16[128,1152]{1,0:T(8,128)(2,1)} %bitcast.20), channel_id=1, source_target_pairs={{0,2},{2,4},{4,6},{6,0},{1,3},{3,5},{5,7},{7,1},{8,10},{10,12},{12... | collective-permute-start | bytes 884744 | tf_op jit(solution)/shard_map/ppermute | solution.py:208
  44.0 5.5 %collective-permute-start.2 = (bf16[128,1152]{1,0:T(8,128)(2,1)}, bf16[128,1152]{1,0:T(8,128)(2,1)}, u32[]{:S(2)}, u32[]{:S(2)}) collective-permute-start(bf16[128,1152]{1,0:T(8,128)(2,1)} %bitcast.21), channel_id=1, source_target_pairs={{0,6},{2,0},{4,2},{6,4},{1,7},{3,1},{5,3},{7,5},{8,14},{10,8},{12,... | collective-permute-start | bytes 884744 | tf_op jit(solution)/shard_map/ppermute | solution.py:208
  49.6 14.1 %collective-permute-start.8 = (bf16[128,1152]{1,0:T(8,128)(2,1)}, bf16[128,1152]{1,0:T(8,128)(2,1)}, u32[]{:S(2)}, u32[]{:S(2)}) collective-permute-start(bf16[128,1152]{1,0:T(8,128)(2,1)} %bitcast.22), channel_id=1, source_target_pairs={{0,1},{1,0},{2,3},{3,2},{4,5},{5,4},{6,7},{7,6},{8,9},{9,8},{10,11... | collective-permute-start | bytes 884744 | tf_op jit(solution)/shard_map/ppermute | solution.py:211
  63.7 9.3 %collective-permute-done.below_ref.refs_2_ = bf16[128,1152]{1,0:T(8,128)(2,1)S(1)} collective-permute-done((bf16[128,1152]{1,0:T(8,128)(2,1)}, bf16[128,1152]{1,0:T(8,128)(2,1)S(1)}, u32[]{:S(2)}, u32[]{:S(2)}) %collective-permute-start) | collective-permute-done | bytes 294944 | tf_op jit(solution)/shard_map/ppermute | solution.py:208
  73.0 1.7 collective-permute-done.2.above_ref.refs_3_
  74.6 1.7 turn.1
  76.3 6.2 %collective-permute-start.4 = (bf16[64,1152]{1,0:T(8,128)(2,1)}, bf16[64,1152]{1,0:T(8,128)(2,1)}, u32[]{:S(2)}, u32[]{:S(2)}) collective-permute-start(bf16[64,1152]{1,0:T(8,128)(2,1)} %get-tuple-element.11), channel_id=1, source_target_pairs={{0,2},{2,4},{4,6},{6,0},{1,3},{3,5},{5,7},{7,1},{8,10},{10,12},{12... | collective-permute-start | bytes 442376 | tf_op jit(solution)/shard_map/ppermute | solution.py:208
  82.5 3.0 %collective-permute-start.5 = (bf16[64,1152]{1,0:T(8,128)(2,1)}, bf16[64,1152]{1,0:T(8,128)(2,1)}, u32[]{:S(2)}, u32[]{:S(2)}) collective-permute-start(bf16[64,1152]{1,0:T(8,128)(2,1)} %get-tuple-element.12), channel_id=1, source_target_pairs={{0,6},{2,0},{4,2},{6,4},{1,7},{3,1},{5,3},{7,5},{8,14},{10,8},{12,... | collective-permute-start | bytes 442376 | tf_op jit(solution)/shard_map/ppermute | solution.py:208
  85.5 3.1 %collective-permute-start.1 = (bf16[128,1152]{1,0:T(8,128)(2,1)S(1)}, bf16[128,1152]{1,0:T(8,128)(2,1)S(1)}, u32[]{:S(2)}, u32[]{:S(2)}) collective-permute-start(bf16[128,1152]{1,0:T(8,128)(2,1)S(1)} %collective-permute-done.below_ref.refs_2_), channel_id=1, source_target_pairs={{0,1},{1,0},{2,3},{3,2},{4,5},{5,4},{6,7},{7,6},{8,9},{9,8},{10,11... | collective-permute-start | bytes 884744 | tf_op jit(solution)/shard_map/ppermute | solution.py:211
  88.6 1.9 %collective-permute-start.3 = (bf16[128,1152]{1,0:T(8,128)(2,1)}, bf16[128,1152]{1,0:T(8,128)(2,1)S(1)}, u32[]{:S(2)}, u32[]{:S(2)}) collective-permute-start(bf16[128,1152]{1,0:T(8,128)(2,1)} %collective-permute-done.2.above_ref.refs_3_), channel_id=1, source_target_pairs={{0,1},{1,0},{2,3},{3,2},{4,5},{5,4},{6,7},{7,6},{8,9},{9,8},{10,11... | collective-permute-start | bytes 884744 | tf_op jit(solution)/shard_map/ppermute | solution.py:211
  90.6 0.0 copy-done.4
  90.6 0.0 copy-done.1
  90.6 0.1 spread.1
  90.8 0.1 stack.35.place_ref
  90.9 0.0 collective-permute-done.4.one_ref
  90.9 2.4 %collective-permute-start.6 = (bf16[64,1152]{1,0:T(8,128)(2,1)}, bf16[64,1152]{1,0:T(8,128)(2,1)S(1)}, u32[]{:S(2)}, u32[]{:S(2)}) collective-permute-start(bf16[64,1152]{1,0:T(8,128)(2,1)} %collective-permute-done.4.one_ref), channel_id=1, source_target_pairs={{0,1},{1,0},{2,3},{3,2},{4,5},{5,4},{6,7},{7,6},{8,9},{9,8},{10,11... | collective-permute-start | bytes 442376 | tf_op jit(solution)/shard_map/ppermute | solution.py:211
  93.3 0.0 collective-permute-done.5.two_ref
  93.3 3.5 %collective-permute-start.7 = (bf16[64,1152]{1,0:T(8,128)(2,1)}, bf16[64,1152]{1,0:T(8,128)(2,1)S(1)}, u32[]{:S(2)}, u32[]{:S(2)}) collective-permute-start(bf16[64,1152]{1,0:T(8,128)(2,1)} %collective-permute-done.5.two_ref), channel_id=1, source_target_pairs={{0,1},{1,0},{2,3},{3,2},{4,5},{5,4},{6,7},{7,6},{8,9},{9,8},{10,11... | collective-permute-start | bytes 442376 | tf_op jit(solution)/shard_map/ppermute | solution.py:211
  96.8 0.0 collective-permute-done.8.refs_1_
  96.8 0.0 copy-start.2
  96.8 1.0 copy-done.2
  97.8 2.7 %early_triples.1 = (bf16[512,512]{1,0:T(8,128)(2,1)S(1)}, bf16[160,512]{1,0:T(8,128)(2,1)S(1)}) custom-call(bf16[128,1152]{1,0:T(8,128)(2,1)S(1)} %bitcast.23, bf16[128,1152]{1,0:T(8,128)(2,1)} %collective-permute-done.8.refs_1_, bf16[128,1152]{1,0:T(8,128)(2,1)S(1)} %collective-permute-done.below_ref.refs_2_, ...), custom_call_target="tpu_custom_call" | custom-call | flops 2000000000 | bytes 5000000 | tf_op jit(solution)/shard_map/early_triples/pallas_call | solution.py:262
  100.5 0.0 copy-start.3
  100.5 0.0 collective-permute-done.6.three_ref
  100.5 0.0 collective-permute-done.7.four_ref
  100.5 0.0 collective-permute-done.1.below_ref
  100.5 0.0 collective-permute-done.3.above_ref
  100.6 7.2 %frame_attention.1 = bf16[8,144,128]{2,1,0:T(8,128)(2,1)S(1)} custom-call(s32[8]{0:T(128)S(1)} %stack.35.place_ref, bf16[128,1152]{1,0:T(8,128)(2,1)S(1)} %collective-permute-done.1.below_ref, bf16[128,1152]{1,0:T(8,128)(2,1)S(1)} %collective-permute-done.3.above_ref, bf16[64,1152]{1,0:T(8,128)(2,1)} %collective-permute-done.4.one_ref, ...), custom_call_target="tpu_custom_call" | custom-call | tf_op jit(solution)/shard_map/frame_attention/pallas_call | solution.py:276
  107.8 21.8 %all_to_all.25.mixed_ref = bf16[8,144,128]{2,1,0:T(8,128)(2,1)S(1)} all-to-all(bf16[8,144,128]{2,1,0:T(8,128)(2,1)S(1)} %frame_attention.1), channel_id=1, replica_groups=mesh['y'=4,'x'=4,'zl'=4,'zh'=4,'c'=2] {'zh','c'}, dimensions={0} | all-to-all | bytes 589824 | tf_op jit(solution)/shard_map/all_to_all | solution.py:289
  129.5 0.8 all-gather.3.cloned.1.call-done
  130.3 0.0 copy-done.3
  130.3 0.0 copy-start
  130.3 2.5 %middle.1 = bf16[128,1152]{1,0:T(8,128)(2,1)S(1)} custom-call(bf16[8,144,128]{2,1,0:T(8,128)(2,1)S(1)} %all_to_all.25.mixed_ref, bf16[16,2,192,1152]{3,2,1,0:T(8,128)(2,1)} %bitcast.25, bf16[128,1152]{1,0:T(8,128)(2,1)S(1)} %bitcast.24, f32[2,3,1152]{2,1,0:T(4,128)S(1)} %copy.7.refs_4_.modulation_ref), custom_call_target="tpu_custom_call" | custom-call | tf_op jit(solution)/shard_map/middle/pallas_call | solution.py:290
  132.9 20.2 %all_to_all.26 = bf16[16,8,1152]{2,1,0:T(8,128)(2,1)S(1)} all-to-all(bf16[16,8,1152]{2,1,0:T(8,128)(2,1)S(1)} %bitcast.18), channel_id=1, replica_groups=mesh['y'=4,'x'=4,'zl'=4,'zh'=4,'c'=2] {'x','zl'}, dimensions={0} | all-to-all | bytes 589824 | tf_op jit(solution)/shard_map/all_to_all | solution.py:300
  153.1 0.0 copy-done
  153.1 7.9 %time_block.1 = bf16[128,1152]{1,0:T(8,128)(2,1)S(1)} custom-call(bf16[128,1152]{1,0:T(8,128)(2,1)S(1)} %bitcast.16, bf16[4,8,192,1152]{3,2,1,0:T(8,128)(2,1)} %bitcast.26, bf16[1152,1152]{1,0:T(8,128)(2,1)S(1)} %copy-done, f32[2,3,1152]{2,1,0:T(4,128)S(1)} %copy.7.refs_4_.modulation_ref), custom_call_target="tpu_custom_call" | custom-call | tf_op jit(solution)/shard_map/time_block/pallas_call | solution.py:302
  161.0 13.9 %all_to_all.27 = bf16[16,8,1152]{2,1,0:T(8,128)(2,1)S(1)} all-to-all(bf16[16,8,1152]{2,1,0:T(8,128)(2,1)S(1)} %bitcast.17), channel_id=1, replica_groups=mesh['y'=4,'x'=4,'zl'=4,'zh'=4,'c'=2] {'x','zl'}, dimensions={0} | all-to-all | bytes 589824 | tf_op jit(solution)/shard_map/all_to_all | solution.py:316
  174.9 0.7 copy.12
  (2 shorter events, 0.0 us)
Async XLA Ops:
  6.5 84.1 %copy-start.4 = (f32[2,3,1152]{2,0,1:T(2,128)S(1)}, f32[2,3,1152]{2,0,1:T(2,128)}, u32[]{:S(2)}) copy-start(f32[2,3,1152]{2,0,1:T(2,128)} %param.11) | copy-start | bytes 82948
  6.5 84.1 %copy-start.1 = (bf16[1152,432]{0,1:T(8,128)(2,1)S(1)}, bf16[1152,432]{0,1:T(8,128)(2,1)}, u32[]{:S(2)}) copy-start(bf16[1152,432]{0,1:T(8,128)(2,1)} %param.7) | copy-start | bytes 2985988
  6.5 123.8 %all-gather.3.cloned.1.call-start = ((), (), s32[]{:S(2)}) async-start(), calls=%async_computation.3 | async-start | bytes 14598144 | tf_op jit(solution)/shard_map/all_gather | solution.py:246
  40.4 32.6 %collective-permute-start = (bf16[128,1152]{1,0:T(8,128)(2,1)}, bf16[128,1152]{1,0:T(8,128)(2,1)S(1)}, u32[]{:S(2)}, u32[]{:S(2)}) collective-permute-start(bf16[128,1152]{1,0:T(8,128)(2,1)} %bitcast.20), channel_id=1, source_target_pairs={{0,2},{2,4},{4,6},{6,0},{1,3},{3,5},{5,7},{7,1},{8,10},{10,12},{12... | collective-permute-start | bytes 884744 | tf_op jit(solution)/shard_map/ppermute | solution.py:208
  44.0 30.6 %collective-permute-start.2 = (bf16[128,1152]{1,0:T(8,128)(2,1)}, bf16[128,1152]{1,0:T(8,128)(2,1)}, u32[]{:S(2)}, u32[]{:S(2)}) collective-permute-start(bf16[128,1152]{1,0:T(8,128)(2,1)} %bitcast.21), channel_id=1, source_target_pairs={{0,6},{2,0},{4,2},{6,4},{1,7},{3,1},{5,3},{7,5},{8,14},{10,8},{12,... | collective-permute-start | bytes 884744 | tf_op jit(solution)/shard_map/ppermute | solution.py:208
  49.6 47.2 %collective-permute-start.8 = (bf16[128,1152]{1,0:T(8,128)(2,1)}, bf16[128,1152]{1,0:T(8,128)(2,1)}, u32[]{:S(2)}, u32[]{:S(2)}) collective-permute-start(bf16[128,1152]{1,0:T(8,128)(2,1)} %bitcast.22), channel_id=1, source_target_pairs={{0,1},{1,0},{2,3},{3,2},{4,5},{5,4},{6,7},{7,6},{8,9},{9,8},{10,11... | collective-permute-start | bytes 884744 | tf_op jit(solution)/shard_map/ppermute | solution.py:211
  76.3 14.6 %collective-permute-start.4 = (bf16[64,1152]{1,0:T(8,128)(2,1)}, bf16[64,1152]{1,0:T(8,128)(2,1)}, u32[]{:S(2)}, u32[]{:S(2)}) collective-permute-start(bf16[64,1152]{1,0:T(8,128)(2,1)} %get-tuple-element.11), channel_id=1, source_target_pairs={{0,2},{2,4},{4,6},{6,0},{1,3},{3,5},{5,7},{7,1},{8,10},{10,12},{12... | collective-permute-start | bytes 442376 | tf_op jit(solution)/shard_map/ppermute | solution.py:208
  82.5 10.8 %collective-permute-start.5 = (bf16[64,1152]{1,0:T(8,128)(2,1)}, bf16[64,1152]{1,0:T(8,128)(2,1)}, u32[]{:S(2)}, u32[]{:S(2)}) collective-permute-start(bf16[64,1152]{1,0:T(8,128)(2,1)} %get-tuple-element.12), channel_id=1, source_target_pairs={{0,6},{2,0},{4,2},{6,4},{1,7},{3,1},{5,3},{7,5},{8,14},{10,8},{12,... | collective-permute-start | bytes 442376 | tf_op jit(solution)/shard_map/ppermute | solution.py:208
  85.5 15.0 %collective-permute-start.1 = (bf16[128,1152]{1,0:T(8,128)(2,1)S(1)}, bf16[128,1152]{1,0:T(8,128)(2,1)S(1)}, u32[]{:S(2)}, u32[]{:S(2)}) collective-permute-start(bf16[128,1152]{1,0:T(8,128)(2,1)S(1)} %collective-permute-done.below_ref.refs_2_), channel_id=1, source_target_pairs={{0,1},{1,0},{2,3},{3,2},{4,5},{5,4},{6,7},{7,6},{8,9},{9,8},{10,11... | collective-permute-start | bytes 884744 | tf_op jit(solution)/shard_map/ppermute | solution.py:211
  88.6 11.9 %collective-permute-start.3 = (bf16[128,1152]{1,0:T(8,128)(2,1)}, bf16[128,1152]{1,0:T(8,128)(2,1)S(1)}, u32[]{:S(2)}, u32[]{:S(2)}) collective-permute-start(bf16[128,1152]{1,0:T(8,128)(2,1)} %collective-permute-done.2.above_ref.refs_3_), channel_id=1, source_target_pairs={{0,1},{1,0},{2,3},{3,2},{4,5},{5,4},{6,7},{7,6},{8,9},{9,8},{10,11... | collective-permute-start | bytes 884744 | tf_op jit(solution)/shard_map/ppermute | solution.py:211
  90.9 9.7 %collective-permute-start.6 = (bf16[64,1152]{1,0:T(8,128)(2,1)}, bf16[64,1152]{1,0:T(8,128)(2,1)S(1)}, u32[]{:S(2)}, u32[]{:S(2)}) collective-permute-start(bf16[64,1152]{1,0:T(8,128)(2,1)} %collective-permute-done.4.one_ref), channel_id=1, source_target_pairs={{0,1},{1,0},{2,3},{3,2},{4,5},{5,4},{6,7},{7,6},{8,9},{9,8},{10,11... | collective-permute-start | bytes 442376 | tf_op jit(solution)/shard_map/ppermute | solution.py:211
  93.3 7.2 %collective-permute-start.7 = (bf16[64,1152]{1,0:T(8,128)(2,1)}, bf16[64,1152]{1,0:T(8,128)(2,1)S(1)}, u32[]{:S(2)}, u32[]{:S(2)}) collective-permute-start(bf16[64,1152]{1,0:T(8,128)(2,1)} %collective-permute-done.5.two_ref), channel_id=1, source_target_pairs={{0,1},{1,0},{2,3},{3,2},{4,5},{5,4},{6,7},{7,6},{8,9},{9,8},{10,11... | collective-permute-start | bytes 442376 | tf_op jit(solution)/shard_map/ppermute | solution.py:211
  96.8 1.0 copy-start.2
  100.5 29.8 %copy-start.3 = (bf16[1,128,1152]{2,1,0:T(8,128)(2,1)S(1)}, bf16[1,128,1152]{2,1,0:T(8,128)(2,1)}, u32[]{:S(2)}) copy-start(bf16[1,128,1152]{2,1,0:T(8,128)(2,1)} %param.6) | copy-start | bytes 884740
  130.3 22.8 %copy-start = (bf16[1152,1152]{1,0:T(8,128)(2,1)S(1)}, bf16[1152,1152]{1,0:T(8,128)(2,1)}, u32[]{:S(2)}) copy-start(bf16[1152,1152]{1,0:T(8,128)(2,1)} %out_table_ref.1) | copy-start | bytes 7962628
Sparse Core Ops, SparseCore 0:
  40.5 89.7 all-gather.2
